TPU v7x, 32 devices: a whole 2x2x4 slice. The times are simulated.
32 devices in a mesh: mol: 8 (over z, y), row: 4 (over x, core).
Axes of the slice: x: 2, y: 2, z: 4, core: 2. Of those that a mesh axis runs over, the one named last changes fastest.
Arguments:
- node_feats: bfloat16 [1024, 29, 128], P(('mol', 'row')), may hold values from -3 to 3
- edge_feats: bfloat16 [5, 65536], P(None, 'mol'), may hold values from -6 to 6
- edge_ends: int32 [2, 1024, 64], P(None, 'mol'), may hold values from 0 to 29, as said below
- atom_counts: int32 [1024], P(('mol', 'row')), may hold values from 8 to 29, as said below
- dataset_flags: int32 [1024], P(('mol', 'row')), may hold values 0 or 1
- targets: float32 [1024, 12], P(('mol', 'row')), may hold values from 0.5 to 2.5
- present: int32 [1024, 12], P(('mol', 'row')), may hold values 0 or 1
- edge_in: float32 [5, 128], replicated, may hold values from -2.5 to 2.5
- edge_out: float32 [128, 16384], P(None, 'row'), may hold values from -0.046875 to 0.046875
- edge_bias: float32 [16384], P('row'), may hold values from -0.75 to 0.75
- gru_weights: float32 [2, 128, 384], replicated, may hold values from -0.5 to 0.5
- lstm_weights: float32 [384, 512], replicated, may hold values from -0.3125 to 0.3125
- head_first: float32 [256, 128], replicated, may hold values from -0.375 to 0.375
- head_second: float32 [128, 12], replicated, may hold values from -0.5 to 0.5
- biases: float32 [1572], replicated, may hold values from -4 to 4
- moment_edge_in: float32 [5, 128], replicated, may hold values from -0.00010681152 to 0.00010681152
- moment_edge_out: float32 [128, 16384], P(None, 'row'), may hold values from -0.00010681152 to 0.00010681152
- moment_edge_bias: float32 [16384], P('row'), may hold values from -0.00010681152 to 0.00010681152
- moment_gru: float32 [2, 128, 384], replicated, may hold values from -0.00010681152 to 0.00010681152
- moment_lstm: float32 [384, 512], replicated, may hold values from -0.00010681152 to 0.00010681152
- moment_head_first: float32 [256, 128], replicated, may hold values from -0.00010681152 to 0.00010681152
- moment_head_second: float32 [128, 12], replicated, may hold values from -0.00010681152 to 0.00010681152
- moment_biases: float32 [1572], replicated, may hold values from -0.00390625 to 0.00390625
- second_edge_in: float32 [5, 128], replicated, may hold values from 4.09004e-12 to 1.636016e-11
- second_edge_out: float32 [128, 16384], P(None, 'row'), may hold values from 4.09004e-12 to 1.636016e-11
- second_edge_bias: float32 [16384], P('row'), may hold values from 4.09004e-12 to 1.636016e-11
- second_gru: float32 [2, 128, 384], replicated, may hold values from 4.09004e-12 to 1.636016e-11
- second_lstm: float32 [384, 512], replicated, may hold values from 4.09004e-12 to 1.636016e-11
- second_head_first: float32 [256, 128], replicated, may hold values from 4.09004e-12 to 1.636016e-11
- second_head_second: float32 [128, 12], replicated, may hold values from 4.09004e-12 to 1.636016e-11
- second_biases: float32 [1572], replicated, may hold values from 6.361323e-09 to 2.5445292e-08
Outputs:
- new_edge_in: float32 [5, 128], replicated
- new_edge_out: float32 [128, 16384], P(None, 'row')
- new_edge_bias: float32 [16384], P('row')
- new_gru: float32 [2, 128, 384], replicated
- new_lstm: float32 [384, 512], replicated
- new_head_first: float32 [256, 128], replicated
- new_head_second: float32 [128, 12], replicated
- new_biases: float32 [1572], replicated
- new_moment_edge_in: float32 [5, 128], replicated
- new_moment_edge_out: float32 [128, 16384], P(None, 'row')
- new_moment_edge_bias: float32 [16384], P('row')
- new_moment_gru: float32 [2, 128, 384], replicated
- new_moment_lstm: float32 [384, 512], replicated
- new_moment_head_first: float32 [256, 128], replicated
- new_moment_head_second: float32 [128, 12], replicated
- new_moment_biases: float32 [1572], replicated
- new_second_edge_in: float32 [5, 128], replicated
- new_second_edge_out: float32 [128, 16384], P(None, 'row')
- new_second_edge_bias: float32 [16384], P('row')
- new_second_gru: float32 [2, 128, 384], replicated
- new_second_lstm: float32 [384, 512], replicated
- new_second_head_first: float32 [256, 128], replicated
- new_second_head_second: float32 [128, 12], replicated
- new_second_biases: float32 [1572], replicated
- loss_sum: float32 [], replicated
- target_count: float32 [], replicated
- grad_norm: float32 [], replicated
Inputs may be any that keep to these rules, and one draw needn't show every extreme that they name: `atom_counts`: some molecule has 29 atoms in every draw. `edge_ends`: slot k of a molecule of c atoms is live exactly when k < 2 (c - 1); empty slots hold 29 in both rows; the live slots hold both directions of the bonds of a tree over the molecule's atoms, each atom j >= 1 bonded to one atom below it.
All inputs are finite; a program needn't handle non-finite values. No bound on the sum of `dataset_flags` or of `present` on one device may be relied on, other than what follows from the above.
Results may differ from a plain program's by a relative error of at most 0.0025.
Values may be sent and summed in bfloat16 or wider, within the bound.
No kernel may reach another device: no remote copies, remote signals or barrier semaphores. Data moves between devices by JAX's collectives and lax.ppermute only.
A program may use at most 256 MiB of HBM per device.

v0:
```python
import math

import jax
import jax.numpy as jnp
from jax import lax
from jax.sharding import PartitionSpec as P

H = 128
EH = 128
EIN = 5
NT = 12
STEPS = 6
ATOMS = 29
EM = 64
LAYERS = 2
STEP_COUNT = 10


highest = lax.Precision.HIGHEST
beta_one = 0.9
beta_two = 0.999
rate = 0.05
epsilon = 1e-08
decay = 0.01
clip_norm = 0.1


def split_biases(biases):
    start = 0
    pieces = []
    for width in (EH, 6 * H, 4 * H, H, NT, 2 * NT):
        pieces.append(biases[start : start + width])
        start = start + width
    return pieces


def gru_cell(message, state_low, state, weights_low, gru_bias):
    from_input = (
        jnp.einsum("mvi,ig->mvg", message, weights_low[0], precision=highest) + gru_bias[: 3 * H]
    )
    from_state = (
        jnp.einsum("mvi,ig->mvg", state_low, weights_low[1], precision=highest) + gru_bias[3 * H :]
    )
    reset = jax.nn.sigmoid(from_input[..., :H] + from_state[..., :H])
    update = jax.nn.sigmoid(from_input[..., H : 2 * H] + from_state[..., H : 2 * H])
    fresh = jnp.tanh(from_input[..., 2 * H :] + reset * from_state[..., 2 * H :])
    return (1.0 - update) * fresh + update * state


def readout(state, counts, flags, targets, present, lstm_weights, head_first, head_second, biases):
    pieces = split_biases(biases)
    live = jnp.arange(ATOMS)[None, :] < counts[:, None]
    live_f = live.astype(jnp.float32)
    molecules = state.shape[0]
    query = jnp.zeros((molecules, 2 * H), jnp.float32)
    hidden = jnp.zeros((molecules, H), jnp.float32)
    cell = jnp.zeros((molecules, H), jnp.float32)
    for repeat in range(STEPS):
        gates = (
            jnp.dot(jnp.concatenate([query, hidden], 1), lstm_weights, precision=highest)
            + pieces[2]
        )
        in_gate = jax.nn.sigmoid(gates[:, :H])
        forget = jax.nn.sigmoid(gates[:, H : 2 * H])
        cell_part = jnp.tanh(gates[:, 2 * H : 3 * H])
        out_gate = jax.nn.sigmoid(gates[:, 3 * H :])
        cell = forget * cell + in_gate * cell_part
        hidden = out_gate * jnp.tanh(cell)
        scores = jnp.einsum("mah,mh->ma", state, hidden, precision=highest)
        scores = jnp.where(live, scores, -1e30)
        weights = jnp.exp(scores - jnp.max(scores, 1, keepdims=True)) * live_f
        weights = weights / jnp.sum(weights, 1, keepdims=True)
        read = jnp.einsum("ma,mah->mh", weights, state, precision=highest)
        query = jnp.concatenate([hidden, read], 1)
    inner = jax.nn.silu(jnp.dot(query, head_first, precision=highest) + pieces[3])
    offsets = pieces[5].reshape(2, NT)
    chosen = jnp.where(flags[:, None] == 1, offsets[1][None, :], offsets[0][None, :])
    predicted = jnp.dot(inner, head_second, precision=highest) + pieces[4] + chosen
    return jnp.sum(present * (predicted - targets) ** 2)


def adamw(weight, grad, moment, second):
    moment_new = beta_one * moment + (1.0 - beta_one) * grad
    second_new = beta_two * second + (1.0 - beta_two) * grad * grad
    mean_hat = moment_new / (1.0 - beta_one**STEP_COUNT)
    square_hat = second_new / (1.0 - beta_two**STEP_COUNT)
    return (
        weight - rate * (mean_hat / (jnp.sqrt(square_hat) + epsilon) + decay * weight),
        moment_new,
        second_new,
    )


def per_device(
    node_feats,
    edge_feats,
    edge_ends,
    atom_counts,
    dataset_flags,
    targets,
    present,
    edge_in,
    edge_out,
    edge_bias,
    gru_weights,
    lstm_weights,
    head_first,
    head_second,
    biases,
    moment_edge_in,
    moment_edge_out,
    moment_edge_bias,
    moment_gru,
    moment_lstm,
    moment_head_first,
    moment_head_second,
    moment_biases,
    second_edge_in,
    second_edge_out,
    second_edge_bias,
    second_gru,
    second_lstm,
    second_head_first,
    second_head_second,
    second_biases,
):
    row_count = lax.axis_size("row")
    quarter = node_feats.shape[0]
    group_mols = quarter * row_count
    own_rows = edge_out.shape[1] // H
    block_mols = math.gcd(group_mols, 32)
    blocks = group_mols // block_mols
    pieces = split_biases(biases)
    atoms = jnp.arange(ATOMS)
    src_hot = (edge_ends[0][..., None] == atoms).astype(jnp.bfloat16)
    dst_hot = (edge_ends[1][..., None] == atoms).astype(jnp.float32)
    features = (
        edge_feats.astype(jnp.float32).reshape(EIN, blocks, block_mols * EM).transpose(1, 2, 0)
    )
    out_low = edge_out.astype(jnp.bfloat16)

    def edge_hidden(feature_block):
        before = jnp.dot(feature_block, edge_in, precision=highest) + pieces[0]
        return (before, jax.nn.silu(before).astype(jnp.bfloat16))

    def edge_forward(feature_block):
        before, hidden = edge_hidden(feature_block)
        amat = jnp.dot(hidden, out_low, preferred_element_type=jnp.float32) + edge_bias
        return amat.astype(jnp.bfloat16).reshape(block_mols, EM, own_rows, H)

    amats = lax.map(edge_forward, features).reshape(group_mols, EM, own_rows, H)
    gru_low = gru_weights.astype(jnp.bfloat16).astype(jnp.float32)
    state = node_feats.astype(jnp.float32)
    sources = []
    pullbacks = []
    for layer in range(LAYERS):
        state_low = state.astype(jnp.bfloat16)
        whole_state = lax.all_gather(state_low, "row", axis=0, tiled=True)
        source = jnp.einsum(
            "mka,mah->mkh", src_hot, whole_state, preferred_element_type=jnp.float32
        ).astype(jnp.bfloat16)
        moved = jnp.einsum("mkij,mkj->mki", amats, source, preferred_element_type=jnp.float32)
        summed = jnp.einsum("mkv,mki->mvi", dst_hot, moved, precision=highest)
        message = summed.astype(jnp.bfloat16)
        full = lax.all_gather(message, "row", axis=2, tiled=True)
        mine = lax.dynamic_slice_in_dim(full, lax.axis_index("row") * quarter, quarter, 0)
        state, pullback = jax.vjp(
            gru_cell,
            mine.astype(jnp.float32),
            state_low.astype(jnp.float32),
            state,
            gru_low,
            pieces[1],
        )
        sources.append(source)
        pullbacks.append(pullback)
    present_f = present.astype(jnp.float32)

    def scored(final_state, lstm_part, first_part, second_part, bias_part):
        return readout(
            final_state,
            atom_counts,
            dataset_flags,
            targets,
            present_f,
            lstm_part,
            first_part,
            second_part,
            bias_part,
        )

    loss_local, read_back = jax.vjp(scored, state, lstm_weights, head_first, head_second, biases)
    grad_state, grad_lstm, grad_first, grad_second, grad_bias = read_back(jnp.ones((), jnp.float32))
    grad_gru = jnp.zeros_like(gru_weights)
    grad_gbias = jnp.zeros((6 * H,), jnp.float32)
    moves = [None] * LAYERS
    for layer in reversed(range(LAYERS)):
        grad_msg, grad_low, grad_prev, grad_weights, grad_cbias = pullbacks[layer](grad_state)
        grad_gru = grad_gru + grad_weights
        grad_gbias = grad_gbias + grad_cbias
        grad_message = grad_msg.astype(jnp.bfloat16)
        full_grad = lax.all_gather(grad_message, "row", axis=0, tiled=True)
        grad_part = lax.dynamic_slice_in_dim(
            full_grad, lax.axis_index("row") * own_rows, own_rows, 2
        )
        grad_moved = jnp.einsum(
            "mkv,mvi->mki", dst_hot, grad_part.astype(jnp.float32), precision=highest
        )
        moves[layer] = grad_moved
        if layer > 0:

            def state_term(start, count, grad_moved=grad_moved):
                grad_rows = grad_moved.astype(jnp.bfloat16)
                pulled = jnp.einsum(
                    "mkij,mki->mkj", amats, grad_rows, preferred_element_type=jnp.float32
                )
                hot_rows = src_hot.astype(jnp.float32)
                return jnp.einsum("mka,mkj->maj", hot_rows, pulled, precision=highest)

            grad_state = (
                grad_prev
                + grad_low
                + lax.psum_scatter(
                    state_term(jnp.int32(0), quarter * lax.axis_size("row")).astype(jnp.bfloat16),
                    "row",
                    scatter_dimension=0,
                    tiled=True,
                ).astype(jnp.float32)
            )
    edge_count = block_mols * EM
    move_blocks = tuple((grad.reshape(blocks, edge_count, own_rows) for grad in moves))
    source_blocks = tuple((item.reshape(blocks, edge_count, H) for item in sources))

    def edge_backward(carry, inputs):
        feature_block, grad_first_layer, grad_second_layer, source_first, source_second = inputs
        before, hidden = edge_hidden(feature_block)
        grad_amat = grad_first_layer[:, :, None] * source_first[:, None, :].astype(
            jnp.float32
        ) + grad_second_layer[:, :, None] * source_second[:, None, :].astype(jnp.float32)
        grad_amat = grad_amat.astype(jnp.bfloat16).reshape(edge_count, own_rows * H)
        grad_out = carry[0] + lax.dot_general(
            hidden, grad_amat, (((0,), (0,)), ((), ())), preferred_element_type=jnp.float32
        )
        grad_ebias = carry[1] + jnp.sum(grad_amat.astype(jnp.float32), 0)
        grad_hidden = lax.dot_general(
            grad_amat, out_low, (((1,), (1,)), ((), ())), preferred_element_type=jnp.float32
        )
        sigmoid_before = jax.nn.sigmoid(before)
        grad_before = grad_hidden * sigmoid_before * (1.0 + before * (1.0 - sigmoid_before))
        grad_in = carry[2] + jnp.dot(feature_block.T, grad_before, precision=highest)
        grad_bin = carry[3] + jnp.sum(grad_before, 0)
        return ((grad_out, grad_ebias, grad_in, grad_bin), None)

    start_carry = (
        jnp.zeros((EH, own_rows * H), jnp.float32),
        jnp.zeros((own_rows * H,), jnp.float32),
        jnp.zeros((EIN, EH), jnp.float32),
        jnp.zeros((EH,), jnp.float32),
    )
    edge_sums, unused = lax.scan(
        edge_backward,
        start_carry,
        (features, move_blocks[0], move_blocks[1], source_blocks[0], source_blocks[1]),
    )
    grad_out_local, grad_ebias_local, grad_in_local, grad_bin_local = edge_sums
    bias_total = grad_bias + jnp.concatenate(
        [grad_bin_local, grad_gbias, jnp.zeros((biases.shape[0] - EH - 6 * H,), jnp.float32)]
    )
    count_local = jnp.sum(present_f)
    shared = lax.psum(
        (
            grad_in_local,
            grad_gru,
            grad_lstm,
            grad_first,
            grad_second,
            bias_total,
            loss_local,
            count_local,
        ),
        ("mol", "row"),
    )
    sharded = lax.psum((grad_out_local, grad_ebias_local), "mol")
    total_count = shared[7]
    grads = [
        shared[0] / total_count,
        sharded[0] / total_count,
        sharded[1] / total_count,
        shared[1] / total_count,
        shared[2] / total_count,
        shared[3] / total_count,
        shared[4] / total_count,
        shared[5] / total_count,
    ]
    edge_squares = lax.psum(jnp.sum(grads[1] * grads[1]) + jnp.sum(grads[2] * grads[2]), "row")
    replicated = grads[0:1] + grads[3:]
    norm = jnp.sqrt(edge_squares + sum((jnp.sum(grad * grad) for grad in replicated)))
    factor = jnp.minimum(1.0, clip_norm / norm)
    params = (
        edge_in,
        edge_out,
        edge_bias,
        gru_weights,
        lstm_weights,
        head_first,
        head_second,
        biases,
    )
    moments = (
        moment_edge_in,
        moment_edge_out,
        moment_edge_bias,
        moment_gru,
        moment_lstm,
        moment_head_first,
        moment_head_second,
        moment_biases,
    )
    seconds = (
        second_edge_in,
        second_edge_out,
        second_edge_bias,
        second_gru,
        second_lstm,
        second_head_first,
        second_head_second,
        second_biases,
    )
    result = [
        adamw(params[index], grads[index] * factor, moments[index], seconds[index])
        for index in range(8)
    ]
    return (
        result[0][0],
        result[1][0],
        result[2][0],
        result[3][0],
        result[4][0],
        result[5][0],
        result[6][0],
        result[7][0],
        result[0][1],
        result[1][1],
        result[2][1],
        result[3][1],
        result[4][1],
        result[5][1],
        result[6][1],
        result[7][1],
        result[0][2],
        result[1][2],
        result[2][2],
        result[3][2],
        result[4][2],
        result[5][2],
        result[6][2],
        result[7][2],
        shared[6],
        total_count,
        norm,
    )


def solution(mesh):
    in_specs = (
        P(("mol", "row"), None, None),
        P(None, "mol"),
        P(None, "mol", None),
        P(("mol", "row")),
        P(("mol", "row")),
        P(("mol", "row"), None),
        P(("mol", "row"), None),
        P(),
        P(None, "row"),
        P("row"),
        P(),
        P(),
        P(),
        P(),
        P(),
        P(),
        P(None, "row"),
        P("row"),
        P(),
        P(),
        P(),
        P(),
        P(),
        P(),
        P(None, "row"),
        P("row"),
        P(),
        P(),
        P(),
        P(),
        P(),
    )
    out_specs = (
        P(),
        P(None, "row"),
        P("row"),
        P(),
        P(),
        P(),
        P(),
        P(),
        P(),
        P(None, "row"),
        P("row"),
        P(),
        P(),
        P(),
        P(),
        P(),
        P(),
        P(None, "row"),
        P("row"),
        P(),
        P(),
        P(),
        P(),
        P(),
        P(),
        P(),
        P(),
    )
    return jax.shard_map(
        per_device, mesh=mesh, in_specs=in_specs, out_specs=out_specs, check_vma=False
    )
```

profile of v0, /device:TPU:0, one launch (start us, length us, event | category | flops | bytes accessed | tf_op | source)
XLA Modules:
  0.0 906.1 jit_solution(10447652789875052109)
XLA Ops:
  12.3 114.8 %while.27 = (s32[]{:T(128)}, bf16[4,32,64,32,128]{4,3,2,1,0:T(8,128)(2,1)}, f32[4,2048,5]{1,2,0:T(8,128)}, f32[5,128]{1,0:T(8,128)}, f32[128]{0:T(128)S(1)}, /*i...) while((s32[]{:T(128)}, bf16[4,32,64,32,128]{4,3,2,1,0:T(8,128)(2,1)}, ...), condition=%wide.region_1.2_spmd, body=%wide.region_0.1_spmd.sunk | while | flops 2181562368 | bytes 86070872 | solution.py:151
  15.0 8.1 fusion.457
  23.1 9.6 %copy.270 = bf16[256,8,32,128]{3,2,1,0:T(8,128)(2,1)S(1)} copy(bf16[256,8,32,128]{3,1,2,0:T(8,128)(2,1)} %fusion.457) | data formatting | bytes 33554432 | tf_op jit(solution)/shard_map/while
  32.8 8.3 constant_dynamic-update-slice_fusion.2
  43.7 8.1 fusion.457
  51.8 9.6 %copy.270 = bf16[256,8,32,128]{3,2,1,0:T(8,128)(2,1)S(1)} copy(bf16[256,8,32,128]{3,1,2,0:T(8,128)(2,1)} %fusion.457) | data formatting | bytes 33554432 | tf_op jit(solution)/shard_map/while
  61.4 8.3 constant_dynamic-update-slice_fusion.2
  72.4 8.1 fusion.457
  80.5 9.6 %copy.270 = bf16[256,8,32,128]{3,2,1,0:T(8,128)(2,1)S(1)} copy(bf16[256,8,32,128]{3,1,2,0:T(8,128)(2,1)} %fusion.457) | data formatting | bytes 33554432 | tf_op jit(solution)/shard_map/while
  90.1 8.3 constant_dynamic-update-slice_fusion.2
  101.1 8.1 fusion.457
  109.1 9.6 %copy.270 = bf16[256,8,32,128]{3,2,1,0:T(8,128)(2,1)S(1)} copy(bf16[256,8,32,128]{3,1,2,0:T(8,128)(2,1)} %fusion.457) | data formatting | bytes 33554432 | tf_op jit(solution)/shard_map/while
  118.8 8.3 constant_dynamic-update-slice_fusion.2
  128.3 11.1 %all_gather.18 = bf16[128,29,128]{2,0,1:T(8,128)(2,1)S(1)} all-gather(bf16[32,29,128]{2,0,1:T(8,128)(2,1)S(1)} %copy-done.19), channel_id=1, replica_groups=mesh['mol'=8,'row'=4] {'row'}, dimensions={0}, use_global_device_ids=true | all-gather | bytes 1187840 | tf_op jit(solution)/shard_map/all_gather | solution.py:158
  142.2 39.7 %fusion.30 = f32[128,64,1,32]{3,2,1,0:T(1,128)S(1)} fusion(bf16[128,64,32,128]{3,2,1,0:T(8,128)(2,1)} %bitcast.5, bf16[128,64,128,1]{2,1,0,3:T(8,128)(2,1)} %bitcast.7), kind=kOutput, calls=%fused_computation.40 | convolution fusion | flops 67108864 | bytes 70254592 | tf_op jit(solution)/shard_map/mkij,mkj->mki/dot_general | solution.py:162
  187.4 9.6 %all_gather.19 = bf16[128,29,128]{0,2,1:T(8,128)(2,1)S(1)} all-gather(bf16[128,29,32]{0,2,1:T(8,128)(2,1)S(1)} %copy.109), channel_id=1, replica_groups=mesh['mol'=8,'row'=4] {'row'}, dimensions={2}, use_global_device_ids=true | all-gather | bytes 1187840 | tf_op jit(solution)/shard_map/all_gather | solution.py:165
  199.6 9.8 %all_gather.20 = bf16[128,29,128]{2,0,1:T(8,128)(2,1)S(1)} all-gather(bf16[32,29,128]{2,0,1:T(8,128)(2,1)S(1)} %get-tuple-element.359), channel_id=1, replica_groups=mesh['mol'=8,'row'=4] {'row'}, dimensions={0}, use_global_device_ids=true | all-gather | bytes 1187840 | tf_op jit(solution)/shard_map/all_gather | solution.py:158
  214.6 41.3 %fusion.28 = f32[128,64,1,32]{3,2,1,0:T(1,128)} fusion(bf16[128,64,32,128]{3,2,1,0:T(8,128)(2,1)} %bitcast.5, bf16[128,64,128,1]{2,1,0,3:T(8,128)(2,1)} %bitcast.13), kind=kOutput, calls=%fused_computation.38 | convolution fusion | flops 67108864 | bytes 70254592 | tf_op jit(solution)/shard_map/mkij,mkj->mki/dot_general | solution.py:162
  255.9 4.6 fusion.43
  262.3 10.4 %all_gather.21 = bf16[128,29,128]{0,2,1:T(8,128)(2,1)S(1)} all-gather(bf16[128,29,32]{0,2,1:T(8,128)(2,1)} %copy.112), channel_id=1, replica_groups=mesh['mol'=8,'row'=4] {'row'}, dimensions={2}, use_global_device_ids=true | all-gather | bytes 1187840 | tf_op jit(solution)/shard_map/all_gather | solution.py:165
  430.4 3.6 fusion.74
  434.1 4.7 fusion.338
  441.0 9.6 %all_gather.22 = bf16[128,29,128]{2,0,1:T(8,128)(2,1)S(1)} all-gather(bf16[32,29,128]{2,0,1:T(8,128)(2,1)S(1)} %convolution_convert_fusion.1), channel_id=1, replica_groups=mesh['mol'=8,'row'=4] {'row'}, dimensions={0}, use_global_device_ids=true | all-gather | bytes 1187840 | tf_op jit(solution)/shard_map/all_gather | solution.py:202
  453.2 8.7 copy.173
  461.8 27.9 %fusion.378 = f32[128,64,1,128]{3,2,1,0:T(1,128)} fusion(bf16[128,64,32,128]{3,2,1,0:T(8,128)(2,1)} %bitcast.5, bf16[128,64,32,1]{2,3,1,0:T(2,128)(2,1)} %copy.173), kind=kOutput, calls=%fused_computation.611 | convolution fusion | flops 67108864 | bytes 71827456 | tf_op jit(solution)/shard_map/mkij,mki->mkj/dot_general | solution.py:214
  489.7 4.6 fusion.33
  501.2 3.6 convolution_bitcast_fusion.1
  512.9 8.1 reduce-scatter.2.cloned.1.call-done
  521.0 3.6 fusion.337
  527.8 9.2 %all_gather.23 = bf16[128,29,128]{2,0,1:T(8,128)(2,1)S(1)} all-gather(bf16[32,29,128]{2,0,1:T(8,128)(2,1)S(1)} %convolution_convert_fusion), channel_id=1, replica_groups=mesh['mol'=8,'row'=4] {'row'}, dimensions={0}, use_global_device_ids=true | all-gather | bytes 1187840 | tf_op jit(solution)/shard_map/all_gather | solution.py:202
  542.6 218.6 %while.28 = (s32[]{:T(128)}, f32[128,4096]{1,0:T(8,128)}, f32[4096]{0:T(1024)}, f32[5,128]{1,0:T(8,128)}, f32[128]{0:T(128)}, /*index=5*/f32[4,2048,5]{1,2,0:T(8...) while((s32[]{:T(128)}, f32[128,4096]{1,0:T(8,128)}, ...), condition=%wide.region_36.37_spmd.clone, body=%wide.region_33.36_spmd.clone.sunk | while | flops 4382266368 | bytes 134953168 | solution.py:260
  545.9 21.3 %convert_reduce_fusion.9 = (f32[32,128]{1,0:T(8,128)}, bf16[2048,32,128]{2,1,0:T(8,128)(2,1)}) fusion(f32[2048,128]{1,0:T(8,128)S(1)} %get-tuple-element.545, f32[2048,32]{1,0:T(8,128)S(1)} %get-tuple-element.546, f32[2048,128]{1,0:T(8,128)S(1)} %get-tuple-element.547, f32[2048,32]{1,0:T(8,128)S(1)} %get-tuple-element.548), kind=kLoop, calls=%fused_computation.8.clone.1 | loop fusion | flops 50327552 | bytes 19415040 | tf_op jit(solution)/shard_map/while/body/eval_jaxpr/reduce_sum | solution.py:244
  569.9 13.3 %fusion.464 = f32[128,4096]{1,0:T(8,128)} fusion(bf16[256,8,32,128]{3,2,1,0:T(8,128)(2,1)} %bitcast.452, f32[128,4096]{1,0:T(8,128)} %get-tuple-element.593, pred[]{:T(512)S(6)} %compare.49, f32[2048,128]{1,0:T(8,128)S(1)} %convolution_add_fusion.22), kind=kOutput, calls=%fused_computation.16.clone.1 | convolution fusion | flops 2149842944 | bytes 22020096 | tf_op jit(solution)/shard_map/while/body/eval_jaxpr/dot_general | solution.py:241
  583.2 8.9 fusion.465
  599.5 21.3 %convert_reduce_fusion.9 = (f32[32,128]{1,0:T(8,128)}, bf16[2048,32,128]{2,1,0:T(8,128)(2,1)}) fusion(f32[2048,128]{1,0:T(8,128)S(1)} %get-tuple-element.545, f32[2048,32]{1,0:T(8,128)S(1)} %get-tuple-element.546, f32[2048,128]{1,0:T(8,128)S(1)} %get-tuple-element.547, f32[2048,32]{1,0:T(8,128)S(1)} %get-tuple-element.548), kind=kLoop, calls=%fused_computation.8.clone.1 | loop fusion | flops 50327552 | bytes 19415040 | tf_op jit(solution)/shard_map/while/body/eval_jaxpr/reduce_sum | solution.py:244
  623.5 13.9 %fusion.464 = f32[128,4096]{1,0:T(8,128)} fusion(bf16[256,8,32,128]{3,2,1,0:T(8,128)(2,1)} %bitcast.452, f32[128,4096]{1,0:T(8,128)} %get-tuple-element.593, pred[]{:T(512)S(6)} %compare.49, f32[2048,128]{1,0:T(8,128)S(1)} %convolution_add_fusion.22), kind=kOutput, calls=%fused_computation.16.clone.1 | convolution fusion | flops 2149842944 | bytes 22020096 | tf_op jit(solution)/shard_map/while/body/eval_jaxpr/dot_general | solution.py:241
  637.4 8.9 fusion.465
  654.4 21.3 %convert_reduce_fusion.9 = (f32[32,128]{1,0:T(8,128)}, bf16[2048,32,128]{2,1,0:T(8,128)(2,1)}) fusion(f32[2048,128]{1,0:T(8,128)S(1)} %get-tuple-element.545, f32[2048,32]{1,0:T(8,128)S(1)} %get-tuple-element.546, f32[2048,128]{1,0:T(8,128)S(1)} %get-tuple-element.547, f32[2048,32]{1,0:T(8,128)S(1)} %get-tuple-element.548), kind=kLoop, calls=%fused_computation.8.clone.1 | loop fusion | flops 50327552 | bytes 19415040 | tf_op jit(solution)/shard_map/while/body/eval_jaxpr/reduce_sum | solution.py:244
  678.3 13.9 %fusion.464 = f32[128,4096]{1,0:T(8,128)} fusion(bf16[256,8,32,128]{3,2,1,0:T(8,128)(2,1)} %bitcast.452, f32[128,4096]{1,0:T(8,128)} %get-tuple-element.593, pred[]{:T(512)S(6)} %compare.49, f32[2048,128]{1,0:T(8,128)S(1)} %convolution_add_fusion.22), kind=kOutput, calls=%fused_computation.16.clone.1 | convolution fusion | flops 2149842944 | bytes 22020096 | tf_op jit(solution)/shard_map/while/body/eval_jaxpr/dot_general | solution.py:241
  692.2 8.9 fusion.465
  709.2 21.3 %convert_reduce_fusion.9 = (f32[32,128]{1,0:T(8,128)}, bf16[2048,32,128]{2,1,0:T(8,128)(2,1)}) fusion(f32[2048,128]{1,0:T(8,128)S(1)} %get-tuple-element.545, f32[2048,32]{1,0:T(8,128)S(1)} %get-tuple-element.546, f32[2048,128]{1,0:T(8,128)S(1)} %get-tuple-element.547, f32[2048,32]{1,0:T(8,128)S(1)} %get-tuple-element.548), kind=kLoop, calls=%fused_computation.8.clone.1 | loop fusion | flops 50327552 | bytes 19415040 | tf_op jit(solution)/shard_map/while/body/eval_jaxpr/reduce_sum | solution.py:244
  733.2 13.9 %fusion.464 = f32[128,4096]{1,0:T(8,128)} fusion(bf16[256,8,32,128]{3,2,1,0:T(8,128)(2,1)} %bitcast.452, f32[128,4096]{1,0:T(8,128)} %get-tuple-element.593, pred[]{:T(512)S(6)} %compare.49, f32[2048,128]{1,0:T(8,128)S(1)} %convolution_add_fusion.22), kind=kOutput, calls=%fused_computation.16.clone.1 | convolution fusion | flops 2149842944 | bytes 22020096 | tf_op jit(solution)/shard_map/while/body/eval_jaxpr/dot_general | solution.py:241
  747.0 8.9 fusion.465
  766.8 42.3 %all-reduce.46 = (f32[]{:T(128)}, f32[5,128]{1,0:T(8,128)S(1)}, f32[128,12]{0,1:T(8,128)S(1)}, f32[1572]{0:T(1024)S(1)}, f32[]{:T(128)}) all-reduce(f32[]{:T(128)} %get-tuple-element.229, f32[5,128]{1,0:T(8,128)} %get-tuple-element.135, f32[128,12]{0,1:T(8,128)S(1)} %fusion.297, ...), channel_id=1, replica_groups=mesh['mol'=8,'row'=4] {'mol','row'}, use_global_device_ids=true, to_apply=%region_39.40 | all-reduce | flops 3750 | bytes 30000 | tf_op jit(solution)/shard_map/psum | solution.py:270
  809.1 36.4 %psum.80 = f32[4096]{0:T(1024)S(1)} all-reduce(f32[4096]{0:T(1024)S(1)} %copy-done.65), channel_id=1, replica_groups=mesh['mol'=8,'row'=4] {'mol'}, use_global_device_ids=true, to_apply=%region_42.43 | all-reduce | flops 4096 | bytes 32768 | tf_op jit(solution)/shard_map/psum | solution.py:283
  861.3 3.6 all-reduce.51.cloned.1.call-done
  870.2 6.8 psum.81
  893.5 4.5 multiply_subtract_fusion
  (655 shorter events, 297.3 us)
Async XLA Ops:
  7.2 513.8 %reduce-scatter.2.cloned.1.call-start = ((), (), s32[]{:S(2)}) async-start(), calls=%async_computation.1 | async-start | bytes 1187840 | tf_op jit(solution)/shard_map/reduce_scatter | solution.py:223
  12.3 114.8 %copy-start.162 = (s32[2,128,64]{1,2,0:T(8,128)S(1)}, s32[2,128,64]{1,2,0:T(8,128)}, u32[]{:S(2)}) copy-start(s32[2,128,64]{1,2,0:T(8,128)} %param.37) | copy-start | bytes 196612
  12.3 115.9 %copy-start.19 = (bf16[32,29,128]{2,0,1:T(8,128)(2,1)S(1)}, bf16[32,29,128]{2,0,1:T(8,128)(2,1)}, u32[]{:S(2)}) copy-start(bf16[32,29,128]{2,0,1:T(8,128)(2,1)} %param.35) | copy-start | bytes 712708
  127.1 15.1 %copy-start.167 = (f32[128]{0:T(128)}, f32[128]{0:T(128)S(1)}, u32[]{:S(2)}) copy-start(f32[128]{0:T(128)S(1)} %get-tuple-element.644) | copy-start | bytes 1540
  139.5 311.4 %copy-start.38 = (s32[128,64]{1,0:T(8,128)}, s32[128,64]{1,0:T(8,128)S(1)}, u32[]{:S(2)}) copy-start(s32[128,64]{1,0:T(8,128)S(1)} %copy.106) | copy-start | bytes 98308
  185.2 11.8 %copy-start.40 = (f32[2,128,384]{2,1,0:T(8,128)S(1)}, f32[2,128,384]{2,1,0:T(8,128)}, u32[]{:S(2)}) copy-start(f32[2,128,384]{2,1,0:T(8,128)} %param.45) | copy-start | bytes 1179652
  185.2 11.9 %copy-start.170 = (f32[384]{0:T(512)S(1)}, f32[384]{0:T(512)}, u32[]{:S(2)}) copy-start(f32[384]{0:T(512)} %get-tuple-element.407) | copy-start | bytes 4612
  187.4 10.0 %copy-start.169 = (f32[384]{0:T(512)S(1)}, f32[384]{0:T(512)}, u32[]{:S(2)}) copy-start(f32[384]{0:T(512)} %get-tuple-element.406) | copy-start | bytes 4612
  197.1 75.6 %copy-start.35 = (bf16[2,128,384]{2,1,0:T(8,128)(2,1)}, bf16[2,128,384]{2,1,0:T(8,128)(2,1)S(1)}, u32[]{:S(2)}) copy-start(bf16[2,128,384]{2,1,0:T(8,128)(2,1)S(1)} %convert_element_type.119) | copy-start | bytes 589828
  262.3 11.2 %copy-start.1 = (f32[384,512]{1,0:T(8,128)S(1)}, f32[384,512]{1,0:T(8,128)}, u32[]{:S(2)}) copy-start(f32[384,512]{1,0:T(8,128)} %param.46) | copy-start | bytes 2359300
  262.3 12.4 %copy-start.14 = (f32[32,29,128]{2,0,1:T(8,128)S(1)}, f32[32,29,128]{2,0,1:T(8,128)}, u32[]{:S(2)}) copy-start(f32[32,29,128]{2,0,1:T(8,128)} %get-tuple-element.360) | copy-start | bytes 1425412
  274.7 10.6 %copy-start.61 = (f32[32,128]{1,0:T(8,128)}, f32[32,128]{1,0:T(8,128)S(1)}, u32[]{:S(2)}) copy-start(f32[32,128]{1,0:T(8,128)S(1)} %get-tuple-element.357) | copy-start | bytes 49156
  275.8 154.6 %copy-start.12 = (f32[32,29,128]{2,0,1:T(8,128)}, f32[32,29,128]{2,0,1:T(8,128)S(1)}, u32[]{:S(2)}) copy-start(f32[32,29,128]{2,0,1:T(8,128)S(1)} %get-tuple-element.356) | copy-start | bytes 1425412
  355.1 27.3 %copy-start.177 = (pred[32,29]{0,1:T(8,128)(4,1)S(1)}, pred[32,29]{0,1:T(8,128)(4,1)}, u32[]{:S(2)}) copy-start(pred[32,29]{0,1:T(8,128)(4,1)} %get-tuple-element.337) | copy-start | bytes 2788
  387.7 19.9 %copy-start.176 = (pred[32,29]{0,1:T(8,128)(4,1)S(1)}, pred[32,29]{0,1:T(8,128)(4,1)}, u32[]{:S(2)}) copy-start(pred[32,29]{0,1:T(8,128)(4,1)} %get-tuple-element.325) | copy-start | bytes 2788
  412.9 17.6 %copy-start.175 = (pred[32,29]{0,1:T(8,128)(4,1)S(1)}, pred[32,29]{0,1:T(8,128)(4,1)}, u32[]{:S(2)}) copy-start(pred[32,29]{0,1:T(8,128)(4,1)} %get-tuple-element.313) | copy-start | bytes 2788
  426.4 12.4 %copy-start.129 = (f32[32,128]{1,0:T(8,128)}, f32[32,128]{1,0:T(8,128)S(1)}, u32[]{:S(2)}) copy-start(f32[32,128]{1,0:T(8,128)S(1)} %split.87) | copy-start | bytes 49156
  438.8 62.4 %copy-start.10 = (f32[32,29,128]{2,0,1:T(8,128)}, f32[32,29,128]{2,0,1:T(8,128)S(1)}, u32[]{:S(2)}) copy-start(f32[32,29,128]{2,0,1:T(8,128)S(1)} %get-tuple-element.309) | copy-start | bytes 1425412
  440.2 10.4 %copy-start.25 = (f32[32,29,128]{2,0,1:T(8,128)}, f32[32,29,128]{2,0,1:T(8,128)S(1)}, u32[]{:S(2)}) copy-start(f32[32,29,128]{2,0,1:T(8,128)S(1)} %fusion.75) | copy-start | bytes 1425412
  495.8 354.7 %all-reduce.53.cloned.1.call-start = ((), (), s32[]{:S(2)}) async-start(), calls=%async_computation.3 | async-start | bytes 2621440 | tf_op jit(solution)/shard_map/psum | solution.py:270
  509.3 11.7 %copy-start.4 = (f32[32,29,384]{2,0,1:T(8,128)S(1)}, f32[32,29,384]{2,0,1:T(8,128)}, u32[]{:S(2)}) copy-start(f32[32,29,384]{2,0,1:T(8,128)} %copy-done.3) | copy-start | bytes 4276228
  509.3 11.7 %copy-start.9 = (f32[32,29,384]{2,0,1:T(8,128)S(1)}, f32[32,29,384]{2,0,1:T(8,128)}, u32[]{:S(2)}) copy-start(f32[32,29,384]{2,0,1:T(8,128)} %copy-done.8) | copy-start | bytes 4276228
  509.3 11.7 %copy-start.13 = (f32[32,29,128]{2,0,1:T(8,128)S(1)}, f32[32,29,128]{2,0,1:T(8,128)}, u32[]{:S(2)}) copy-start(f32[32,29,128]{2,0,1:T(8,128)} %copy-done.12) | copy-start | bytes 1425412
  509.4 11.7 %copy-start.37 = (bf16[2,128,384]{2,1,0:T(8,128)(2,1)S(1)}, bf16[2,128,384]{2,1,0:T(8,128)(2,1)}, u32[]{:S(2)}) copy-start(bf16[2,128,384]{2,1,0:T(8,128)(2,1)} %copy-done.35) | copy-start | bytes 589828
  524.7 16.1 %copy-start.67 = (f32[32,29,128]{2,0,1:T(8,128)}, f32[32,29,128]{2,0,1:T(8,128)S(1)}, u32[]{:S(2)}) copy-start(f32[32,29,128]{2,0,1:T(8,128)S(1)} %get-tuple-element.306) | copy-start | bytes 1425412
  524.7 16.1 %copy-start.69 = (f32[32,29,128]{2,0,1:T(8,128)}, f32[32,29,128]{2,0,1:T(8,128)S(1)}, u32[]{:S(2)}) copy-start(f32[32,29,128]{2,0,1:T(8,128)S(1)} %get-tuple-element.370) | copy-start | bytes 1425412
  524.9 15.8 %copy-start.30 = (f32[32,29,128]{2,0,1:T(8,128)}, f32[32,29,128]{2,0,1:T(8,128)S(1)}, u32[]{:S(2)}) copy-start(f32[32,29,128]{2,0,1:T(8,128)S(1)} %fusion.76) | copy-start | bytes 1425412
  527.8 9.6 %copy-start.39 = (s32[128,64]{1,0:T(8,128)S(1)}, s32[128,64]{1,0:T(8,128)}, u32[]{:S(2)}) copy-start(s32[128,64]{1,0:T(8,128)} %copy-done.38) | copy-start | bytes 98308
  542.6 322.3 %all-reduce.51.cloned.1.call-start = ((), (), s32[]{:S(2)}) async-start(), calls=%async_computation.2 | async-start | bytes 4194304 | tf_op jit(solution)/shard_map/psum | solution.py:283
  569.8 13.4 %copy-start = (bf16[2048,32,128]{2,1,0:T(8,128)(2,1)S(1)}, bf16[2048,32,128]{2,1,0:T(8,128)(2,1)}, u32[]{:S(2)}) copy-start(bf16[2048,32,128]{2,1,0:T(8,128)(2,1)} %get-tuple-element.549) | copy-start | bytes 50331652 | tf_op jit(solution)/shard_map/while
  623.5 13.9 %copy-start = (bf16[2048,32,128]{2,1,0:T(8,128)(2,1)S(1)}, bf16[2048,32,128]{2,1,0:T(8,128)(2,1)}, u32[]{:S(2)}) copy-start(bf16[2048,32,128]{2,1,0:T(8,128)(2,1)} %get-tuple-element.549) | copy-start | bytes 50331652 | tf_op jit(solution)/shard_map/while
  678.3 13.9 %copy-start = (bf16[2048,32,128]{2,1,0:T(8,128)(2,1)S(1)}, bf16[2048,32,128]{2,1,0:T(8,128)(2,1)}, u32[]{:S(2)}) copy-start(bf16[2048,32,128]{2,1,0:T(8,128)(2,1)} %get-tuple-element.549) | copy-start | bytes 50331652 | tf_op jit(solution)/shard_map/while
  733.1 13.9 %copy-start = (bf16[2048,32,128]{2,1,0:T(8,128)(2,1)S(1)}, bf16[2048,32,128]{2,1,0:T(8,128)(2,1)}, u32[]{:S(2)}) copy-start(bf16[2048,32,128]{2,1,0:T(8,128)(2,1)} %get-tuple-element.549) | copy-start | bytes 50331652 | tf_op jit(solution)/shard_map/while
  763.0 46.2 %copy-start.65 = (f32[4096]{0:T(1024)S(1)}, f32[4096]{0:T(1024)}, u32[]{:S(2)}) copy-start(f32[4096]{0:T(1024)} %get-tuple-element.137) | copy-start | bytes 49156
  766.0 115.9 %copy-start.43 = (f32[256,128]{1,0:T(8,128)S(1)}, f32[256,128]{1,0:T(8,128)}, u32[]{:S(2)}) copy-start(f32[256,128]{1,0:T(8,128)} %param.47) | copy-start | bytes 393220
  766.0 115.9 %copy-start.161 = (f32[256,128]{1,0:T(8,128)S(1)}, f32[256,128]{1,0:T(8,128)}, u32[]{:S(2)}) copy-start(f32[256,128]{1,0:T(8,128)} %param.55) | copy-start | bytes 393220
  809.1 41.4 %copy-start.165 = (f32[128,12]{0,1:T(8,128)}, f32[128,12]{0,1:T(8,128)S(1)}, u32[]{:S(2)}) copy-start(f32[128,12]{0,1:T(8,128)S(1)} %get-tuple-element.273) | copy-start | bytes 18436
  809.1 41.4 %copy-start.166 = (f32[1572]{0:T(1024)}, f32[1572]{0:T(1024)S(1)}, u32[]{:S(2)}) copy-start(f32[1572]{0:T(1024)S(1)} %get-tuple-element.274) | copy-start | bytes 18868
  809.1 41.4 %copy-start.178 = (f32[5,128]{1,0:T(8,128)}, f32[5,128]{1,0:T(8,128)S(1)}, u32[]{:S(2)}) copy-start(f32[5,128]{1,0:T(8,128)S(1)} %get-tuple-element.272) | copy-start | bytes 7684
  850.5 31.3 %copy-start.66 = (f32[256,128]{1,0:T(8,128)S(1)}, f32[256,128]{1,0:T(8,128)}, u32[]{:S(2)}) copy-start(f32[256,128]{1,0:T(8,128)} %get-tuple-element.278) | copy-start | bytes 393220
  852.9 31.4 %copy-start.2 = (f32[384,512]{1,0:T(8,128)S(1)}, f32[384,512]{1,0:T(8,128)}, u32[]{:S(2)}) copy-start(f32[384,512]{1,0:T(8,128)} %param.46) | copy-start | bytes 2359300
  852.9 31.4 %copy-start.18 = (f32[384,512]{1,0:T(8,128)S(1)}, f32[384,512]{1,0:T(8,128)}, u32[]{:S(2)}) copy-start(f32[384,512]{1,0:T(8,128)} %get-tuple-element.277) | copy-start | bytes 2359300
  852.9 31.4 %copy-start.52 = (f32[384,512]{1,0:T(8,128)S(1)}, f32[384,512]{1,0:T(8,128)}, u32[]{:S(2)}) copy-start(f32[384,512]{1,0:T(8,128)} %param.54) | copy-start | bytes 2359300
  853.0 31.4 %copy-start.53 = (f32[384,512]{1,0:T(8,128)S(1)}, f32[384,512]{1,0:T(8,128)}, u32[]{:S(2)}) copy-start(f32[384,512]{1,0:T(8,128)} %param.62) | copy-start | bytes 2359300
  881.9 9.6 %copy-start.179 = (f32[5,128]{1,0:T(8,128)S(1)}, f32[5,128]{1,0:T(8,128)}, u32[]{:S(2)}) copy-start(f32[5,128]{1,0:T(8,128)} %copy-done.178) | copy-start | bytes 7684
  881.9 9.6 %copy-start.193 = (f32[5,128]{1,0:T(8,128)S(1)}, f32[5,128]{1,0:T(8,128)}, u32[]{:S(2)}) copy-start(f32[5,128]{1,0:T(8,128)} %param.50) | copy-start | bytes 7684
  881.9 9.5 %copy-start.194 = (f32[5,128]{1,0:T(8,128)S(1)}, f32[5,128]{1,0:T(8,128)}, u32[]{:S(2)}) copy-start(f32[5,128]{1,0:T(8,128)} %param.58) | copy-start | bytes 7684
  884.4 9.0 copy-start.7
  (157 other events, 387.4 us)
Sparse Core Ops, SparseCore 0:
  495.8 25.1 reduce-scatter.1
  542.7 132.7 all-reduce.52
  761.6 103.2 all-reduce.50
where the time goes:
time: 920 us; the launch traced here: 906 us
  matrix products  360 us (39%)
  other arithmetic  219 us (24%)
  local copies, waits for them, and re-layouts  145 us (16%)
  blocking collectives  145 us (16%)
  between operations  24.3 us (3%)
  waiting for transfers between devices  11.7 us (1%)
    reduce_sum x4, other arithmetic, edge_backward(): grad_ebias = carry[1] + jnp.sum(grad_amat.astype(jnp.float32), 0)  85.2 us
    dot_general x2, matrix products, per_device(): jnp.einsum('mkij,mkj->mki', amats, source, preferred_element_type=jnp.flo...  81 us
    dot_general x4, matrix products, edge_backward(): lax.dot_general(hidden, grad_amat, (((0,), (0,)), ((), ())), preferred_el...  55 us
    psum x1, blocking collectives, per_device(): lax.psum((grad_in_local, grad_gru, grad_lstm, grad_first, grad_second, bi...  42.3 us
    while x12, local copies, waits for them, and re-layouts  38.6 us
    psum x1, blocking collectives, per_device(): sharded = lax.psum((grad_out_local, grad_ebias_local), 'mol')  36.4 us
    dot_general x4, matrix products, edge_backward(): lax.dot_general(grad_amat, out_low, (((1,), (1,)), ((), ())), preferred_e...  35.8 us
    dynamic_update_slice x4, local copies, waits for them, and re-layouts, per_device(): amats = lax.map(edge_forward, features).reshape(group_mols, EM, own_rows, H)  33.1 us
  transfers between devices with their start and end apart: 3, of which 2 were waited for; matrix products, arithmetic and copies ran while one was open for 28% of the time, Pallas kernels for 0%

commit v1 on v0

v1 whole, which is shorter than its diff:
```python
import functools
import math

import jax
import jax.numpy as jnp
from jax import lax
from jax.experimental import pallas as pl
from jax.experimental.pallas import tpu as pltpu
from jax.sharding import PartitionSpec as P

H = 128
EH = 128
EIN = 5
NT = 12
STEPS = 6
ATOMS = 29
EM = 64
LAYERS = 2
STEP_COUNT = 10

PAD = 32
LIVE = 2 * (ATOMS - 1)
LB = 256
MIB = 2**20

f32 = jnp.float32
bf16 = jnp.bfloat16
highest = lax.Precision.HIGHEST
beta_one = 0.9
beta_two = 0.999
rate = 0.05
epsilon = 1e-08
decay = 0.01
clip_norm = 0.1

R_LSTM, R_FIRST, R_GRU, R_SECOND, R_MISC, R_EBIAS, R_END = 0, 1024, 1280, 2048, 2176, 2192, 2320

NN = ((1,), (0,))
NTR = ((1,), (1,))
TN = ((0,), (0,))


def mm(a, b, dims=NN):
    return lax.dot_general(a, b, (dims, ((), ())), preferred_element_type=f32)


def split(x):
    high = x.astype(bf16)
    return high, (x - high.astype(f32)).astype(bf16)


def mm3(a, b, dims=NN):
    return mm(a[0], b[0], dims) + (mm(a[0], b[1], dims) + mm(a[1], b[0], dims))


def mm2(a, b, dims=NN):
    high, low = split(a)
    return mm(high, b, dims) + mm(low, b, dims)


def columns(start, size):
    return pl.ds(pl.multiple_of(start, size), size)


def sigmoid(v):
    return jax.nn.sigmoid(v)


def body_main(
    mols,
    counts_s,
    counts_col,
    flags_col,
    targets,
    present,
    tab,
    nodes,
    edge_in_t,
    b_in_col,
    w_fwd,
    w_back,
    ebias,
    gru_t,
    gru_n,
    gbias_col,
    lstm,
    c_lstm,
    first,
    c_head,
    second,
    c_out,
    offsets,
    pack,
    src_o,
    g_o,
    hid_o,
    before_o,
    feat_o,
    z,
    hot_src,
    hot_dst,
    st,
    low,
    msg,
    keep,
    acc,
    dst_acc,
    gm,
    w_all,
    ds_all,
):
    atoms = mols * PAD
    total = jnp.int32(0)
    for m in range(mols):
        total = total + 2 * (counts_s[m] - 1)
    blocks = lax.div(total + (LB - 1), jnp.int32(LB))

    live_col = 2.0 * (counts_col[...].astype(f32) - 1.0)
    below = (
        lax.broadcasted_iota(jnp.int32, (mols, mols), 1)
        < lax.broadcasted_iota(jnp.int32, (mols, mols), 0)
    ).astype(bf16)
    start_col = mm(below, jnp.broadcast_to(live_col, (mols, 128)).astype(bf16))[:, :1]
    e_high, e_low = split(edge_in_t[...])
    e_rest = (edge_in_t[...] - e_high.astype(f32) - e_low.astype(f32)).astype(bf16)

    def prepare(b, carry):
        c = columns(b * LB, LB)
        place = (lax.broadcasted_iota(jnp.int32, (mols, LB), 1) + b * LB).astype(f32)
        mol_hot = ((place >= start_col) & (place < start_col + live_col)).astype(f32)
        rows = mm(tab[...], mol_hot.astype(bf16))
        start_row = jnp.sum(mol_hot * start_col, axis=0, keepdims=True)
        mol_row = jnp.sum(
            mol_hot * lax.broadcasted_iota(jnp.int32, (mols, LB), 0).astype(f32),
            axis=0,
            keepdims=True,
        )
        valid = jnp.sum(mol_hot, axis=0, keepdims=True)
        slot = place[:1] - start_row
        slot_hot = (lax.broadcasted_iota(jnp.int32, (EM, LB), 0).astype(f32) == slot).astype(f32)
        picked = [
            jnp.sum(rows[r * EM : (r + 1) * EM] * slot_hot, axis=0, keepdims=True)
            for r in range(EIN + 2)
        ]
        feat = jnp.concatenate(
            picked[:EIN] + [valid, jnp.zeros((2, LB), f32)], axis=0
        )
        feat_o[:, c] = feat
        feat_low = feat.astype(bf16)
        before = (
            mm(e_high, feat_low) + mm(e_low, feat_low) + mm(e_rest, feat_low) + b_in_col[...]
        )
        before_o[:, c] = before
        hid_o[:, c] = (before * sigmoid(before)).astype(bf16)
        atom = lax.broadcasted_iota(jnp.int32, (atoms, LB), 0)
        base = mol_row * PAD
        src = jnp.where(valid > 0.5, base + picked[EIN], -1.0).astype(jnp.int32)
        dst = jnp.where(valid > 0.5, base + picked[EIN + 1], -1.0).astype(jnp.int32)
        hot_src[:, c] = (atom == src).astype(f32).astype(bf16)
        hot_dst[:, c] = (atom == dst).astype(f32).astype(bf16)
        return carry

    lax.fori_loop(0, blocks, prepare, 0)

    b_high, b_low = split(ebias[...])
    chunks = atoms // LB

    low[0] = nodes[...]
    st[0] = nodes[...].astype(f32)
    for layer in range(LAYERS):
        acc[...] = jnp.zeros_like(acc)

        def move(b, carry, layer=layer):
            c = columns(b * LB, LB)
            source = mm(low[layer], hot_src[:, c]).astype(bf16)
            src_o[layer, :, c] = source
            for h in range(EH):
                z[h * H : (h + 1) * H, :] = hid_o[pl.ds(h, 1), c] * source
            moved = mm(w_fwd[...], z[...])
            moved = moved + (mm(b_high, source) + mm(b_low, source))
            acc[...] += mm2(moved, hot_dst[:, c], NTR)
            return carry

        lax.fori_loop(0, blocks, move, 0)
        msg[layer] = acc[...].astype(bf16)

        def update(k, carry, layer=layer):
            c = columns(k * LB, LB)
            from_in = mm(gru_t[0], msg[layer, :, c]) + gbias_col[0]
            from_st = mm(gru_t[1], low[layer, :, c]) + gbias_col[1]
            reset = sigmoid(from_in[:H] + from_st[:H])
            upd = sigmoid(from_in[H : 2 * H] + from_st[H : 2 * H])
            fresh = jnp.tanh(from_in[2 * H :] + reset * from_st[2 * H :])
            new = (1.0 - upd) * fresh + upd * st[layer, :, c]
            st[layer + 1, :, c] = new
            if layer + 1 < LAYERS:
                low[layer + 1, :, c] = new.astype(bf16)
            keep[layer, 0, :, c] = reset
            keep[layer, 1, :, c] = upd
            keep[layer, 2, :, c] = fresh
            keep[layer, 3, :, c] = from_st[2 * H :]
            return carry

        lax.fori_loop(0, chunks, update, 0)

    lane = lax.broadcasted_iota(jnp.int32, (mols, atoms), 1)
    own = lax.broadcasted_iota(jnp.int32, (mols, atoms), 0)
    slot_of = lane - own * PAD
    alive = (slot_of >= 0) & (slot_of < counts_col[...])
    x = split(st[LAYERS])
    lstm_w = split(lstm[...])
    zeros = jnp.zeros((mols, H), f32)
    hidden, read, cell = zeros, zeros, zeros
    saved = []
    for step in range(STEPS):
        query = jnp.concatenate([hidden, read], axis=1)
        if step == 0:
            gates = jnp.broadcast_to(c_lstm[...], (mols, 4 * H))
        else:
            gates = mm3(split(query), lstm_w) + c_lstm[...]
        in_gate = sigmoid(gates[:, :H])
        forget = sigmoid(gates[:, H : 2 * H])
        part = jnp.tanh(gates[:, 2 * H : 3 * H])
        out_gate = sigmoid(gates[:, 3 * H :])
        before_cell = cell
        cell = forget * cell + in_gate * part
        squashed = jnp.tanh(cell)
        hidden = out_gate * squashed
        scores = jnp.where(alive, mm3(split(hidden), x), -1e30)
        weights = jnp.where(alive, jnp.exp(scores - jnp.max(scores, axis=1, keepdims=True)), 0.0)
        weights = weights / jnp.sum(weights, axis=1, keepdims=True)
        w_all[step * mols : (step + 1) * mols, :] = weights
        read = mm3(split(weights), x, NTR)
        saved.append((query, in_gate, forget, part, out_gate, before_cell, squashed, hidden))
    query = jnp.concatenate([hidden, read], axis=1)
    first_w = split(first[...])
    second_w = split(second[...])
    query_s = split(query)
    inner_pre = mm3(query_s, first_w) + c_head[...]
    inner_sig = sigmoid(inner_pre)
    inner = inner_pre * inner_sig
    inner_s = split(inner)
    is_one = flags_col[...] == 1
    predicted = (
        mm3(inner_s, second_w)
        + c_out[...]
        + jnp.where(is_one, offsets[1:2, :], offsets[0:1, :])
    )
    there = present[...].astype(f32)
    diff = predicted - targets[...]
    loss = jnp.sum(jnp.sum(there * diff * diff, axis=1, keepdims=True), axis=0, keepdims=True)
    count = jnp.sum(jnp.sum(there, axis=1, keepdims=True), axis=0, keepdims=True)

    d_pred = 2.0 * there * diff
    d_pred_s = split(d_pred)
    pack[R_SECOND:R_MISC, :] = jnp.zeros((H, 128), f32)
    pack[R_SECOND:R_MISC, :NT] = mm3(inner_s, d_pred_s, TN)
    misc = jnp.zeros((16, 128), f32)
    pack[R_MISC:R_EBIAS, :] = misc
    pack[R_MISC + 11 : R_MISC + 12, :NT] = jnp.sum(d_pred, axis=0, keepdims=True)
    pack[R_MISC + 12 : R_MISC + 13, :NT] = jnp.sum(
        jnp.where(is_one, 0.0, d_pred), axis=0, keepdims=True
    )
    pack[R_MISC + 13 : R_MISC + 14, :NT] = jnp.sum(
        jnp.where(is_one, d_pred, 0.0), axis=0, keepdims=True
    )
    pack[R_MISC + 14 : R_MISC + 15, 0:1] = loss
    pack[R_MISC + 14 : R_MISC + 15, 1:2] = count
    d_inner = mm3(d_pred_s, second_w, NTR)
    d_pre = d_inner * inner_sig * (1.0 + inner_pre * (1.0 - inner_sig))
    d_pre_s = split(d_pre)
    pack[R_FIRST:R_GRU, :] = mm3(query_s, d_pre_s, TN)
    pack[R_MISC + 10 : R_MISC + 11, :] = jnp.sum(d_pre, axis=0, keepdims=True)
    d_query = mm3(d_pre_s, first_w, NTR)
    d_hidden, d_read = d_query[:, :H], d_query[:, H:]
    d_cell = zeros
    d_gates_all = [None] * STEPS
    d_reads = [None] * STEPS
    for step in reversed(range(STEPS)):
        query, in_gate, forget, part, out_gate, before_cell, squashed, hid_t = saved[step]
        weights = w_all[step * mols : (step + 1) * mols, :]
        d_read_s = split(d_read)
        d_reads[step] = d_read
        d_weights = mm3(d_read_s, x)
        d_scores = weights * (d_weights - jnp.sum(weights * d_weights, axis=1, keepdims=True))
        ds_all[step * mols : (step + 1) * mols, :] = d_scores
        d_hidden = d_hidden + mm3(split(d_scores), x, NTR)
        d_out = d_hidden * squashed * out_gate * (1.0 - out_gate)
        d_cell = d_cell + d_hidden * out_gate * (1.0 - squashed * squashed)
        d_forget = d_cell * before_cell * forget * (1.0 - forget)
        d_in = d_cell * part * in_gate * (1.0 - in_gate)
        d_part = d_cell * in_gate * (1.0 - part * part)
        d_cell = d_cell * forget
        d_gates = jnp.concatenate([d_in, d_forget, d_part, d_out], axis=1)
        d_gates_all[step] = d_gates
        if step > 0:
            d_query = mm3(split(d_gates), lstm_w, NTR)
            d_hidden, d_read = d_query[:, :H], d_query[:, H:]
    queries = split(jnp.concatenate([saved[s][0] for s in range(STEPS)], axis=0))
    d_gates_cat = jnp.concatenate(d_gates_all, axis=0)
    d_gates_s = split(d_gates_cat)
    grad_lstm = mm3(queries, d_gates_s, TN)
    d_gates_sum = jnp.sum(d_gates_cat, axis=0, keepdims=True)
    for k in range(4):
        pack[R_LSTM + k * 256 : R_LSTM + (k + 1) * 256, :] = grad_lstm[:, k * H : (k + 1) * H]
        pack[R_MISC + 6 + k : R_MISC + 7 + k, :] = d_gates_sum[:, k * H : (k + 1) * H]
    left = jnp.concatenate(d_reads + [saved[s][7] for s in range(STEPS)], axis=0)
    left_s = split(left)

    def spread(k, carry):
        c = columns(k * LB, LB)
        right = split(jnp.concatenate([w_all[:, c], ds_all[:, c]], axis=0))
        dst_acc[:, c] = mm3(left_s, right, TN)
        return carry

    lax.fori_loop(0, chunks, spread, 0)

    pack[R_GRU:R_SECOND, :] = jnp.zeros((6 * H, 128), f32)
    for layer in reversed(range(LAYERS)):

        def back(k, carry, layer=layer):
            c = columns(k * LB, LB)
            d_state = dst_acc[:, c]
            reset, upd = keep[layer, 0, :, c], keep[layer, 1, :, c]
            fresh, from_st = keep[layer, 2, :, c], keep[layer, 3, :, c]
            d_upd = d_state * (st[layer, :, c] - fresh) * upd * (1.0 - upd)
            d_fresh = d_state * (1.0 - upd) * (1.0 - fresh * fresh)
            d_reset = d_fresh * from_st * reset * (1.0 - reset)
            d_from_in = jnp.concatenate([d_reset, d_upd, d_fresh], axis=0)
            d_from_st = jnp.concatenate([d_reset, d_upd, d_fresh * reset], axis=0)
            in_s, st_s = split(d_from_in), split(d_from_st)
            gm[:, c] = (mm(gru_n[0], in_s[0]) + mm(gru_n[0], in_s[1])).astype(bf16)
            if layer > 0:
                dst_acc[:, c] = d_state * upd + (mm(gru_n[1], st_s[0]) + mm(gru_n[1], st_s[1]))
            ones = jnp.ones((8, LB), bf16)
            message, state_low = msg[layer, :, c], low[layer, :, c]
            for half, left_m, right_m in ((0, message, in_s), (1, state_low, st_s)):
                grad = mm(left_m, right_m[0], NTR) + mm(left_m, right_m[1], NTR)
                sums = (mm(ones, right_m[0], NTR) + mm(ones, right_m[1], NTR))[:1]
                for q in range(3):
                    r = R_GRU + (half * 3 + q) * H
                    pack[r : r + H, :] += grad[:, q * H : (q + 1) * H]
                    m = R_MISC + half * 3 + q
                    pack[m : m + 1, :] += sums[:, q * H : (q + 1) * H]
            return carry

        lax.fori_loop(0, chunks, back, 0)
        if layer > 0:
            bt_high, bt_low = split(jnp.transpose(ebias[...]))

            def pull(b, carry, layer=layer):
                c = columns(b * LB, LB)
                grad = mm(gm[...], hot_dst[:, c])
                grad_low = grad.astype(bf16)
                g_o[layer, :, c] = grad_low
                hid = hid_o[:, c]
                for i in range(H):
                    z[i * EH : (i + 1) * EH, :] = g_o[layer, pl.ds(i, 1), c] * hid
                pulled = mm(w_back[...], z[...])
                pulled = pulled + (mm(bt_high, grad_low) + mm(bt_low, grad_low))
                dst_acc[...] += mm2(pulled, hot_src[:, c], NTR)
                return carry

            lax.fori_loop(0, blocks, pull, 0)
        else:

            def take(b, carry, layer=layer):
                c = columns(b * LB, LB)
                g_o[layer, :, c] = mm(gm[...], hot_dst[:, c]).astype(bf16)
                return carry

            lax.fori_loop(0, blocks, take, 0)
    acc_b = acc.at[:, :H]
    acc_b[...] = jnp.zeros((H, H), f32)

    def bias_sum(b, carry):
        c = columns(b * LB, LB)
        acc_b[...] += mm(g_o[0, :, c], src_o[0, :, c], NTR) + mm(
            g_o[1, :, c], src_o[1, :, c], NTR
        )
        return carry

    lax.fori_loop(0, blocks, bias_sum, 0)
    pack[R_EBIAS:R_END, :] = acc_b[...]


def body_edges(mols, counts_s, w, src, g, hid, before, feat, out, grad_in, grid_z, grad_hid, acc):
    part = pl.program_id(0)
    total = jnp.int32(0)
    for m in range(mols):
        total = total + 2 * (counts_s[m] - 1)
    blocks = lax.div(total + (LB - 1), jnp.int32(LB))
    rows = w.shape[2] // H

    def edges(b, carry):
        c = columns(b * LB, LB)
        base = part * rows
        g0 = g[0, pl.ds(pl.multiple_of(base, rows), rows), c].astype(f32)
        g1 = g[1, pl.ds(pl.multiple_of(base, rows), rows), c].astype(f32)
        s0, s1 = src[0, :, c].astype(f32), src[1, :, c].astype(f32)
        for i in range(rows):
            grid_z[i * H : (i + 1) * H, :] = (g0[i : i + 1] * s0 + g1[i : i + 1] * s1).astype(bf16)
        pulled = mm(w[0], grid_z[...])

        @pl.when(part == 0)
        def _():
            grad_hid[:, c] = pulled

        @pl.when(part > 0)
        def _():
            grad_hid[:, c] += pulled

        product = mm(hid[:, c], grid_z[...], NTR)

        @pl.when(b == 0)
        def _():
            acc[...] = product

        @pl.when(b > 0)
        def _():
            acc[...] += product

        return carry

    lax.fori_loop(0, blocks, edges, 0)
    out[0] = acc[...].astype(out.dtype)

    @pl.when(part == pl.num_programs(0) - 1)
    def _():
        grad_in[...] = jnp.zeros_like(grad_in)

        def finish(b, carry):
            c = columns(b * LB, LB)
            ahead = before[:, c]
            sig = sigmoid(ahead)
            grad = split(grad_hid[:, c] * sig * (1.0 + ahead * (1.0 - sig)))
            rows_low = feat[:, c].astype(bf16)
            grad_in[...] += mm(rows_low, grad[0], NTR) + mm(rows_low, grad[1], NTR)
            return carry

        lax.fori_loop(0, blocks, finish, 0)


def split_biases(biases):
    start = 0
    pieces = []
    for width in (EH, 6 * H, 4 * H, H, NT, 2 * NT):
        pieces.append(biases[start : start + width])
        start = start + width
    return pieces


def adamw(weight, grad, moment, second):
    moment_new = beta_one * moment + (1.0 - beta_one) * grad
    second_new = beta_two * second + (1.0 - beta_two) * grad * grad
    mean_hat = moment_new / (1.0 - beta_one**STEP_COUNT)
    square_hat = second_new / (1.0 - beta_two**STEP_COUNT)
    return (
        weight - rate * (mean_hat / (jnp.sqrt(square_hat) + epsilon) + decay * weight),
        moment_new,
        second_new,
    )


VM = pl.BlockSpec(memory_space=pltpu.VMEM)
SM = pl.BlockSpec(memory_space=pltpu.SMEM)


def per_device(
    node_feats,
    edge_feats,
    edge_ends,
    atom_counts,
    dataset_flags,
    targets,
    present,
    edge_in,
    edge_out,
    edge_bias,
    gru_weights,
    lstm_weights,
    head_first,
    head_second,
    biases,
    *moments_seconds,
):
    row = lax.axis_index("row")
    row_count = lax.axis_size("row")
    mols = node_feats.shape[0]
    own_rows = edge_out.shape[1] // H
    atoms = mols * PAD
    space = -(-mols * LIVE // LB) * LB
    b_in, b_gru, c_lstm, c_head, c_out, offsets = split_biases(biases)

    out_low = edge_out.astype(bf16)
    w_all = lax.all_gather(out_low, "row", axis=0)
    ebias = lax.all_gather(edge_bias, "row", axis=0).reshape(H, H)
    w4 = w_all.reshape(row_count, EH, own_rows, H)
    w_fwd = w4.transpose(0, 2, 1, 3).reshape(H, EH * H)
    w_back = w4.transpose(3, 0, 2, 1).reshape(H, H * EH)

    ends = lax.dynamic_slice_in_dim(edge_ends, row * mols, mols, 1)
    feats = lax.dynamic_slice_in_dim(edge_feats, row * mols * EM, mols * EM, 1)
    tab = jnp.concatenate(
        [
            feats.reshape(EIN, mols, EM),
            ends.astype(bf16),
            jnp.zeros((1, mols, EM), bf16),
        ],
        axis=0,
    )
    tab = tab.transpose(0, 2, 1).reshape(8 * EM, mols)
    nodes = jnp.pad(node_feats, ((0, 0), (0, PAD - ATOMS), (0, 0))).reshape(atoms, H).T
    gru_low = gru_weights.astype(bf16)
    lstm = jnp.concatenate([lstm_weights[:H] + lstm_weights[2 * H :], lstm_weights[H : 2 * H]], 0)
    edge_in_t = jnp.pad(edge_in, ((0, 3), (0, 0))).T

    sds = jax.ShapeDtypeStruct
    pack, src, g, hid, before, feat = pl.pallas_call(
        functools.partial(body_main, mols),
        out_shape=(
            sds((R_END, 128), f32),
            sds((LAYERS, H, space), bf16),
            sds((LAYERS, H, space), bf16),
            sds((EH, space), bf16),
            sds((EH, space), f32),
            sds((8, space), f32),
        ),
        in_specs=[SM] + [VM] * 21,
        out_specs=(VM,) * 6,
        scratch_shapes=[
            pltpu.VMEM((H * EH, LB), bf16),
            pltpu.VMEM((atoms, space), bf16),
            pltpu.VMEM((atoms, space), bf16),
            pltpu.VMEM((LAYERS + 1, H, atoms), f32),
            pltpu.VMEM((LAYERS, H, atoms), bf16),
            pltpu.VMEM((LAYERS, H, atoms), bf16),
            pltpu.VMEM((LAYERS, 4, H, atoms), f32),
            pltpu.VMEM((H, atoms), f32),
            pltpu.VMEM((H, atoms), f32),
            pltpu.VMEM((H, atoms), bf16),
            pltpu.VMEM((STEPS * mols, atoms), f32),
            pltpu.VMEM((STEPS * mols, atoms), f32),
        ],
        compiler_params=pltpu.CompilerParams(vmem_limit_bytes=60 * MIB),
    )(
        atom_counts,
        atom_counts.reshape(mols, 1),
        dataset_flags.reshape(mols, 1),
        targets,
        present,
        tab,
        nodes,
        edge_in_t,
        b_in.reshape(EH, 1),
        w_fwd,
        w_back,
        ebias,
        gru_low.transpose(0, 2, 1),
        gru_low,
        b_gru.reshape(2, 3 * H, 1),
        lstm,
        c_lstm.reshape(1, 4 * H),
        head_first,
        c_head.reshape(1, H),
        head_second,
        c_out.reshape(1, NT),
        offsets.reshape(2, NT),
    )
    shared = lax.psum(pack, ("mol", "row"))

    grad_out, grad_in = pl.pallas_call(
        functools.partial(body_edges, mols),
        out_shape=(sds((row_count, EH, own_rows * H), bf16), sds((8, EH), f32)),
        grid=(row_count,),
        in_specs=[SM, pl.BlockSpec((1, EH, own_rows * H), lambda q: (q, 0, 0))] + [VM] * 5,
        out_specs=(pl.BlockSpec((1, EH, own_rows * H), lambda q: (q, 0, 0)), VM),
        scratch_shapes=[
            pltpu.VMEM((own_rows * H, LB), bf16),
            pltpu.VMEM((EH, space), f32),
            pltpu.VMEM((EH, own_rows * H), f32),
        ],
        compiler_params=pltpu.CompilerParams(vmem_limit_bytes=56 * MIB),
    )(atom_counts, w_all, src, g, hid, before, feat)
    own = lax.psum_scatter(grad_out, "row", scatter_dimension=0, tiled=False)
    own = lax.psum(own.astype(f32), "mol")
    grad_in = lax.psum(grad_in, ("mol", "row"))

    misc = shared[R_MISC:R_EBIAS]
    loss, total_count = misc[14, 0], misc[14, 1]
    lstm_rows = shared[R_LSTM:R_FIRST].reshape(4, 2 * H, H).transpose(1, 0, 2).reshape(2 * H, 4 * H)
    grad_lstm = jnp.concatenate([lstm_rows, lstm_rows[:H]], axis=0)
    grad_gru = (
        shared[R_GRU:R_SECOND].reshape(2, 3, H, H).transpose(0, 2, 1, 3).reshape(2, H, 3 * H)
    )
    grad_bias = jnp.concatenate(
        [
            grad_in[EIN],
            misc[:11].reshape(11 * H),
            misc[11, :NT],
            misc[12, :NT],
            misc[13, :NT],
        ]
    )
    ebias_rows = lax.dynamic_slice_in_dim(shared[R_EBIAS:R_END], row * own_rows, own_rows, 0)
    sums = [
        grad_in[:EIN],
        own,
        ebias_rows.reshape(own_rows * H),
        grad_gru,
        grad_lstm,
        shared[R_FIRST:R_GRU],
        shared[R_SECOND:R_MISC, :NT],
        grad_bias,
    ]
    grads = [grad / total_count for grad in sums]
    edge_squares = lax.psum(jnp.sum(grads[1] * grads[1]) + jnp.sum(grads[2] * grads[2]), "row")
    replicated = grads[0:1] + grads[3:]
    norm = jnp.sqrt(edge_squares + sum((jnp.sum(grad * grad) for grad in replicated)))
    factor = jnp.minimum(1.0, clip_norm / norm)
    params = (
        edge_in,
        edge_out,
        edge_bias,
        gru_weights,
        lstm_weights,
        head_first,
        head_second,
        biases,
    )
    moments, seconds = moments_seconds[:8], moments_seconds[8:]
    result = [
        adamw(params[index], grads[index] * factor, moments[index], seconds[index])
        for index in range(8)
    ]
    return (
        tuple(item[0] for item in result)
        + tuple(item[1] for item in result)
        + tuple(item[2] for item in result)
        + (loss, total_count, norm)
    )


def solution(mesh):
    weights = (P(), P(None, "row"), P("row"), P(), P(), P(), P(), P())
    in_specs = (
        P(("mol", "row"), None, None),
        P(None, "mol"),
        P(None, "mol", None),
        P(("mol", "row")),
        P(("mol", "row")),
        P(("mol", "row"), None),
        P(("mol", "row"), None),
    ) + weights * 3
    out_specs = weights * 3 + (P(), P(), P())
    return jax.shard_map(
        per_device, mesh=mesh, in_specs=in_specs, out_specs=out_specs, check_vma=False
    )
```

time: 920 us -> 545 us (0.59)
  matrix products: 360 us -> 0 us
  waiting for transfers between devices: 11.7 us -> 245 us
  other arithmetic: 219 us -> 40.4 us
  Pallas kernels: 0 us -> 121 us
  blocking collectives: 145 us -> 53.5 us
  local copies, waits for them, and re-layouts: 145 us -> 56.1 us
    dot_general x90 -> x0, matrix products: 356 us -> none  [the longest x2 81 us: per_device(): jnp.einsum('mkij,mkj->mki', amats, source, preferred_element_type=jnp.flo...]
    psum x2, waiting for transfers between devices: 3.56 us -> 183 us  [the longest x1 92.2 us: per_device(): shared = lax.psum(pack, ('mol', 'row'))]
    pallas_call x0 -> x2, Pallas kernels: none -> 121 us  [the longest x1 75.9 us: per_device(): pl.pallas_call(functools.partial(body_main, mols), out_shape=(sds((R_END,...]
    reduce_sum x33 -> x0, other arithmetic: 112 us -> none  [the longest x4 85.2 us: edge_backward(): grad_ebias = carry[1] + jnp.sum(grad_amat.astype(jnp.float32), 0)]
    all_gather x6 -> x1, blocking collectives: 59.8 us -> 7.01 us  [per_device(): ebias = lax.all_gather(edge_bias, 'row', axis=0).reshape(H, H)]
    psum x2 -> x1, blocking collectives: 78.7 us -> 39.7 us  [per_device(): grad_in = lax.psum(grad_in, ('mol', 'row'))]
    while x12 -> x0, local copies, waits for them, and re-layouts: 38.6 us -> none
    reduce_scatter x1, waiting for transfers between devices: 8.13 us -> 43.5 us  [per_device(): own = lax.psum_scatter(grad_out, 'row', scatter_dimension=0, tiled=False)]
  transfers between devices with their start and end apart: 3 -> 4, of which waited for: 2 -> 4; matrix products, arithmetic and copies ran while one was open for 28% -> 6% of each run, Pallas kernels for 0% -> 0%
where the time goes in v1:
time: 545 us; the launch traced here: 537 us
  waiting for transfers between devices  245 us (45%)
  Pallas kernels  121 us (22%)
  local copies, waits for them, and re-layouts  56.1 us (10%)
  blocking collectives  53.5 us (10%)
  other arithmetic  40.4 us (7%)
  between operations  21.2 us (4%)
    psum x1, waiting for transfers between devices, per_device(): shared = lax.psum(pack, ('mol', 'row'))  92.2 us
    psum x1, waiting for transfers between devices, per_device(): own = lax.psum(own.astype(f32), 'mol')  91.3 us
    pallas_call x1, Pallas kernels, per_device(): pl.pallas_call(functools.partial(body_main, mols), out_shape=(sds((R_END,...  75.9 us
    pallas_call x1, Pallas kernels, per_device(): pl.pallas_call(functools.partial(body_edges, mols), out_shape=(sds((row_c...  45.1 us
    reduce_scatter x1, waiting for transfers between devices, per_device(): own = lax.psum_scatter(grad_out, 'row', scatter_dimension=0, tiled=False)  43.5 us
    psum x1, blocking collectives, per_device(): grad_in = lax.psum(grad_in, ('mol', 'row'))  39.7 us
    sub x8, other arithmetic, adamw(): weight - rate * (mean_hat / (jnp.sqrt(square_hat) + epsilon) + decay * we...  19.8 us
    unnamed x84, local copies, waits for them, and re-layouts  17.7 us
  transfers between devices with their start and end apart: 4, of which 4 were waited for; matrix products, arithmetic and copies ran while one was open for 6% of the time, Pallas kernels for 0%

profile of v1, /device:TPU:0, one launch (start us, length us, event | category | flops | bytes accessed | tf_op | source)
XLA Modules:
  0.0 537.0 jit_solution(2028783023668900925)
XLA Ops:
  7.3 2.9 convert_element_type.19
  11.5 0.8 copy.153
  12.7 0.7 copy.163.b_in_col
  13.5 0.7 copy.166.second
  14.4 0.9 copy.155
  15.2 1.0 reshape.160.gbias_col
  17.0 0.8 copy.164.gru_t
  21.3 7.0 %all-gather.1 = f32[16384]{0:T(1024)} all-gather(f32[4096]{0:T(1024)S(1)} %copy-done.16), channel_id=3, replica_groups=mesh['mol'=8,'row'=4] {'row'}, dimensions={0}, use_global_device_ids=true | all-gather | bytes 81920 | tf_op jit(solution)/shard_map/all_gather | solution.py:497
  29.0 0.8 pad_maximum_fusion.lstm
  30.4 17.5 %all-gather.4.cloned.1.call-done = bf16[512,4096]{1,0:T(8,128)(2,1)} async-done(((bf16[128,4096]{1,0:T(8,128)(2,1)}), bf16[512,4096]{1,0:T(8,128)(2,1)}) %all-gather.4.cloned.1.call-update) | async-done | bytes 4194320 | tf_op jit(solution)/shard_map/all_gather | solution.py:496
  47.9 3.4 copy.189
  51.4 2.0 copy-done.2
  53.4 3.6 copy.157
  56.9 9.0 %copy.158 = bf16[4,128,32,128]{1,2,0,3:T(8,128)(2,1)} copy(bf16[4,128,32,128]{3,2,1,0:T(8,128)(2,1)} %bitcast.79) | data formatting | bytes 8388608 | tf_op jit(solution)/shard_map/reshape | solution.py:498
  66.0 12.6 %copy_bitcast_fusion = (bf16[128,16384]{1,0:T(8,128)(2,1)}, bf16[128,16384]{1,0:T(8,128)(2,1)}) fusion(bf16[16,8,128,128]{3,2,1,0:T(8,128)(2,1)} %bitcast.83, bf16[16,8,128,128]{3,2,1,0:T(8,128)(2,1)} %bitcast.82), kind=kLoop, calls=%fused_computation | loop fusion | bytes 16777216 | tf_op jit(solution)/shard_map/reshape | solution.py:500
  78.6 75.9 %shard_map.502 = (f32[2320,128]{1,0:T(8,128)}, bf16[2,128,1792]{2,1,0:T(8,128)(2,1)}, bf16[2,128,1792]{2,1,0:T(8,128)(2,1)}, bf16[128,1792]{1,0:T(8,128)(2,1)}, f32[128,1792]{1,0:T(8,128)}, /*index=5*/f32[8,1792]{1,0:T(8,128)}) custom-call(s32[32]{0:T(128)} %counts_s.3, s32[32,1]{1,0:T(8,128)} %copy.159.counts_col, s32[32,1]{1,0:T(8,128)} %copy.160.flags_col, ...), custom_call_target="tpu_custom_call" | custom-call | tf_op jit(solution)/shard_map/pallas_call | solution.py:519
  154.5 45.1 %shard_map.503 = (bf16[4,128,4096]{2,1,0:T(8,128)(2,1)}, f32[8,128]{1,0:T(8,128)}) custom-call(s32[32]{0:T(128)} %counts_s.3, bf16[4,128,4096]{2,1,0:T(8,128)(2,1)} %bitcast.81, bf16[2,128,1792]{2,1,0:T(8,128)(2,1)} %get-tuple-element.35.src, bf16[2,128,1792]{2,1,0:T(8,128)(2,1)} %get-tuple-element.36.g, bf16[128,1792]{1,0:T(8,128)(2,1)} %get-tuple-element.37.hid, ...), custom_call_target="tpu_custom_call" | custom-call | tf_op jit(solution)/shard_map/pallas_call | solution.py:572
  199.7 0.9 copy.174
  200.8 43.5 %reduce-scatter.2.cloned.1.call-done = bf16[1,128,4096]{2,1,0:T(8,128)(2,1)} async-done(((bf16[4,128,4096]{2,1,0:T(8,128)(2,1)}), bf16[1,128,4096]{2,1,0:T(8,128)(2,1)}) %reduce-scatter.2.cloned.1.call-update) | async-done | bytes 1048592 | tf_op jit(solution)/shard_map/reduce_scatter | solution.py:585
  244.3 2.8 bitcast_convert_fusion
  247.3 0.9 copy.170
  248.3 0.9 copy.172
  249.2 39.7 %psum.28 = f32[8,128]{1,0:T(8,128)S(1)} all-reduce(f32[8,128]{1,0:T(8,128)S(1)} %copy-done.30), channel_id=1, replica_groups=mesh['mol'=8,'row'=4] {'mol','row'}, use_global_device_ids=true, to_apply=%region_0.1 | all-reduce | flops 1024 | bytes 8192 | tf_op jit(solution)/shard_map/psum | solution.py:587
  289.4 92.2 %all-reduce.5.cloned.1.call-done = f32[2320,128]{1,0:T(8,128)} async-done(((f32[2320,128]{1,0:T(8,128)}), f32[2320,128]{1,0:T(8,128)}) %all-reduce.5.cloned.1.call-update) | async-done | bytes 1187856 | tf_op jit(solution)/shard_map/psum | solution.py:570
  381.6 1.2 slice.114
  383.6 1.2 multiply_reduce_fusion.7
  384.8 1.4 multiply_reduce_fusion.2
  387.5 1.5 multiply_reduce_fusion.1
  389.6 1.3 multiply_reduce_fusion.3
  391.6 1.3 multiply_reduce_fusion.4
  393.5 0.7 concatenate.15
  394.3 1.3 multiply_reduce_fusion.5
  395.5 1.3 multiply_reduce_fusion.6
  396.8 91.3 %all-reduce.7.cloned.1.call-done = f32[128,4096]{1,0:T(8,128)} async-done(((f32[128,4096]{1,0:T(8,128)}), f32[128,4096]{1,0:T(8,128)}) %all-reduce.7.cloned.1.call-update) | async-done | bytes 2097168 | tf_op jit(solution)/shard_map/psum | solution.py:586
  488.1 3.4 multiply_reduce_fusion
  493.4 6.8 %psum.31 = f32[]{:T(128)} all-reduce(f32[]{:T(128)S(6)} %add.168), channel_id=1, replica_groups=mesh['mol'=8,'row'=4] {'row'}, use_global_device_ids=true, to_apply=%region_6.7 | all-reduce | flops 1 | bytes 8 | tf_op jit(solution)/shard_map/psum | solution.py:617
  501.0 0.7 multiply_subtract_fusion.4
  504.4 0.9 copy.171
  505.3 2.5 multiply_subtract_fusion.2
  507.8 1.9 copy.179
  509.8 2.0 copy.181
  511.7 0.9 copy.183
  512.7 2.0 multiply_subtract_fusion.6
  514.7 4.4 multiply_subtract_fusion.1
  519.1 1.3 multiply_subtract_fusion.5
  520.4 1.3 multiply_subtract_fusion.7
  521.7 1.5 multiply_subtract_fusion.3
  523.2 6.2 %multiply_subtract_fusion = (f32[128,4096]{1,0:T(8,128)}, f32[128,4096]{1,0:T(8,128)}, f32[128,4096]{1,0:T(8,128)}) fusion(f32[128,4096]{1,0:T(8,128)S(1)} %copy-done.3, f32[]{:T(128)S(6)} %min_shard_map.3, f32[128,4096]{1,0:T(8,128)S(1)} %copy-done.4, f32[]{:T(128)} %bitcast.16, f32[128,4096]{1,0:T(8,128)S(1)} %copy-done.8, f32[128,4096]{1,0:T(8,128)} %param.55), kind=kLoop, calls=%fused_computation.4 | loop fusion | flops 8912896 | bytes 14680072 | tf_op jit(solution)/shard_map/sub | solution.py:459
  (116 shorter events, 12.0 us)
Async XLA Ops:
  7.2 3.9 copy-start
  7.2 3.0 copy-start.20
  7.2 3.7 copy-start.18
  7.2 6.2 %copy-start.19 = (f32[128,12]{0,1:T(8,128)S(1)}, f32[128,12]{0,1:T(8,128)}, u32[]{:S(2)}) copy-start(f32[128,12]{0,1:T(8,128)} %param.44) | copy-start | bytes 18436
  7.3 7.0 %copy-start.13 = (bf16[32,29,128]{2,0,1:T(8,128)(2,1)S(1)}, bf16[32,29,128]{2,0,1:T(8,128)(2,1)}, u32[]{:S(2)}) copy-start(bf16[32,29,128]{2,0,1:T(8,128)(2,1)} %param.31) | copy-start | bytes 712708
  7.3 40.7 %all-gather.4.cloned.1.call-start = ((), (), s32[]{:S(2)}) async-start(), calls=%async_computation.4 | async-start | bytes 5242880 | tf_op jit(solution)/shard_map/all_gather | solution.py:496
  10.2 6.1 %copy-start.5 = (f32[2,128,384]{2,1,0:T(8,128)S(1)}, f32[2,128,384]{2,1,0:T(8,128)}, u32[]{:S(2)}) copy-start(f32[2,128,384]{2,1,0:T(8,128)} %param.41) | copy-start | bytes 1179652
  10.2 234.1 %reduce-scatter.2.cloned.1.call-start = ((), (), s32[]{:S(2)}) async-start(), calls=%async_computation.2 | async-start | bytes 5242880 | tf_op jit(solution)/shard_map/reduce_scatter | solution.py:585
  11.1 6.7 %copy-start.24 = (f32[5,128]{1,0:T(8,128)S(1)}, f32[5,128]{1,0:T(8,128)}, u32[]{:S(2)}) copy-start(f32[5,128]{1,0:T(8,128)} %param.38) | copy-start | bytes 7684
  11.1 6.8 %copy-start.29 = (s32[32]{0:T(128)S(1)}, s32[32]{0:T(128)}, u32[]{:S(2)}) copy-start(s32[32]{0:T(128)} %counts_s.3) | copy-start | bytes 388
  11.1 7.5 %copy-start.33 = (s32[32]{0:T(128)S(1)}, s32[32]{0:T(128)}, u32[]{:S(2)}) copy-start(s32[32]{0:T(128)} %param.35) | copy-start | bytes 388
  11.2 8.2 %copy-start.25 = (f32[32,12]{0,1:T(8,128)S(1)}, f32[32,12]{0,1:T(8,128)}, u32[]{:S(2)}) copy-start(f32[32,12]{0,1:T(8,128)} %param.36) | copy-start | bytes 4612
  11.2 8.8 %copy-start.26 = (s32[32,12]{0,1:T(8,128)S(1)}, s32[32,12]{0,1:T(8,128)}, u32[]{:S(2)}) copy-start(s32[32,12]{0,1:T(8,128)} %param.37) | copy-start | bytes 4612
  11.2 10.1 %copy-start.16 = (f32[4096]{0:T(1024)S(1)}, f32[4096]{0:T(1024)}, u32[]{:S(2)}) copy-start(f32[4096]{0:T(1024)} %param.40) | copy-start | bytes 49156
  11.5 17.5 %copy-start.6 = (f32[384,512]{1,0:T(8,128)S(1)}, f32[384,512]{1,0:T(8,128)}, u32[]{:S(2)}) copy-start(f32[384,512]{1,0:T(8,128)} %param.42) | copy-start | bytes 2359300
  51.4 2.0 copy-start.2
  199.6 1.0 copy-start.27
  199.6 182.0 %all-reduce.5.cloned.1.call-start = ((), (), s32[]{:S(2)}) async-start(), calls=%async_computation.1 | async-start | bytes 2375680 | tf_op jit(solution)/shard_map/psum | solution.py:570
  200.7 46.4 %copy-start.28 = (f32[128,12]{0,1:T(8,128)S(1)}, f32[128,12]{0,1:T(8,128)}, u32[]{:S(2)}) copy-start(f32[128,12]{0,1:T(8,128)} %param.60) | copy-start | bytes 18436
  200.7 46.6 %copy-start.11 = (f32[2,128,384]{2,1,0:T(8,128)S(1)}, f32[2,128,384]{2,1,0:T(8,128)}, u32[]{:S(2)}) copy-start(f32[2,128,384]{2,1,0:T(8,128)} %param.49) | copy-start | bytes 1179652
  200.7 287.3 %all-reduce.7.cloned.1.call-start = ((), (), s32[]{:S(2)}) async-start(), calls=%async_computation.3 | async-start | bytes 4194304 | tf_op jit(solution)/shard_map/psum | solution.py:586
  247.1 1.2 copy-start.12
  247.1 2.1 copy-start.30
  381.6 1.4 copy-start.7
  384.8 116.1 %copy-start.9 = (f32[128,12]{1,0:T(8,128)S(1)}, f32[128,12]{1,0:T(8,128)}, u32[]{:S(2)}) copy-start(f32[128,12]{1,0:T(8,128)} %copy.166.second) | copy-start | bytes 18436
  505.3 7.3 %copy-start.21 = (f32[1572]{0:T(1024)S(1)}, f32[1572]{0:T(1024)}, u32[]{:S(2)}) copy-start(f32[1572]{0:T(1024)} %param.45) | copy-start | bytes 18868
  509.7 9.4 %copy-start.17 = (f32[4096]{0:T(1024)S(1)}, f32[4096]{0:T(1024)}, u32[]{:S(2)}) copy-start(f32[4096]{0:T(1024)} %param.40) | copy-start | bytes 49156
  509.8 9.4 %copy-start.22 = (f32[4096]{0:T(1024)S(1)}, f32[4096]{0:T(1024)}, u32[]{:S(2)}) copy-start(f32[4096]{0:T(1024)} %param.48) | copy-start | bytes 49156
  509.8 9.4 %copy-start.23 = (f32[4096]{0:T(1024)S(1)}, f32[4096]{0:T(1024)}, u32[]{:S(2)}) copy-start(f32[4096]{0:T(1024)} %param.56) | copy-start | bytes 49156
  509.8 11.9 %copy-start.10 = (f32[256,128]{1,0:T(8,128)S(1)}, f32[256,128]{1,0:T(8,128)}, u32[]{:S(2)}) copy-start(f32[256,128]{1,0:T(8,128)} %first.1) | copy-start | bytes 393220
  509.8 11.9 %copy-start.14 = (f32[256,128]{1,0:T(8,128)S(1)}, f32[256,128]{1,0:T(8,128)}, u32[]{:S(2)}) copy-start(f32[256,128]{1,0:T(8,128)} %param.51) | copy-start | bytes 393220
  512.7 7.7 %copy-start.31 = (f32[5,128]{1,0:T(8,128)S(1)}, f32[5,128]{1,0:T(8,128)}, u32[]{:S(2)}) copy-start(f32[5,128]{1,0:T(8,128)} %param.46) | copy-start | bytes 7684
  512.7 7.7 %copy-start.32 = (f32[5,128]{1,0:T(8,128)S(1)}, f32[5,128]{1,0:T(8,128)}, u32[]{:S(2)}) copy-start(f32[5,128]{1,0:T(8,128)} %param.54) | copy-start | bytes 7684
  512.7 9.0 %copy-start.15 = (f32[256,128]{1,0:T(8,128)S(1)}, f32[256,128]{1,0:T(8,128)}, u32[]{:S(2)}) copy-start(f32[256,128]{1,0:T(8,128)} %param.59) | copy-start | bytes 393220
  514.7 8.5 %copy-start.3 = (f32[128,4096]{1,0:T(8,128)S(1)}, f32[128,4096]{1,0:T(8,128)}, u32[]{:S(2)}) copy-start(f32[128,4096]{1,0:T(8,128)} %param.39) | copy-start | bytes 6291460
  514.7 8.5 %copy-start.4 = (f32[128,4096]{1,0:T(8,128)S(1)}, f32[128,4096]{1,0:T(8,128)}, u32[]{:S(2)}) copy-start(f32[128,4096]{1,0:T(8,128)} %all-reduce.7.cloned.1.call-done) | copy-start | bytes 6291460
  514.7 8.5 %copy-start.8 = (f32[128,4096]{1,0:T(8,128)S(1)}, f32[128,4096]{1,0:T(8,128)}, u32[]{:S(2)}) copy-start(f32[128,4096]{1,0:T(8,128)} %param.47) | copy-start | bytes 6291460
  523.2 6.2 %copy-start.1 = (bf16[5,8192]{1,0:T(8,128)(2,1)S(1)}, bf16[5,8192]{1,0:T(8,128)(2,1)}, u32[]{:S(2)}) copy-start(bf16[5,8192]{1,0:T(8,128)(2,1)} %param.32) | copy-start | bytes 245764
Sparse Core Ops, SparseCore 0:
  10.3 37.5 all-gather.3
  199.7 44.5 reduce-scatter.1
  251.2 130.3 all-reduce.4
  386.1 101.9 all-reduce.6

commit v2 on v1

--- a/solution.py
+++ b/solution.py
@@ -34,6 +34,8 @@
 clip_norm = 0.1
 
 R_LSTM, R_FIRST, R_GRU, R_SECOND, R_MISC, R_EBIAS, R_END = 0, 1024, 1280, 2048, 2176, 2192, 2320
+R_PACK = 2560
+M_INPUT, M_STATE, M_LSTM, M_HEAD, M_OUT, M_SUMS = 1, 4, 7, 11, 12, 13
 
 NN = ((1,), (0,))
 NTR = ((1,), (1,))
@@ -68,7 +70,9 @@
 
 def body_main(
     mols,
+    own_rows,
     counts_s,
+    places,
     counts_col,
     flags_col,
     targets,
@@ -78,8 +82,8 @@
     edge_in_t,
     b_in_col,
     w_fwd,
-    w_back,
-    ebias,
+    w_nat,
+    ebias_parts,
     gru_t,
     gru_n,
     gbias_col,
@@ -106,14 +110,20 @@
     acc,
     dst_acc,
     gm,
+    gm_rel,
+    w_back,
     w_all,
     ds_all,
 ):
     atoms = mols * PAD
+    parts = len(w_fwd)
     total = jnp.int32(0)
     for m in range(mols):
         total = total + 2 * (counts_s[m] - 1)
     blocks = lax.div(total + (LB - 1), jnp.int32(LB))
+
+    def place(k):
+        return pl.ds(pl.multiple_of(places[k], own_rows), own_rows)
 
     live_col = 2.0 * (counts_col[...].astype(f32) - 1.0)
     below = (
@@ -126,8 +136,8 @@
 
     def prepare(b, carry):
         c = columns(b * LB, LB)
-        place = (lax.broadcasted_iota(jnp.int32, (mols, LB), 1) + b * LB).astype(f32)
-        mol_hot = ((place >= start_col) & (place < start_col + live_col)).astype(f32)
+        spot = (lax.broadcasted_iota(jnp.int32, (mols, LB), 1) + b * LB).astype(f32)
+        mol_hot = ((spot >= start_col) & (spot < start_col + live_col)).astype(f32)
         rows = mm(tab[...], mol_hot.astype(bf16))
         start_row = jnp.sum(mol_hot * start_col, axis=0, keepdims=True)
         mol_row = jnp.sum(
@@ -136,7 +146,7 @@
             keepdims=True,
         )
         valid = jnp.sum(mol_hot, axis=0, keepdims=True)
-        slot = place[:1] - start_row
+        slot = spot[:1] - start_row
         slot_hot = (lax.broadcasted_iota(jnp.int32, (EM, LB), 0).astype(f32) == slot).astype(f32)
         picked = [
             jnp.sum(rows[r * EM : (r + 1) * EM] * slot_hot, axis=0, keepdims=True)
@@ -162,7 +172,17 @@
 
     lax.fori_loop(0, blocks, prepare, 0)
 
-    b_high, b_low = split(ebias[...])
+    ebias = jnp.concatenate([part[...] for part in ebias_parts], axis=0)
+    b_high, b_low = split(ebias)
+
+    def turn(i, carry):
+        for k in range(parts):
+            w_back[:, pl.ds(pl.multiple_of(k * own_rows * H + i * H, H), H)] = jnp.transpose(
+                w_nat[k][:, columns(i * H, H)]
+            )
+        return carry
+
+    lax.fori_loop(0, own_rows, turn, 0)
     chunks = atoms // LB
 
     low[0] = nodes[...]
@@ -176,13 +196,14 @@
             src_o[layer, :, c] = source
             for h in range(EH):
                 z[h * H : (h + 1) * H, :] = hid_o[pl.ds(h, 1), c] * source
-            moved = mm(w_fwd[...], z[...])
+            moved = mm(jnp.concatenate([part[...] for part in w_fwd], axis=0), z[...])
             moved = moved + (mm(b_high, source) + mm(b_low, source))
             acc[...] += mm2(moved, hot_dst[:, c], NTR)
             return carry
 
         lax.fori_loop(0, blocks, move, 0)
-        msg[layer] = acc[...].astype(bf16)
+        for k in range(parts):
+            msg[layer, place(k), :] = acc[k * own_rows : (k + 1) * own_rows, :].astype(bf16)
 
         def update(k, carry, layer=layer):
             c = columns(k * LB, LB)
@@ -257,20 +278,20 @@
     pack[R_SECOND:R_MISC, :NT] = mm3(inner_s, d_pred_s, TN)
     misc = jnp.zeros((16, 128), f32)
     pack[R_MISC:R_EBIAS, :] = misc
-    pack[R_MISC + 11 : R_MISC + 12, :NT] = jnp.sum(d_pred, axis=0, keepdims=True)
-    pack[R_MISC + 12 : R_MISC + 13, :NT] = jnp.sum(
+    pack[R_MISC + M_OUT : R_MISC + M_OUT + 1, :NT] = jnp.sum(d_pred, axis=0, keepdims=True)
+    pack[R_MISC + M_OUT : R_MISC + M_OUT + 1, NT : 2 * NT] = jnp.sum(
         jnp.where(is_one, 0.0, d_pred), axis=0, keepdims=True
     )
-    pack[R_MISC + 13 : R_MISC + 14, :NT] = jnp.sum(
+    pack[R_MISC + M_OUT : R_MISC + M_OUT + 1, 2 * NT : 3 * NT] = jnp.sum(
         jnp.where(is_one, d_pred, 0.0), axis=0, keepdims=True
     )
-    pack[R_MISC + 14 : R_MISC + 15, 0:1] = loss
-    pack[R_MISC + 14 : R_MISC + 15, 1:2] = count
+    pack[R_MISC + M_SUMS : R_MISC + M_SUMS + 1, 0:1] = loss
+    pack[R_MISC + M_SUMS : R_MISC + M_SUMS + 1, 1:2] = count
     d_inner = mm3(d_pred_s, second_w, NTR)
     d_pre = d_inner * inner_sig * (1.0 + inner_pre * (1.0 - inner_sig))
     d_pre_s = split(d_pre)
     pack[R_FIRST:R_GRU, :] = mm3(query_s, d_pre_s, TN)
-    pack[R_MISC + 10 : R_MISC + 11, :] = jnp.sum(d_pre, axis=0, keepdims=True)
+    pack[R_MISC + M_HEAD : R_MISC + M_HEAD + 1, :] = jnp.sum(d_pre, axis=0, keepdims=True)
     d_query = mm3(d_pre_s, first_w, NTR)
     d_hidden, d_read = d_query[:, :H], d_query[:, H:]
     d_cell = zeros
@@ -303,7 +324,7 @@
     d_gates_sum = jnp.sum(d_gates_cat, axis=0, keepdims=True)
     for k in range(4):
         pack[R_LSTM + k * 256 : R_LSTM + (k + 1) * 256, :] = grad_lstm[:, k * H : (k + 1) * H]
-        pack[R_MISC + 6 + k : R_MISC + 7 + k, :] = d_gates_sum[:, k * H : (k + 1) * H]
+        pack[R_MISC + M_LSTM + k : R_MISC + M_LSTM + k + 1, :] = d_gates_sum[:, k * H : (k + 1) * H]
     left = jnp.concatenate(d_reads + [saved[s][7] for s in range(STEPS)], axis=0)
     left_s = split(left)
 
@@ -340,17 +361,19 @@
                 for q in range(3):
                     r = R_GRU + (half * 3 + q) * H
                     pack[r : r + H, :] += grad[:, q * H : (q + 1) * H]
-                    m = R_MISC + half * 3 + q
+                    m = R_MISC + M_INPUT + half * 3 + q
                     pack[m : m + 1, :] += sums[:, q * H : (q + 1) * H]
             return carry
 
         lax.fori_loop(0, chunks, back, 0)
+        for k in range(parts):
+            gm_rel[k * own_rows : (k + 1) * own_rows, :] = gm[place(k), :]
         if layer > 0:
-            bt_high, bt_low = split(jnp.transpose(ebias[...]))
+            bt_high, bt_low = split(jnp.transpose(ebias))
 
             def pull(b, carry, layer=layer):
                 c = columns(b * LB, LB)
-                grad = mm(gm[...], hot_dst[:, c])
+                grad = mm(gm_rel[...], hot_dst[:, c])
                 grad_low = grad.astype(bf16)
                 g_o[layer, :, c] = grad_low
                 hid = hid_o[:, c]
@@ -366,7 +389,7 @@
 
             def take(b, carry, layer=layer):
                 c = columns(b * LB, LB)
-                g_o[layer, :, c] = mm(gm[...], hot_dst[:, c]).astype(bf16)
+                g_o[layer, :, c] = mm(gm_rel[...], hot_dst[:, c]).astype(bf16)
                 return carry
 
             lax.fori_loop(0, blocks, take, 0)
@@ -381,52 +404,54 @@
         return carry
 
     lax.fori_loop(0, blocks, bias_sum, 0)
-    pack[R_EBIAS:R_END, :] = acc_b[...]
-
-
-def body_edges(mols, counts_s, w, src, g, hid, before, feat, out, grad_in, grid_z, grad_hid, acc):
-    part = pl.program_id(0)
+    for k in range(parts):
+        row = pl.multiple_of(R_EBIAS + places[k], 8)
+        pack[pl.ds(row, own_rows), :] = acc_b[k * own_rows : (k + 1) * own_rows, :]
+    pack[R_END:R_PACK, :] = jnp.zeros((R_PACK - R_END, 128), f32)
+
+
+def body_edges(mols, rels, last, counts_s, *refs):
+    n = len(rels)
+    ws, (src, g, hid) = refs[:n], refs[n : n + 3]
+    if last:
+        hid_before, before, feat = refs[n + 3 : n + 6]
+        outs, grad_in = refs[n + 6 : 2 * n + 6], refs[2 * n + 6]
+        built, acc, grad_hid = refs[2 * n + 7 :]
+    else:
+        outs, grad_hid = refs[n + 3 : 2 * n + 3], refs[2 * n + 3]
+        built, acc = refs[2 * n + 4 :]
     total = jnp.int32(0)
     for m in range(mols):
         total = total + 2 * (counts_s[m] - 1)
     blocks = lax.div(total + (LB - 1), jnp.int32(LB))
-    rows = w.shape[2] // H
-
-    def edges(b, carry):
-        c = columns(b * LB, LB)
-        base = part * rows
-        g0 = g[0, pl.ds(pl.multiple_of(base, rows), rows), c].astype(f32)
-        g1 = g[1, pl.ds(pl.multiple_of(base, rows), rows), c].astype(f32)
-        s0, s1 = src[0, :, c].astype(f32), src[1, :, c].astype(f32)
-        for i in range(rows):
-            grid_z[i * H : (i + 1) * H, :] = (g0[i : i + 1] * s0 + g1[i : i + 1] * s1).astype(bf16)
-        pulled = mm(w[0], grid_z[...])
-
-        @pl.when(part == 0)
-        def _():
-            grad_hid[:, c] = pulled
-
-        @pl.when(part > 0)
-        def _():
-            grad_hid[:, c] += pulled
-
-        product = mm(hid[:, c], grid_z[...], NTR)
-
-        @pl.when(b == 0)
-        def _():
-            acc[...] = product
-
-        @pl.when(b > 0)
-        def _():
-            acc[...] += product
-
-        return carry
-
-    lax.fori_loop(0, blocks, edges, 0)
-    out[0] = acc[...].astype(out.dtype)
-
-    @pl.when(part == pl.num_programs(0) - 1)
-    def _():
+    rows = ws[0].shape[1] // H
+
+    for q, rel in enumerate(rels):
+        acc[...] = jnp.zeros_like(acc)
+
+        def edges(b, carry, q=q, rel=rel):
+            c = columns(b * LB, LB)
+            g0 = g[0, rel * rows : (rel + 1) * rows, c].astype(f32)
+            g1 = g[1, rel * rows : (rel + 1) * rows, c].astype(f32)
+            s0, s1 = src[0, :, c].astype(f32), src[1, :, c].astype(f32)
+            for i in range(rows):
+                built[i * H : (i + 1) * H, :] = (g0[i : i + 1] * s0 + g1[i : i + 1] * s1).astype(
+                    bf16
+                )
+            pulled = mm(ws[q][...], built[...])
+            if q > 0:
+                grad_hid[:, c] += pulled
+            elif last:
+                grad_hid[:, c] = hid_before[:, c] + pulled
+            else:
+                grad_hid[:, c] = pulled
+            acc[...] += mm(hid[:, c], built[...], NTR)
+            return carry
+
+        lax.fori_loop(0, blocks, edges, 0)
+        outs[q][...] = acc[...].astype(outs[q].dtype)
+
+    if last:
         grad_in[...] = jnp.zeros_like(grad_in)
 
         def finish(b, carry):
@@ -439,15 +464,6 @@
             return carry
 
         lax.fori_loop(0, blocks, finish, 0)
-
-
-def split_biases(biases):
-    start = 0
-    pieces = []
-    for width in (EH, 6 * H, 4 * H, H, NT, 2 * NT):
-        pieces.append(biases[start : start + width])
-        start = start + width
-    return pieces
 
 
 def adamw(weight, grad, moment, second):
@@ -460,6 +476,68 @@
         moment_new,
         second_new,
     )
+
+
+def squares(x):
+    return jnp.sum(jnp.sum(x * x, axis=1, keepdims=True), axis=0, keepdims=True)
+
+
+def body_adamw(own_rows, place, own, pack, grad_in, edge_squares, *refs):
+    params, moments, seconds = refs[0:8], refs[8:16], refs[16:24]
+    outs = refs[24:48]
+    loss, count, norm, scale = refs[48:52]
+
+    def step(index, grad, at=...):
+        new = adamw(params[index][at], grad, moments[index][at], seconds[index][at])
+        for kind in range(3):
+            outs[kind * 8 + index][at] = new[kind]
+
+    @pl.when(pl.program_id(0) == 0)
+    def _():
+        sums = pack[R_MISC + M_SUMS : R_MISC + M_SUMS + 1, :]
+        total = (
+            edge_squares[:, 0:1]
+            + squares(grad_in[: EIN + 1, :])
+            + squares(pack[: R_MISC + M_SUMS, :])
+            + squares(pack[R_EBIAS:R_END, :])
+        )
+        for k in range(4):
+            total = total + squares(pack[R_LSTM + k * 2 * H : R_LSTM + k * 2 * H + H, :])
+        loss[...] = sums[:, 0:1]
+        count[...] = sums[:, 1:2]
+        grad_norm = jnp.sqrt(total) / sums[:, 1:2]
+        norm[...] = grad_norm
+        factor = jnp.minimum(1.0, clip_norm / grad_norm) / sums[:, 1:2]
+        scale[...] = jnp.broadcast_to(factor, scale.shape)
+        step(0, grad_in[:EIN, :] * factor)
+        step(2, pack[pl.ds(pl.multiple_of(R_EBIAS + place[0], 8), own_rows), :] * factor)
+        for half in range(2):
+            for q in range(3):
+                r = R_GRU + (half * 3 + q) * H
+                step(3, pack[r : r + H, :] * factor, (half, slice(None), slice(q * H, (q + 1) * H)))
+        for k in range(4):
+            r = R_LSTM + k * 2 * H
+            for block, start in ((0, 0), (1, H), (2, 0)):
+                step(
+                    4,
+                    pack[r + start : r + start + H, :] * factor,
+                    (slice(block * H, (block + 1) * H), slice(k * H, (k + 1) * H)),
+                )
+        step(5, pack[R_FIRST:R_GRU, :] * factor)
+        step(6, pack[R_SECOND:R_MISC, :NT] * factor)
+        bias = jnp.concatenate([grad_in[EIN : EIN + 1, :], pack[R_MISC + 1 : R_EBIAS, :]], axis=0)
+        step(7, bias * factor)
+
+    step(1, own[...] * scale[0:1, 0:1])
+
+
+def split_biases(biases):
+    start = 0
+    pieces = []
+    for width in (EH, 6 * H, 4 * H, H, NT, 2 * NT):
+        pieces.append(biases[start : start + width])
+        start = start + width
+    return pieces
 
 
 VM = pl.BlockSpec(memory_space=pltpu.VMEM)
@@ -486,18 +564,44 @@
 ):
     row = lax.axis_index("row")
     row_count = lax.axis_size("row")
+    mol = lax.axis_index("mol")
+    mol_bits = lax.axis_size("mol").bit_length() - 1
+    row_bits = row_count.bit_length() - 1
     mols = node_feats.shape[0]
     own_rows = edge_out.shape[1] // H
     atoms = mols * PAD
     space = -(-mols * LIVE // LB) * LB
     b_in, b_gru, c_lstm, c_head, c_out, offsets = split_biases(biases)
 
+    def row_swap(x, k):
+        return lax.ppermute(x, "row", [(i, i ^ k) for i in range(row_count)])
+
+    def mol_swap(x, bit):
+        return lax.ppermute(x, "mol", [(i, i ^ (1 << bit)) for i in range(2**mol_bits)])
+
+    def halve(x, swap, bit, send_type):
+        halves = x.reshape((2, x.shape[0] // 2) + x.shape[1:])
+        sent = lax.dynamic_index_in_dim(halves, 1 - bit, 0, False).astype(send_type)
+        kept = lax.dynamic_index_in_dim(halves, bit, 0, False)
+        return kept + swap(sent).astype(f32)
+
+    def double(x, swap, bit):
+        other = swap(x)
+        return jnp.concatenate(
+            [jnp.where(bit == 0, x, other), jnp.where(bit == 0, other, x)], axis=0
+        )
+
     out_low = edge_out.astype(bf16)
-    w_all = lax.all_gather(out_low, "row", axis=0)
-    ebias = lax.all_gather(edge_bias, "row", axis=0).reshape(H, H)
-    w4 = w_all.reshape(row_count, EH, own_rows, H)
-    w_fwd = w4.transpose(0, 2, 1, 3).reshape(H, EH * H)
-    w_back = w4.transpose(3, 0, 2, 1).reshape(H, H * EH)
+    parts, bias_parts = [out_low], [edge_bias.reshape(own_rows, H)]
+    for bit in range(row_bits):
+        for k in range(1 << bit):
+            parts.append(row_swap(parts[k], 1 << bit))
+            bias_parts.append(row_swap(bias_parts[k], 1 << bit))
+    places = jnp.stack([(row ^ k) * own_rows for k in range(row_count)]).astype(jnp.int32)
+    w_fwd = [
+        part.reshape(EH, own_rows, H).transpose(1, 0, 2).reshape(own_rows, EH * H)
+        for part in parts
+    ]
 
     ends = lax.dynamic_slice_in_dim(edge_ends, row * mols, mols, 1)
     feats = lax.dynamic_slice_in_dim(edge_feats, row * mols * EM, mols * EM, 1)
@@ -516,17 +620,31 @@
     edge_in_t = jnp.pad(edge_in, ((0, 3), (0, 0))).T
 
     sds = jax.ShapeDtypeStruct
+    n = row_count
+
+    def main(*refs):
+        at = 10
+        body_main(
+            mols,
+            own_rows,
+            *refs[:at],
+            refs[at : at + n],
+            refs[at + n : at + 2 * n],
+            refs[at + 2 * n : at + 3 * n],
+            *refs[at + 3 * n :],
+        )
+
     pack, src, g, hid, before, feat = pl.pallas_call(
-        functools.partial(body_main, mols),
+        main,
         out_shape=(
-            sds((R_END, 128), f32),
+            sds((R_PACK, 128), f32),
             sds((LAYERS, H, space), bf16),
             sds((LAYERS, H, space), bf16),
             sds((EH, space), bf16),
             sds((EH, space), f32),
             sds((8, space), f32),
         ),
-        in_specs=[SM] + [VM] * 21,
+        in_specs=[SM, SM] + [VM] * (18 + 3 * n),
         out_specs=(VM,) * 6,
         scratch_shapes=[
             pltpu.VMEM((H * EH, LB), bf16),
@@ -539,12 +657,15 @@
             pltpu.VMEM((H, atoms), f32),
             pltpu.VMEM((H, atoms), f32),
             pltpu.VMEM((H, atoms), bf16),
+            pltpu.VMEM((H, atoms), bf16),
+            pltpu.VMEM((H, H * EH), bf16),
             pltpu.VMEM((STEPS * mols, atoms), f32),
             pltpu.VMEM((STEPS * mols, atoms), f32),
         ],
         compiler_params=pltpu.CompilerParams(vmem_limit_bytes=60 * MIB),
     )(
         atom_counts,
+        places,
         atom_counts.reshape(mols, 1),
         dataset_flags.reshape(mols, 1),
         targets,
@@ -553,9 +674,9 @@
         nodes,
         edge_in_t,
         b_in.reshape(EH, 1),
-        w_fwd,
-        w_back,
-        ebias,
+        *w_fwd,
+        *parts,
+        *bias_parts,
         gru_low.transpose(0, 2, 1),
         gru_low,
         b_gru.reshape(2, 3 * H, 1),
@@ -567,58 +688,67 @@
         c_out.reshape(1, NT),
         offsets.reshape(2, NT),
     )
-    shared = lax.psum(pack, ("mol", "row"))
-
-    grad_out, grad_in = pl.pallas_call(
-        functools.partial(body_edges, mols),
-        out_shape=(sds((row_count, EH, own_rows * H), bf16), sds((8, EH), f32)),
-        grid=(row_count,),
-        in_specs=[SM, pl.BlockSpec((1, EH, own_rows * H), lambda q: (q, 0, 0))] + [VM] * 5,
-        out_specs=(pl.BlockSpec((1, EH, own_rows * H), lambda q: (q, 0, 0)), VM),
-        scratch_shapes=[
-            pltpu.VMEM((own_rows * H, LB), bf16),
-            pltpu.VMEM((EH, space), f32),
-            pltpu.VMEM((EH, own_rows * H), f32),
-        ],
-        compiler_params=pltpu.CompilerParams(vmem_limit_bytes=56 * MIB),
-    )(atom_counts, w_all, src, g, hid, before, feat)
-    own = lax.psum_scatter(grad_out, "row", scatter_dimension=0, tiled=False)
-    own = lax.psum(own.astype(f32), "mol")
-    grad_in = lax.psum(grad_in, ("mol", "row"))
-
-    misc = shared[R_MISC:R_EBIAS]
-    loss, total_count = misc[14, 0], misc[14, 1]
-    lstm_rows = shared[R_LSTM:R_FIRST].reshape(4, 2 * H, H).transpose(1, 0, 2).reshape(2 * H, 4 * H)
-    grad_lstm = jnp.concatenate([lstm_rows, lstm_rows[:H]], axis=0)
-    grad_gru = (
-        shared[R_GRU:R_SECOND].reshape(2, 3, H, H).transpose(0, 2, 1, 3).reshape(2, H, 3 * H)
+
+    far, near = tuple(range(n // 2, n)), tuple(range(n // 2))
+    part_scratch = [pltpu.VMEM((own_rows * H, LB), bf16), pltpu.VMEM((EH, own_rows * H), f32)]
+    params = pltpu.CompilerParams(vmem_limit_bytes=56 * MIB)
+    part_shape = sds((EH, own_rows * H), bf16)
+    *far_parts, grad_hid = pl.pallas_call(
+        functools.partial(body_edges, mols, far, False),
+        out_shape=(part_shape,) * len(far) + (sds((EH, space), f32),),
+        in_specs=[SM] + [VM] * (len(far) + 3),
+        out_specs=(VM,) * (len(far) + 1),
+        scratch_shapes=part_scratch,
+        compiler_params=params,
+    )(atom_counts, *(parts[k] for k in far), src, g, hid)
+    *near_parts, grad_in = pl.pallas_call(
+        functools.partial(body_edges, mols, near, True),
+        out_shape=(part_shape,) * len(near) + (sds((8, EH), f32),),
+        in_specs=[SM] + [VM] * (len(near) + 6),
+        out_specs=(VM,) * (len(near) + 1),
+        scratch_shapes=part_scratch + [pltpu.VMEM((EH, space), f32)],
+        compiler_params=params,
+    )(atom_counts, *(parts[k] for k in near), src, g, hid, grad_hid, before, feat)
+
+    row_bit = [(row >> bit) & 1 for bit in range(row_bits)]
+    mol_bit = [(mol >> bit) & 1 for bit in range(mol_bits)]
+    steps = [
+        (functools.partial(row_swap, k=1 << bit), row_bit[bit]) for bit in range(row_bits)
+    ] + [(functools.partial(mol_swap, bit=bit), mol_bit[bit]) for bit in range(mol_bits)]
+    for swap, bit in steps:
+        pack = halve(pack, swap, bit, f32)
+    for swap, bit in reversed(steps):
+        pack = double(pack, swap, bit)
+    for swap, bit in steps:
+        grad_in = grad_in + swap(grad_in)
+
+    slots = near_parts + far_parts
+    for bit in reversed(range(row_bits)):
+        k = 1 << bit
+        slots = [
+            slots[i].astype(f32) + row_swap(slots[i + k].astype(bf16), k).astype(f32)
+            for i in range(k)
+        ]
+    own = slots[0]
+    mol_steps = steps[row_bits:]
+    for swap, bit in mol_steps:
+        own = halve(own, swap, bit, bf16)
+    largest = jnp.maximum(jnp.max(jnp.abs(own)), 1e-30)
+    note = jnp.concatenate(
+        [jnp.sum(own * own).reshape(1, 1), largest.reshape(1, 1), jnp.zeros((1, 126), f32)], axis=1
     )
-    grad_bias = jnp.concatenate(
-        [
-            grad_in[EIN],
-            misc[:11].reshape(11 * H),
-            misc[11, :NT],
-            misc[12, :NT],
-            misc[13, :NT],
-        ]
-    )
-    ebias_rows = lax.dynamic_slice_in_dim(shared[R_EBIAS:R_END], row * own_rows, own_rows, 0)
-    sums = [
-        grad_in[:EIN],
-        own,
-        ebias_rows.reshape(own_rows * H),
-        grad_gru,
-        grad_lstm,
-        shared[R_FIRST:R_GRU],
-        shared[R_SECOND:R_MISC, :NT],
-        grad_bias,
-    ]
-    grads = [grad / total_count for grad in sums]
-    edge_squares = lax.psum(jnp.sum(grads[1] * grads[1]) + jnp.sum(grads[2] * grads[2]), "row")
-    replicated = grads[0:1] + grads[3:]
-    norm = jnp.sqrt(edge_squares + sum((jnp.sum(grad * grad) for grad in replicated)))
-    factor = jnp.minimum(1.0, clip_norm / norm)
-    params = (
+    own = (own * (16384.0 / largest)).astype(jnp.float16)
+    for swap, bit in reversed(mol_steps):
+        own = double(own, swap, bit)
+        note = double(note, swap, bit)
+    pieces = note.shape[0]
+    own = own.astype(f32).reshape(pieces, -1) * (note[:, 1:2] * (1.0 / 16384.0))
+    own = own.reshape(EH, own_rows * H)
+    edge_squares = jnp.broadcast_to(jnp.sum(note[:, 0]), (1, 128))
+    for swap, bit in steps[:row_bits]:
+        edge_squares = edge_squares + swap(edge_squares)
+
+    weights = [
         edge_in,
         edge_out,
         edge_bias,
@@ -627,18 +757,36 @@
         head_first,
         head_second,
         biases,
-    )
-    moments, seconds = moments_seconds[:8], moments_seconds[8:]
-    result = [
-        adamw(params[index], grads[index] * factor, moments[index], seconds[index])
-        for index in range(8)
     ]
-    return (
-        tuple(item[0] for item in result)
-        + tuple(item[1] for item in result)
-        + tuple(item[2] for item in result)
-        + (loss, total_count, norm)
-    )
+    states = []
+    for group in (weights, moments_seconds[:8], moments_seconds[8:]):
+        group = list(group)
+        group[2] = group[2].reshape(own_rows, H)
+        group[7] = jnp.pad(group[7], (0, 16 * 128 - group[7].shape[0])).reshape(16, 128)
+        states += group
+    grid = 4
+    block = pl.BlockSpec((EH // grid, own_rows * H), lambda i: (i, 0))
+
+    def state_specs():
+        return [block if index == 1 else VM for index in range(8)] * 3
+
+    shapes = [sds(state.shape, f32) for state in states]
+    results = pl.pallas_call(
+        functools.partial(body_adamw, own_rows),
+        grid=(grid,),
+        out_shape=tuple(shapes) + (sds((1, 1), f32),) * 3,
+        in_specs=[SM, block, VM, VM, VM] + state_specs(),
+        out_specs=tuple(state_specs()) + (VM,) * 3,
+        scratch_shapes=[pltpu.VMEM((8, 128), f32)],
+        compiler_params=params,
+    )(places, own, pack, grad_in, edge_squares, *states)
+    results = list(results)
+    for kind in range(3):
+        results[kind * 8 + 2] = results[kind * 8 + 2].reshape(own_rows * H)
+        results[kind * 8 + 7] = results[kind * 8 + 7].reshape(-1)[: biases.shape[0]]
+    for index in range(24, 27):
+        results[index] = results[index].reshape(())
+    return tuple(results)
 
 
 def solution(mesh):

time: 545 us -> 303 us (0.56)
  waiting for transfers between devices: 245 us -> 71.1 us
  blocking collectives: 53.5 us -> 0 us
  starting transfers between devices: 0.16 us -> 41.2 us
  local copies, waits for them, and re-layouts: 56.1 us -> 34.8 us
  between operations: 21.2 us -> 1.91 us
  other arithmetic: 40.4 us -> 24.1 us
    psum x2 -> x0, waiting for transfers between devices: 183 us -> none  [the longest x1 92.2 us: per_device(): shared = lax.psum(pack, ('mol', 'row'))]
    ppermute x0 -> x35, waiting for transfers between devices: none -> 71.1 us  [the longest x18 35.6 us: mol_swap(): lax.ppermute(x, 'mol', [(i, i ^ 1 << bit) for i in range(2 ** mol_bits)])]
    psum x2 -> x0, blocking collectives: 46.5 us -> none  [the longest x1 39.7 us: per_device(): grad_in = lax.psum(grad_in, ('mol', 'row'))]
    reduce_scatter x1 -> x0, waiting for transfers between devices: 43.5 us -> none  [per_device(): own = lax.psum_scatter(grad_out, 'row', scatter_dimension=0, tiled=False)]
    ppermute x0 -> x35, starting transfers between devices: none -> 41.2 us  [the longest x18 28.7 us: mol_swap(): lax.ppermute(x, 'mol', [(i, i ^ 1 << bit) for i in range(2 ** mol_bits)])]
    sub x8 -> x0, other arithmetic: 19.8 us -> none  [adamw(): weight - rate * (mean_hat / (jnp.sqrt(square_hat) + epsilon) + decay * we...]
    reshape x5 -> x6, local copies, waits for them, and re-layouts: 25.3 us -> 6.58 us  [the longest x4 4.67 us: per_device(): part.reshape(EH, own_rows, H).transpose(1, 0, 2).reshape(own_rows, EH * H)]
    all_gather x1 -> x0, waiting for transfers between devices: 17.5 us -> none  [per_device(): w_all = lax.all_gather(out_low, 'row', axis=0)]
  transfers between devices with their start and end apart: 4 -> 35, of which waited for: 4 -> 17; matrix products, arithmetic and copies ran while one was open for 6% -> 15% of each run, Pallas kernels for 0% -> 11%
where the time goes in v2:
time: 303 us; the launch traced here: 298 us
  Pallas kernels  125 us (41%)
  waiting for transfers between devices  71.1 us (23%)
  starting transfers between devices  41.2 us (14%)
  local copies, waits for them, and re-layouts  34.8 us (11%)
  other arithmetic  24.1 us (8%)
    pallas_call x1, Pallas kernels, per_device(): pl.pallas_call(main, out_shape=(sds((R_PACK, 128), f32), sds((LAYERS, H,...  79.1 us
    ppermute x18, waiting for transfers between devices, mol_swap(): lax.ppermute(x, 'mol', [(i, i ^ 1 << bit) for i in range(2 ** mol_bits)])  35.6 us
    ppermute x17, waiting for transfers between devices, row_swap(): return lax.ppermute(x, 'row', [(i, i ^ k) for i in range(row_count)])  35.4 us
    ppermute x18, starting transfers between devices, mol_swap(): lax.ppermute(x, 'mol', [(i, i ^ 1 << bit) for i in range(2 ** mol_bits)])  28.7 us
    pallas_call x1, Pallas kernels, per_device(): pl.pallas_call(functools.partial(body_edges, mols, near, True), out_shape...  17.4 us
    pallas_call x1, Pallas kernels, per_device(): pl.pallas_call(functools.partial(body_edges, mols, far, False), out_shape...  16.5 us
    unnamed x61, local copies, waits for them, and re-layouts  15.9 us
    ppermute x17, starting transfers between devices, row_swap(): return lax.ppermute(x, 'row', [(i, i ^ k) for i in range(row_count)])  12.5 us
  transfers between devices with their start and end apart: 35, of which 17 were waited for; matrix products, arithmetic and copies ran while one was open for 15% of the time, Pallas kernels for 11%

profile of v2, /device:TPU:0, one launch (start us, length us, event | category | flops | bytes accessed | tf_op | source)
XLA Modules:
  0.0 298.3 jit_solution(2674141440051050915)
XLA Ops:
  0.7 1.8 convert_element_type.70.refs_14_.refs_0_
  3.1 2.6 collective-permute-start.1
  9.1 1.8 collective-permute-start.2
  15.2 1.7 convert_element_type.72.refs_23_
  18.3 1.4 copy.136.refs_9_
  20.5 1.5 copy.151
  29.4 1.4 copy.152
  32.0 1.4 copy.153
  34.7 17.8 %collective-permute-done.2.refs_17_.refs_1_ = bf16[128,4096]{1,0:T(8,128)(2,1)} collective-permute-done((bf16[128,4096]{1,0:T(8,128)(2,1)}, bf16[128,4096]{1,0:T(8,128)(2,1)}, u32[]{:S(2)}, u32[]{:S(2)}) %collective-permute-start.2) | collective-permute-done | bytes 1048608 | tf_op jit(solution)/shard_map/ppermute | solution.py:577
  52.5 1.4 copy.154
  55.7 79.1 %shard_map.502 = (f32[2560,128]{1,0:T(8,128)}, bf16[2,128,1792]{2,1,0:T(8,128)(2,1)}, bf16[2,128,1792]{2,1,0:T(8,128)(2,1)}, bf16[128,1792]{1,0:T(8,128)(2,1)}, f32[128,1792]{1,0:T(8,128)}, /*index=5*/f32[8,1792]{1,0:T(8,128)}) custom-call(s32[32]{0:T(128)} %counts_s.3, s32[4]{0:T(128)} %pad_add_fusion.refs_1_.place, s32[32,1]{1,0:T(8,128)} %copy.132.refs_2_, ...), custom_call_target="tpu_custom_call" | custom-call | tf_op jit(solution)/shard_map/pallas_call | solution.py:637
  136.1 16.5 %shard_map.503 = (bf16[128,4096]{1,0:T(8,128)(2,1)}, bf16[128,4096]{1,0:T(8,128)(2,1)}, f32[128,1792]{1,0:T(8,128)}) custom-call(s32[32]{0:T(128)} %counts_s.3, bf16[128,4096]{1,0:T(8,128)(2,1)} %collective-permute-done.1.refs_16_.refs_0_, bf16[128,4096]{1,0:T(8,128)(2,1)} %collective-permute-done.2.refs_17_.refs_1_, ...), custom_call_target="tpu_custom_call" | custom-call | tf_op jit(solution)/shard_map/pallas_call | solution.py:696
  152.5 1.8 collective-permute-start.7
  155.4 1.8 collective-permute-start.6
  157.1 17.4 %shard_map.504 = (bf16[128,4096]{1,0:T(8,128)(2,1)}, bf16[128,4096]{1,0:T(8,128)(2,1)}, f32[8,128]{1,0:T(8,128)}) custom-call(s32[32]{0:T(128)} %counts_s.3, bf16[128,4096]{1,0:T(8,128)(2,1)} %copy-done.3, bf16[128,4096]{1,0:T(8,128)(2,1)} %collective-permute-done.refs_15_.refs_1_, bf16[2,128,1792]{2,1,0:T(8,128)(2,1)} %get-tuple-element.66.refs_2_, ...), custom_call_target="tpu_custom_call" | custom-call | tf_op jit(solution)/shard_map/pallas_call | solution.py:704
  174.5 11.2 %collective-permute-done.19 = f32[640,128]{1,0:T(8,128)S(1)} collective-permute-done((f32[640,128]{1,0:T(8,128)}, f32[640,128]{1,0:T(8,128)S(1)}, u32[]{:S(2)}, u32[]{:S(2)}) %collective-permute-start.19) | collective-permute-done | bytes 327712 | tf_op jit(solution)/shard_map/ppermute | solution.py:577
  185.8 1.9 collective-permute-start.20
  187.6 2.4 add_convert_fusion
  191.3 1.9 collective-permute-start.21
  193.2 2.6 collective-permute-done.21
  195.9 2.9 collective-permute-start.22
  198.7 2.1 collective-permute-done.22
  200.8 2.9 collective-permute-start.23
  203.7 2.1 collective-permute-done.23
  205.8 2.0 collective-permute-done.6
  208.8 2.0 convert_add_fusion
  210.8 1.8 collective-permute-start.9
  212.7 1.6 collective-permute-start.24
  215.7 3.3 %collective-permute-done.29 = f32[8,128]{1,0:T(8,128)S(1)} collective-permute-done((f32[8,128]{1,0:T(8,128)S(1)}, f32[8,128]{1,0:T(8,128)S(1)}, u32[]{:S(2)}, u32[]{:S(2)}) %collective-permute-start.29) | collective-permute-done | bytes 4128 | tf_op jit(solution)/shard_map/ppermute | solution.py:577
  219.5 5.1 %collective-permute-done.30 = f32[8,128]{1,0:T(8,128)S(1)} collective-permute-done((f32[8,128]{1,0:T(8,128)S(1)}, f32[8,128]{1,0:T(8,128)S(1)}, u32[]{:S(2)}, u32[]{:S(2)}) %collective-permute-start.30) | collective-permute-done | bytes 4128 | tf_op jit(solution)/shard_map/ppermute | solution.py:580
  224.6 1.8 collective-permute-start.31
  226.4 1.6 collective-permute-start.25
  231.1 2.6 collective-permute-start.32
  236.0 3.3 %collective-permute-start.11 = (bf16[16,4096]{1,0:T(8,128)(2,1)S(1)}, bf16[16,4096]{1,0:T(8,128)(2,1)S(1)}, u32[]{:S(2)}, u32[]{:S(2)}) collective-permute-start(bf16[16,4096]{1,0:T(8,128)(2,1)S(1)} %fusion.2), channel_id=1, source_target_pairs={{0,16},{4,20},{8,24},{12,28},{16,0},{20,4},{24,8},{28,12},{1,17},{... | collective-permute-start | bytes 393224 | tf_op jit(solution)/shard_map/ppermute | solution.py:580
  239.3 1.6 collective-permute-start.26
  245.6 1.6 collective-permute-start.15
  247.3 2.8 collective-permute-done.15
  251.1 3.4 %collective-permute-done.16 = f32[2,128]{1,0:T(2,128)S(1)} collective-permute-done((f32[2,128]{1,0:T(2,128)S(1)}, f32[2,128]{1,0:T(2,128)S(1)}, u32[]{:S(2)}, u32[]{:S(2)}) %collective-permute-start.16) | collective-permute-done | bytes 1056 | tf_op jit(solution)/shard_map/ppermute | solution.py:580
  255.2 1.6 collective-permute-start.12
  259.5 2.5 collective-permute-done.12
  264.0 4.6 %collective-permute-done.13 = f16[32,4096]{1,0:T(8,128)(2,1)S(1)} collective-permute-done((f16[32,4096]{1,0:T(8,128)(2,1)S(1)}, f16[32,4096]{1,0:T(8,128)(2,1)S(1)}, u32[]{:S(2)}, u32[]{:S(2)}) %collective-permute-start.13) | collective-permute-done | bytes 262176 | tf_op jit(solution)/shard_map/ppermute | solution.py:580
  268.8 1.5 collective-permute-start.14
  272.9 6.7 %collective-permute-done.14 = f16[64,4096]{1,0:T(8,128)(2,1)S(1)} collective-permute-done((f16[64,4096]{1,0:T(8,128)(2,1)S(1)}, f16[64,4096]{1,0:T(8,128)(2,1)S(1)}, u32[]{:S(2)}, u32[]{:S(2)}) %collective-permute-start.14) | collective-permute-done | bytes 524320 | tf_op jit(solution)/shard_map/ppermute | solution.py:580
  279.9 1.6 convert_multiply_fusion.own
  281.5 12.2 %shard_map.505 = (f32[5,128]{1,0:T(8,128)}, f32[128,4096]{1,0:T(8,128)}, f32[32,128]{1,0:T(8,128)}, f32[2,128,384]{2,1,0:T(8,128)}, f32[384,512]{1,0:T(8,128)}, ...) custom-call(s32[4]{0:T(128)} %pad_add_fusion.refs_1_.place, ...), custom_call_target="tpu_custom_call" | custom-call | tf_op jit(solution)/shard_map/pallas_call | solution.py:774
  293.7 1.5 copy.143
  295.2 1.5 copy.144
  296.7 1.5 copy.145
  (175 shorter events, 47.5 us)
Async XLA Ops:
  0.7 8.4 %copy-start = (bf16[5,8192]{1,0:T(8,128)(2,1)S(1)}, bf16[5,8192]{1,0:T(8,128)(2,1)}, u32[]{:S(2)}) copy-start(bf16[5,8192]{1,0:T(8,128)(2,1)} %param.32) | copy-start | bytes 245764
  0.7 7.4 %copy-start.9 = (f32[1572]{0:T(1024)S(1)}, f32[1572]{0:T(1024)}, u32[]{:S(2)}) copy-start(f32[1572]{0:T(1024)} %param.45) | copy-start | bytes 18868
  0.7 10.2 %copy-start.8 = (s32[2,128,64]{1,2,0:T(8,128)S(1)}, s32[2,128,64]{1,2,0:T(8,128)}, u32[]{:S(2)}) copy-start(s32[2,128,64]{1,2,0:T(8,128)} %param.33) | copy-start | bytes 196612
  2.5 11.2 %copy-start.3 = (bf16[128,4096]{1,0:T(8,128)(2,1)}, bf16[128,4096]{1,0:T(8,128)(2,1)S(1)}, u32[]{:S(2)}) copy-start(bf16[128,4096]{1,0:T(8,128)(2,1)S(1)} %convert_element_type.70.refs_14_.refs_0_) | copy-start | bytes 3145732
  2.5 8.7 %copy-start.10 = (f32[5,128]{1,0:T(8,128)S(1)}, f32[5,128]{1,0:T(8,128)}, u32[]{:S(2)}) copy-start(f32[5,128]{1,0:T(8,128)} %refs_0_.3) | copy-start | bytes 7684
  2.5 10.0 %copy-start.2 = (f32[128,4096]{1,0:T(8,128)S(1)}, f32[128,4096]{1,0:T(8,128)}, u32[]{:S(2)}) copy-start(f32[128,4096]{1,0:T(8,128)} %refs_1_.1) | copy-start | bytes 6291460
  2.6 6.6 %collective-permute-start = (bf16[128,4096]{1,0:T(8,128)(2,1)S(1)}, bf16[128,4096]{1,0:T(8,128)(2,1)}, u32[]{:S(2)}, u32[]{:S(2)}) collective-permute-start(bf16[128,4096]{1,0:T(8,128)(2,1)S(1)} %convert_element_type.70.refs_14_.refs_0_), channel_id=1, source_target_pairs={{0,1},{1,0},{2,3},{3,2},{4,5},{5,4},{6,7},{7,6},{8,9},{9,8},{10,11... | collective-permute-start | bytes 3145736 | tf_op jit(solution)/shard_map/ppermute | solution.py:577
  3.1 29.0 %collective-permute-start.1 = (bf16[128,4096]{1,0:T(8,128)(2,1)S(1)}, bf16[128,4096]{1,0:T(8,128)(2,1)}, u32[]{:S(2)}, u32[]{:S(2)}) collective-permute-start(bf16[128,4096]{1,0:T(8,128)(2,1)S(1)} %convert_element_type.70.refs_14_.refs_0_), channel_id=1, source_target_pairs={{0,2},{1,3},{2,0},{3,1},{4,6},{5,7},{6,4},{7,5},{8,10},{9,11},{10,... | collective-permute-start | bytes 3145736 | tf_op jit(solution)/shard_map/ppermute | solution.py:577
  5.6 8.7 %collective-permute-start.3 = (f32[32,128]{1,0:T(8,128)S(1)}, f32[32,128]{1,0:T(8,128)S(1)}, u32[]{:S(2)}, u32[]{:S(2)}) collective-permute-start(f32[32,128]{1,0:T(8,128)S(1)} %bitcast.159), channel_id=1, source_target_pairs={{0,1},{1,0},{2,3},{3,2},{4,5},{5,4},{6,7},{7,6},{8,9},{9,8},{10,11... | collective-permute-start | bytes 49160 | tf_op jit(solution)/shard_map/ppermute | solution.py:577
  5.8 49.3 %collective-permute-start.4 = (f32[32,128]{1,0:T(8,128)S(1)}, f32[32,128]{1,0:T(8,128)S(1)}, u32[]{:S(2)}, u32[]{:S(2)}) collective-permute-start(f32[32,128]{1,0:T(8,128)S(1)} %bitcast.160), channel_id=1, source_target_pairs={{0,2},{1,3},{2,0},{3,1},{4,6},{5,7},{6,4},{7,5},{8,10},{9,11},{10,... | collective-permute-start | bytes 49160 | tf_op jit(solution)/shard_map/ppermute | solution.py:577
  9.1 43.4 %collective-permute-start.2 = (bf16[128,4096]{1,0:T(8,128)(2,1)}, bf16[128,4096]{1,0:T(8,128)(2,1)}, u32[]{:S(2)}, u32[]{:S(2)}) collective-permute-start(bf16[128,4096]{1,0:T(8,128)(2,1)} %collective-permute-done.refs_15_.refs_1_), channel_id=1, source_target_pairs={{0,2},{1,3},{2,0},{3,1},{4,6},{5,7},{6,4},{7,5},{8,10},{9,11},{10,... | collective-permute-start | bytes 3145736 | tf_op jit(solution)/shard_map/ppermute | solution.py:577
  12.5 7.2 %copy-start.15 = (f32[128,12]{0,1:T(8,128)S(1)}, f32[128,12]{0,1:T(8,128)}, u32[]{:S(2)}) copy-start(f32[128,12]{0,1:T(8,128)} %param.44) | copy-start | bytes 18436
  14.3 8.8 %copy-start.11 = (f32[32,128]{1,0:T(8,128)}, f32[32,128]{1,0:T(8,128)S(1)}, u32[]{:S(2)}) copy-start(f32[32,128]{1,0:T(8,128)S(1)} %collective-permute-done.3.refs_19_) | copy-start | bytes 49156
  14.3 40.8 %collective-permute-start.5 = (f32[32,128]{1,0:T(8,128)S(1)}, f32[32,128]{1,0:T(8,128)S(1)}, u32[]{:S(2)}, u32[]{:S(2)}) collective-permute-start(f32[32,128]{1,0:T(8,128)S(1)} %collective-permute-done.3.refs_19_), channel_id=1, source_target_pairs={{0,2},{1,3},{2,0},{3,1},{4,6},{5,7},{6,4},{7,5},{8,10},{9,11},{10,... | collective-permute-start | bytes 49160 | tf_op jit(solution)/shard_map/ppermute | solution.py:577
  136.0 18.3 %collective-permute-start.18 = (f32[1280,128]{1,0:T(8,128)S(1)}, f32[1280,128]{1,0:T(8,128)S(1)}, u32[]{:S(2)}, u32[]{:S(2)}) collective-permute-start(f32[1280,128]{1,0:T(8,128)S(1)} %dynamic-slice_bitcast_fusion), channel_id=1, source_target_pairs={{0,1},{1,0},{2,3},{3,2},{4,5},{5,4},{6,7},{7,6},{8,9},{9,8},{10,11... | collective-permute-start | bytes 1966088 | tf_op jit(solution)/shard_map/ppermute | solution.py:577
  136.0 18.2 %copy-start.4 = (f32[2560,128]{1,0:T(8,128)S(1)}, f32[2560,128]{1,0:T(8,128)}, u32[]{:S(2)}) copy-start(f32[2560,128]{1,0:T(8,128)} %get-tuple-element.76) | copy-start | bytes 3932164
  152.5 35.1 %collective-permute-start.7 = (bf16[128,4096]{1,0:T(8,128)(2,1)}, bf16[128,4096]{1,0:T(8,128)(2,1)S(1)}, u32[]{:S(2)}, u32[]{:S(2)}) collective-permute-start(bf16[128,4096]{1,0:T(8,128)(2,1)} %get-tuple-element.75), channel_id=1, source_target_pairs={{0,2},{1,3},{2,0},{3,1},{4,6},{5,7},{6,4},{7,5},{8,10},{9,11},{10,... | collective-permute-start | bytes 3145736 | tf_op jit(solution)/shard_map/ppermute | solution.py:577
  155.1 30.6 %collective-permute-start.19 = (f32[640,128]{1,0:T(8,128)}, f32[640,128]{1,0:T(8,128)S(1)}, u32[]{:S(2)}, u32[]{:S(2)}) collective-permute-start(f32[640,128]{1,0:T(8,128)} %dynamic-slice_bitcast_fusion.1), channel_id=1, source_target_pairs={{0,2},{1,3},{2,0},{3,1},{4,6},{5,7},{6,4},{7,5},{8,10},{9,11},{10,... | collective-permute-start | bytes 983048 | tf_op jit(solution)/shard_map/ppermute | solution.py:577
  155.4 52.4 %collective-permute-start.6 = (bf16[128,4096]{1,0:T(8,128)(2,1)}, bf16[128,4096]{1,0:T(8,128)(2,1)S(1)}, u32[]{:S(2)}, u32[]{:S(2)}) collective-permute-start(bf16[128,4096]{1,0:T(8,128)(2,1)} %get-tuple-element.73), channel_id=1, source_target_pairs={{0,2},{1,3},{2,0},{3,1},{4,6},{5,7},{6,4},{7,5},{8,10},{9,11},{10,... | collective-permute-start | bytes 3145736 | tf_op jit(solution)/shard_map/ppermute | solution.py:577
  185.8 5.5 %collective-permute-start.20 = (f32[320,128]{1,0:T(8,128)S(1)}, f32[320,128]{1,0:T(8,128)S(1)}, u32[]{:S(2)}, u32[]{:S(2)}) collective-permute-start(f32[320,128]{1,0:T(8,128)S(1)} %dynamic-slice_bitcast_fusion.2), channel_id=1, source_target_pairs={{0,4},{4,0},{8,12},{12,8},{16,20},{20,16},{24,28},{28,24},{1,5},{5... | collective-permute-start | bytes 491528 | tf_op jit(solution)/shard_map/ppermute | solution.py:580
  190.1 17.7 %collective-permute-start.8 = (bf16[128,4096]{1,0:T(8,128)(2,1)}, bf16[128,4096]{1,0:T(8,128)(2,1)S(1)}, u32[]{:S(2)}, u32[]{:S(2)}) collective-permute-start(bf16[128,4096]{1,0:T(8,128)(2,1)} %add_convert_fusion), channel_id=1, source_target_pairs={{0,1},{1,0},{2,3},{3,2},{4,5},{5,4},{6,7},{7,6},{8,9},{9,8},{10,11... | collective-permute-start | bytes 3145736 | tf_op jit(solution)/shard_map/ppermute | solution.py:577
  191.3 4.5 %collective-permute-start.21 = (f32[160,128]{1,0:T(8,128)S(1)}, f32[160,128]{1,0:T(8,128)S(1)}, u32[]{:S(2)}, u32[]{:S(2)}) collective-permute-start(f32[160,128]{1,0:T(8,128)S(1)} %dynamic-slice_bitcast_fusion.3), channel_id=1, source_target_pairs={{0,8},{4,12},{8,0},{12,4},{16,24},{20,28},{24,16},{28,20},{1,9},{5... | collective-permute-start | bytes 245768 | tf_op jit(solution)/shard_map/ppermute | solution.py:580
  195.9 5.0 %collective-permute-start.22 = (f32[80,128]{1,0:T(8,128)S(1)}, f32[80,128]{1,0:T(8,128)S(1)}, u32[]{:S(2)}, u32[]{:S(2)}) collective-permute-start(f32[80,128]{1,0:T(8,128)S(1)} %dynamic-slice_bitcast_fusion.4), channel_id=1, source_target_pairs={{0,16},{4,20},{8,24},{12,28},{16,0},{20,4},{24,8},{28,12},{1,17},{... | collective-permute-start | bytes 122888 | tf_op jit(solution)/shard_map/ppermute | solution.py:580
  200.8 5.0 %collective-permute-start.23 = (f32[80,128]{1,0:T(8,128)S(1)}, f32[80,128]{1,0:T(8,128)S(1)}, u32[]{:S(2)}, u32[]{:S(2)}) collective-permute-start(f32[80,128]{1,0:T(8,128)S(1)} %bitcast_add_fusion.7), channel_id=1, source_target_pairs={{0,16},{4,20},{8,24},{12,28},{16,0},{20,4},{24,8},{28,12},{1,17},{... | collective-permute-start | bytes 122888 | tf_op jit(solution)/shard_map/ppermute | solution.py:580
  210.8 18.9 %copy-start.20 = (f32[1572]{0:T(1024)S(1)}, f32[1572]{0:T(1024)}, u32[]{:S(2)}) copy-start(f32[1572]{0:T(1024)} %param.61) | copy-start | bytes 18868
  210.8 17.2 %collective-permute-start.9 = (bf16[64,4096]{1,0:T(8,128)(2,1)S(1)}, bf16[64,4096]{1,0:T(8,128)(2,1)}, u32[]{:S(2)}, u32[]{:S(2)}) collective-permute-start(bf16[64,4096]{1,0:T(8,128)(2,1)S(1)} %fusion), channel_id=1, source_target_pairs={{0,4},{4,0},{8,12},{12,8},{16,20},{20,16},{24,28},{28,24},{1,5},{5... | collective-permute-start | bytes 1572872 | tf_op jit(solution)/shard_map/ppermute | solution.py:580
  212.7 13.7 %collective-permute-start.24 = (f32[160,128]{1,0:T(8,128)S(1)}, f32[160,128]{1,0:T(8,128)S(1)}, u32[]{:S(2)}, u32[]{:S(2)}) collective-permute-start(f32[160,128]{1,0:T(8,128)S(1)} %pad_maximum_fusion.7), channel_id=1, source_target_pairs={{0,8},{4,12},{8,0},{12,4},{16,24},{20,28},{24,16},{28,20},{1,9},{5... | collective-permute-start | bytes 245768 | tf_op jit(solution)/shard_map/ppermute | solution.py:580
  214.2 1.2 collective-permute-start.28
  215.4 3.6 %collective-permute-start.29 = (f32[8,128]{1,0:T(8,128)S(1)}, f32[8,128]{1,0:T(8,128)S(1)}, u32[]{:S(2)}, u32[]{:S(2)}) collective-permute-start(f32[8,128]{1,0:T(8,128)S(1)} %add.146), channel_id=1, source_target_pairs={{0,2},{1,3},{2,0},{3,1},{4,6},{5,7},{6,4},{7,5},{8,10},{9,11},{10,... | collective-permute-start | bytes 12296 | tf_op jit(solution)/shard_map/ppermute | solution.py:577
  219.0 5.6 %collective-permute-start.30 = (f32[8,128]{1,0:T(8,128)S(1)}, f32[8,128]{1,0:T(8,128)S(1)}, u32[]{:S(2)}, u32[]{:S(2)}) collective-permute-start(f32[8,128]{1,0:T(8,128)S(1)} %add.147), channel_id=1, source_target_pairs={{0,4},{4,0},{8,12},{12,8},{16,20},{20,16},{24,28},{28,24},{1,5},{5... | collective-permute-start | bytes 12296 | tf_op jit(solution)/shard_map/ppermute | solution.py:580
  224.6 6.5 %collective-permute-start.31 = (f32[8,128]{1,0:T(8,128)S(1)}, f32[8,128]{1,0:T(8,128)S(1)}, u32[]{:S(2)}, u32[]{:S(2)}) collective-permute-start(f32[8,128]{1,0:T(8,128)S(1)} %add.148), channel_id=1, source_target_pairs={{0,8},{4,12},{8,0},{12,4},{16,24},{20,28},{24,16},{28,20},{1,9},{5... | collective-permute-start | bytes 12296 | tf_op jit(solution)/shard_map/ppermute | solution.py:580
  226.4 7.3 %collective-permute-start.25 = (f32[320,128]{1,0:T(8,128)S(1)}, f32[320,128]{1,0:T(8,128)}, u32[]{:S(2)}, u32[]{:S(2)}) collective-permute-start(f32[320,128]{1,0:T(8,128)S(1)} %pad_maximum_fusion.6), channel_id=1, source_target_pairs={{0,4},{4,0},{8,12},{12,8},{16,20},{20,16},{24,28},{28,24},{1,5},{5... | collective-permute-start | bytes 491528 | tf_op jit(solution)/shard_map/ppermute | solution.py:580
  229.2 12.3 %copy-start.18 = (f32[128,12]{0,1:T(8,128)S(1)}, f32[128,12]{0,1:T(8,128)}, u32[]{:S(2)}) copy-start(f32[128,12]{0,1:T(8,128)} %param.52) | copy-start | bytes 18436
  229.2 13.1 %copy-start.19 = (f32[128,12]{0,1:T(8,128)S(1)}, f32[128,12]{0,1:T(8,128)}, u32[]{:S(2)}) copy-start(f32[128,12]{0,1:T(8,128)} %param.60) | copy-start | bytes 18436
  229.2 6.6 %collective-permute-start.10 = (bf16[32,4096]{1,0:T(8,128)(2,1)S(1)}, bf16[32,4096]{1,0:T(8,128)(2,1)S(1)}, u32[]{:S(2)}, u32[]{:S(2)}) collective-permute-start(bf16[32,4096]{1,0:T(8,128)(2,1)S(1)} %fusion.1), channel_id=1, source_target_pairs={{0,8},{4,12},{8,0},{12,4},{16,24},{20,28},{24,16},{28,20},{1,9},{5... | collective-permute-start | bytes 786440 | tf_op jit(solution)/shard_map/ppermute | solution.py:580
  231.1 11.9 %collective-permute-start.32 = (f32[8,128]{1,0:T(8,128)S(1)}, f32[8,128]{1,0:T(8,128)S(1)}, u32[]{:S(2)}, u32[]{:S(2)}) collective-permute-start(f32[8,128]{1,0:T(8,128)S(1)} %add.149), channel_id=1, source_target_pairs={{0,16},{4,20},{8,24},{12,28},{16,0},{20,4},{24,8},{28,12},{1,17},{... | collective-permute-start | bytes 12296 | tf_op jit(solution)/shard_map/ppermute | solution.py:580
  236.0 7.6 %collective-permute-start.11 = (bf16[16,4096]{1,0:T(8,128)(2,1)S(1)}, bf16[16,4096]{1,0:T(8,128)(2,1)S(1)}, u32[]{:S(2)}, u32[]{:S(2)}) collective-permute-start(bf16[16,4096]{1,0:T(8,128)(2,1)S(1)} %fusion.2), channel_id=1, source_target_pairs={{0,16},{4,20},{8,24},{12,28},{16,0},{20,4},{24,8},{28,12},{1,17},{... | collective-permute-start | bytes 393224 | tf_op jit(solution)/shard_map/ppermute | solution.py:580
  239.3 7.9 %collective-permute-start.26 = (f32[640,128]{1,0:T(8,128)S(1)}, f32[640,128]{1,0:T(8,128)S(1)}, u32[]{:S(2)}, u32[]{:S(2)}) collective-permute-start(f32[640,128]{1,0:T(8,128)S(1)} %pad_maximum_fusion.4), channel_id=1, source_target_pairs={{0,2},{1,3},{2,0},{3,1},{4,6},{5,7},{6,4},{7,5},{8,10},{9,11},{10,... | collective-permute-start | bytes 983048 | tf_op jit(solution)/shard_map/ppermute | solution.py:577
  245.6 4.4 %collective-permute-start.15 = (f32[1,128]{1,0:T(1,128)S(1)}, f32[1,128]{1,0:T(1,128)S(1)}, u32[]{:S(2)}, u32[]{:S(2)}) collective-permute-start(f32[1,128]{1,0:T(1,128)S(1)} %bitcast_maximum_fusion), channel_id=1, source_target_pairs={{0,16},{4,20},{8,24},{12,28},{16,0},{20,4},{24,8},{28,12},{1,17},{... | collective-permute-start | bytes 1544 | tf_op jit(solution)/shard_map/ppermute | solution.py:580
  250.8 3.6 %collective-permute-start.16 = (f32[2,128]{1,0:T(2,128)S(1)}, f32[2,128]{1,0:T(2,128)S(1)}, u32[]{:S(2)}, u32[]{:S(2)}) collective-permute-start(f32[2,128]{1,0:T(2,128)S(1)} %pad_maximum_fusion.10), channel_id=1, source_target_pairs={{0,8},{4,12},{8,0},{12,4},{16,24},{20,28},{24,16},{28,20},{1,9},{5... | collective-permute-start | bytes 3080 | tf_op jit(solution)/shard_map/ppermute | solution.py:580
  250.9 11.2 %collective-permute-start.27 = (f32[1280,128]{1,0:T(8,128)S(1)}, f32[1280,128]{1,0:T(8,128)S(1)}, u32[]{:S(2)}, u32[]{:S(2)}) collective-permute-start(f32[1280,128]{1,0:T(8,128)S(1)} %pad_maximum_fusion.1), channel_id=1, source_target_pairs={{0,1},{1,0},{2,3},{3,2},{4,5},{5,4},{6,7},{7,6},{8,9},{9,8},{10,11... | collective-permute-start | bytes 1966088 | tf_op jit(solution)/shard_map/ppermute | solution.py:577
  254.5 3.7 %collective-permute-start.17 = (f32[4,128]{1,0:T(4,128)S(1)}, f32[4,128]{1,0:T(4,128)S(1)}, u32[]{:S(2)}, u32[]{:S(2)}) collective-permute-start(f32[4,128]{1,0:T(4,128)S(1)} %pad_maximum_fusion.9), channel_id=1, source_target_pairs={{0,4},{4,0},{8,12},{12,8},{16,20},{20,16},{24,28},{28,24},{1,5},{5... | collective-permute-start | bytes 6152 | tf_op jit(solution)/shard_map/ppermute | solution.py:580
  255.2 6.8 %collective-permute-start.12 = (f16[16,4096]{1,0:T(8,128)(2,1)S(1)}, f16[16,4096]{1,0:T(8,128)(2,1)S(1)}, u32[]{:S(2)}, u32[]{:S(2)}) collective-permute-start(f16[16,4096]{1,0:T(8,128)(2,1)S(1)} %multiply_convert_fusion), channel_id=1, source_target_pairs={{0,16},{4,20},{8,24},{12,28},{16,0},{20,4},{24,8},{28,12},{1,17},{... | collective-permute-start | bytes 393224 | tf_op jit(solution)/shard_map/ppermute | solution.py:580
  259.4 2.9 collective-permute-start.33
  262.1 6.4 %collective-permute-start.13 = (f16[32,4096]{1,0:T(8,128)(2,1)S(1)}, f16[32,4096]{1,0:T(8,128)(2,1)S(1)}, u32[]{:S(2)}, u32[]{:S(2)}) collective-permute-start(f16[32,4096]{1,0:T(8,128)(2,1)S(1)} %pad_maximum_fusion.5), channel_id=1, source_target_pairs={{0,8},{4,12},{8,0},{12,4},{16,24},{20,28},{24,16},{28,20},{1,9},{5... | collective-permute-start | bytes 786440 | tf_op jit(solution)/shard_map/ppermute | solution.py:580
  263.0 8.7 %collective-permute-start.34 = (f32[1,128]{1,0:T(1,128)S(1)}, f32[1,128]{1,0:T(1,128)S(1)}, u32[]{:S(2)}, u32[]{:S(2)}) collective-permute-start(f32[1,128]{1,0:T(1,128)S(1)} %broadcast_add_fusion), channel_id=1, source_target_pairs={{0,2},{1,3},{2,0},{3,1},{4,6},{5,7},{6,4},{7,5},{8,10},{9,11},{10,... | collective-permute-start | bytes 1544 | tf_op jit(solution)/shard_map/ppermute | solution.py:577
  268.8 10.8 %collective-permute-start.14 = (f16[64,4096]{1,0:T(8,128)(2,1)S(1)}, f16[64,4096]{1,0:T(8,128)(2,1)S(1)}, u32[]{:S(2)}, u32[]{:S(2)}) collective-permute-start(f16[64,4096]{1,0:T(8,128)(2,1)S(1)} %pad_maximum_fusion.3), channel_id=1, source_target_pairs={{0,4},{4,0},{8,12},{12,8},{16,20},{20,16},{24,28},{28,24},{1,5},{5... | collective-permute-start | bytes 1572872 | tf_op jit(solution)/shard_map/ppermute | solution.py:580
  281.5 16.8 %copy-start.1 = (bf16[5,8192]{1,0:T(8,128)(2,1)S(1)}, bf16[5,8192]{1,0:T(8,128)(2,1)}, u32[]{:S(2)}) copy-start(bf16[5,8192]{1,0:T(8,128)(2,1)} %param.32) | copy-start | bytes 245764
  (10 other events, 35.6 us)

commit v3 on v2

v3 whole, which is shorter than its diff:
```python
import functools
import math

import jax
import jax.numpy as jnp
from jax import lax
from jax.experimental import pallas as pl
from jax.experimental.pallas import tpu as pltpu
from jax.sharding import PartitionSpec as P

H = 128
EH = 128
EIN = 5
NT = 12
STEPS = 6
ATOMS = 29
EM = 64
LAYERS = 2
STEP_COUNT = 10

PAD = 32
LIVE = 2 * (ATOMS - 1)
LB = 256
MIB = 2**20

f32 = jnp.float32
bf16 = jnp.bfloat16
highest = lax.Precision.HIGHEST
beta_one = 0.9
beta_two = 0.999
rate = 0.05
epsilon = 1e-08
decay = 0.01
clip_norm = 0.1

R_LSTM, R_FIRST, R_GRU, R_SECOND, R_MISC, R_EBIAS, R_END = 0, 1024, 1280, 2048, 2064, 2080, 2208
R_PACK = 2560
M_INPUT, M_LSTM, M_HEAD, M_OUT = 1, 7, 11, 12
G_BIAS, G_SUMS = EIN, EIN + 1
WINDOW = 384
CHUNKS = 2

NN = ((1,), (0,))
NTR = ((1,), (1,))
TN = ((0,), (0,))


def mm(a, b, dims=NN):
    return lax.dot_general(a, b, (dims, ((), ())), preferred_element_type=f32)


def split(x):
    high = x.astype(bf16)
    return high, (x - high.astype(f32)).astype(bf16)


def mm3(a, b, dims=NN):
    return mm(a[0], b[0], dims) + (mm(a[0], b[1], dims) + mm(a[1], b[0], dims))


def mm2(a, b, dims=NN):
    high, low = split(a)
    return mm(high, b, dims) + mm(low, b, dims)


def total_of(x):
    return jnp.sum(jnp.sum(x, axis=1, keepdims=True), axis=0, keepdims=True)


def columns(start, size):
    return pl.ds(pl.multiple_of(start, size), size)


def sigmoid(v):
    return jax.nn.sigmoid(v)


def column_of(values, size):
    at = lax.broadcasted_iota(jnp.int32, (size, 1), 0)
    found = jnp.zeros((size, 1), jnp.int32)
    for m in range(size):
        found = jnp.where(at == m, values[m], found)
    return found


def row_of(values, size):
    at = lax.broadcasted_iota(jnp.int32, (1, size), 1)
    found = jnp.zeros((1, size), jnp.int32)
    for m in range(size):
        found = jnp.where(at == m, values[m], found)
    return found


def starts_of(column, size):
    below = (
        lax.broadcasted_iota(jnp.int32, (size, size), 1)
        < lax.broadcasted_iota(jnp.int32, (size, size), 0)
    ).astype(bf16)
    return mm(below, jnp.broadcast_to(column, (size, 128)).astype(bf16))[:, :1]


def body_prepare(
    mols,
    counts_s,
    table,
    node_feats,
    edge_in,
    bias_rows,
    meta,
    nodes_o,
    hid_o,
    before_o,
    feat_o,
    hot_src,
    hot_dst,
    square,
    flat,
):
    lanes = nodes_o.shape[1]
    space = hid_o.shape[1]
    for b in range(space // LB):
        meta[2 + b] = jnp.int32(0)
    edges, atoms = jnp.int32(0), jnp.int32(0)
    for m in range(mols):
        live = 2 * (counts_s[m] - 1)
        block = lax.div(edges + (LB - 1), jnp.int32(LB))

        @pl.when(block * LB < edges + live)
        def _(block=block, atoms=atoms):
            meta[2 + block] = lax.div(atoms, jnp.int32(128)) * 128

        edges = edges + live
        atoms = atoms + counts_s[m]
    blocks = lax.div(edges + (LB - 1), jnp.int32(LB))
    meta[0] = blocks
    meta[1] = lax.div(atoms + (LB - 1), jnp.int32(LB))

    count_col = column_of(counts_s, mols).astype(f32)
    live_col = 2.0 * (count_col - 1.0)
    start_col = starts_of(live_col, mols)
    atom_col = starts_of(count_col, mols)

    square[...] = jnp.zeros_like(square)
    square[0:EIN, :] = edge_in[...]
    square[8:24, :] = bias_rows[...]
    turned = jnp.transpose(square[...])
    in_t, b_in_col = turned[:, :8], turned[:, 8:9]
    e_high, e_low = split(in_t)
    e_rest = (in_t - e_high.astype(f32) - e_low.astype(f32)).astype(bf16)

    flat[...] = jnp.zeros_like(flat)
    for m in range(mols):
        flat[m * PAD : m * PAD + ATOMS, :] = node_feats[m].astype(f32)
    flat_low = flat[...].astype(bf16)
    nodes_o[...] = jnp.zeros_like(nodes_o)
    atom_at = lax.broadcasted_iota(jnp.int32, (mols * PAD, 1), 0)
    spread = (
        lax.broadcasted_iota(jnp.int32, (mols * PAD, mols), 0) // PAD
        == lax.broadcasted_iota(jnp.int32, (mols * PAD, mols), 1)
    ).astype(bf16)
    goal_high = jnp.floor(atom_col * (1.0 / 8.0))
    goal_parts = jnp.concatenate([goal_high, atom_col - 8.0 * goal_high, count_col], axis=1)
    goal = mm(
        spread,
        jnp.concatenate([goal_parts, jnp.zeros((mols, 125), f32)], axis=1).astype(bf16),
    )
    within = lax.rem(atom_at, jnp.int32(PAD)).astype(f32)
    target = jnp.where(
        within < goal[:, 2:3], 8.0 * goal[:, 0:1] + goal[:, 1:2] + within, -1.0
    ).astype(jnp.int32)

    def pack_atoms(k, carry):
        c = columns(k * LB, LB)
        at = lax.broadcasted_iota(jnp.int32, (mols * PAD, LB), 1) + k * LB
        hot = (at == target).astype(f32).astype(bf16)
        nodes_o[:, c] = mm(flat_low, hot, TN).astype(bf16)
        return carry

    lax.fori_loop(0, meta[1], pack_atoms, 0)

    def prepare(b, carry):
        c = columns(b * LB, LB)
        spot = (lax.broadcasted_iota(jnp.int32, (mols, LB), 1) + b * LB).astype(f32)
        mol_hot = ((spot >= start_col) & (spot < start_col + live_col)).astype(f32)
        rows = mm(table[...], mol_hot.astype(bf16), TN)
        start_row = jnp.sum(mol_hot * start_col, axis=0, keepdims=True)
        base = jnp.sum(mol_hot * atom_col, axis=0, keepdims=True)
        valid = jnp.sum(mol_hot, axis=0, keepdims=True)
        slot = spot[:1] - start_row
        slot_hot = (lax.broadcasted_iota(jnp.int32, (EM, LB), 0).astype(f32) == slot).astype(f32)
        picked = [
            jnp.sum(rows[r * EM : (r + 1) * EM] * slot_hot, axis=0, keepdims=True)
            for r in range(EIN + 2)
        ]
        feat = jnp.concatenate(picked[:EIN] + [valid, jnp.zeros((2, LB), f32)], axis=0)
        feat_o[:, c] = feat
        feat_low = feat.astype(bf16)
        before = mm(e_high, feat_low) + mm(e_low, feat_low) + mm(e_rest, feat_low) + b_in_col
        before_o[:, c] = before
        hid_o[:, c] = (before * sigmoid(before)).astype(bf16)
        atom = lax.broadcasted_iota(jnp.int32, (WINDOW, LB), 0)
        base = base - meta[2 + b].astype(f32)
        src = jnp.where(valid > 0.5, base + picked[EIN], -1.0).astype(jnp.int32)
        dst = jnp.where(valid > 0.5, base + picked[EIN + 1], -1.0).astype(jnp.int32)
        hot_src[:, c] = (atom == src).astype(f32).astype(bf16)
        hot_dst[:, c] = (atom == dst).astype(f32).astype(bf16)
        return carry

    lax.fori_loop(0, blocks, prepare, 0)


def body_main(
    mols,
    own_rows,
    counts_s,
    flags_s,
    places,
    meta,
    targets,
    present,
    nodes,
    hid_i,
    hot_src,
    hot_dst,
    w_fwd,
    w_nat,
    ebias_parts,
    gru,
    bias_rows,
    lstm_rows,
    first,
    second,
    pack,
    sums_o,
    src_o,
    g_o,
    z,
    st,
    low,
    msg,
    keep,
    acc,
    dst_acc,
    gm,
    gm_rel,
    w_back,
    w_all,
    ds_all,
    gru_n,
    gru_t,
    square,
):
    parts = len(w_fwd)
    blocks, chunks = meta[0], meta[1]
    atoms = w_all.shape[1]

    def place(k):
        return pl.ds(pl.multiple_of(places[k], own_rows), own_rows)

    def window(b):
        return pl.ds(pl.multiple_of(meta[2 + b], 128), WINDOW)

    square[...] = jnp.zeros_like(square)
    square[0:16, :] = bias_rows[...]
    turned = jnp.transpose(square[...])
    gbias_col = [
        jnp.concatenate([turned[:, r + q : r + q + 1] for q in range(3)], axis=0)
        for r in (M_INPUT, M_INPUT + 3)
    ]
    c_lstm = jnp.concatenate(
        [bias_rows[M_LSTM + k : M_LSTM + k + 1, :] for k in range(4)], axis=1
    )
    c_head = bias_rows[M_HEAD : M_HEAD + 1, :]
    out_cols = [turned[k * NT : (k + 1) * NT, M_OUT : M_OUT + 1] for k in range(3)]
    gru_n[...] = gru[...].astype(bf16)
    for half in range(2):
        for q in range(3):
            gru_t[half, q * H : (q + 1) * H, :] = jnp.transpose(
                gru_n[half, :, q * H : (q + 1) * H]
            )
    ebias = jnp.concatenate([part[...] for part in ebias_parts], axis=0)
    b_high, b_low = split(ebias)

    def turn(i, carry):
        for k in range(parts):
            w_back[:, pl.ds(pl.multiple_of(k * own_rows * H + i * H, H), H)] = jnp.transpose(
                w_nat[k][:, columns(i * H, H)]
            )
        return carry

    lax.fori_loop(0, own_rows, turn, 0)

    for layer in range(LAYERS):
        low[layer] = jnp.zeros_like(low[layer])
    low[0, :, :atoms] = nodes[...]
    st[0] = nodes[...].astype(f32)
    st[LAYERS] = jnp.zeros_like(st[LAYERS])
    gm_rel[...] = jnp.zeros_like(gm_rel)
    for layer in range(LAYERS):
        acc[...] = jnp.zeros_like(acc)

        def move(b, carry, layer=layer):
            c, w = columns(b * LB, LB), window(b)
            source = mm(low[layer, :, w], hot_src[:, c]).astype(bf16)
            src_o[layer, :, c] = source
            for h in range(EH):
                z[h * H : (h + 1) * H, :] = hid_i[pl.ds(h, 1), c] * source
            moved = mm(jnp.concatenate([part[...] for part in w_fwd], axis=0), z[...])
            moved = moved + (mm(b_high, source) + mm(b_low, source))
            acc[:, w] += mm2(moved, hot_dst[:, c], NTR)
            return carry

        lax.fori_loop(0, blocks, move, 0)
        for k in range(parts):
            msg[layer, place(k), :] = acc[k * own_rows : (k + 1) * own_rows, :atoms].astype(bf16)

        def update(k, carry, layer=layer):
            c = columns(k * LB, LB)
            from_in = mm(gru_t[0], msg[layer, :, c]) + gbias_col[0]
            from_st = mm(gru_t[1], low[layer, :, c]) + gbias_col[1]
            reset = sigmoid(from_in[:H] + from_st[:H])
            upd = sigmoid(from_in[H : 2 * H] + from_st[H : 2 * H])
            fresh = jnp.tanh(from_in[2 * H :] + reset * from_st[2 * H :])
            new = (1.0 - upd) * fresh + upd * st[layer, :, c]
            st[layer + 1, :, c] = new
            if layer + 1 < LAYERS:
                low[layer + 1, :, c] = new.astype(bf16)
            keep[layer, 0, :, c] = reset
            keep[layer, 1, :, c] = upd
            keep[layer, 2, :, c] = fresh
            keep[layer, 3, :, c] = from_st[2 * H :]
            return carry

        lax.fori_loop(0, chunks, update, 0)

    lane = lax.broadcasted_iota(jnp.int32, (mols, atoms), 1).astype(f32)
    count_col = column_of(counts_s, mols).astype(f32)
    slot_of = lane - starts_of(count_col, mols)
    alive = (slot_of >= 0.0) & (slot_of < count_col)
    x = split(st[LAYERS])
    lstm = jnp.concatenate(
        [lstm_rows[0:H, :] + lstm_rows[2 * H : 3 * H, :], lstm_rows[H : 2 * H, :]], axis=0
    )
    lstm_w = split(lstm)
    zeros = jnp.zeros((mols, H), f32)
    hidden, read, cell = zeros, zeros, zeros
    saved = []
    for step in range(STEPS):
        query = jnp.concatenate([hidden, read], axis=1)
        if step == 0:
            gates = jnp.broadcast_to(c_lstm, (mols, 4 * H))
        else:
            gates = mm3(split(query), lstm_w) + c_lstm
        in_gate = sigmoid(gates[:, :H])
        forget = sigmoid(gates[:, H : 2 * H])
        part = jnp.tanh(gates[:, 2 * H : 3 * H])
        out_gate = sigmoid(gates[:, 3 * H :])
        before_cell = cell
        cell = forget * cell + in_gate * part
        squashed = jnp.tanh(cell)
        hidden = out_gate * squashed
        scores = jnp.where(alive, mm3(split(hidden), x), -1e30)
        weights = jnp.where(alive, jnp.exp(scores - jnp.max(scores, axis=1, keepdims=True)), 0.0)
        weights = weights / jnp.sum(weights, axis=1, keepdims=True)
        w_all[step * mols : (step + 1) * mols, :] = weights
        read = mm3(split(weights), x, NTR)
        saved.append((query, in_gate, forget, part, out_gate, before_cell, squashed, hidden))
    query = jnp.concatenate([hidden, read], axis=1)
    first_w = split(first[...])
    second_w = split(second[...])
    query_s = split(query)
    inner_pre = mm3(query_s, first_w) + c_head
    inner_sig = sigmoid(inner_pre)
    inner = inner_pre * inner_sig
    inner_s = split(inner)
    is_one = row_of(flags_s, mols) == 1
    predicted = (
        mm3(second_w, inner_s, NTR)
        + out_cols[0]
        + jnp.where(is_one, out_cols[2], out_cols[1])
    )
    there = present[...].astype(f32)
    diff = predicted - targets[...]
    lanes = lax.broadcasted_iota(jnp.int32, (1, 128), 1)
    loss = total_of(there * diff * diff)
    count = total_of(there)
    sums_o[...] = jnp.zeros_like(sums_o)
    sums_o[G_SUMS : G_SUMS + 1, :] = jnp.where(lanes == 0, loss, jnp.where(lanes == 1, count, 0.0))

    d_pred = 2.0 * there * diff
    d_pred_s = split(d_pred)
    pack[R_SECOND:R_MISC, :] = jnp.zeros((R_MISC - R_SECOND, 128), f32)
    pack[R_SECOND : R_SECOND + NT, :] = mm3(d_pred_s, inner_s)
    pack[R_MISC:R_EBIAS, :] = jnp.zeros((R_EBIAS - R_MISC, 128), f32)
    zero_pred = jnp.where(is_one, 0.0, d_pred)
    out_sums = jnp.concatenate([d_pred, zero_pred, d_pred - zero_pred], axis=0)
    out_high, out_low = split(out_sums)
    out_ones = jnp.ones((8, mols), bf16)
    pack[R_MISC + M_OUT : R_MISC + M_OUT + 1, : 3 * NT] = (
        mm(out_ones, out_high, NTR) + mm(out_ones, out_low, NTR)
    )[:1]
    d_inner = mm3(d_pred_s, second_w, TN)
    d_pre = d_inner * inner_sig * (1.0 + inner_pre * (1.0 - inner_sig))
    d_pre_s = split(d_pre)
    pack[R_FIRST:R_GRU, :] = mm3(query_s, d_pre_s, TN)
    pack[R_MISC + M_HEAD : R_MISC + M_HEAD + 1, :] = jnp.sum(d_pre, axis=0, keepdims=True)
    d_query = mm3(d_pre_s, first_w, NTR)
    d_hidden, d_read = d_query[:, :H], d_query[:, H:]
    d_cell = zeros
    d_gates_all = [None] * STEPS
    d_reads = [None] * STEPS
    for step in reversed(range(STEPS)):
        query, in_gate, forget, part, out_gate, before_cell, squashed, hid_t = saved[step]
        weights = w_all[step * mols : (step + 1) * mols, :]
        d_read_s = split(d_read)
        d_reads[step] = d_read
        d_weights = mm3(d_read_s, x)
        d_scores = weights * (d_weights - jnp.sum(weights * d_weights, axis=1, keepdims=True))
        ds_all[step * mols : (step + 1) * mols, :] = d_scores
        d_hidden = d_hidden + mm3(split(d_scores), x, NTR)
        d_out = d_hidden * squashed * out_gate * (1.0 - out_gate)
        d_cell = d_cell + d_hidden * out_gate * (1.0 - squashed * squashed)
        d_forget = d_cell * before_cell * forget * (1.0 - forget)
        d_in = d_cell * part * in_gate * (1.0 - in_gate)
        d_part = d_cell * in_gate * (1.0 - part * part)
        d_cell = d_cell * forget
        d_gates = jnp.concatenate([d_in, d_forget, d_part, d_out], axis=1)
        d_gates_all[step] = d_gates
        if step > 0:
            d_query = mm3(split(d_gates), lstm_w, NTR)
            d_hidden, d_read = d_query[:, :H], d_query[:, H:]
    queries = split(jnp.concatenate([saved[s][0] for s in range(STEPS)], axis=0))
    d_gates_cat = jnp.concatenate(d_gates_all, axis=0)
    d_gates_s = split(d_gates_cat)
    grad_lstm = mm3(queries, d_gates_s, TN)
    d_gates_sum = jnp.sum(d_gates_cat, axis=0, keepdims=True)
    for k in range(4):
        pack[R_LSTM + k * 256 : R_LSTM + (k + 1) * 256, :] = grad_lstm[:, k * H : (k + 1) * H]
        pack[R_MISC + M_LSTM + k : R_MISC + M_LSTM + k + 1, :] = d_gates_sum[:, k * H : (k + 1) * H]
    left = jnp.concatenate(d_reads + [saved[s][7] for s in range(STEPS)], axis=0)
    left_s = split(left)

    def spread(k, carry):
        c = columns(k * LB, LB)
        right = split(jnp.concatenate([w_all[:, c], ds_all[:, c]], axis=0))
        dst_acc[:, c] = mm3(left_s, right, TN)
        return carry

    dst_acc[...] = jnp.zeros_like(dst_acc)
    lax.fori_loop(0, chunks, spread, 0)

    pack[R_GRU:R_SECOND, :] = jnp.zeros((6 * H, 128), f32)
    gm[...] = jnp.zeros_like(gm)
    for layer in reversed(range(LAYERS)):

        def back(k, carry, layer=layer):
            c = columns(k * LB, LB)
            d_state = dst_acc[:, c]
            reset, upd = keep[layer, 0, :, c], keep[layer, 1, :, c]
            fresh, from_st = keep[layer, 2, :, c], keep[layer, 3, :, c]
            d_upd = d_state * (st[layer, :, c] - fresh) * upd * (1.0 - upd)
            d_fresh = d_state * (1.0 - upd) * (1.0 - fresh * fresh)
            d_reset = d_fresh * from_st * reset * (1.0 - reset)
            d_from_in = jnp.concatenate([d_reset, d_upd, d_fresh], axis=0)
            d_from_st = jnp.concatenate([d_reset, d_upd, d_fresh * reset], axis=0)
            in_s, st_s = split(d_from_in), split(d_from_st)
            gm[:, c] = (mm(gru_n[0], in_s[0]) + mm(gru_n[0], in_s[1])).astype(bf16)
            if layer > 0:
                dst_acc[:, c] = d_state * upd + (mm(gru_n[1], st_s[0]) + mm(gru_n[1], st_s[1]))
            ones = jnp.ones((8, LB), bf16)
            message, state_low = msg[layer, :, c], low[layer, :, c]
            for half, left_m, right_m in ((0, message, in_s), (1, state_low, st_s)):
                grad = mm(left_m, right_m[0], NTR) + mm(left_m, right_m[1], NTR)
                sums = (mm(ones, right_m[0], NTR) + mm(ones, right_m[1], NTR))[:1]
                for q in range(3):
                    r = R_GRU + (half * 3 + q) * H
                    pack[r : r + H, :] += grad[:, q * H : (q + 1) * H]
                    m = R_MISC + M_INPUT + half * 3 + q
                    pack[m : m + 1, :] += sums[:, q * H : (q + 1) * H]
            return carry

        lax.fori_loop(0, chunks, back, 0)
        for k in range(parts):
            gm_rel[k * own_rows : (k + 1) * own_rows, :atoms] = gm[place(k), :]
        if layer > 0:
            bt_high, bt_low = split(jnp.transpose(ebias))

            def pull(b, carry, layer=layer):
                c = columns(b * LB, LB)
                w = window(b)
                grad = mm(gm_rel[:, w], hot_dst[:, c])
                grad_low = grad.astype(bf16)
                g_o[layer, :, c] = grad_low
                hid = hid_i[:, c]
                for i in range(H):
                    z[i * EH : (i + 1) * EH, :] = g_o[layer, pl.ds(i, 1), c] * hid
                pulled = mm(w_back[...], z[...])
                pulled = pulled + (mm(bt_high, grad_low) + mm(bt_low, grad_low))
                dst_acc[:, w] += mm2(pulled, hot_src[:, c], NTR)
                return carry

            lax.fori_loop(0, blocks, pull, 0)
        else:

            def take(b, carry, layer=layer):
                c = columns(b * LB, LB)
                g_o[layer, :, c] = mm(gm_rel[:, window(b)], hot_dst[:, c]).astype(bf16)
                return carry

            lax.fori_loop(0, blocks, take, 0)
    acc_b = acc.at[:, :H]
    acc_b[...] = jnp.zeros((H, H), f32)

    def bias_sum(b, carry):
        c = columns(b * LB, LB)
        acc_b[...] += mm(g_o[0, :, c], src_o[0, :, c], NTR) + mm(
            g_o[1, :, c], src_o[1, :, c], NTR
        )
        return carry

    lax.fori_loop(0, blocks, bias_sum, 0)
    for k in range(parts):
        row = pl.multiple_of(R_EBIAS + places[k], 8)
        pack[pl.ds(row, own_rows), :] = acc_b[k * own_rows : (k + 1) * own_rows, :]
    pack[R_END:R_PACK, :] = jnp.zeros((R_PACK - R_END, 128), f32)


def body_edges(jobs, start, last, meta, *refs):
    n = len(jobs)
    ws, (src, g, hid), refs = refs[:n], refs[n : n + 3], refs[n + 3 :]
    if not start:
        hid_before, refs = refs[0], refs[1:]
    if last:
        (before, feat, sums), refs = refs[:3], refs[3:]
    outs, result, built, acc = refs[:n], refs[n], refs[n + 1], refs[n + 2]
    grad_hid = refs[n + 3] if last else result
    blocks = meta[0]
    rows = ws[0].shape[1] // H

    acc[...] = jnp.zeros_like(acc)

    def edges(b, carry):
        c = columns(b * LB, LB)
        s0, s1 = src[0, :, c].astype(f32), src[1, :, c].astype(f32)
        pulled = None if start else hid_before[:, c]
        for q, (rel, chunk) in enumerate(jobs):
            at = (rel * CHUNKS + chunk) * rows
            g0 = g[0, at : at + rows, c].astype(f32)
            g1 = g[1, at : at + rows, c].astype(f32)
            for i in range(rows):
                built[q % 2, i * H : (i + 1) * H, :] = (
                    g0[i : i + 1] * s0 + g1[i : i + 1] * s1
                ).astype(bf16)
            part = mm(ws[q][...], built[q % 2])
            pulled = part if pulled is None else pulled + part
            acc[q] += mm(hid[:, c], built[q % 2], NTR)
        grad_hid[:, c] = pulled
        return carry

    lax.fori_loop(0, blocks, edges, 0)
    for q in range(n):
        for i in range(rows):
            outs[q][i * EH : (i + 1) * EH, :] = acc[q, :, i * H : (i + 1) * H].astype(
                outs[q].dtype
            )

    if last:
        result[...] = sums[...]

        def finish(b, carry):
            c = columns(b * LB, LB)
            ahead = before[:, c]
            sig = sigmoid(ahead)
            grad = split(grad_hid[:, c] * sig * (1.0 + ahead * (1.0 - sig)))
            rows_low = feat[:, c].astype(bf16)
            result[...] += mm(rows_low, grad[0], NTR) + mm(rows_low, grad[1], NTR)
            return carry

        lax.fori_loop(0, blocks, finish, 0)


def adamw(weight, grad, moment, second):
    moment_new = beta_one * moment + (1.0 - beta_one) * grad
    second_new = beta_two * second + (1.0 - beta_two) * grad * grad
    mean_hat = moment_new / (1.0 - beta_one**STEP_COUNT)
    square_hat = second_new / (1.0 - beta_two**STEP_COUNT)
    return (
        weight - rate * (mean_hat / (jnp.sqrt(square_hat) + epsilon) + decay * weight),
        moment_new,
        second_new,
    )


def body_adamw(own_rows, place, *refs):
    owns, refs = refs[:CHUNKS], refs[CHUNKS:]
    (pack, grad_in, squares), refs = refs[:3], refs[3:]
    params, moments, seconds = refs[0:8], refs[8:16], refs[16:24]
    outs = refs[24:48]
    loss, count, norm, scale = refs[48:52]

    def step(index, grad, at=...):
        new = adamw(params[index][at], grad, moments[index][at], seconds[index][at])
        for kind in range(3):
            outs[kind * 8 + index][at] = new[kind]

    @pl.when(pl.program_id(0) == 0)
    def _():
        total = squares[0:1, 0:1] + total_of(jnp.square(grad_in[: G_BIAS + 1, :]))
        for k in range(4):
            total = total + total_of(jnp.square(pack[R_LSTM + k * 2 * H : R_LSTM + k * 2 * H + H, :]))
        loss[...] = grad_in[G_SUMS : G_SUMS + 1, 0:1]
        number = grad_in[G_SUMS : G_SUMS + 1, 1:2]
        count[...] = number
        grad_norm = jnp.sqrt(total) / number
        norm[...] = grad_norm
        factor = jnp.minimum(1.0, clip_norm / grad_norm) / number
        scale[...] = jnp.broadcast_to(factor, scale.shape)
        step(0, grad_in[:EIN, :] * factor)
        step(2, pack[pl.ds(pl.multiple_of(R_EBIAS + place[0], 8), own_rows), :] * factor)
        for half in range(2):
            for q in range(3):
                r = R_GRU + (half * 3 + q) * H
                step(3, pack[r : r + H, :] * factor, (half, slice(None), slice(q * H, (q + 1) * H)))
        for k in range(4):
            r = R_LSTM + k * 2 * H
            for block, start in ((0, 0), (1, H), (2, 0)):
                step(
                    4,
                    pack[r + start : r + start + H, :] * factor,
                    (slice(block * H, (block + 1) * H), slice(k * H, (k + 1) * H)),
                )
        step(5, pack[R_FIRST:R_GRU, :] * factor)
        step(6, pack[R_SECOND : R_SECOND + NT, :] * factor)
        bias = jnp.concatenate(
            [grad_in[G_BIAS : G_BIAS + 1, :], pack[R_MISC + 1 : R_EBIAS, :]], axis=0
        )
        step(7, bias * factor)

    per = pl.num_programs(0) // CHUNKS
    for c in range(CHUNKS):

        @pl.when(pl.program_id(0) // per == c)
        def _(c=c):
            for i in range(params[1].shape[1] // H):
                step(
                    1,
                    owns[c][i * EH : (i + 1) * EH, :] * scale[0:1, 0:1],
                    (slice(None), slice(i * H, (i + 1) * H)),
                )


VM = pl.BlockSpec(memory_space=pltpu.VMEM)
SM = pl.BlockSpec(memory_space=pltpu.SMEM)


def per_device(
    node_feats,
    edge_feats,
    edge_ends,
    atom_counts,
    dataset_flags,
    targets,
    present,
    edge_in,
    edge_out,
    edge_bias,
    gru_weights,
    lstm_weights,
    head_first,
    head_second,
    biases,
    *moments_seconds,
):
    row = lax.axis_index("row")
    row_count = lax.axis_size("row")
    mol = lax.axis_index("mol")
    mol_bits = lax.axis_size("mol").bit_length() - 1
    row_bits = row_count.bit_length() - 1
    mols = node_feats.shape[0]
    own_rows = edge_out.shape[1] // H
    atoms = -(-mols * ATOMS // LB) * LB
    space = -(-mols * LIVE // LB) * LB

    def row_swap(x, k):
        return lax.ppermute(x, "row", [(i, i ^ k) for i in range(row_count)])

    def mol_swap(x, bit):
        return lax.ppermute(x, "mol", [(i, i ^ (1 << bit)) for i in range(2**mol_bits)])

    def double(x, swap, bit):
        other = swap(x)
        return jnp.concatenate(
            [jnp.where(bit == 0, x, other), jnp.where(bit == 0, other, x)], axis=0
        )

    sds = jax.ShapeDtypeStruct
    n = row_count
    al = atoms + WINDOW - 128
    params = pltpu.CompilerParams(vmem_limit_bytes=56 * MIB)

    sent = edge_out.astype(bf16)
    bias_sent = edge_bias.reshape(own_rows, H)

    def forward_order(part):
        part = part.reshape(EH, own_rows, H)
        return part.transpose(1, 0, 2).reshape(own_rows, EH * H)

    parts, bias_parts = {0: sent}, {0: bias_sent}
    for bit in reversed(range(row_bits)):
        parts[1 << bit] = row_swap(sent, 1 << bit)
        bias_parts[1 << bit] = row_swap(bias_sent, 1 << bit)

    ends = lax.dynamic_slice_in_dim(edge_ends, row * mols, mols, 1)
    feats = lax.dynamic_slice_in_dim(edge_feats, row * mols * EM, mols * EM, 1)
    table = jnp.concatenate([feats.reshape(EIN, mols, EM), ends.astype(bf16)], axis=0)
    table = table.transpose(1, 0, 2).reshape(mols, (EIN + 2) * EM)
    places = jnp.stack([(row ^ k) * own_rows for k in range(row_count)]).astype(jnp.int32)
    bias_rows = jnp.pad(biases, (0, 16 * 128 - biases.shape[0])).reshape(16, 128)

    prepared = pl.pallas_call(
        functools.partial(body_prepare, mols),
        out_shape=(
            sds((2 + space // LB,), jnp.int32),
            sds((H, atoms), bf16),
            sds((EH, space), bf16),
            sds((EH, space), f32),
            sds((8, space), f32),
            sds((WINDOW, space), bf16),
            sds((WINDOW, space), bf16),
        ),
        in_specs=[SM] + [VM] * 4,
        out_specs=(SM,) + (VM,) * 6,
        scratch_shapes=[pltpu.VMEM((128, 128), f32), pltpu.VMEM((mols * PAD, H), f32)],
        compiler_params=params,
    )(atom_counts, table, node_feats, edge_in, bias_rows)
    forward = {k: forward_order(part) for k, part in parts.items() if k < n // 2}
    parts, bias_parts, prepared, forward = lax.optimization_barrier(
        (parts, bias_parts, prepared, forward)
    )
    meta, nodes, hid, before, feat, hot_src, hot_dst = prepared
    for bit in reversed(range(row_bits)):
        for k in [k for k in parts if k > 1 << bit and not k & (1 << bit)]:
            parts[k + (1 << bit)] = row_swap(parts[k], 1 << bit)
            bias_parts[k + (1 << bit)] = row_swap(bias_parts[k], 1 << bit)
    parts = [parts[k] for k in range(n)]
    bias_parts = [bias_parts[k] for k in range(n)]
    w_fwd = [forward[k] if k in forward else forward_order(parts[k]) for k in range(n)]

    def main(*refs):
        at = 10
        body_main(
            mols,
            own_rows,
            *refs[:at],
            refs[at : at + n],
            refs[at + n : at + 2 * n],
            refs[at + 2 * n : at + 3 * n],
            *refs[at + 3 * n :],
        )

    pack, sums, src, g = pl.pallas_call(
        main,
        out_shape=(
            sds((R_PACK, 128), f32),
            sds((8, 128), f32),
            sds((LAYERS, H, space), bf16),
            sds((LAYERS, H, space), bf16),
        ),
        in_specs=[SM] * 4 + [VM] * (11 + 3 * n),
        out_specs=(VM,) * 4,
        scratch_shapes=[
            pltpu.VMEM((H * EH, LB), bf16),
            pltpu.VMEM((LAYERS + 1, H, atoms), f32),
            pltpu.VMEM((LAYERS, H, al), bf16),
            pltpu.VMEM((LAYERS, H, atoms), bf16),
            pltpu.VMEM((LAYERS, 4, H, atoms), f32),
            pltpu.VMEM((H, al), f32),
            pltpu.VMEM((H, al), f32),
            pltpu.VMEM((H, atoms), bf16),
            pltpu.VMEM((H, al), bf16),
            pltpu.VMEM((H, H * EH), bf16),
            pltpu.VMEM((STEPS * mols, atoms), f32),
            pltpu.VMEM((STEPS * mols, atoms), f32),
            pltpu.VMEM((2, H, 3 * H), bf16),
            pltpu.VMEM((2, 3 * H, H), bf16),
            pltpu.VMEM((128, 128), f32),
        ],
        compiler_params=pltpu.CompilerParams(vmem_limit_bytes=60 * MIB),
    )(
        atom_counts,
        dataset_flags,
        places,
        meta,
        targets.T,
        present.T,
        nodes,
        hid,
        hot_src,
        hot_dst,
        *w_fwd,
        *parts,
        *bias_parts,
        gru_weights,
        bias_rows,
        lstm_weights,
        head_first,
        head_second.T,
    )

    span = own_rows * H // CHUNKS

    def edge_parts(jobs, before_hid, last):
        start = before_hid is None
        extra = () if start else (before_hid,)
        if last:
            extra = extra + (before, feat, sums)
        *found, result = pl.pallas_call(
            functools.partial(body_edges, jobs, start, last),
            grid=(1,),
            out_shape=(sds((span, EH), bf16),) * len(jobs)
            + (sds((8, EH) if last else (EH, space), f32),),
            in_specs=[SM]
            + [pl.BlockSpec((EH, span), lambda i, c=chunk: (0, c)) for _, chunk in jobs]
            + [VM] * (3 + len(extra)),
            out_specs=(VM,) * (len(jobs) + 1),
            scratch_shapes=[
                pltpu.VMEM((2, span, LB), bf16),
                pltpu.VMEM((len(jobs), EH, span), f32),
            ]
            + ([pltpu.VMEM((EH, space), f32)] if last else []),
            compiler_params=params,
        )(meta, *(parts[k] for k, _ in jobs), src, g, hid, *extra)
        return found, result

    row_steps = [(functools.partial(row_swap, k=1 << b), (row >> b) & 1) for b in range(row_bits)]
    mol_steps = [(functools.partial(mol_swap, bit=b), (mol >> b) & 1) for b in range(mol_bits)]
    tie = lax.optimization_barrier
    (core, core_bit), (cross, cross_bit) = row_steps

    def halves(x, bit):
        both = x.reshape((2, x.shape[0] // 2) + x.shape[1:])
        return (
            lax.dynamic_index_in_dim(both, 1 - bit, 0, False),
            lax.dynamic_index_in_dim(both, bit, 0, False),
        )

    def as_low(x, count):
        found = []
        for _ in range(count):
            high = lax.reduce_precision(x, 8, 7)
            found.append(high)
            x = x - high
        return jnp.concatenate(found, axis=0).astype(bf16)

    def from_low(x, count):
        x = x.astype(f32).reshape(count, -1, 128)
        found = x[count - 1]
        for k in reversed(range(count - 1)):
            found = found + x[k]
        return found

    (far, far_core), carry = edge_parts(((2, 0), (3, 0)), None, False)
    pack_sent, pack = halves(pack, core_bit)
    came = core(jnp.concatenate([far_core, as_low(pack_sent, 2)], axis=0))
    pack_sent, pack = halves(pack + from_low(came[span:], 2), cross_bit)
    sent = (far.astype(f32) + came[:span].astype(f32)).astype(bf16)
    sent = jnp.concatenate([sent, as_low(pack_sent, 2)], axis=0)
    sent, carry = tie((sent, carry))
    arrived = cross(sent)
    (near, near_core, far, far_core), carry = edge_parts(
        ((0, 0), (1, 0), (2, 1), (3, 1)), carry, False
    )
    sent, arrived = tie((jnp.concatenate([near_core, far_core], axis=0), arrived))
    came = core(sent)
    own = near.astype(f32) + came[:span].astype(f32) + arrived[:span].astype(f32)
    pack = pack + from_low(arrived[span:], 2)
    sent = (far.astype(f32) + came[span:].astype(f32)).astype(bf16)

    def first_stage(own, pack, swap, bit):
        own_sent, own = halves(own, bit)
        pack_sent, pack = halves(pack, bit)
        half = own.shape[0]

        def take(came):
            return own + came[:half].astype(f32), pack + from_low(came[half:], 2)

        return jnp.concatenate([own_sent.astype(bf16), as_low(pack_sent, 2)], axis=0), take

    first_sent, take = first_stage(own, pack, *mol_steps[0])
    sent, first_sent, carry = tie((sent, first_sent, carry))
    arrived = cross(sent)
    first_came = mol_steps[0][0](first_sent)
    (near, near_core), grad_in = edge_parts(((0, 1), (1, 1)), carry, True)
    sent = jnp.concatenate([near_core, as_low(grad_in, 3)], axis=0)
    sent, arrived, first_came = tie((sent, arrived, first_came))
    came = core(sent)
    grad_in = grad_in + from_low(came[span:], 3)
    own = near.astype(f32) + came[:span].astype(f32) + arrived.astype(f32)
    first, pack = take(first_came)
    grad_in = grad_in + cross(grad_in)
    grad_in = grad_in + mol_steps[0][0](grad_in)
    for index, (swap, bit) in enumerate(mol_steps):
        if index > 0:
            first_sent, take = first_stage(first, pack, swap, bit)
            first, pack = take(swap(first_sent))
        own_sent, own = halves(own, bit)
        half = own.shape[0]
        sent = own_sent.astype(bf16)
        if index > 0:
            sent = jnp.concatenate([sent, as_low(grad_in, 3)], axis=0)
        came = swap(sent)
        own = own + came[:half].astype(f32)
        if index > 0:
            grad_in = grad_in + from_low(came[half:], 3)
    owns = [first, own]
    own_rest = owns[0].shape[0]
    pieces = [jnp.concatenate([owns[0], pack], axis=0)] + owns[1:]
    squares = jnp.broadcast_to(sum(jnp.sum(piece * piece) for piece in pieces), (8, 128))

    travel = []
    for piece in pieces:
        largest = jnp.maximum(jnp.max(jnp.abs(piece)), 1e-30)
        power = 14.0 - jnp.ceil(jnp.log2(largest))
        travel.append(
            jnp.concatenate(
                [piece * jnp.exp2(power), jnp.broadcast_to(power, (16, 128))], axis=0
            ).astype(jnp.float16)
        )
    squares, travel[-1] = tie((squares, travel[-1]))
    squares = (squares + row_swap(squares, 1)) + (row_swap(squares, 2) + row_swap(squares, 3))
    for swap, bit in reversed(mol_steps):
        squares = squares + swap(squares)
    for swap, bit in reversed(mol_steps):
        travel = [double(sent, swap, bit) for sent in travel]
    owns = []
    for piece, sent in zip(pieces, travel):
        height = piece.shape[0]
        sent = sent.astype(f32).reshape(-1, height + 16, 128)
        owns.append(sent[:, :height] * jnp.exp2(-sent[:, height : height + 1, 0:1]))
    pack = owns[0][:, own_rest:].reshape(-1, 128)
    owns[0] = owns[0][:, :own_rest]
    owns = [own.reshape(-1, 128) for own in owns]
    for swap, bit in reversed(row_steps):
        pack = double(pack, swap, bit)

    weights = [
        edge_in,
        edge_out,
        edge_bias,
        gru_weights,
        lstm_weights,
        head_first,
        head_second,
        biases,
    ]
    states = []
    for group in (weights, moments_seconds[:8], moments_seconds[8:]):
        group = list(group)
        group[2] = group[2].reshape(own_rows, H)
        group[6] = group[6].T
        if group[7] is biases:
            group[7] = bias_rows
        else:
            group[7] = jnp.pad(group[7], (0, 16 * 128 - group[7].shape[0])).reshape(16, 128)
        states += group
    grid = 2 * CHUNKS
    block = pl.BlockSpec((EH, own_rows * H // grid), lambda i: (0, i))
    own_specs = [
        pl.BlockSpec((span // 2, EH), lambda i, c=c: (jnp.clip(i - 2 * c, 0, 1), 0))
        for c in range(CHUNKS)
    ]

    def state_specs():
        return [block if index == 1 else VM for index in range(8)] * 3

    shapes = [sds(state.shape, f32) for state in states]
    results = pl.pallas_call(
        functools.partial(body_adamw, own_rows),
        grid=(grid,),
        out_shape=tuple(shapes) + (sds((1, 1), f32),) * 3,
        in_specs=[SM] + own_specs + [VM, VM, VM] + state_specs(),
        out_specs=tuple(state_specs()) + (VM,) * 3,
        scratch_shapes=[pltpu.VMEM((8, 128), f32)],
        compiler_params=params,
    )(places, *owns, pack, grad_in, squares, *states)
    results = list(results)
    for kind in range(3):
        results[kind * 8 + 2] = results[kind * 8 + 2].reshape(own_rows * H)
        results[kind * 8 + 6] = results[kind * 8 + 6].T
        results[kind * 8 + 7] = results[kind * 8 + 7].reshape(-1)[: biases.shape[0]]
    for index in range(24, 27):
        results[index] = results[index].reshape(())
    return tuple(results)


def solution(mesh):
    weights = (P(), P(None, "row"), P("row"), P(), P(), P(), P(), P())
    in_specs = (
        P(("mol", "row"), None, None),
        P(None, "mol"),
        P(None, "mol", None),
        P(("mol", "row")),
        P(("mol", "row")),
        P(("mol", "row"), None),
        P(("mol", "row"), None),
    ) + weights * 3
    out_specs = weights * 3 + (P(), P(), P())
    return jax.shard_map(
        per_device, mesh=mesh, in_specs=in_specs, out_specs=out_specs, check_vma=False
    )
```

time: 303 us -> 253 us (0.83); the launches traced: 298 us -> 255 us
  local copies, waits for them, and re-layouts: 34.8 us -> 14.1 us
  waiting for transfers between devices: 71.1 us -> 62.9 us
  starting transfers between devices: 41.2 us -> 34.9 us
  Pallas kernels: 125 us -> 119 us
  other arithmetic: 24.1 us -> 19.7 us
    ppermute x18 -> x16, starting transfers between devices: 28.7 us -> 14.3 us  [mol_swap(): lax.ppermute(x, 'mol', [(i, i ^ 1 << bit) for i in range(2 ** mol_bits)])]
    ppermute x17, waiting for transfers between devices: 35.4 us -> 23.5 us  [row_swap(): return lax.ppermute(x, 'row', [(i, i ^ k) for i in range(row_count)])]
    unnamed x61 -> x44, local copies, waits for them, and re-layouts: 15.9 us -> 5.84 us
    ppermute x17, starting transfers between devices: 12.5 us -> 20.6 us  [row_swap(): return lax.ppermute(x, 'row', [(i, i ^ k) for i in range(row_count)])]
    pallas_call x3 -> x5, Pallas kernels: 113 us -> 107 us  [the longest x1 64 us: per_device(): pl.pallas_call(main, out_shape=(sds((R_PACK, 128), f32), sds((8, 128), f3...]
    reshape x12 -> x6, local copies, waits for them, and re-layouts: 11 us -> 6.09 us  [the longest x4 4.78 us: forward_order(): return part.transpose(1, 0, 2).reshape(own_rows, EH * H)]
    add x16 -> x22, other arithmetic: 6.96 us -> 2.16 us  [the longest x3 0.6 us: per_device(): squares = squares + swap(squares)]
    ppermute x18 -> x16, waiting for transfers between devices: 35.6 us -> 39.4 us  [mol_swap(): lax.ppermute(x, 'mol', [(i, i ^ 1 << bit) for i in range(2 ** mol_bits)])]
  transfers between devices with their start and end apart: 35 -> 33, of which waited for: 17 -> 23; matrix products, arithmetic and copies ran while one was open for 15% -> 9% of each run, Pallas kernels for 11% -> 13%
where the time goes in v3:
time: 253 us; the launch traced here: 255 us
  Pallas kernels  119 us (47%)
  waiting for transfers between devices  62.9 us (25%)
  starting transfers between devices  34.9 us (14%)
  other arithmetic  19.7 us (8%)
  local copies, waits for them, and re-layouts  14.1 us (6%)
  between operations  4.41 us (2%)
    pallas_call x1, Pallas kernels, per_device(): pl.pallas_call(main, out_shape=(sds((R_PACK, 128), f32), sds((8, 128), f3...  64 us
    ppermute x16, waiting for transfers between devices, mol_swap(): lax.ppermute(x, 'mol', [(i, i ^ 1 << bit) for i in range(2 ** mol_bits)])  39.4 us
    pallas_call x3, Pallas kernels, edge_parts(): pl.pallas_call(functools.partial(body_edges, jobs, start, last), grid=(1,...  34.5 us
    ppermute x17, waiting for transfers between devices, row_swap(): return lax.ppermute(x, 'row', [(i, i ^ k) for i in range(row_count)])  23.5 us
    ppermute x17, starting transfers between devices, row_swap(): return lax.ppermute(x, 'row', [(i, i ^ k) for i in range(row_count)])  20.6 us
    ppermute x16, starting transfers between devices, mol_swap(): lax.ppermute(x, 'mol', [(i, i ^ 1 << bit) for i in range(2 ** mol_bits)])  14.3 us
    pallas_call x1, Pallas kernels, per_device(): pl.pallas_call(functools.partial(body_adamw, own_rows), grid=(grid,), out...  12.3 us
    pallas_call x1, Pallas kernels, per_device(): pl.pallas_call(functools.partial(body_prepare, mols), out_shape=(sds((2 +...  8.07 us
  transfers between devices with their start and end apart: 33, of which 23 were waited for; matrix products, arithmetic and copies ran while one was open for 9% of the time, Pallas kernels for 13%

profile of v3, /device:TPU:0, one launch (start us, length us, event | category | flops | bytes accessed | tf_op | source)
XLA Modules:
  0.0 254.9 jit_solution(10806153889556064059)
XLA Ops:
  0.7 2.9 %convert_element_type.148.refs_14_.refs_0_ = bf16[128,4096]{1,0:T(8,128)(2,1)} convert(f32[128,4096]{1,0:T(8,128)} %refs_6_.1) | non-fusion elementwise | flops 524288 | bytes 3145728 | tf_op jit(solution)/shard_map/convert_element_type | solution.py:701
  4.1 2.5 collective-permute-start.1
  7.4 1.2 convert_bitcast_fusion
  10.8 1.4 copy.86
  12.2 1.2 copy.97
  13.4 8.1 %shard_map.502 = (s32[9]{0:T(128)}, bf16[128,1024]{1,0:T(8,128)(2,1)}, bf16[128,1792]{1,0:T(8,128)(2,1)}, f32[128,1792]{1,0:T(8,128)}, f32[8,1792]{1,0:T(8,128)}...) custom-call(s32[32]{0:T(128)} %refs_0_.1, bf16[32,448]{1,0:T(8,128)(2,1)} %reshape.242.table, ...), custom_call_target="tpu_custom_call" | custom-call | tf_op jit(solution)/shard_map/pallas_call | solution.py:720
  21.5 1.4 copy.87
  22.9 1.2 copy.96
  24.1 6.9 %collective-permute-done.3.refs_20_ = f32[32,128]{1,0:T(8,128)} collective-permute-done((f32[32,128]{1,0:T(8,128)S(1)}, f32[32,128]{1,0:T(8,128)}, u32[]{:S(2)}, u32[]{:S(2)}) %collective-permute-start.3) | collective-permute-done | bytes 16416 | tf_op jit(solution)/shard_map/ppermute | solution.py:685
  32.4 1.2 copy.95
  34.0 1.3 copy.94
  35.9 64.0 %shard_map.503 = (f32[2560,128]{1,0:T(8,128)}, f32[8,128]{1,0:T(8,128)}, bf16[2,128,1792]{2,1,0:T(8,128)(2,1)}, bf16[2,128,1792]{2,1,0:T(8,128)(2,1)}) custom-call(s32[32]{0:T(128)} %refs_0_.1, s32[32]{0:T(128)} %refs_1_.1, s32[4]{0:T(128)} %pad_add_fusion.refs_2_.place, s32[9]{0:T(128)} %get-tuple-element.110.refs_3_.meta, f32[12,32]{1,0:T(8,128)} %bitcast.187, ...), custom_call_target="tpu_custom_call" | custom-call | tf_op jit(solution)/shard_map/pallas_call | solution.py:761
  99.9 1.2 reduce-precision_convert_fusion
  101.1 9.1 %shard_map.504 = (bf16[2048,128]{1,0:T(8,128)(2,1)}, bf16[2048,128]{1,0:T(8,128)(2,1)}, f32[128,1792]{1,0:T(8,128)}) custom-call(s32[9]{0:T(128)} %get-tuple-element.110.refs_3_.meta, bf16[128,4096]{1,0:T(8,128)(2,1)} %copy-done.3, bf16[128,4096]{1,0:T(8,128)(2,1)} %copy-done.4, bf16[2,128,1792]{2,1,0:T(8,128)(2,1)} %get-tuple-element.123.refs_2_.refs_4_, ...), custom_call_target="tpu_custom_call" | custom-call | tf_op jit(solution)/shard_map/pallas_call | solution.py:817
  110.1 2.2 pad_maximum_fusion.1
  112.4 3.0 %collective-permute-done.6 = bf16[4608,128]{1,0:T(8,128)(2,1)S(1)} collective-permute-done((bf16[4608,128]{1,0:T(8,128)(2,1)}, bf16[4608,128]{1,0:T(8,128)(2,1)S(1)}, u32[]{:S(2)}, u32[]{:S(2)}) %collective-permute-start.6) | collective-permute-done | bytes 1179680 | tf_op jit(solution)/shard_map/ppermute | solution.py:685
  116.9 8.9 %collective-permute-start.7 = (bf16[3328,128]{1,0:T(8,128)(2,1)S(1)}, bf16[3328,128]{1,0:T(8,128)(2,1)S(1)}, u32[]{:S(2)}, u32[]{:S(2)}) collective-permute-start(bf16[3328,128]{1,0:T(8,128)(2,1)S(1)} %pad_maximum_fusion.3), channel_id=1, source_target_pairs={{0,2},{1,3},{2,0},{3,1},{4,6},{5,7},{6,4},{7,5},{8,10},{9,11},{10,... | collective-permute-start | bytes 2555912 | tf_op jit(solution)/shard_map/ppermute | solution.py:685
  125.8 15.2 %shard_map.505 = (bf16[2048,128]{1,0:T(8,128)(2,1)}, bf16[2048,128]{1,0:T(8,128)(2,1)}, bf16[2048,128]{1,0:T(8,128)(2,1)}, bf16[2048,128]{1,0:T(8,128)(2,1)}, f32[128,1792]{1,0:T(8,128)}) custom-call(s32[9]{0:T(128)} %get-tuple-element.110.refs_3_.meta, bf16[128,4096]{1,0:T(8,128)(2,1)} %convert_element_type.148.refs_14_.refs_0_, ...), custom_call_target="tpu_custom_call" | custom-call | tf_op jit(solution)/shard_map/pallas_call | solution.py:817
  141.0 1.3 pad_maximum_fusion.2
  142.2 3.0 %collective-permute-done.7 = bf16[3328,128]{1,0:T(8,128)(2,1)S(1)} collective-permute-done((bf16[3328,128]{1,0:T(8,128)(2,1)S(1)}, bf16[3328,128]{1,0:T(8,128)(2,1)S(1)}, u32[]{:S(2)}, u32[]{:S(2)}) %collective-permute-start.7) | collective-permute-done | bytes 852000 | tf_op jit(solution)/shard_map/ppermute | solution.py:685
  145.5 2.4 collective-permute-done.8
  148.3 1.8 collective-permute-start.9
  150.1 10.3 %shard_map.506 = (bf16[2048,128]{1,0:T(8,128)(2,1)}, bf16[2048,128]{1,0:T(8,128)(2,1)}, f32[8,128]{1,0:T(8,128)}) custom-call(s32[9]{0:T(128)} %get-tuple-element.110.refs_3_.meta, bf16[128,4096]{1,0:T(8,128)(2,1)} %convert_element_type.148.refs_14_.refs_0_, bf16[128,4096]{1,0:T(8,128)(2,1)} %collective-permute-done.refs_15_.refs_1_, ...), custom_call_target="tpu_custom_call" | custom-call | tf_op jit(solution)/shard_map/pallas_call | solution.py:817
  161.1 1.1 pad_maximum_fusion.7
  162.8 7.6 %collective-permute-done.11 = bf16[832,128]{1,0:T(8,128)(2,1)S(1)} collective-permute-done((bf16[832,128]{1,0:T(8,128)(2,1)S(1)}, bf16[832,128]{1,0:T(8,128)(2,1)S(1)}, u32[]{:S(2)}, u32[]{:S(2)}) %collective-permute-start.11) | collective-permute-done | bytes 213024 | tf_op jit(solution)/shard_map/ppermute | solution.py:688
  170.4 1.8 collective-permute-start.18
  172.4 1.7 collective-permute-done.18
  174.1 1.9 collective-permute-start.19
  176.2 1.5 collective-permute-done.19
  177.7 4.9 %collective-permute-done.17 = bf16[1024,128]{1,0:T(8,128)(2,1)S(1)} collective-permute-done((bf16[1024,128]{1,0:T(8,128)(2,1)S(1)}, bf16[1024,128]{1,0:T(8,128)(2,1)S(1)}, u32[]{:S(2)}, u32[]{:S(2)}) %collective-permute-start.17) | collective-permute-done | bytes 262176 | tf_op jit(solution)/shard_map/ppermute | solution.py:688
  183.3 4.5 %collective-permute-done.20 = bf16[536,128]{1,0:T(8,128)(2,1)S(1)} collective-permute-done((bf16[536,128]{1,0:T(8,128)(2,1)S(1)}, bf16[536,128]{1,0:T(8,128)(2,1)S(1)}, u32[]{:S(2)}, u32[]{:S(2)}) %collective-permute-start.20) | collective-permute-done | bytes 137248 | tf_op jit(solution)/shard_map/ppermute | solution.py:688
  188.1 3.0 %collective-permute-start.12 = (bf16[416,128]{1,0:T(8,128)(2,1)S(1)}, bf16[416,128]{1,0:T(8,128)(2,1)S(1)}, u32[]{:S(2)}, u32[]{:S(2)}) collective-permute-start(bf16[416,128]{1,0:T(8,128)(2,1)S(1)} %pad_maximum_fusion.16), channel_id=1, source_target_pairs={{0,16},{4,20},{8,24},{12,28},{16,0},{20,4},{24,8},{28,12},{1,17},{... | collective-permute-start | bytes 319496 | tf_op jit(solution)/shard_map/ppermute | solution.py:688
  191.1 2.2 collective-permute-done.21
  194.7 1.6 collective-permute-done.12
  198.8 1.5 collective-permute-start.29
  200.9 1.2 collective-permute-done.28
  203.3 3.3 %collective-permute-done.30 = f32[8,128]{1,0:T(8,128)S(1)} collective-permute-done((f32[8,128]{1,0:T(8,128)S(1)}, f32[8,128]{1,0:T(8,128)S(1)}, u32[]{:S(2)}, u32[]{:S(2)}) %collective-permute-start.30) | collective-permute-done | bytes 4128 | tf_op jit(solution)/shard_map/ppermute | solution.py:688
  206.7 2.8 %collective-permute-start.13 = (f16[352,128]{1,0:T(8,128)(2,1)S(1)}, f16[352,128]{1,0:T(8,128)(2,1)S(1)}, u32[]{:S(2)}, u32[]{:S(2)}) collective-permute-start(f16[352,128]{1,0:T(8,128)(2,1)S(1)} %concatenate.96), channel_id=1, source_target_pairs={{0,16},{4,20},{8,24},{12,28},{16,0},{20,4},{24,8},{28,12},{1,17},{... | collective-permute-start | bytes 270344 | tf_op jit(solution)/shard_map/ppermute | solution.py:688
  210.3 1.3 collective-permute-start.32
  214.6 1.1 collective-permute-start.14
  215.7 2.1 collective-permute-done.22
  218.2 3.1 %collective-permute-done.14 = f16[704,128]{1,0:T(8,128)(2,1)S(1)} collective-permute-done((f16[704,128]{1,0:T(8,128)(2,1)S(1)}, f16[704,128]{1,0:T(8,128)(2,1)S(1)}, u32[]{:S(2)}, u32[]{:S(2)}) %collective-permute-start.14) | collective-permute-done | bytes 180256 | tf_op jit(solution)/shard_map/ppermute | solution.py:688
  224.1 6.3 %collective-permute-done.15 = f16[1408,128]{1,0:T(8,128)(2,1)S(1)} collective-permute-done((f16[1408,128]{1,0:T(8,128)(2,1)S(1)}, f16[1408,128]{1,0:T(8,128)(2,1)S(1)}, u32[]{:S(2)}, u32[]{:S(2)}) %collective-permute-start.15) | collective-permute-done | bytes 360480 | tf_op jit(solution)/shard_map/ppermute | solution.py:688
  231.2 2.1 collective-permute-start.25
  233.5 4.9 %collective-permute-done.25 = f32[640,128]{1,0:T(8,128)S(1)} collective-permute-done((f32[640,128]{1,0:T(8,128)S(1)}, f32[640,128]{1,0:T(8,128)S(1)}, u32[]{:S(2)}, u32[]{:S(2)}) %collective-permute-start.25) | collective-permute-done | bytes 327712 | tf_op jit(solution)/shard_map/ppermute | solution.py:685
  238.9 1.1 slice_multiply_fusion.1
  241.2 1.2 pad_maximum_fusion.refs_2_
  242.4 12.3 %shard_map.507 = (f32[5,128]{1,0:T(8,128)}, f32[128,4096]{1,0:T(8,128)}, f32[32,128]{1,0:T(8,128)}, f32[2,128,384]{2,1,0:T(8,128)}, f32[384,512]{1,0:T(8,128)}, ...) custom-call(s32[4]{0:T(128)} %pad_add_fusion.refs_2_.place, ...), custom_call_target="tpu_custom_call" | custom-call | tf_op jit(solution)/shard_map/pallas_call | solution.py:977
  (175 shorter events, 23.0 us)
Async XLA Ops:
  0.7 6.6 %copy-start = (bf16[5,8192]{1,0:T(8,128)(2,1)S(1)}, bf16[5,8192]{1,0:T(8,128)(2,1)}, u32[]{:S(2)}) copy-start(bf16[5,8192]{1,0:T(8,128)(2,1)} %param.32) | copy-start | bytes 245764
  0.7 6.7 %copy-start.2 = (f32[128,4096]{1,0:T(8,128)S(1)}, f32[128,4096]{1,0:T(8,128)}, u32[]{:S(2)}) copy-start(f32[128,4096]{1,0:T(8,128)} %refs_6_.1) | copy-start | bytes 6291460
  0.7 5.9 %copy-start.11 = (f32[4096]{0:T(1024)S(1)}, f32[4096]{0:T(1024)}, u32[]{:S(2)}) copy-start(f32[4096]{0:T(1024)} %param.40) | copy-start | bytes 49156
  0.7 6.4 %copy-start.12 = (s32[2,128,64]{1,2,0:T(8,128)S(1)}, s32[2,128,64]{1,2,0:T(8,128)}, u32[]{:S(2)}) copy-start(s32[2,128,64]{1,2,0:T(8,128)} %param.33) | copy-start | bytes 196612
  3.6 17.8 %collective-permute-start = (bf16[128,4096]{1,0:T(8,128)(2,1)}, bf16[128,4096]{1,0:T(8,128)(2,1)}, u32[]{:S(2)}, u32[]{:S(2)}) collective-permute-start(bf16[128,4096]{1,0:T(8,128)(2,1)} %convert_element_type.148.refs_14_.refs_0_), channel_id=1, source_target_pairs={{0,1},{1,0},{2,3},{3,2},{4,5},{5,4},{6,7},{7,6},{8,9},{9,8},{10,11... | collective-permute-start | bytes 3145736 | tf_op jit(solution)/shard_map/ppermute | solution.py:685
  4.1 27.0 %collective-permute-start.1 = (bf16[128,4096]{1,0:T(8,128)(2,1)}, bf16[128,4096]{1,0:T(8,128)(2,1)S(1)}, u32[]{:S(2)}, u32[]{:S(2)}) collective-permute-start(bf16[128,4096]{1,0:T(8,128)(2,1)} %convert_element_type.148.refs_14_.refs_0_), channel_id=1, source_target_pairs={{0,2},{1,3},{2,0},{3,1},{4,6},{5,7},{6,4},{7,5},{8,10},{9,11},{10,... | collective-permute-start | bytes 3145736 | tf_op jit(solution)/shard_map/ppermute | solution.py:685
  6.6 17.6 %collective-permute-start.2 = (f32[32,128]{1,0:T(8,128)S(1)}, f32[32,128]{1,0:T(8,128)S(1)}, u32[]{:S(2)}, u32[]{:S(2)}) collective-permute-start(f32[32,128]{1,0:T(8,128)S(1)} %bitcast.179), channel_id=1, source_target_pairs={{0,1},{1,0},{2,3},{3,2},{4,5},{5,4},{6,7},{7,6},{8,9},{9,8},{10,11... | collective-permute-start | bytes 49160 | tf_op jit(solution)/shard_map/ppermute | solution.py:685
  6.8 24.3 %collective-permute-start.3 = (f32[32,128]{1,0:T(8,128)S(1)}, f32[32,128]{1,0:T(8,128)}, u32[]{:S(2)}, u32[]{:S(2)}) collective-permute-start(f32[32,128]{1,0:T(8,128)S(1)} %bitcast.180), channel_id=1, source_target_pairs={{0,2},{1,3},{2,0},{3,1},{4,6},{5,7},{6,4},{7,5},{8,10},{9,11},{10,... | collective-permute-start | bytes 49160 | tf_op jit(solution)/shard_map/ppermute | solution.py:685
  7.4 2.5 copy-start.10
  24.1 9.4 %copy-start.13 = (f32[32,128]{1,0:T(8,128)}, f32[32,128]{1,0:T(8,128)S(1)}, u32[]{:S(2)}) copy-start(f32[32,128]{1,0:T(8,128)S(1)} %collective-permute-done.2.refs_19_) | copy-start | bytes 49156
  31.1 2.5 copy-start.3
  31.1 2.7 %collective-permute-start.4 = (bf16[128,4096]{1,0:T(8,128)(2,1)S(1)}, bf16[128,4096]{1,0:T(8,128)(2,1)S(1)}, u32[]{:S(2)}, u32[]{:S(2)}) collective-permute-start(bf16[128,4096]{1,0:T(8,128)(2,1)S(1)} %collective-permute-done.1.refs_16_.refs_0_.refs_2_), channel_id=1, source_target_pairs={{0,1},{1,0},{2,3},{3,2},{4,5},{5,4},{6,7},{7,6},{8,9},{9,8},{10,11... | collective-permute-start | bytes 3145736 | tf_op jit(solution)/shard_map/ppermute | solution.py:685
  31.1 4.2 %collective-permute-start.5 = (f32[32,128]{1,0:T(8,128)}, f32[32,128]{1,0:T(8,128)S(1)}, u32[]{:S(2)}, u32[]{:S(2)}) collective-permute-start(f32[32,128]{1,0:T(8,128)} %collective-permute-done.3.refs_20_), channel_id=1, source_target_pairs={{0,1},{1,0},{2,3},{3,2},{4,5},{5,4},{6,7},{7,6},{8,9},{9,8},{10,11... | collective-permute-start | bytes 49160 | tf_op jit(solution)/shard_map/ppermute | solution.py:685
  110.1 2.2 copy-start.5
  112.4 3.1 %collective-permute-start.6 = (bf16[4608,128]{1,0:T(8,128)(2,1)}, bf16[4608,128]{1,0:T(8,128)(2,1)S(1)}, u32[]{:S(2)}, u32[]{:S(2)}) collective-permute-start(bf16[4608,128]{1,0:T(8,128)(2,1)} %pad_maximum_fusion.1), channel_id=1, source_target_pairs={{0,1},{1,0},{2,3},{3,2},{4,5},{5,4},{6,7},{7,6},{8,9},{9,8},{10,11... | collective-permute-start | bytes 3538952 | tf_op jit(solution)/shard_map/ppermute | solution.py:685
  116.9 28.4 %collective-permute-start.7 = (bf16[3328,128]{1,0:T(8,128)(2,1)S(1)}, bf16[3328,128]{1,0:T(8,128)(2,1)S(1)}, u32[]{:S(2)}, u32[]{:S(2)}) collective-permute-start(bf16[3328,128]{1,0:T(8,128)(2,1)S(1)} %pad_maximum_fusion.3), channel_id=1, source_target_pairs={{0,2},{1,3},{2,0},{3,1},{4,6},{5,7},{6,4},{7,5},{8,10},{9,11},{10,... | collective-permute-start | bytes 2555912 | tf_op jit(solution)/shard_map/ppermute | solution.py:685
  145.2 2.7 %collective-permute-start.8 = (bf16[4096,128]{1,0:T(8,128)(2,1)S(1)}, bf16[4096,128]{1,0:T(8,128)(2,1)S(1)}, u32[]{:S(2)}, u32[]{:S(2)}) collective-permute-start(bf16[4096,128]{1,0:T(8,128)(2,1)S(1)} %pad_maximum_fusion.2), channel_id=1, source_target_pairs={{0,1},{1,0},{2,3},{3,2},{4,5},{5,4},{6,7},{7,6},{8,9},{9,8},{10,11... | collective-permute-start | bytes 3145736 | tf_op jit(solution)/shard_map/ppermute | solution.py:685
  145.3 2.6 %copy-start.8 = (bf16[2048,128]{1,0:T(8,128)(2,1)S(1)}, bf16[2048,128]{1,0:T(8,128)(2,1)}, u32[]{:S(2)}) copy-start(bf16[2048,128]{1,0:T(8,128)(2,1)} %get-tuple-element.130) | copy-start | bytes 1572868
  145.3 2.6 %copy-start.9 = (bf16[2048,128]{1,0:T(8,128)(2,1)S(1)}, bf16[2048,128]{1,0:T(8,128)(2,1)}, u32[]{:S(2)}) copy-start(bf16[2048,128]{1,0:T(8,128)(2,1)} %get-tuple-element.136) | copy-start | bytes 1572868
  148.3 14.0 %collective-permute-start.9 = (bf16[2048,128]{1,0:T(8,128)(2,1)S(1)}, bf16[2048,128]{1,0:T(8,128)(2,1)S(1)}, u32[]{:S(2)}, u32[]{:S(2)}) collective-permute-start(bf16[2048,128]{1,0:T(8,128)(2,1)S(1)} %get-tuple-element.144), channel_id=1, source_target_pairs={{0,2},{1,3},{2,0},{3,1},{4,6},{5,7},{6,4},{7,5},{8,10},{9,11},{10,... | collective-permute-start | bytes 1572872 | tf_op jit(solution)/shard_map/ppermute | solution.py:685
  150.1 12.0 %collective-permute-start.10 = (bf16[1664,128]{1,0:T(8,128)(2,1)S(1)}, bf16[1664,128]{1,0:T(8,128)(2,1)S(1)}, u32[]{:S(2)}, u32[]{:S(2)}) collective-permute-start(bf16[1664,128]{1,0:T(8,128)(2,1)S(1)} %pad_maximum_fusion.8), channel_id=1, source_target_pairs={{0,4},{4,0},{8,12},{12,8},{16,20},{20,16},{24,28},{28,24},{1,5},{5... | collective-permute-start | bytes 1277960 | tf_op jit(solution)/shard_map/ppermute | solution.py:688
  162.4 8.0 %copy-start.15 = (f32[8,128]{1,0:T(8,128)S(1)}, f32[8,128]{1,0:T(8,128)}, u32[]{:S(2)}) copy-start(f32[8,128]{1,0:T(8,128)} %get-tuple-element.143) | copy-start | bytes 12292
  162.4 9.8 %copy-start.6 = (bf16[2048,128]{1,0:T(8,128)(2,1)S(1)}, bf16[2048,128]{1,0:T(8,128)(2,1)}, u32[]{:S(2)}) copy-start(bf16[2048,128]{1,0:T(8,128)(2,1)} %get-tuple-element.147) | copy-start | bytes 1572868
  162.4 8.0 %collective-permute-start.16 = (bf16[2072,128]{1,0:T(8,128)(2,1)S(1)}, bf16[2072,128]{1,0:T(8,128)(2,1)S(1)}, u32[]{:S(2)}, u32[]{:S(2)}) collective-permute-start(bf16[2072,128]{1,0:T(8,128)(2,1)S(1)} %pad_maximum_fusion.7), channel_id=1, source_target_pairs={{0,1},{1,0},{2,3},{3,2},{4,5},{5,4},{6,7},{7,6},{8,9},{9,8},{10,11... | collective-permute-start | bytes 1591304 | tf_op jit(solution)/shard_map/ppermute | solution.py:685
  162.7 7.7 %collective-permute-start.11 = (bf16[832,128]{1,0:T(8,128)(2,1)S(1)}, bf16[832,128]{1,0:T(8,128)(2,1)S(1)}, u32[]{:S(2)}, u32[]{:S(2)}) collective-permute-start(bf16[832,128]{1,0:T(8,128)(2,1)S(1)} %pad_maximum_fusion.11), channel_id=1, source_target_pairs={{0,8},{4,12},{8,0},{12,4},{16,24},{20,28},{24,16},{28,20},{1,9},{5... | collective-permute-start | bytes 638984 | tf_op jit(solution)/shard_map/ppermute | solution.py:688
  170.4 3.7 %collective-permute-start.18 = (f32[8,128]{1,0:T(8,128)S(1)}, f32[8,128]{1,0:T(8,128)S(1)}, u32[]{:S(2)}, u32[]{:S(2)}) collective-permute-start(f32[8,128]{1,0:T(8,128)S(1)} %fusion.27), channel_id=1, source_target_pairs={{0,2},{1,3},{2,0},{3,1},{4,6},{5,7},{6,4},{7,5},{8,10},{9,11},{10,... | collective-permute-start | bytes 12296 | tf_op jit(solution)/shard_map/ppermute | solution.py:685
  174.1 3.6 %collective-permute-start.19 = (f32[8,128]{1,0:T(8,128)S(1)}, f32[8,128]{1,0:T(8,128)S(1)}, u32[]{:S(2)}, u32[]{:S(2)}) collective-permute-start(f32[8,128]{1,0:T(8,128)S(1)} %add.250), channel_id=1, source_target_pairs={{0,4},{4,0},{8,12},{12,8},{16,20},{20,16},{24,28},{28,24},{1,5},{5... | collective-permute-start | bytes 12296 | tf_op jit(solution)/shard_map/ppermute | solution.py:688
  176.0 6.6 %collective-permute-start.17 = (bf16[1024,128]{1,0:T(8,128)(2,1)S(1)}, bf16[1024,128]{1,0:T(8,128)(2,1)S(1)}, u32[]{:S(2)}, u32[]{:S(2)}) collective-permute-start(bf16[1024,128]{1,0:T(8,128)(2,1)S(1)} %fusion.5), channel_id=1, source_target_pairs={{0,4},{4,0},{8,12},{12,8},{16,20},{20,16},{24,28},{28,24},{1,5},{5... | collective-permute-start | bytes 786440 | tf_op jit(solution)/shard_map/ppermute | solution.py:688
  182.7 5.1 %collective-permute-start.20 = (bf16[536,128]{1,0:T(8,128)(2,1)S(1)}, bf16[536,128]{1,0:T(8,128)(2,1)S(1)}, u32[]{:S(2)}, u32[]{:S(2)}) collective-permute-start(bf16[536,128]{1,0:T(8,128)(2,1)S(1)} %pad_maximum_fusion.15), channel_id=1, source_target_pairs={{0,8},{4,12},{8,0},{12,4},{16,24},{20,28},{24,16},{28,20},{1,9},{5... | collective-permute-start | bytes 411656 | tf_op jit(solution)/shard_map/ppermute | solution.py:688
  187.8 12.4 %copy-start.17 = (f32[1572]{0:T(1024)S(1)}, f32[1572]{0:T(1024)}, u32[]{:S(2)}) copy-start(f32[1572]{0:T(1024)} %param.61) | copy-start | bytes 18868
  187.9 12.4 %copy-start.18 = (f32[1572]{0:T(1024)S(1)}, f32[1572]{0:T(1024)}, u32[]{:S(2)}) copy-start(f32[1572]{0:T(1024)} %param.53) | copy-start | bytes 18868
  188.0 5.3 %collective-permute-start.21 = (bf16[280,128]{1,0:T(8,128)(2,1)S(1)}, bf16[280,128]{1,0:T(8,128)(2,1)S(1)}, u32[]{:S(2)}, u32[]{:S(2)}) collective-permute-start(bf16[280,128]{1,0:T(8,128)(2,1)S(1)} %pad_maximum_fusion.17), channel_id=1, source_target_pairs={{0,16},{4,20},{8,24},{12,28},{16,0},{20,4},{24,8},{28,12},{1,17},{... | collective-permute-start | bytes 215048 | tf_op jit(solution)/shard_map/ppermute | solution.py:688
  188.1 8.2 %collective-permute-start.12 = (bf16[416,128]{1,0:T(8,128)(2,1)S(1)}, bf16[416,128]{1,0:T(8,128)(2,1)S(1)}, u32[]{:S(2)}, u32[]{:S(2)}) collective-permute-start(bf16[416,128]{1,0:T(8,128)(2,1)S(1)} %pad_maximum_fusion.16), channel_id=1, source_target_pairs={{0,16},{4,20},{8,24},{12,28},{16,0},{20,4},{24,8},{28,12},{1,17},{... | collective-permute-start | bytes 319496 | tf_op jit(solution)/shard_map/ppermute | solution.py:688
  198.3 2.6 %collective-permute-start.27 = (f32[8,128]{1,0:T(8,128)S(1)}, f32[8,128]{1,0:T(8,128)S(1)}, u32[]{:S(2)}, u32[]{:S(2)}) collective-permute-start(f32[8,128]{1,0:T(8,128)S(1)} %broadcast_in_dim.2), channel_id=1, source_target_pairs={{0,1},{1,0},{2,3},{3,2},{4,5},{5,4},{6,7},{7,6},{8,9},{9,8},{10,11... | collective-permute-start | bytes 12296 | tf_op jit(solution)/shard_map/ppermute | solution.py:685
  198.4 3.7 %collective-permute-start.28 = (f32[8,128]{1,0:T(8,128)S(1)}, f32[8,128]{1,0:T(8,128)S(1)}, u32[]{:S(2)}, u32[]{:S(2)}) collective-permute-start(f32[8,128]{1,0:T(8,128)S(1)} %broadcast_in_dim.2), channel_id=1, source_target_pairs={{0,2},{1,3},{2,0},{3,1},{4,6},{5,7},{6,4},{7,5},{8,10},{9,11},{10,... | collective-permute-start | bytes 12296 | tf_op jit(solution)/shard_map/ppermute | solution.py:685
  198.8 3.3 %collective-permute-start.29 = (f32[8,128]{1,0:T(8,128)S(1)}, f32[8,128]{1,0:T(8,128)S(1)}, u32[]{:S(2)}, u32[]{:S(2)}) collective-permute-start(f32[8,128]{1,0:T(8,128)S(1)} %broadcast_in_dim.2), channel_id=1, source_target_pairs={{0,3},{1,2},{2,1},{3,0},{4,7},{5,6},{6,5},{7,4},{8,11},{9,10},{10,... | collective-permute-start | bytes 12296 | tf_op jit(solution)/shard_map/ppermute | solution.py:685
  202.1 4.6 %collective-permute-start.30 = (f32[8,128]{1,0:T(8,128)S(1)}, f32[8,128]{1,0:T(8,128)S(1)}, u32[]{:S(2)}, u32[]{:S(2)}) collective-permute-start(f32[8,128]{1,0:T(8,128)S(1)} %add_add_fusion), channel_id=1, source_target_pairs={{0,16},{4,20},{8,24},{12,28},{16,0},{20,4},{24,8},{28,12},{1,17},{... | collective-permute-start | bytes 12296 | tf_op jit(solution)/shard_map/ppermute | solution.py:688
  206.7 3.6 %collective-permute-start.31 = (f32[8,128]{1,0:T(8,128)S(1)}, f32[8,128]{1,0:T(8,128)S(1)}, u32[]{:S(2)}, u32[]{:S(2)}) collective-permute-start(f32[8,128]{1,0:T(8,128)S(1)} %add.264), channel_id=1, source_target_pairs={{0,8},{4,12},{8,0},{12,4},{16,24},{20,28},{24,16},{28,20},{1,9},{5... | collective-permute-start | bytes 12296 | tf_op jit(solution)/shard_map/ppermute | solution.py:688
  206.7 7.7 %collective-permute-start.13 = (f16[352,128]{1,0:T(8,128)(2,1)S(1)}, f16[352,128]{1,0:T(8,128)(2,1)S(1)}, u32[]{:S(2)}, u32[]{:S(2)}) collective-permute-start(f16[352,128]{1,0:T(8,128)(2,1)S(1)} %concatenate.96), channel_id=1, source_target_pairs={{0,16},{4,20},{8,24},{12,28},{16,0},{20,4},{24,8},{28,12},{1,17},{... | collective-permute-start | bytes 270344 | tf_op jit(solution)/shard_map/ppermute | solution.py:688
  210.3 3.6 %collective-permute-start.32 = (f32[8,128]{1,0:T(8,128)S(1)}, f32[8,128]{1,0:T(8,128)S(1)}, u32[]{:S(2)}, u32[]{:S(2)}) collective-permute-start(f32[8,128]{1,0:T(8,128)S(1)} %add.265), channel_id=1, source_target_pairs={{0,4},{4,0},{8,12},{12,8},{16,20},{20,16},{24,28},{28,24},{1,5},{5... | collective-permute-start | bytes 12296 | tf_op jit(solution)/shard_map/ppermute | solution.py:688
  212.2 5.6 %collective-permute-start.22 = (f16[272,128]{1,0:T(8,128)(2,1)S(1)}, f16[272,128]{1,0:T(8,128)(2,1)S(1)}, u32[]{:S(2)}, u32[]{:S(2)}) collective-permute-start(f16[272,128]{1,0:T(8,128)(2,1)S(1)} %concatenate.102), channel_id=1, source_target_pairs={{0,16},{4,20},{8,24},{12,28},{16,0},{20,4},{24,8},{28,12},{1,17},{... | collective-permute-start | bytes 208904 | tf_op jit(solution)/shard_map/ppermute | solution.py:688
  214.6 6.7 %collective-permute-start.14 = (f16[704,128]{1,0:T(8,128)(2,1)S(1)}, f16[704,128]{1,0:T(8,128)(2,1)S(1)}, u32[]{:S(2)}, u32[]{:S(2)}) collective-permute-start(f16[704,128]{1,0:T(8,128)(2,1)S(1)} %pad_maximum_fusion.12), channel_id=1, source_target_pairs={{0,8},{4,12},{8,0},{12,4},{16,24},{20,28},{24,16},{28,20},{1,9},{5... | collective-permute-start | bytes 540680 | tf_op jit(solution)/shard_map/ppermute | solution.py:688
  217.9 5.1 %collective-permute-start.23 = (f16[544,128]{1,0:T(8,128)(2,1)S(1)}, f16[544,128]{1,0:T(8,128)(2,1)S(1)}, u32[]{:S(2)}, u32[]{:S(2)}) collective-permute-start(f16[544,128]{1,0:T(8,128)(2,1)S(1)} %pad_maximum_fusion.14), channel_id=1, source_target_pairs={{0,8},{4,12},{8,0},{12,4},{16,24},{20,28},{24,16},{28,20},{1,9},{5... | collective-permute-start | bytes 417800 | tf_op jit(solution)/shard_map/ppermute | solution.py:688
  221.5 8.9 %collective-permute-start.15 = (f16[1408,128]{1,0:T(8,128)(2,1)S(1)}, f16[1408,128]{1,0:T(8,128)(2,1)S(1)}, u32[]{:S(2)}, u32[]{:S(2)}) collective-permute-start(f16[1408,128]{1,0:T(8,128)(2,1)S(1)} %pad_maximum_fusion.9), channel_id=1, source_target_pairs={{0,4},{4,0},{8,12},{12,8},{16,20},{20,16},{24,28},{28,24},{1,5},{5... | collective-permute-start | bytes 1081352 | tf_op jit(solution)/shard_map/ppermute | solution.py:688
  223.2 10.1 %collective-permute-start.24 = (f16[1088,128]{1,0:T(8,128)(2,1)S(1)}, f16[1088,128]{1,0:T(8,128)(2,1)S(1)}, u32[]{:S(2)}, u32[]{:S(2)}) collective-permute-start(f16[1088,128]{1,0:T(8,128)(2,1)S(1)} %pad_maximum_fusion.10), channel_id=1, source_target_pairs={{0,4},{4,0},{8,12},{12,8},{16,20},{20,16},{24,28},{28,24},{1,5},{5... | collective-permute-start | bytes 835592 | tf_op jit(solution)/shard_map/ppermute | solution.py:688
  231.2 7.1 %collective-permute-start.25 = (f32[640,128]{1,0:T(8,128)S(1)}, f32[640,128]{1,0:T(8,128)S(1)}, u32[]{:S(2)}, u32[]{:S(2)}) collective-permute-start(f32[640,128]{1,0:T(8,128)S(1)} %bitcast.168), channel_id=1, source_target_pairs={{0,2},{1,3},{2,0},{3,1},{4,6},{5,7},{6,4},{7,5},{8,10},{9,11},{10,... | collective-permute-start | bytes 983048 | tf_op jit(solution)/shard_map/ppermute | solution.py:685
  238.5 2.7 %collective-permute-start.26 = (f32[1280,128]{1,0:T(8,128)S(1)}, f32[1280,128]{1,0:T(8,128)S(1)}, u32[]{:S(2)}, u32[]{:S(2)}) collective-permute-start(f32[1280,128]{1,0:T(8,128)S(1)} %pad_maximum_fusion.5), channel_id=1, source_target_pairs={{0,1},{1,0},{2,3},{3,2},{4,5},{5,4},{6,7},{7,6},{8,9},{9,8},{10,11... | collective-permute-start | bytes 1966088 | tf_op jit(solution)/shard_map/ppermute | solution.py:685
  242.4 12.3 %copy-start.1 = (bf16[5,8192]{1,0:T(8,128)(2,1)S(1)}, bf16[5,8192]{1,0:T(8,128)(2,1)}, u32[]{:S(2)}) copy-start(bf16[5,8192]{1,0:T(8,128)(2,1)} %param.32) | copy-start | bytes 245764
  (4 other events, 4.3 us)

commit v4 on v3

--- a/solution.py
+++ b/solution.py
@@ -525,24 +525,36 @@
     pack[R_END:R_PACK, :] = jnp.zeros((R_PACK - R_END, 128), f32)
 
 
-def body_edges(jobs, start, last, meta, *refs):
+def body_edges(jobs, slots, extra_in, last, meta, *refs):
     n = len(jobs)
     ws, (src, g, hid), refs = refs[:n], refs[n : n + 3], refs[n + 3 :]
-    if not start:
+    if extra_in == "pack":
+        (place, pack), refs = refs[:2], refs[2:]
+    else:
         hid_before, refs = refs[0], refs[1:]
     if last:
         (before, feat, sums), refs = refs[:3], refs[3:]
-    outs, result, built, acc = refs[:n], refs[n], refs[n + 1], refs[n + 2]
-    grad_hid = refs[n + 3] if last else result
+    count = 1 + max(slot for slot, _ in slots)
+    outs, result, refs = refs[:count], refs[count], refs[count + 1 :]
+    built, acc = refs[:2]
+    grad_hid = refs[2] if last else result
     blocks = meta[0]
     rows = ws[0].shape[1] // H
+    span = rows * EH
+
+    if extra_in == "pack":
+        half = pack.shape[0] // 2
+        sent = pack[pl.ds(pl.multiple_of(place[0] * half, half), half), :]
+        high, low = split(sent)
+        outs[0][span : span + half, :] = high
+        outs[0][span + half : span + 2 * half, :] = low
 
     acc[...] = jnp.zeros_like(acc)
 
     def edges(b, carry):
         c = columns(b * LB, LB)
         s0, s1 = src[0, :, c].astype(f32), src[1, :, c].astype(f32)
-        pulled = None if start else hid_before[:, c]
+        pulled = None if extra_in == "pack" else hid_before[:, c]
         for q, (rel, chunk) in enumerate(jobs):
             at = (rel * CHUNKS + chunk) * rows
             g0 = g[0, at : at + rows, c].astype(f32)
@@ -558,11 +570,10 @@
         return carry
 
     lax.fori_loop(0, blocks, edges, 0)
-    for q in range(n):
+    for q, (slot, at) in enumerate(slots):
         for i in range(rows):
-            outs[q][i * EH : (i + 1) * EH, :] = acc[q, :, i * H : (i + 1) * H].astype(
-                outs[q].dtype
-            )
+            r = at + i * EH
+            outs[slot][r : r + EH, :] = acc[q, :, i * H : (i + 1) * H].astype(bf16)
 
     if last:
         result[...] = sums[...]
@@ -577,6 +588,11 @@
             return carry
 
         lax.fori_loop(0, blocks, finish, 0)
+        high, low = split(result[...])
+        rest = result[...] - high.astype(f32) - low.astype(f32)
+        outs[0][span : span + 32, :] = jnp.concatenate(
+            [high.astype(f32), low.astype(f32), rest, jnp.zeros_like(rest)], axis=0
+        ).astype(bf16)
 
 
 def adamw(weight, grad, moment, second):
@@ -596,57 +612,48 @@
     (pack, grad_in, squares), refs = refs[:3], refs[3:]
     params, moments, seconds = refs[0:8], refs[8:16], refs[16:24]
     outs = refs[24:48]
-    loss, count, norm, scale = refs[48:52]
+    loss, count, norm = refs[48:51]
 
     def step(index, grad, at=...):
         new = adamw(params[index][at], grad, moments[index][at], seconds[index][at])
         for kind in range(3):
             outs[kind * 8 + index][at] = new[kind]
 
-    @pl.when(pl.program_id(0) == 0)
-    def _():
-        total = squares[0:1, 0:1] + total_of(jnp.square(grad_in[: G_BIAS + 1, :]))
-        for k in range(4):
-            total = total + total_of(jnp.square(pack[R_LSTM + k * 2 * H : R_LSTM + k * 2 * H + H, :]))
-        loss[...] = grad_in[G_SUMS : G_SUMS + 1, 0:1]
-        number = grad_in[G_SUMS : G_SUMS + 1, 1:2]
-        count[...] = number
-        grad_norm = jnp.sqrt(total) / number
-        norm[...] = grad_norm
-        factor = jnp.minimum(1.0, clip_norm / grad_norm) / number
-        scale[...] = jnp.broadcast_to(factor, scale.shape)
-        step(0, grad_in[:EIN, :] * factor)
-        step(2, pack[pl.ds(pl.multiple_of(R_EBIAS + place[0], 8), own_rows), :] * factor)
-        for half in range(2):
-            for q in range(3):
-                r = R_GRU + (half * 3 + q) * H
-                step(3, pack[r : r + H, :] * factor, (half, slice(None), slice(q * H, (q + 1) * H)))
-        for k in range(4):
-            r = R_LSTM + k * 2 * H
-            for block, start in ((0, 0), (1, H), (2, 0)):
-                step(
-                    4,
-                    pack[r + start : r + start + H, :] * factor,
-                    (slice(block * H, (block + 1) * H), slice(k * H, (k + 1) * H)),
-                )
-        step(5, pack[R_FIRST:R_GRU, :] * factor)
-        step(6, pack[R_SECOND : R_SECOND + NT, :] * factor)
-        bias = jnp.concatenate(
-            [grad_in[G_BIAS : G_BIAS + 1, :], pack[R_MISC + 1 : R_EBIAS, :]], axis=0
-        )
-        step(7, bias * factor)
-
-    per = pl.num_programs(0) // CHUNKS
+    total = squares[0:1, 0:1] + total_of(jnp.square(grad_in[: G_BIAS + 1, :]))
+    for k in range(4):
+        total = total + total_of(jnp.square(pack[R_LSTM + k * 2 * H : R_LSTM + k * 2 * H + H, :]))
+    loss[...] = grad_in[G_SUMS : G_SUMS + 1, 0:1]
+    number = grad_in[G_SUMS : G_SUMS + 1, 1:2]
+    count[...] = number
+    grad_norm = jnp.sqrt(total) / number
+    norm[...] = grad_norm
+    factor = jnp.minimum(1.0, clip_norm / grad_norm) / number
+    step(0, grad_in[:EIN, :] * factor)
+    step(2, pack[pl.ds(pl.multiple_of(R_EBIAS + place[0], 8), own_rows), :] * factor)
+    for half in range(2):
+        for q in range(3):
+            r = R_GRU + (half * 3 + q) * H
+            step(3, pack[r : r + H, :] * factor, (half, slice(None), slice(q * H, (q + 1) * H)))
+    for k in range(4):
+        r = R_LSTM + k * 2 * H
+        for block, start in ((0, 0), (1, H), (2, 0)):
+            step(
+                4,
+                pack[r + start : r + start + H, :] * factor,
+                (slice(block * H, (block + 1) * H), slice(k * H, (k + 1) * H)),
+            )
+    step(5, pack[R_FIRST:R_GRU, :] * factor)
+    step(6, pack[R_SECOND : R_SECOND + NT, :] * factor)
+    bias = jnp.concatenate(
+        [grad_in[G_BIAS : G_BIAS + 1, :], pack[R_MISC + 1 : R_EBIAS, :]], axis=0
+    )
+    step(7, bias * factor)
+
+    rows = own_rows // CHUNKS
     for c in range(CHUNKS):
-
-        @pl.when(pl.program_id(0) // per == c)
-        def _(c=c):
-            for i in range(params[1].shape[1] // H):
-                step(
-                    1,
-                    owns[c][i * EH : (i + 1) * EH, :] * scale[0:1, 0:1],
-                    (slice(None), slice(i * H, (i + 1) * H)),
-                )
+        for i in range(rows):
+            at = (c * rows + i) * H
+            step(1, owns[c][i * EH : (i + 1) * EH, :] * factor, (slice(None), slice(at, at + H)))
 
 
 VM = pl.BlockSpec(memory_space=pltpu.VMEM)
@@ -809,20 +816,20 @@
 
     span = own_rows * H // CHUNKS
 
-    def edge_parts(jobs, before_hid, last):
-        start = before_hid is None
-        extra = () if start else (before_hid,)
+    def edge_parts(jobs, slots, heights, extra, last):
+        kind = "pack" if len(extra) == 2 else "sum"
         if last:
             extra = extra + (before, feat, sums)
         *found, result = pl.pallas_call(
-            functools.partial(body_edges, jobs, start, last),
+            functools.partial(body_edges, jobs, slots, kind, last),
             grid=(1,),
-            out_shape=(sds((span, EH), bf16),) * len(jobs)
+            out_shape=tuple(sds((height, EH), bf16) for height in heights)
             + (sds((8, EH) if last else (EH, space), f32),),
             in_specs=[SM]
             + [pl.BlockSpec((EH, span), lambda i, c=chunk: (0, c)) for _, chunk in jobs]
-            + [VM] * (3 + len(extra)),
-            out_specs=(VM,) * (len(jobs) + 1),
+            + [VM] * 3
+            + ([SM, VM] if kind == "pack" else [VM] * len(extra)),
+            out_specs=(VM,) * (len(heights) + 1),
             scratch_shapes=[
                 pltpu.VMEM((2, span, LB), bf16),
                 pltpu.VMEM((len(jobs), EH, span), f32),
@@ -859,89 +866,113 @@
             found = found + x[k]
         return found
 
-    (far, far_core), carry = edge_parts(((2, 0), (3, 0)), None, False)
-    pack_sent, pack = halves(pack, core_bit)
-    came = core(jnp.concatenate([far_core, as_low(pack_sent, 2)], axis=0))
+    def chain(own, pack, beside):
+        for swap, bit in mol_steps:
+            own_sent, own = halves(own, bit)
+            half = own.shape[0]
+            sent = [own_sent.astype(bf16)]
+            if pack is not None:
+                pack_sent, pack = halves(pack, bit)
+                sent.append(as_low(pack_sent, 2))
+            if beside is not None:
+                sent.append(as_low(beside["rows"], 3))
+            came = yield swap, jnp.concatenate(sent, axis=0) if len(sent) > 1 else sent[0]
+            own = own + came[:half].astype(f32)
+            if pack is not None:
+                pack = pack + from_low(came[half : half + 2 * pack.shape[0]], 2)
+            if beside is not None:
+                beside["rows"] = beside["rows"] + from_low(came[half:], 3)
+        piece = own if pack is None else jnp.concatenate([own, pack], axis=0)
+        height, rest = piece.shape[0], own.shape[0]
+        largest = jnp.maximum(jnp.max(jnp.abs(piece)), 1e-30)
+        power = 14.0 - jnp.ceil(jnp.log2(largest))
+        sent = jnp.concatenate(
+            [piece * jnp.exp2(power), jnp.broadcast_to(power, (16, 128))], axis=0
+        ).astype(jnp.float16)
+        for swap, bit in reversed(mol_steps):
+            came = yield swap, sent
+            sent = jnp.concatenate(
+                [jnp.where(bit == 0, sent, came), jnp.where(bit == 0, came, sent)], axis=0
+            )
+        sent = sent.astype(f32).reshape(-1, height + 16, 128)
+        back = jnp.exp2(-sent[:, height : height + 1, 0:1])
+        own = (sent[:, :rest] * back).reshape(-1, 128)
+        square = jnp.sum(own * own)
+        if pack is not None:
+            pack = (sent[:, rest:height] * back).reshape(-1, 128)
+            square = square + jnp.sum(pack * pack)
+        return own, pack, square
+
+    core_place = (1 - core_bit).reshape(1).astype(jnp.int32)
+    half = pack.shape[0] // 2
+    (message, far), carry = edge_parts(
+        ((2, 0), (3, 0)),
+        ((1, 0), (0, 0)),
+        (span + 2 * half, span),
+        (core_place, pack),
+        False,
+    )
+    came = core(message)
+    pack = halves(pack, core_bit)[1]
     pack_sent, pack = halves(pack + from_low(came[span:], 2), cross_bit)
     sent = (far.astype(f32) + came[:span].astype(f32)).astype(bf16)
     sent = jnp.concatenate([sent, as_low(pack_sent, 2)], axis=0)
     sent, carry = tie((sent, carry))
     arrived = cross(sent)
-    (near, near_core, far, far_core), carry = edge_parts(
-        ((0, 0), (1, 0), (2, 1), (3, 1)), carry, False
-    )
-    sent, arrived = tie((jnp.concatenate([near_core, far_core], axis=0), arrived))
-    came = core(sent)
+    (message, near, far), carry = edge_parts(
+        ((0, 0), (1, 0), (2, 1), (3, 1)),
+        ((1, 0), (0, 0), (2, 0), (0, span)),
+        (2 * span, span, span),
+        (carry,),
+        False,
+    )
+    message, arrived = tie((message, arrived))
+    came = core(message)
     own = near.astype(f32) + came[:span].astype(f32) + arrived[:span].astype(f32)
     pack = pack + from_low(arrived[span:], 2)
     sent = (far.astype(f32) + came[span:].astype(f32)).astype(bf16)
 
-    def first_stage(own, pack, swap, bit):
-        own_sent, own = halves(own, bit)
-        pack_sent, pack = halves(pack, bit)
-        half = own.shape[0]
-
-        def take(came):
-            return own + came[:half].astype(f32), pack + from_low(came[half:], 2)
-
-        return jnp.concatenate([own_sent.astype(bf16), as_low(pack_sent, 2)], axis=0), take
-
-    first_sent, take = first_stage(own, pack, *mol_steps[0])
+    first = chain(own, pack, None)
+    first_swap, first_sent = next(first)
     sent, first_sent, carry = tie((sent, first_sent, carry))
     arrived = cross(sent)
-    first_came = mol_steps[0][0](first_sent)
-    (near, near_core), grad_in = edge_parts(((0, 1), (1, 1)), carry, True)
-    sent = jnp.concatenate([near_core, as_low(grad_in, 3)], axis=0)
-    sent, arrived, first_came = tie((sent, arrived, first_came))
-    came = core(sent)
-    grad_in = grad_in + from_low(came[span:], 3)
+    first_came = first_swap(first_sent)
+    (message, near), grad_in = edge_parts(
+        ((0, 1), (1, 1)), ((1, 0), (0, 0)), (span + 32, span), (carry,), True
+    )
+    message, arrived, first_came = tie((message, arrived, first_came))
+    came = core(message)
+    beside = {"rows": grad_in + from_low(came[span : span + 24], 3)}
     own = near.astype(f32) + came[:span].astype(f32) + arrived.astype(f32)
-    first, pack = take(first_came)
-    grad_in = grad_in + cross(grad_in)
-    grad_in = grad_in + mol_steps[0][0](grad_in)
-    for index, (swap, bit) in enumerate(mol_steps):
-        if index > 0:
-            first_sent, take = first_stage(first, pack, swap, bit)
-            first, pack = take(swap(first_sent))
-        own_sent, own = halves(own, bit)
-        half = own.shape[0]
-        sent = own_sent.astype(bf16)
-        if index > 0:
-            sent = jnp.concatenate([sent, as_low(grad_in, 3)], axis=0)
-        came = swap(sent)
-        own = own + came[:half].astype(f32)
-        if index > 0:
-            grad_in = grad_in + from_low(came[half:], 3)
-    owns = [first, own]
-    own_rest = owns[0].shape[0]
-    pieces = [jnp.concatenate([owns[0], pack], axis=0)] + owns[1:]
-    squares = jnp.broadcast_to(sum(jnp.sum(piece * piece) for piece in pieces), (8, 128))
-
-    travel = []
-    for piece in pieces:
-        largest = jnp.maximum(jnp.max(jnp.abs(piece)), 1e-30)
-        power = 14.0 - jnp.ceil(jnp.log2(largest))
-        travel.append(
-            jnp.concatenate(
-                [piece * jnp.exp2(power), jnp.broadcast_to(power, (16, 128))], axis=0
-            ).astype(jnp.float16)
-        )
-    squares, travel[-1] = tie((squares, travel[-1]))
+
+    second = chain(own, None, beside)
+    second_swap, second_sent = next(second)
+    first_swap, first_sent = first.send(first_came)
+    while True:
+        first_sent, second_sent = tie((first_sent, second_sent))
+        first_came, second_came = first_swap(first_sent), second_swap(second_sent)
+        second_swap, second_sent = second.send(second_came)
+        try:
+            first_swap, first_sent = first.send(first_came)
+        except StopIteration as end:
+            first_own, pack, square = end.value
+            break
+    quarters = jnp.concatenate([pack, beside["rows"]], axis=0)
+    quarters, second_sent = tie((quarters, second_sent))
+    came, second_came = cross(quarters), second_swap(second_sent)
+    try:
+        second.send(second_came)
+    except StopIteration as end:
+        second_own, _, more = end.value
+    grad_in = beside["rows"] + came[-8:]
+    came = came[:-8]
+    pack = jnp.concatenate(
+        [jnp.where(cross_bit == 0, pack, came), jnp.where(cross_bit == 0, came, pack)], axis=0
+    )
+    pack = double(pack, core, core_bit)
+    squares = jnp.broadcast_to(square + more, (8, 128))
     squares = (squares + row_swap(squares, 1)) + (row_swap(squares, 2) + row_swap(squares, 3))
-    for swap, bit in reversed(mol_steps):
-        squares = squares + swap(squares)
-    for swap, bit in reversed(mol_steps):
-        travel = [double(sent, swap, bit) for sent in travel]
-    owns = []
-    for piece, sent in zip(pieces, travel):
-        height = piece.shape[0]
-        sent = sent.astype(f32).reshape(-1, height + 16, 128)
-        owns.append(sent[:, :height] * jnp.exp2(-sent[:, height : height + 1, 0:1]))
-    pack = owns[0][:, own_rest:].reshape(-1, 128)
-    owns[0] = owns[0][:, :own_rest]
-    owns = [own.reshape(-1, 128) for own in owns]
-    for swap, bit in reversed(row_steps):
-        pack = double(pack, swap, bit)
+    owns = [first_own, second_own]
 
     weights = [
         edge_in,
@@ -963,24 +994,12 @@
         else:
             group[7] = jnp.pad(group[7], (0, 16 * 128 - group[7].shape[0])).reshape(16, 128)
         states += group
-    grid = 2 * CHUNKS
-    block = pl.BlockSpec((EH, own_rows * H // grid), lambda i: (0, i))
-    own_specs = [
-        pl.BlockSpec((span // 2, EH), lambda i, c=c: (jnp.clip(i - 2 * c, 0, 1), 0))
-        for c in range(CHUNKS)
-    ]
-
-    def state_specs():
-        return [block if index == 1 else VM for index in range(8)] * 3
-
     shapes = [sds(state.shape, f32) for state in states]
     results = pl.pallas_call(
         functools.partial(body_adamw, own_rows),
-        grid=(grid,),
         out_shape=tuple(shapes) + (sds((1, 1), f32),) * 3,
-        in_specs=[SM] + own_specs + [VM, VM, VM] + state_specs(),
-        out_specs=tuple(state_specs()) + (VM,) * 3,
-        scratch_shapes=[pltpu.VMEM((8, 128), f32)],
+        in_specs=[SM] + [VM] * (CHUNKS + 3 + len(shapes)),
+        out_specs=(VM,) * (len(shapes) + 3),
         compiler_params=params,
     )(places, *owns, pack, grad_in, squares, *states)
     results = list(results)

time: 253 us -> 238 us (0.941); the launches traced: 255 us -> 233 us
  waiting for transfers between devices: 62.9 us -> 49.5 us
  starting transfers between devices: 34.9 us -> 29 us
  other arithmetic: 19.7 us -> 16.1 us
    ppermute x16 -> x12, waiting for transfers between devices: 39.4 us -> 26.5 us  [mol_swap(): lax.ppermute(x, 'mol', [(i, i ^ 1 << bit) for i in range(2 ** mol_bits)])]
    ppermute x17 -> x16, starting transfers between devices: 20.6 us -> 10.6 us  [row_swap(): return lax.ppermute(x, 'row', [(i, i ^ k) for i in range(row_count)])]
    ppermute x16 -> x12, starting transfers between devices: 14.3 us -> 18.4 us  [mol_swap(): lax.ppermute(x, 'mol', [(i, i ^ 1 << bit) for i in range(2 ** mol_bits)])]
    concatenate x8 -> x14, other arithmetic: 4.66 us -> 0.77 us  [the longest x6 0.61 us: chain(): jnp.concatenate([jnp.where(bit == 0, sent, came), jnp.where(bit == 0, cam...]
    reduce_sum x1 -> x3, other arithmetic: 0.65 us -> 4.26 us  [the longest x2 3.49 us: chain(): square = jnp.sum(own * own)]
    ppermute x17 -> x16, waiting for transfers between devices: 23.5 us -> 23 us  [row_swap(): return lax.ppermute(x, 'row', [(i, i ^ k) for i in range(row_count)])]
  transfers between devices with their start and end apart: 33 -> 28, of which waited for: 23 -> 20; matrix products, arithmetic and copies ran while one was open for 9% -> 9% of each run, Pallas kernels for 13% -> 14%
where the time goes in v4:
time: 238 us; the launch traced here: 233 us
  Pallas kernels  119 us (50%)
  waiting for transfers between devices  49.5 us (21%)
  starting transfers between devices  29 us (12%)
  other arithmetic  16.1 us (7%)
  local copies, waits for them, and re-layouts  14.6 us (6%)
  between operations  5.04 us (2%)
    pallas_call x1, Pallas kernels, per_device(): pl.pallas_call(main, out_shape=(sds((R_PACK, 128), f32), sds((8, 128), f3...  64 us
    pallas_call x3, Pallas kernels, edge_parts(): pl.pallas_call(functools.partial(body_edges, jobs, slots, kind, last), gr...  35.4 us
    ppermute x12, waiting for transfers between devices, mol_swap(): lax.ppermute(x, 'mol', [(i, i ^ 1 << bit) for i in range(2 ** mol_bits)])  26.5 us
    ppermute x16, waiting for transfers between devices, row_swap(): return lax.ppermute(x, 'row', [(i, i ^ k) for i in range(row_count)])  23 us
    ppermute x12, starting transfers between devices, mol_swap(): lax.ppermute(x, 'mol', [(i, i ^ 1 << bit) for i in range(2 ** mol_bits)])  18.4 us
    pallas_call x1, Pallas kernels, per_device(): pl.pallas_call(functools.partial(body_adamw, own_rows), out_shape=tuple(s...  11.4 us
    ppermute x16, starting transfers between devices, row_swap(): return lax.ppermute(x, 'row', [(i, i ^ k) for i in range(row_count)])  10.6 us
    pallas_call x1, Pallas kernels, per_device(): pl.pallas_call(functools.partial(body_prepare, mols), out_shape=(sds((2 +...  8.07 us
  transfers between devices with their start and end apart: 28, of which 20 were waited for; matrix products, arithmetic and copies ran while one was open for 9% of the time, Pallas kernels for 14%

profile of v4, /device:TPU:0, one launch (start us, length us, event | category | flops | bytes accessed | tf_op | source)
XLA Modules:
  0.0 233.1 jit_solution(13900820548100000660)
XLA Ops:
  0.7 1.9 convert_element_type.150.refs_14_.refs_0_
  3.1 2.6 %collective-permute-start.1 = (bf16[128,4096]{1,0:T(8,128)(2,1)S(1)}, bf16[128,4096]{1,0:T(8,128)(2,1)}, u32[]{:S(2)}, u32[]{:S(2)}) collective-permute-start(bf16[128,4096]{1,0:T(8,128)(2,1)S(1)} %convert_element_type.150.refs_14_.refs_0_), channel_id=1, source_target_pairs={{0,2},{1,3},{2,0},{3,1},{4,6},{5,7},{6,4},{7,5},{8,10},{9,11},{10,... | collective-permute-start | bytes 3145736 | tf_op jit(solution)/shard_map/ppermute | solution.py:692
  6.5 1.2 convert_bitcast_fusion
  9.8 1.4 copy.86
  11.3 1.2 copy.97
  12.4 8.1 %shard_map.502 = (s32[9]{0:T(128)}, bf16[128,1024]{1,0:T(8,128)(2,1)}, bf16[128,1792]{1,0:T(8,128)(2,1)}, f32[128,1792]{1,0:T(8,128)}, f32[8,1792]{1,0:T(8,128)}...) custom-call(s32[32]{0:T(128)} %refs_0_.1, bf16[32,448]{1,0:T(8,128)(2,1)} %reshape.252.table, ...), custom_call_target="tpu_custom_call" | custom-call | tf_op jit(solution)/shard_map/pallas_call | solution.py:727
  20.5 1.4 copy.87
  22.0 1.2 copy.96
  23.1 6.8 %collective-permute-done.3.refs_20_ = f32[32,128]{1,0:T(8,128)} collective-permute-done((f32[32,128]{1,0:T(8,128)S(1)}, f32[32,128]{1,0:T(8,128)}, u32[]{:S(2)}, u32[]{:S(2)}) %collective-permute-start.3) | collective-permute-done | bytes 16416 | tf_op jit(solution)/shard_map/ppermute | solution.py:692
  31.1 1.4 copy.88
  32.5 1.1 copy.95
  33.9 1.2 copy.94
  35.8 64.0 %shard_map.503 = (f32[2560,128]{1,0:T(8,128)}, f32[8,128]{1,0:T(8,128)}, bf16[2,128,1792]{2,1,0:T(8,128)(2,1)}, bf16[2,128,1792]{2,1,0:T(8,128)(2,1)}) custom-call(s32[32]{0:T(128)} %refs_0_.1, s32[32]{0:T(128)} %refs_1_.1, s32[4]{0:T(128)} %pad_add_fusion.refs_2_.place, s32[9]{0:T(128)} %get-tuple-element.119.refs_3_.meta, f32[12,32]{1,0:T(8,128)} %bitcast.181, ...), custom_call_target="tpu_custom_call" | custom-call | tf_op jit(solution)/shard_map/pallas_call | solution.py:768
  99.8 9.9 %shard_map.504 = (bf16[4608,128]{1,0:T(8,128)(2,1)}, bf16[2048,128]{1,0:T(8,128)(2,1)}, f32[128,1792]{1,0:T(8,128)}) custom-call(s32[9]{0:T(128)} %get-tuple-element.119.refs_3_.meta, bf16[128,4096]{1,0:T(8,128)(2,1)} %collective-permute-done.1.refs_16_.refs_0_.refs_2_, bf16[128,4096]{1,0:T(8,128)(2,1)} %copy-done.4, ...), custom_call_target="tpu_custom_call" | custom-call | tf_op jit(solution)/shard_map/pallas_call | solution.py:823
  109.8 3.0 %collective-permute-done.6 = bf16[4608,128]{1,0:T(8,128)(2,1)S(1)} collective-permute-done((bf16[4608,128]{1,0:T(8,128)(2,1)}, bf16[4608,128]{1,0:T(8,128)(2,1)S(1)}, u32[]{:S(2)}, u32[]{:S(2)}) %collective-permute-start.6) | collective-permute-done | bytes 1179680 | tf_op jit(solution)/shard_map/ppermute | solution.py:692
  113.1 0.9 copy-done.7
  114.2 1.8 collective-permute-start.7
  116.0 15.2 %shard_map.505 = (bf16[4096,128]{1,0:T(8,128)(2,1)}, bf16[2048,128]{1,0:T(8,128)(2,1)}, bf16[2048,128]{1,0:T(8,128)(2,1)}, f32[128,1792]{1,0:T(8,128)}) custom-call(s32[9]{0:T(128)} %get-tuple-element.119.refs_3_.meta, bf16[128,4096]{1,0:T(8,128)(2,1)} %copy-done.3, bf16[128,4096]{1,0:T(8,128)(2,1)} %collective-permute-done.refs_15_.refs_1_, ...), custom_call_target="tpu_custom_call" | custom-call | tf_op jit(solution)/shard_map/pallas_call | solution.py:823
  131.2 4.0 %collective-permute-done.7 = bf16[3328,128]{1,0:T(8,128)(2,1)S(1)} collective-permute-done((bf16[3328,128]{1,0:T(8,128)(2,1)S(1)}, bf16[3328,128]{1,0:T(8,128)(2,1)S(1)}, u32[]{:S(2)}, u32[]{:S(2)}) %collective-permute-start.7) | collective-permute-done | bytes 852000 | tf_op jit(solution)/shard_map/ppermute | solution.py:692
  135.5 2.6 %collective-permute-done.8 = bf16[4096,128]{1,0:T(8,128)(2,1)S(1)} collective-permute-done((bf16[4096,128]{1,0:T(8,128)(2,1)}, bf16[4096,128]{1,0:T(8,128)(2,1)S(1)}, u32[]{:S(2)}, u32[]{:S(2)}) %collective-permute-start.8) | collective-permute-done | bytes 1048608 | tf_op jit(solution)/shard_map/ppermute | solution.py:692
  138.1 1.1 convert_add_fusion.1
  139.3 1.8 collective-permute-start.9
  141.2 1.4 collective-permute-start.10
  142.5 10.3 %shard_map.506 = (bf16[2080,128]{1,0:T(8,128)(2,1)}, bf16[2048,128]{1,0:T(8,128)(2,1)}, f32[8,128]{1,0:T(8,128)}) custom-call(s32[9]{0:T(128)} %get-tuple-element.119.refs_3_.meta, bf16[128,4096]{1,0:T(8,128)(2,1)} %copy-done.3, bf16[128,4096]{1,0:T(8,128)(2,1)} %collective-permute-done.refs_15_.refs_1_, ...), custom_call_target="tpu_custom_call" | custom-call | tf_op jit(solution)/shard_map/pallas_call | solution.py:823
  153.8 1.9 collective-permute-done.11
  156.5 1.9 collective-permute-start.12
  158.4 1.5 collective-permute-start.13
  159.9 4.0 %collective-permute-done.12 = bf16[832,128]{1,0:T(8,128)(2,1)S(1)} collective-permute-done((bf16[832,128]{1,0:T(8,128)(2,1)S(1)}, bf16[832,128]{1,0:T(8,128)(2,1)S(1)}, u32[]{:S(2)}, u32[]{:S(2)}) %collective-permute-start.12) | collective-permute-done | bytes 213024 | tf_op jit(solution)/shard_map/ppermute | solution.py:695
  164.1 2.5 %collective-permute-done.13 = bf16[1048,128]{1,0:T(8,128)(2,1)S(1)} collective-permute-done((bf16[1048,128]{1,0:T(8,128)(2,1)S(1)}, bf16[1048,128]{1,0:T(8,128)(2,1)S(1)}, u32[]{:S(2)}, u32[]{:S(2)}) %collective-permute-start.13) | collective-permute-done | bytes 268320 | tf_op jit(solution)/shard_map/ppermute | solution.py:695
  166.7 2.6 %collective-permute-start.14 = (bf16[416,128]{1,0:T(8,128)(2,1)S(1)}, bf16[416,128]{1,0:T(8,128)(2,1)S(1)}, u32[]{:S(2)}, u32[]{:S(2)}) collective-permute-start(bf16[416,128]{1,0:T(8,128)(2,1)S(1)} %pad_maximum_fusion.15), channel_id=1, source_target_pairs={{0,16},{4,20},{8,24},{12,28},{16,0},{20,4},{24,8},{28,12},{1,17},{... | collective-permute-start | bytes 319496 | tf_op jit(solution)/shard_map/ppermute | solution.py:695
  169.8 4.1 %collective-permute-done.14 = bf16[416,128]{1,0:T(8,128)(2,1)S(1)} collective-permute-done((bf16[416,128]{1,0:T(8,128)(2,1)S(1)}, bf16[416,128]{1,0:T(8,128)(2,1)S(1)}, u32[]{:S(2)}, u32[]{:S(2)}) %collective-permute-start.14) | collective-permute-done | bytes 106528 | tf_op jit(solution)/shard_map/ppermute | solution.py:695
  175.7 1.6 collective-permute-start.17
  177.3 1.4 collective-permute-start.16
  178.7 4.9 %collective-permute-done.17 = bf16[280,128]{1,0:T(8,128)(2,1)S(1)} collective-permute-done((bf16[280,128]{1,0:T(8,128)(2,1)S(1)}, bf16[280,128]{1,0:T(8,128)(2,1)S(1)}, u32[]{:S(2)}, u32[]{:S(2)}) %collective-permute-start.17) | collective-permute-done | bytes 71712 | tf_op jit(solution)/shard_map/ppermute | solution.py:695
  185.6 1.9 collective-permute-start.18
  187.5 3.4 %collective-permute-done.19 = f16[272,128]{1,0:T(8,128)(2,1)S(1)} collective-permute-done((f16[272,128]{1,0:T(8,128)(2,1)S(1)}, f16[272,128]{1,0:T(8,128)(2,1)S(1)}, u32[]{:S(2)}, u32[]{:S(2)}) %collective-permute-start.19) | collective-permute-done | bytes 69664 | tf_op jit(solution)/shard_map/ppermute | solution.py:695
  190.9 1.1 collective-permute-done.18
  192.3 1.0 collective-permute-start.21
  193.3 2.0 collective-permute-start.20
  195.3 2.1 collective-permute-done.21
  197.6 3.2 %collective-permute-done.20 = f16[1408,128]{1,0:T(8,128)(2,1)S(1)} collective-permute-done((f16[1408,128]{1,0:T(8,128)(2,1)S(1)}, f16[1408,128]{1,0:T(8,128)(2,1)S(1)}, u32[]{:S(2)}, u32[]{:S(2)}) %collective-permute-start.20) | collective-permute-done | bytes 360480 | tf_op jit(solution)/shard_map/ppermute | solution.py:695
  202.3 2.5 %collective-permute-start.22 = (f16[1088,128]{1,0:T(8,128)(2,1)S(1)}, f16[1088,128]{1,0:T(8,128)(2,1)S(1)}, u32[]{:S(2)}, u32[]{:S(2)}) collective-permute-start(f16[1088,128]{1,0:T(8,128)(2,1)S(1)} %pad_maximum_fusion.8), channel_id=1, source_target_pairs={{0,4},{4,0},{8,12},{12,8},{16,20},{20,16},{24,28},{28,24},{1,5},{5... | collective-permute-start | bytes 835592 | tf_op jit(solution)/shard_map/ppermute | solution.py:695
  205.7 1.7 multiply_reduce_fusion.1
  209.9 2.0 collective-permute-done.23
  212.1 1.7 multiply_reduce_fusion
  217.1 1.6 collective-permute-done.26
  220.3 1.2 pad_maximum_fusion.refs_2_
  221.5 11.4 %shard_map.507 = (f32[5,128]{1,0:T(8,128)}, f32[128,4096]{1,0:T(8,128)}, f32[32,128]{1,0:T(8,128)}, f32[2,128,384]{2,1,0:T(8,128)}, f32[384,512]{1,0:T(8,128)}, ...) custom-call(s32[4]{0:T(128)} %pad_add_fusion.refs_2_.place, ...), custom_call_target="tpu_custom_call" | custom-call | tf_op jit(solution)/shard_map/pallas_call | solution.py:998
  (161 shorter events, 19.1 us)
Async XLA Ops:
  0.7 5.6 %copy-start = (bf16[5,8192]{1,0:T(8,128)(2,1)S(1)}, bf16[5,8192]{1,0:T(8,128)(2,1)}, u32[]{:S(2)}) copy-start(bf16[5,8192]{1,0:T(8,128)(2,1)} %param.32) | copy-start | bytes 245764
  0.7 5.8 %copy-start.2 = (f32[128,4096]{1,0:T(8,128)S(1)}, f32[128,4096]{1,0:T(8,128)}, u32[]{:S(2)}) copy-start(f32[128,4096]{1,0:T(8,128)} %refs_6_.1) | copy-start | bytes 6291460
  0.7 5.0 %copy-start.11 = (f32[4096]{0:T(1024)S(1)}, f32[4096]{0:T(1024)}, u32[]{:S(2)}) copy-start(f32[4096]{0:T(1024)} %param.40) | copy-start | bytes 49156
  0.7 5.4 %copy-start.12 = (s32[2,128,64]{1,2,0:T(8,128)S(1)}, s32[2,128,64]{1,2,0:T(8,128)}, u32[]{:S(2)}) copy-start(s32[2,128,64]{1,2,0:T(8,128)} %param.33) | copy-start | bytes 196612
  2.6 5.1 %copy-start.3 = (bf16[128,4096]{1,0:T(8,128)(2,1)}, bf16[128,4096]{1,0:T(8,128)(2,1)S(1)}, u32[]{:S(2)}) copy-start(bf16[128,4096]{1,0:T(8,128)(2,1)S(1)} %convert_element_type.150.refs_14_.refs_0_) | copy-start | bytes 3145732
  2.6 17.9 %collective-permute-start = (bf16[128,4096]{1,0:T(8,128)(2,1)S(1)}, bf16[128,4096]{1,0:T(8,128)(2,1)}, u32[]{:S(2)}, u32[]{:S(2)}) collective-permute-start(bf16[128,4096]{1,0:T(8,128)(2,1)S(1)} %convert_element_type.150.refs_14_.refs_0_), channel_id=1, source_target_pairs={{0,1},{1,0},{2,3},{3,2},{4,5},{5,4},{6,7},{7,6},{8,9},{9,8},{10,11... | collective-permute-start | bytes 3145736 | tf_op jit(solution)/shard_map/ppermute | solution.py:692
  3.1 26.8 %collective-permute-start.1 = (bf16[128,4096]{1,0:T(8,128)(2,1)S(1)}, bf16[128,4096]{1,0:T(8,128)(2,1)}, u32[]{:S(2)}, u32[]{:S(2)}) collective-permute-start(bf16[128,4096]{1,0:T(8,128)(2,1)S(1)} %convert_element_type.150.refs_14_.refs_0_), channel_id=1, source_target_pairs={{0,2},{1,3},{2,0},{3,1},{4,6},{5,7},{6,4},{7,5},{8,10},{9,11},{10,... | collective-permute-start | bytes 3145736 | tf_op jit(solution)/shard_map/ppermute | solution.py:692
  5.7 17.4 %collective-permute-start.2 = (f32[32,128]{1,0:T(8,128)S(1)}, f32[32,128]{1,0:T(8,128)S(1)}, u32[]{:S(2)}, u32[]{:S(2)}) collective-permute-start(f32[32,128]{1,0:T(8,128)S(1)} %bitcast.173), channel_id=1, source_target_pairs={{0,1},{1,0},{2,3},{3,2},{4,5},{5,4},{6,7},{7,6},{8,9},{9,8},{10,11... | collective-permute-start | bytes 49160 | tf_op jit(solution)/shard_map/ppermute | solution.py:692
  5.9 24.0 %collective-permute-start.3 = (f32[32,128]{1,0:T(8,128)S(1)}, f32[32,128]{1,0:T(8,128)}, u32[]{:S(2)}, u32[]{:S(2)}) collective-permute-start(f32[32,128]{1,0:T(8,128)S(1)} %bitcast.174), channel_id=1, source_target_pairs={{0,2},{1,3},{2,0},{3,1},{4,6},{5,7},{6,4},{7,5},{8,10},{9,11},{10,... | collective-permute-start | bytes 49160 | tf_op jit(solution)/shard_map/ppermute | solution.py:692
  6.5 1.2 copy-start.15
  6.5 2.5 %copy-start.10 = (bf16[32,29,128]{2,0,1:T(8,128)(2,1)S(1)}, bf16[32,29,128]{2,0,1:T(8,128)(2,1)}, u32[]{:S(2)}) copy-start(bf16[32,29,128]{2,0,1:T(8,128)(2,1)} %param.31) | copy-start | bytes 712708
  23.1 10.5 %copy-start.13 = (f32[32,128]{1,0:T(8,128)}, f32[32,128]{1,0:T(8,128)S(1)}, u32[]{:S(2)}) copy-start(f32[32,128]{1,0:T(8,128)S(1)} %collective-permute-done.2.refs_19_) | copy-start | bytes 49156
  29.9 3.8 %collective-permute-start.4 = (bf16[128,4096]{1,0:T(8,128)(2,1)}, bf16[128,4096]{1,0:T(8,128)(2,1)S(1)}, u32[]{:S(2)}, u32[]{:S(2)}) collective-permute-start(bf16[128,4096]{1,0:T(8,128)(2,1)} %collective-permute-done.1.refs_16_.refs_0_.refs_2_), channel_id=1, source_target_pairs={{0,1},{1,0},{2,3},{3,2},{4,5},{5,4},{6,7},{7,6},{8,9},{9,8},{10,11... | collective-permute-start | bytes 3145736 | tf_op jit(solution)/shard_map/ppermute | solution.py:692
  29.9 5.3 %collective-permute-start.5 = (f32[32,128]{1,0:T(8,128)}, f32[32,128]{1,0:T(8,128)S(1)}, u32[]{:S(2)}, u32[]{:S(2)}) collective-permute-start(f32[32,128]{1,0:T(8,128)} %collective-permute-done.3.refs_20_), channel_id=1, source_target_pairs={{0,1},{1,0},{2,3},{3,2},{4,5},{5,4},{6,7},{7,6},{8,9},{9,8},{10,11... | collective-permute-start | bytes 49160 | tf_op jit(solution)/shard_map/ppermute | solution.py:692
  33.7 1.5 copy-start.4
  35.2 0.6 copy-start.14
  99.8 10.0 %copy-start.5 = (f32[2560,128]{1,0:T(8,128)S(1)}, f32[2560,128]{1,0:T(8,128)}, u32[]{:S(2)}) copy-start(f32[2560,128]{1,0:T(8,128)} %get-tuple-element.134.refs_6_) | copy-start | bytes 3932164
  109.7 3.1 %collective-permute-start.6 = (bf16[4608,128]{1,0:T(8,128)(2,1)}, bf16[4608,128]{1,0:T(8,128)(2,1)S(1)}, u32[]{:S(2)}, u32[]{:S(2)}) collective-permute-start(bf16[4608,128]{1,0:T(8,128)(2,1)} %get-tuple-element.136), channel_id=1, source_target_pairs={{0,1},{1,0},{2,3},{3,2},{4,5},{5,4},{6,7},{7,6},{8,9},{9,8},{10,11... | collective-permute-start | bytes 3538952 | tf_op jit(solution)/shard_map/ppermute | solution.py:692
  113.0 1.0 copy-start.7
  114.2 21.1 %collective-permute-start.7 = (bf16[3328,128]{1,0:T(8,128)(2,1)S(1)}, bf16[3328,128]{1,0:T(8,128)(2,1)S(1)}, u32[]{:S(2)}, u32[]{:S(2)}) collective-permute-start(bf16[3328,128]{1,0:T(8,128)(2,1)S(1)} %pad_maximum_fusion.1), channel_id=1, source_target_pairs={{0,2},{1,3},{2,0},{3,1},{4,6},{5,7},{6,4},{7,5},{8,10},{9,11},{10,... | collective-permute-start | bytes 2555912 | tf_op jit(solution)/shard_map/ppermute | solution.py:692
  135.3 2.9 %collective-permute-start.8 = (bf16[4096,128]{1,0:T(8,128)(2,1)}, bf16[4096,128]{1,0:T(8,128)(2,1)S(1)}, u32[]{:S(2)}, u32[]{:S(2)}) collective-permute-start(bf16[4096,128]{1,0:T(8,128)(2,1)} %get-tuple-element.142), channel_id=1, source_target_pairs={{0,1},{1,0},{2,3},{3,2},{4,5},{5,4},{6,7},{7,6},{8,9},{9,8},{10,11... | collective-permute-start | bytes 3145736 | tf_op jit(solution)/shard_map/ppermute | solution.py:692
  135.4 2.8 %copy-start.8 = (bf16[2048,128]{1,0:T(8,128)(2,1)S(1)}, bf16[2048,128]{1,0:T(8,128)(2,1)}, u32[]{:S(2)}) copy-start(bf16[2048,128]{1,0:T(8,128)(2,1)} %get-tuple-element.139) | copy-start | bytes 1572868
  135.4 2.8 %copy-start.9 = (bf16[2048,128]{1,0:T(8,128)(2,1)S(1)}, bf16[2048,128]{1,0:T(8,128)(2,1)}, u32[]{:S(2)}) copy-start(bf16[2048,128]{1,0:T(8,128)(2,1)} %get-tuple-element.144) | copy-start | bytes 1572868
  139.3 14.2 %collective-permute-start.9 = (bf16[2048,128]{1,0:T(8,128)(2,1)}, bf16[2048,128]{1,0:T(8,128)(2,1)S(1)}, u32[]{:S(2)}, u32[]{:S(2)}) collective-permute-start(bf16[2048,128]{1,0:T(8,128)(2,1)} %get-tuple-element.151), channel_id=1, source_target_pairs={{0,2},{1,3},{2,0},{3,1},{4,6},{5,7},{6,4},{7,5},{8,10},{9,11},{10,... | collective-permute-start | bytes 1572872 | tf_op jit(solution)/shard_map/ppermute | solution.py:692
  141.2 11.7 %collective-permute-start.10 = (bf16[1664,128]{1,0:T(8,128)(2,1)S(1)}, bf16[1664,128]{1,0:T(8,128)(2,1)S(1)}, u32[]{:S(2)}, u32[]{:S(2)}) collective-permute-start(bf16[1664,128]{1,0:T(8,128)(2,1)S(1)} %pad_maximum_fusion.5), channel_id=1, source_target_pairs={{0,4},{4,0},{8,12},{12,8},{16,20},{20,16},{24,28},{28,24},{1,5},{5... | collective-permute-start | bytes 1277960 | tf_op jit(solution)/shard_map/ppermute | solution.py:695
  153.6 2.1 collective-permute-start.11
  153.6 2.1 copy-start.6
  155.7 0.7 copy-start.18
  156.5 7.4 %collective-permute-start.12 = (bf16[832,128]{1,0:T(8,128)(2,1)S(1)}, bf16[832,128]{1,0:T(8,128)(2,1)S(1)}, u32[]{:S(2)}, u32[]{:S(2)}) collective-permute-start(bf16[832,128]{1,0:T(8,128)(2,1)S(1)} %pad_maximum_fusion.10), channel_id=1, source_target_pairs={{0,8},{4,12},{8,0},{12,4},{16,24},{20,28},{24,16},{28,20},{1,9},{5... | collective-permute-start | bytes 638984 | tf_op jit(solution)/shard_map/ppermute | solution.py:695
  158.4 8.2 %collective-permute-start.13 = (bf16[1048,128]{1,0:T(8,128)(2,1)S(1)}, bf16[1048,128]{1,0:T(8,128)(2,1)S(1)}, u32[]{:S(2)}, u32[]{:S(2)}) collective-permute-start(bf16[1048,128]{1,0:T(8,128)(2,1)S(1)} %pad_maximum_fusion.9), channel_id=1, source_target_pairs={{0,4},{4,0},{8,12},{12,8},{16,20},{20,16},{24,28},{28,24},{1,5},{5... | collective-permute-start | bytes 804872 | tf_op jit(solution)/shard_map/ppermute | solution.py:695
  166.7 7.2 %collective-permute-start.14 = (bf16[416,128]{1,0:T(8,128)(2,1)S(1)}, bf16[416,128]{1,0:T(8,128)(2,1)S(1)}, u32[]{:S(2)}, u32[]{:S(2)}) collective-permute-start(bf16[416,128]{1,0:T(8,128)(2,1)S(1)} %pad_maximum_fusion.15), channel_id=1, source_target_pairs={{0,16},{4,20},{8,24},{12,28},{16,0},{20,4},{24,8},{28,12},{1,17},{... | collective-permute-start | bytes 319496 | tf_op jit(solution)/shard_map/ppermute | solution.py:695
  169.3 6.3 %collective-permute-start.15 = (bf16[536,128]{1,0:T(8,128)(2,1)S(1)}, bf16[536,128]{1,0:T(8,128)(2,1)S(1)}, u32[]{:S(2)}, u32[]{:S(2)}) collective-permute-start(bf16[536,128]{1,0:T(8,128)(2,1)S(1)} %pad_maximum_fusion.14), channel_id=1, source_target_pairs={{0,8},{4,12},{8,0},{12,4},{16,24},{20,28},{24,16},{28,20},{1,9},{5... | collective-permute-start | bytes 411656 | tf_op jit(solution)/shard_map/ppermute | solution.py:695
  175.7 7.9 %collective-permute-start.17 = (bf16[280,128]{1,0:T(8,128)(2,1)S(1)}, bf16[280,128]{1,0:T(8,128)(2,1)S(1)}, u32[]{:S(2)}, u32[]{:S(2)}) collective-permute-start(bf16[280,128]{1,0:T(8,128)(2,1)S(1)} %pad_maximum_fusion.16), channel_id=1, source_target_pairs={{0,16},{4,20},{8,24},{12,28},{16,0},{20,4},{24,8},{28,12},{1,17},{... | collective-permute-start | bytes 215048 | tf_op jit(solution)/shard_map/ppermute | solution.py:695
  177.3 8.1 %collective-permute-start.16 = (f16[352,128]{1,0:T(8,128)(2,1)S(1)}, f16[352,128]{1,0:T(8,128)(2,1)S(1)}, u32[]{:S(2)}, u32[]{:S(2)}) collective-permute-start(f16[352,128]{1,0:T(8,128)(2,1)S(1)} %concatenate.89), channel_id=1, source_target_pairs={{0,16},{4,20},{8,24},{12,28},{16,0},{20,4},{24,8},{28,12},{1,17},{... | collective-permute-start | bytes 270344 | tf_op jit(solution)/shard_map/ppermute | solution.py:695
  185.5 5.4 %collective-permute-start.19 = (f16[272,128]{1,0:T(8,128)(2,1)S(1)}, f16[272,128]{1,0:T(8,128)(2,1)S(1)}, u32[]{:S(2)}, u32[]{:S(2)}) collective-permute-start(f16[272,128]{1,0:T(8,128)(2,1)S(1)} %concatenate.92), channel_id=1, source_target_pairs={{0,16},{4,20},{8,24},{12,28},{16,0},{20,4},{24,8},{28,12},{1,17},{... | collective-permute-start | bytes 208904 | tf_op jit(solution)/shard_map/ppermute | solution.py:695
  185.6 6.5 %collective-permute-start.18 = (f16[704,128]{1,0:T(8,128)(2,1)S(1)}, f16[704,128]{1,0:T(8,128)(2,1)S(1)}, u32[]{:S(2)}, u32[]{:S(2)}) collective-permute-start(f16[704,128]{1,0:T(8,128)(2,1)S(1)} %pad_maximum_fusion.11), channel_id=1, source_target_pairs={{0,8},{4,12},{8,0},{12,4},{16,24},{20,28},{24,16},{28,20},{1,9},{5... | collective-permute-start | bytes 540680 | tf_op jit(solution)/shard_map/ppermute | solution.py:695
  192.3 5.1 %collective-permute-start.21 = (f16[544,128]{1,0:T(8,128)(2,1)S(1)}, f16[544,128]{1,0:T(8,128)(2,1)S(1)}, u32[]{:S(2)}, u32[]{:S(2)}) collective-permute-start(f16[544,128]{1,0:T(8,128)(2,1)S(1)} %pad_maximum_fusion.13), channel_id=1, source_target_pairs={{0,8},{4,12},{8,0},{12,4},{16,24},{20,28},{24,16},{28,20},{1,9},{5... | collective-permute-start | bytes 417800 | tf_op jit(solution)/shard_map/ppermute | solution.py:695
  193.3 7.5 %collective-permute-start.20 = (f16[1408,128]{1,0:T(8,128)(2,1)S(1)}, f16[1408,128]{1,0:T(8,128)(2,1)S(1)}, u32[]{:S(2)}, u32[]{:S(2)}) collective-permute-start(f16[1408,128]{1,0:T(8,128)(2,1)S(1)} %pad_maximum_fusion.6), channel_id=1, source_target_pairs={{0,4},{4,0},{8,12},{12,8},{16,20},{20,16},{24,28},{28,24},{1,5},{5... | collective-permute-start | bytes 1081352 | tf_op jit(solution)/shard_map/ppermute | solution.py:695
  202.3 7.1 %collective-permute-start.22 = (f16[1088,128]{1,0:T(8,128)(2,1)S(1)}, f16[1088,128]{1,0:T(8,128)(2,1)S(1)}, u32[]{:S(2)}, u32[]{:S(2)}) collective-permute-start(f16[1088,128]{1,0:T(8,128)(2,1)S(1)} %pad_maximum_fusion.8), channel_id=1, source_target_pairs={{0,4},{4,0},{8,12},{12,8},{16,20},{20,16},{24,28},{28,24},{1,5},{5... | collective-permute-start | bytes 835592 | tf_op jit(solution)/shard_map/ppermute | solution.py:695
  204.8 7.1 %collective-permute-start.23 = (f32[648,128]{1,0:T(8,128)S(1)}, f32[648,128]{1,0:T(8,128)S(1)}, u32[]{:S(2)}, u32[]{:S(2)}) collective-permute-start(f32[648,128]{1,0:T(8,128)S(1)} %pad_maximum_fusion.7), channel_id=1, source_target_pairs={{0,2},{1,3},{2,0},{3,1},{4,6},{5,7},{6,4},{7,5},{8,10},{9,11},{10,... | collective-permute-start | bytes 995336 | tf_op jit(solution)/shard_map/ppermute | solution.py:692
  212.0 4.5 %copy-start.16 = (f32[1572]{0:T(1024)S(1)}, f32[1572]{0:T(1024)}, u32[]{:S(2)}) copy-start(f32[1572]{0:T(1024)} %param.61) | copy-start | bytes 18868
  212.0 4.5 %copy-start.17 = (f32[1572]{0:T(1024)S(1)}, f32[1572]{0:T(1024)}, u32[]{:S(2)}) copy-start(f32[1572]{0:T(1024)} %param.53) | copy-start | bytes 18868
  212.0 8.2 %collective-permute-start.24 = (f32[1280,128]{1,0:T(8,128)S(1)}, f32[1280,128]{1,0:T(8,128)S(1)}, u32[]{:S(2)}, u32[]{:S(2)}) collective-permute-start(f32[1280,128]{1,0:T(8,128)S(1)} %pad_maximum_fusion.3), channel_id=1, source_target_pairs={{0,1},{1,0},{2,3},{3,2},{4,5},{5,4},{6,7},{7,6},{8,9},{9,8},{10,11... | collective-permute-start | bytes 1966088 | tf_op jit(solution)/shard_map/ppermute | solution.py:692
  214.5 2.6 %collective-permute-start.25 = (f32[8,128]{1,0:T(8,128)S(1)}, f32[8,128]{1,0:T(8,128)S(1)}, u32[]{:S(2)}, u32[]{:S(2)}) collective-permute-start(f32[8,128]{1,0:T(8,128)S(1)} %broadcast_in_dim.2), channel_id=1, source_target_pairs={{0,1},{1,0},{2,3},{3,2},{4,5},{5,4},{6,7},{7,6},{8,9},{9,8},{10,11... | collective-permute-start | bytes 12296 | tf_op jit(solution)/shard_map/ppermute | solution.py:692
  215.1 3.6 %collective-permute-start.26 = (f32[8,128]{1,0:T(8,128)S(1)}, f32[8,128]{1,0:T(8,128)S(1)}, u32[]{:S(2)}, u32[]{:S(2)}) collective-permute-start(f32[8,128]{1,0:T(8,128)S(1)} %broadcast_in_dim.2), channel_id=1, source_target_pairs={{0,2},{1,3},{2,0},{3,1},{4,6},{5,7},{6,4},{7,5},{8,10},{9,11},{10,... | collective-permute-start | bytes 12296 | tf_op jit(solution)/shard_map/ppermute | solution.py:692
  216.0 3.1 %collective-permute-start.27 = (f32[8,128]{1,0:T(8,128)S(1)}, f32[8,128]{1,0:T(8,128)S(1)}, u32[]{:S(2)}, u32[]{:S(2)}) collective-permute-start(f32[8,128]{1,0:T(8,128)S(1)} %broadcast_in_dim.2), channel_id=1, source_target_pairs={{0,3},{1,2},{2,1},{3,0},{4,7},{5,6},{6,5},{7,4},{8,11},{9,10},{10,... | collective-permute-start | bytes 12296 | tf_op jit(solution)/shard_map/ppermute | solution.py:692
  221.5 11.4 %copy-start.1 = (bf16[5,8192]{1,0:T(8,128)(2,1)S(1)}, bf16[5,8192]{1,0:T(8,128)(2,1)}, u32[]{:S(2)}) copy-start(bf16[5,8192]{1,0:T(8,128)(2,1)} %param.32) | copy-start | bytes 245764

commit v5 on v4

--- a/solution.py
+++ b/solution.py
@@ -55,6 +55,10 @@
 
 
 def mm3(a, b, dims=NN):
+    if dims[0] == (1,) and a[0].shape[0] in (16, 32, 64):
+        rows = a[0].shape[0]
+        both = mm(jnp.concatenate(a, axis=0), b[0], dims)
+        return both[:rows] + (both[rows:] + mm(a[0], b[1], dims))
     return mm(a[0], b[0], dims) + (mm(a[0], b[1], dims) + mm(a[1], b[0], dims))
 
 
@@ -106,6 +110,7 @@
     node_feats,
     edge_in,
     bias_rows,
+    nat,
     meta,
     nodes_o,
     hid_o,
@@ -113,6 +118,7 @@
     feat_o,
     hot_src,
     hot_dst,
+    turned_o,
     square,
     flat,
 ):
@@ -139,6 +145,17 @@
     live_col = 2.0 * (count_col - 1.0)
     start_col = starts_of(live_col, mols)
     atom_col = starts_of(count_col, mols)
+
+    width = nat[0].shape[1]
+
+    def turn(i, carry):
+        for k, part in enumerate(nat):
+            turned_o[:, pl.ds(pl.multiple_of(k * width + i * H, H), H)] = jnp.transpose(
+                part[:, columns(i * H, H)]
+            )
+        return carry
+
+    lax.fori_loop(0, width // H, turn, 0)
 
     square[...] = jnp.zeros_like(square)
     square[0:EIN, :] = edge_in[...]
@@ -206,7 +223,7 @@
         hot_dst[:, c] = (atom == dst).astype(f32).astype(bf16)
         return carry
 
-    lax.fori_loop(0, blocks, prepare, 0)
+    lax.fori_loop(0, 2 * lax.div(blocks + 1, jnp.int32(2)), prepare, 0)
 
 
 def body_main(
@@ -223,7 +240,8 @@
     hot_src,
     hot_dst,
     w_fwd,
-    w_nat,
+    turned_h,
+    nat_h,
     ebias_parts,
     gru,
     bias_rows,
@@ -249,9 +267,18 @@
     gru_n,
     gru_t,
     square,
+    moved_s,
+    w_nat,
+    late_sem,
 ):
     parts = len(w_fwd)
     blocks, chunks = meta[0], meta[1]
+    turned_width = turned_h.shape[1]
+    late = [pltpu.make_async_copy(turned_h, w_back.at[:, :turned_width], late_sem.at[0])]
+    for k in range(len(nat_h)):
+        late.append(pltpu.make_async_copy(nat_h[k], w_nat.at[k], late_sem.at[1 + k]))
+    for copy in late:
+        copy.start()
     atoms = w_all.shape[1]
 
     def place(k):
@@ -281,14 +308,28 @@
     ebias = jnp.concatenate([part[...] for part in ebias_parts], axis=0)
     b_high, b_low = split(ebias)
 
-    def turn(i, carry):
-        for k in range(parts):
-            w_back[:, pl.ds(pl.multiple_of(k * own_rows * H + i * H, H), H)] = jnp.transpose(
-                w_nat[k][:, columns(i * H, H)]
-            )
-        return carry
-
-    lax.fori_loop(0, own_rows, turn, 0)
+    def in_pairs(step):
+        def both(p, carry):
+            step(2 * p)
+            step(2 * p + 1)
+            return carry
+
+        lax.fori_loop(0, lax.div(blocks + 1, jnp.int32(2)), both, 0)
+
+    def deliver(into, hot):
+        def both(p, carry):
+            found = []
+            for u in range(2):
+                c = columns((2 * p + u) * LB, LB)
+                found.append(mm2(moved_s[:, c], hot[:, c], NTR))
+            for u in range(2):
+                into[:, window(2 * p + u)] += found[u]
+            return carry
+
+        lax.fori_loop(0, lax.div(blocks + 1, jnp.int32(2)), both, 0)
+
+    b_fwd = jnp.concatenate([b_high, b_low], axis=1)
+    moved_s[...] = jnp.zeros_like(moved_s)
 
     for layer in range(LAYERS):
         low[layer] = jnp.zeros_like(low[layer])
@@ -299,18 +340,23 @@
     for layer in range(LAYERS):
         acc[...] = jnp.zeros_like(acc)
 
+        def fetch(b, layer=layer):
+            c = columns(b * LB, LB)
+            src_o[layer, :, c] = mm(low[layer, :, window(b)], hot_src[:, c]).astype(bf16)
+
         def move(b, carry, layer=layer):
-            c, w = columns(b * LB, LB), window(b)
-            source = mm(low[layer, :, w], hot_src[:, c]).astype(bf16)
-            src_o[layer, :, c] = source
+            c = columns(b * LB, LB)
+            source = src_o[layer, :, c]
             for h in range(EH):
                 z[h * H : (h + 1) * H, :] = hid_i[pl.ds(h, 1), c] * source
-            moved = mm(jnp.concatenate([part[...] for part in w_fwd], axis=0), z[...])
-            moved = moved + (mm(b_high, source) + mm(b_low, source))
-            acc[:, w] += mm2(moved, hot_dst[:, c], NTR)
+            moved_s[:, c] = mm(jnp.concatenate([part[...] for part in w_fwd], axis=0), z[...]) + mm(
+                b_fwd, jnp.concatenate([source, source], axis=0)
+            )
             return carry
 
+        in_pairs(fetch)
         lax.fori_loop(0, blocks, move, 0)
+        deliver(acc, hot_dst)
         for k in range(parts):
             msg[layer, place(k), :] = acc[k * own_rows : (k + 1) * own_rows, :atoms].astype(bf16)
 
@@ -483,31 +529,43 @@
         for k in range(parts):
             gm_rel[k * own_rows : (k + 1) * own_rows, :atoms] = gm[place(k), :]
         if layer > 0:
-            bt_high, bt_low = split(jnp.transpose(ebias))
+            b_pull = jnp.concatenate(split(jnp.transpose(ebias)), axis=1)
+            for copy in late:
+                copy.wait()
+
+            def turn(i, carry):
+                for k in range(len(nat_h)):
+                    at = pl.multiple_of(turned_width + k * own_rows * H + i * H, H)
+                    w_back[:, pl.ds(at, H)] = jnp.transpose(w_nat[k, :, columns(i * H, H)])
+                return carry
+
+            lax.fori_loop(0, own_rows, turn, 0)
+
+            def take(b, layer=layer):
+                c = columns(b * LB, LB)
+                g_o[layer, :, c] = mm(gm_rel[:, window(b)], hot_dst[:, c]).astype(bf16)
 
             def pull(b, carry, layer=layer):
                 c = columns(b * LB, LB)
-                w = window(b)
-                grad = mm(gm_rel[:, w], hot_dst[:, c])
-                grad_low = grad.astype(bf16)
-                g_o[layer, :, c] = grad_low
                 hid = hid_i[:, c]
+                grad = g_o[layer, :, c]
                 for i in range(H):
                     z[i * EH : (i + 1) * EH, :] = g_o[layer, pl.ds(i, 1), c] * hid
-                pulled = mm(w_back[...], z[...])
-                pulled = pulled + (mm(bt_high, grad_low) + mm(bt_low, grad_low))
-                dst_acc[:, w] += mm2(pulled, hot_src[:, c], NTR)
+                moved_s[:, c] = mm(w_back[...], z[...]) + mm(
+                    b_pull, jnp.concatenate([grad, grad], axis=0)
+                )
                 return carry
 
+            in_pairs(take)
             lax.fori_loop(0, blocks, pull, 0)
+            deliver(dst_acc, hot_src)
         else:
 
-            def take(b, carry, layer=layer):
+            def take(b, layer=layer):
                 c = columns(b * LB, LB)
                 g_o[layer, :, c] = mm(gm_rel[:, window(b)], hot_dst[:, c]).astype(bf16)
-                return carry
-
-            lax.fori_loop(0, blocks, take, 0)
+
+            in_pairs(take)
     acc_b = acc.at[:, :H]
     acc_b[...] = jnp.zeros((H, H), f32)
 
@@ -598,8 +656,8 @@
 def adamw(weight, grad, moment, second):
     moment_new = beta_one * moment + (1.0 - beta_one) * grad
     second_new = beta_two * second + (1.0 - beta_two) * grad * grad
-    mean_hat = moment_new / (1.0 - beta_one**STEP_COUNT)
-    square_hat = second_new / (1.0 - beta_two**STEP_COUNT)
+    mean_hat = moment_new * (1.0 / (1.0 - beta_one**STEP_COUNT))
+    square_hat = second_new * (1.0 / (1.0 - beta_two**STEP_COUNT))
     return (
         weight - rate * (mean_hat / (jnp.sqrt(square_hat) + epsilon) + decay * weight),
         moment_new,
@@ -607,18 +665,63 @@
     )
 
 
+BIG = (1, 3, 4, 5)
+WIDE = 1024
+
+
 def body_adamw(own_rows, place, *refs):
-    owns, refs = refs[:CHUNKS], refs[CHUNKS:]
-    (pack, grad_in, squares), refs = refs[:3], refs[3:]
-    params, moments, seconds = refs[0:8], refs[8:16], refs[16:24]
-    outs = refs[24:48]
-    loss, count, norm = refs[48:51]
+    owns_h, refs = refs[:CHUNKS], refs[CHUNKS:]
+    (pack_h, grad_in, squares), refs = refs[:3], refs[3:]
+    states, outs, refs = refs[:24], refs[24:48], refs[48:]
+    (loss, count, norm), refs = refs[:3], refs[3:]
+    owns, pack, bufs, made, in_sem, out_sem = refs[0:CHUNKS], refs[2], refs[3:15], refs[15:27], refs[27], refs[28]
+    columns_out = states[1].shape[1]
+    waits, ins, going = {}, 0, []
+
+    def fetch(key, source, target):
+        nonlocal ins
+        copy = pltpu.make_async_copy(source, target, in_sem.at[ins])
+        copy.start()
+        waits.setdefault(key, []).append(copy)
+        ins += 1
+
+    def buffer_of(group, kind, index):
+        return group[kind * 4 + BIG.index(index)]
+
+    fetch("pack", pack_h, pack)
+    spans = [pl.ds(at, WIDE) for at in range(0, columns_out, WIDE)]
+    per = len(spans) // CHUNKS
+    for c in range(CHUNKS):
+        fetch(("own", c), owns_h[c], owns[c])
+        for k in range(c * per, (c + 1) * per):
+            for kind in range(3):
+                fetch(
+                    (1, k),
+                    states[kind * 8 + 1].at[:, spans[k]],
+                    buffer_of(bufs, kind, 1).at[:, spans[k]],
+                )
+    for index in BIG[1:]:
+        for kind in range(3):
+            fetch((index, 0), states[kind * 8 + index], buffer_of(bufs, kind, index))
+
+    def arrive(key):
+        for copy in waits[key]:
+            copy.wait()
+
+    def send(source, target):
+        copy = pltpu.make_async_copy(source, target, out_sem.at[len(going)])
+        copy.start()
+        going.append(copy)
 
     def step(index, grad, at=...):
-        new = adamw(params[index][at], grad, moments[index][at], seconds[index][at])
+        big = index in BIG
+        now = [buffer_of(bufs, k, index) if big else states[k * 8 + index] for k in range(3)]
+        new = adamw(now[0][at], grad, now[1][at], now[2][at])
         for kind in range(3):
-            outs[kind * 8 + index][at] = new[kind]
-
+            target = buffer_of(made, kind, index) if big else outs[kind * 8 + index]
+            target[at] = new[kind]
+
+    arrive("pack")
     total = squares[0:1, 0:1] + total_of(jnp.square(grad_in[: G_BIAS + 1, :]))
     for k in range(4):
         total = total + total_of(jnp.square(pack[R_LSTM + k * 2 * H : R_LSTM + k * 2 * H + H, :]))
@@ -628,12 +731,29 @@
     grad_norm = jnp.sqrt(total) / number
     norm[...] = grad_norm
     factor = jnp.minimum(1.0, clip_norm / grad_norm) / number
-    step(0, grad_in[:EIN, :] * factor)
-    step(2, pack[pl.ds(pl.multiple_of(R_EBIAS + place[0], 8), own_rows), :] * factor)
+    rows = WIDE // H
+    for k, span in enumerate(spans):
+        c = k // per
+        if k % per == 0:
+            arrive(("own", c))
+        arrive((1, k))
+        for i in range(rows):
+            at, r = k * WIDE + i * H, ((k % per) * rows + i) * EH
+            step(1, owns[c][r : r + EH, :] * factor, (slice(None), slice(at, at + H)))
+        for kind in range(3):
+            send(buffer_of(made, kind, 1).at[:, span], outs[kind * 8 + 1].at[:, span])
+
+    def finish(index):
+        for kind in range(3):
+            send(buffer_of(made, kind, index), outs[kind * 8 + index])
+
+    arrive((3, 0))
     for half in range(2):
         for q in range(3):
             r = R_GRU + (half * 3 + q) * H
             step(3, pack[r : r + H, :] * factor, (half, slice(None), slice(q * H, (q + 1) * H)))
+    finish(3)
+    arrive((4, 0))
     for k in range(4):
         r = R_LSTM + k * 2 * H
         for block, start in ((0, 0), (1, H), (2, 0)):
@@ -642,22 +762,22 @@
                 pack[r + start : r + start + H, :] * factor,
                 (slice(block * H, (block + 1) * H), slice(k * H, (k + 1) * H)),
             )
+    finish(4)
+    arrive((5, 0))
     step(5, pack[R_FIRST:R_GRU, :] * factor)
+    finish(5)
+    step(0, grad_in[:EIN, :] * factor)
+    step(2, pack[pl.ds(pl.multiple_of(R_EBIAS + place[0], 8), own_rows), :] * factor)
     step(6, pack[R_SECOND : R_SECOND + NT, :] * factor)
-    bias = jnp.concatenate(
-        [grad_in[G_BIAS : G_BIAS + 1, :], pack[R_MISC + 1 : R_EBIAS, :]], axis=0
-    )
+    bias = jnp.concatenate([grad_in[G_BIAS : G_BIAS + 1, :], pack[R_MISC + 1 : R_EBIAS, :]], axis=0)
     step(7, bias * factor)
-
-    rows = own_rows // CHUNKS
-    for c in range(CHUNKS):
-        for i in range(rows):
-            at = (c * rows + i) * H
-            step(1, owns[c][i * EH : (i + 1) * EH, :] * factor, (slice(None), slice(at, at + H)))
+    for copy in going:
+        copy.wait()
 
 
 VM = pl.BlockSpec(memory_space=pltpu.VMEM)
 SM = pl.BlockSpec(memory_space=pltpu.SMEM)
+HBM = pl.BlockSpec(memory_space=pl.ANY)
 
 
 def per_device(
@@ -686,7 +806,7 @@
     mols = node_feats.shape[0]
     own_rows = edge_out.shape[1] // H
     atoms = -(-mols * ATOMS // LB) * LB
-    space = -(-mols * LIVE // LB) * LB
+    space = -(-mols * LIVE // (2 * LB)) * 2 * LB
 
     def row_swap(x, k):
         return lax.ppermute(x, "row", [(i, i ^ k) for i in range(row_count)])
@@ -724,8 +844,13 @@
     places = jnp.stack([(row ^ k) * own_rows for k in range(row_count)]).astype(jnp.int32)
     bias_rows = jnp.pad(biases, (0, 16 * 128 - biases.shape[0])).reshape(16, 128)
 
+    at_hand = [parts[k] for k in range(n // 2)]
+
+    def prepare(*refs):
+        body_prepare(mols, *refs[:5], refs[5 : 5 + n // 2], *refs[5 + n // 2 :])
+
     prepared = pl.pallas_call(
-        functools.partial(body_prepare, mols),
+        prepare,
         out_shape=(
             sds((2 + space // LB,), jnp.int32),
             sds((H, atoms), bf16),
@@ -734,17 +859,18 @@
             sds((8, space), f32),
             sds((WINDOW, space), bf16),
             sds((WINDOW, space), bf16),
+            sds((H, n // 2 * own_rows * H), bf16),
         ),
-        in_specs=[SM] + [VM] * 4,
-        out_specs=(SM,) + (VM,) * 6,
+        in_specs=[SM] + [VM] * (4 + n // 2),
+        out_specs=(SM,) + (VM,) * 7,
         scratch_shapes=[pltpu.VMEM((128, 128), f32), pltpu.VMEM((mols * PAD, H), f32)],
         compiler_params=params,
-    )(atom_counts, table, node_feats, edge_in, bias_rows)
+    )(atom_counts, table, node_feats, edge_in, bias_rows, *at_hand)
     forward = {k: forward_order(part) for k, part in parts.items() if k < n // 2}
     parts, bias_parts, prepared, forward = lax.optimization_barrier(
         (parts, bias_parts, prepared, forward)
     )
-    meta, nodes, hid, before, feat, hot_src, hot_dst = prepared
+    meta, nodes, hid, before, feat, hot_src, hot_dst, turned = prepared
     for bit in reversed(range(row_bits)):
         for k in [k for k in parts if k > 1 << bit and not k & (1 << bit)]:
             parts[k + (1 << bit)] = row_swap(parts[k], 1 << bit)
@@ -753,6 +879,8 @@
     bias_parts = [bias_parts[k] for k in range(n)]
     w_fwd = [forward[k] if k in forward else forward_order(parts[k]) for k in range(n)]
 
+    away = n - n // 2
+
     def main(*refs):
         at = 10
         body_main(
@@ -760,9 +888,10 @@
             own_rows,
             *refs[:at],
             refs[at : at + n],
-            refs[at + n : at + 2 * n],
-            refs[at + 2 * n : at + 3 * n],
-            *refs[at + 3 * n :],
+            refs[at + n],
+            refs[at + n + 1 : at + n + 1 + away],
+            refs[at + n + 1 + away : at + 2 * n + 1 + away],
+            *refs[at + 2 * n + 1 + away :],
         )
 
     pack, sums, src, g = pl.pallas_call(
@@ -773,7 +902,7 @@
             sds((LAYERS, H, space), bf16),
             sds((LAYERS, H, space), bf16),
         ),
-        in_specs=[SM] * 4 + [VM] * (11 + 3 * n),
+        in_specs=[SM] * 4 + [VM] * (6 + n) + [HBM] * (1 + away) + [VM] * (n + 5),
         out_specs=(VM,) * 4,
         scratch_shapes=[
             pltpu.VMEM((H * EH, LB), bf16),
@@ -791,6 +920,9 @@
             pltpu.VMEM((2, H, 3 * H), bf16),
             pltpu.VMEM((2, 3 * H, H), bf16),
             pltpu.VMEM((128, 128), f32),
+            pltpu.VMEM((H, space), f32),
+            pltpu.VMEM((n - n // 2, EH, own_rows * H), bf16),
+            pltpu.SemaphoreType.DMA((1 + n - n // 2,)),
         ],
         compiler_params=pltpu.CompilerParams(vmem_limit_bytes=60 * MIB),
     )(
@@ -805,7 +937,8 @@
         hot_src,
         hot_dst,
         *w_fwd,
-        *parts,
+        turned,
+        *parts[n // 2 :],
         *bias_parts,
         gru_weights,
         bias_rows,
@@ -894,13 +1027,13 @@
             sent = jnp.concatenate(
                 [jnp.where(bit == 0, sent, came), jnp.where(bit == 0, came, sent)], axis=0
             )
-        sent = sent.astype(f32).reshape(-1, height + 16, 128)
+        raw, sent = sent, sent.astype(f32).reshape(-1, height + 16, 128)
         back = jnp.exp2(-sent[:, height : height + 1, 0:1])
         own = (sent[:, :rest] * back).reshape(-1, 128)
         square = jnp.sum(own * own)
         if pack is not None:
-            pack = (sent[:, rest:height] * back).reshape(-1, 128)
-            square = square + jnp.sum(pack * pack)
+            pack = raw.reshape(-1, height + 16, 128)[:, rest:].reshape(-1, 128)
+            square = square + jnp.sum(jnp.square(sent[:, rest:height] * back))
         return own, pack, square
 
     core_place = (1 - core_bit).reshape(1).astype(jnp.int32)
@@ -957,21 +1090,25 @@
         except StopIteration as end:
             first_own, pack, square = end.value
             break
-    quarters = jnp.concatenate([pack, beside["rows"]], axis=0)
-    quarters, second_sent = tie((quarters, second_sent))
-    came, second_came = cross(quarters), second_swap(second_sent)
+    second_came, came = second_swap(second_sent), cross(pack)
+    grad_in = beside["rows"] + cross(beside["rows"])
+    pack = jnp.concatenate(
+        [jnp.where(cross_bit == 0, pack, came), jnp.where(cross_bit == 0, came, pack)], axis=0
+    )
+    came = core(pack)
+    pack = jnp.concatenate(
+        [jnp.where(core_bit == 0, pack, came), jnp.where(core_bit == 0, came, pack)], axis=0
+    )
+    pack = pack.astype(f32).reshape(n * 2**mol_bits, -1, 128)
+    pack = (pack[:, :-16] * jnp.exp2(-pack[:, -16:-15, 0:1])).reshape(-1, 128)
     try:
         second.send(second_came)
     except StopIteration as end:
         second_own, _, more = end.value
-    grad_in = beside["rows"] + came[-8:]
-    came = came[:-8]
-    pack = jnp.concatenate(
-        [jnp.where(cross_bit == 0, pack, came), jnp.where(cross_bit == 0, came, pack)], axis=0
-    )
-    pack = double(pack, core, core_bit)
     squares = jnp.broadcast_to(square + more, (8, 128))
-    squares = (squares + row_swap(squares, 1)) + (row_swap(squares, 2) + row_swap(squares, 3))
+    came = row_swap(squares, 3)
+    came, pack, grad_in = tie((came, pack, grad_in))
+    squares = (squares + row_swap(squares, 1)) + (row_swap(squares, 2) + came)
     owns = [first_own, second_own]
 
     weights = [
@@ -994,12 +1131,18 @@
         else:
             group[7] = jnp.pad(group[7], (0, 16 * 128 - group[7].shape[0])).reshape(16, 128)
         states += group
+    spots = [HBM if index in BIG else VM for index in range(8)] * 3
+    copies = 3 * (own_rows * H // WIDE + len(BIG) - 1)
     shapes = [sds(state.shape, f32) for state in states]
     results = pl.pallas_call(
         functools.partial(body_adamw, own_rows),
         out_shape=tuple(shapes) + (sds((1, 1), f32),) * 3,
-        in_specs=[SM] + [VM] * (CHUNKS + 3 + len(shapes)),
-        out_specs=(VM,) * (len(shapes) + 3),
+        in_specs=[SM] + [HBM] * (CHUNKS + 1) + [VM] * 2 + spots,
+        out_specs=tuple(spots) + (VM,) * 3,
+        scratch_shapes=[pltpu.VMEM(own.shape, f32) for own in owns]
+        + [pltpu.VMEM(pack.shape, f32)]
+        + [pltpu.VMEM(shapes[index].shape, f32) for _ in range(6) for index in BIG]
+        + [pltpu.SemaphoreType.DMA((copies + CHUNKS + 1,)), pltpu.SemaphoreType.DMA((copies,))],
         compiler_params=params,
     )(places, *owns, pack, grad_in, squares, *states)
     results = list(results)

time: 238 us -> 227 us (0.954); the launches traced: 233 us -> 228 us
  starting transfers between devices: 29 us -> 18.3 us
  Pallas kernels: 119 us -> 124 us
    ppermute x12, starting transfers between devices: 18.4 us -> 10.8 us  [mol_swap(): lax.ppermute(x, 'mol', [(i, i ^ 1 << bit) for i in range(2 ** mol_bits)])]
    pallas_call x3, Pallas kernels: 35.4 us -> 40.5 us  [edge_parts(): pl.pallas_call(functools.partial(body_edges, jobs, slots, kind, last), gr...]
    pallas_call x1, Pallas kernels: 8.07 us -> 13.2 us  [per_device(): pl.pallas_call(prepare, out_shape=(sds((2 + space // LB,), jnp.int32), sd...]
    pallas_call x1, Pallas kernels: 64 us -> 59.1 us  [per_device(): pl.pallas_call(main, out_shape=(sds((R_PACK, 128), f32), sds((8, 128), f3...]
    ppermute x16 -> x17, waiting for transfers between devices: 23 us -> 18.9 us  [row_swap(): return lax.ppermute(x, 'row', [(i, i ^ k) for i in range(row_count)])]
    ppermute x12, waiting for transfers between devices: 26.5 us -> 29.9 us  [mol_swap(): lax.ppermute(x, 'mol', [(i, i ^ 1 << bit) for i in range(2 ** mol_bits)])]
    ppermute x16 -> x17, starting transfers between devices: 10.6 us -> 7.45 us  [row_swap(): return lax.ppermute(x, 'row', [(i, i ^ k) for i in range(row_count)])]
  transfers between devices with their start and end apart: 28 -> 29, of which waited for: 20 -> 16; matrix products, arithmetic and copies ran while one was open for 9% -> 10% of each run, Pallas kernels for 14% -> 19%
where the time goes in v5:
time: 227 us; the launch traced here: 228 us
  Pallas kernels  124 us (55%)
  waiting for transfers between devices  48.8 us (21%)
  starting transfers between devices  18.3 us (8%)
  other arithmetic  18 us (8%)
  local copies, waits for them, and re-layouts  13.5 us (6%)
  between operations  5.14 us (2%)
    pallas_call x1, Pallas kernels, per_device(): pl.pallas_call(main, out_shape=(sds((R_PACK, 128), f32), sds((8, 128), f3...  59.1 us
    pallas_call x3, Pallas kernels, edge_parts(): pl.pallas_call(functools.partial(body_edges, jobs, slots, kind, last), gr...  40.5 us
    ppermute x12, waiting for transfers between devices, mol_swap(): lax.ppermute(x, 'mol', [(i, i ^ 1 << bit) for i in range(2 ** mol_bits)])  29.9 us
    ppermute x17, waiting for transfers between devices, row_swap(): return lax.ppermute(x, 'row', [(i, i ^ k) for i in range(row_count)])  18.9 us
    pallas_call x1, Pallas kernels, per_device(): pl.pallas_call(prepare, out_shape=(sds((2 + space // LB,), jnp.int32), sd...  13.2 us
    pallas_call x1, Pallas kernels, per_device(): pl.pallas_call(functools.partial(body_adamw, own_rows), out_shape=tuple(s...  11.4 us
    ppermute x12, starting transfers between devices, mol_swap(): lax.ppermute(x, 'mol', [(i, i ^ 1 << bit) for i in range(2 ** mol_bits)])  10.8 us
    ppermute x17, starting transfers between devices, row_swap(): return lax.ppermute(x, 'row', [(i, i ^ k) for i in range(row_count)])  7.45 us
  transfers between devices with their start and end apart: 29, of which 16 were waited for; matrix products, arithmetic and copies ran while one was open for 10% of the time, Pallas kernels for 19%

profile of v5, /device:TPU:0, one launch (start us, length us, event | category | flops | bytes accessed | tf_op | source)
XLA Modules:
  0.0 228.0 jit_solution(5080790913679961006)
XLA Ops:
  0.7 2.9 %convert_element_type.154.refs_5_.refs_0_ = bf16[128,4096]{1,0:T(8,128)(2,1)} convert(f32[128,4096]{1,0:T(8,128)} %refs_6_.1) | non-fusion elementwise | flops 524288 | bytes 3145728 | tf_op jit(solution)/shard_map/convert_element_type | solution.py:828
  4.0 2.5 %collective-permute-start.1 = (bf16[128,4096]{1,0:T(8,128)(2,1)}, bf16[128,4096]{1,0:T(8,128)(2,1)S(1)}, u32[]{:S(2)}, u32[]{:S(2)}) collective-permute-start(bf16[128,4096]{1,0:T(8,128)(2,1)} %convert_element_type.154.refs_5_.refs_0_), channel_id=1, source_target_pairs={{0,2},{1,3},{2,0},{3,1},{4,6},{5,7},{6,4},{7,5},{8,10},{9,11},{10,... | collective-permute-start | bytes 3145736 | tf_op jit(solution)/shard_map/ppermute | solution.py:812
  7.4 1.2 convert_bitcast_fusion
  9.2 0.7 reshape.258.refs_1_
  9.9 0.8 copy.76.refs_2_
  10.7 1.4 copy.86
  12.2 1.2 copy.97
  13.4 1.4 copy.87
  14.8 1.1 copy.96
  16.0 13.2 %shard_map.502 = (s32[10]{0:T(128)}, bf16[128,1024]{1,0:T(8,128)(2,1)}, bf16[128,2048]{1,0:T(8,128)(2,1)}, f32[128,2048]{1,0:T(8,128)}, f32[8,2048]{1,0:T(8,128)...) custom-call(s32[32]{0:T(128)} %refs_0_.3, bf16[32,448]{1,0:T(8,128)(2,1)} %reshape.258.refs_1_, ...), custom_call_target="tpu_custom_call" | custom-call | tf_op jit(solution)/shard_map/pallas_call | solution.py:852
  29.2 1.9 collective-permute-done.3.refs_19_
  32.4 1.2 copy.95
  34.0 1.2 copy.94
  35.8 59.1 %shard_map.503 = (f32[2560,128]{1,0:T(8,128)}, f32[8,128]{1,0:T(8,128)}, bf16[2,128,2048]{2,1,0:T(8,128)(2,1)}, bf16[2,128,2048]{2,1,0:T(8,128)(2,1)}) custom-call(s32[32]{0:T(128)} %refs_0_.3, s32[32]{0:T(128)} %refs_1_.1, s32[4]{0:T(128)} %pad_add_fusion.refs_2_.place, s32[10]{0:T(128)} %get-tuple-element.123.refs_3_.meta, f32[12,32]{1,0:T(8,128)} %bitcast.187, ...), custom_call_target="tpu_custom_call" | custom-call | tf_op jit(solution)/shard_map/pallas_call | solution.py:897
  95.0 11.2 %shard_map.504 = (bf16[4608,128]{1,0:T(8,128)(2,1)}, bf16[2048,128]{1,0:T(8,128)(2,1)}, f32[128,2048]{1,0:T(8,128)}) custom-call(s32[10]{0:T(128)} %get-tuple-element.123.refs_3_.meta, bf16[128,4096]{1,0:T(8,128)(2,1)} %copy-done.3, bf16[128,4096]{1,0:T(8,128)(2,1)} %copy-done.4, bf16[2,128,2048]{2,1,0:T(8,128)(2,1)} %get-tuple-element.137.refs_2_.refs_4_, ...), custom_call_target="tpu_custom_call" | custom-call | tf_op jit(solution)/shard_map/pallas_call | solution.py:956
  106.3 2.9 %collective-permute-done.6 = bf16[4608,128]{1,0:T(8,128)(2,1)S(1)} collective-permute-done((bf16[4608,128]{1,0:T(8,128)(2,1)}, bf16[4608,128]{1,0:T(8,128)(2,1)S(1)}, u32[]{:S(2)}, u32[]{:S(2)}) %collective-permute-start.6) | collective-permute-done | bytes 1179680 | tf_op jit(solution)/shard_map/ppermute | solution.py:812
  109.5 0.9 copy-done.7
  110.7 17.6 %shard_map.505 = (bf16[4096,128]{1,0:T(8,128)(2,1)}, bf16[2048,128]{1,0:T(8,128)(2,1)}, bf16[2048,128]{1,0:T(8,128)(2,1)}, f32[128,2048]{1,0:T(8,128)}) custom-call(s32[10]{0:T(128)} %get-tuple-element.123.refs_3_.meta, bf16[128,4096]{1,0:T(8,128)(2,1)} %convert_element_type.154.refs_5_.refs_0_, bf16[128,4096]{1,0:T(8,128)(2,1)} %collective-permute-done.refs_6_.refs_1_, ...), custom_call_target="tpu_custom_call" | custom-call | tf_op jit(solution)/shard_map/pallas_call | solution.py:956
  128.3 3.4 %collective-permute-done.7 = bf16[3328,128]{1,0:T(8,128)(2,1)S(1)} collective-permute-done((bf16[3328,128]{1,0:T(8,128)(2,1)S(1)}, bf16[3328,128]{1,0:T(8,128)(2,1)S(1)}, u32[]{:S(2)}, u32[]{:S(2)}) %collective-permute-start.7) | collective-permute-done | bytes 852000 | tf_op jit(solution)/shard_map/ppermute | solution.py:812
  131.9 2.6 %collective-permute-done.8 = bf16[4096,128]{1,0:T(8,128)(2,1)S(1)} collective-permute-done((bf16[4096,128]{1,0:T(8,128)(2,1)}, bf16[4096,128]{1,0:T(8,128)(2,1)S(1)}, u32[]{:S(2)}, u32[]{:S(2)}) %collective-permute-start.8) | collective-permute-done | bytes 1048608 | tf_op jit(solution)/shard_map/ppermute | solution.py:812
  134.6 1.1 convert_add_fusion.1
  136.1 11.8 %shard_map.506 = (bf16[2080,128]{1,0:T(8,128)(2,1)}, bf16[2048,128]{1,0:T(8,128)(2,1)}, f32[8,128]{1,0:T(8,128)}) custom-call(s32[10]{0:T(128)} %get-tuple-element.123.refs_3_.meta, bf16[128,4096]{1,0:T(8,128)(2,1)} %convert_element_type.154.refs_5_.refs_0_, bf16[128,4096]{1,0:T(8,128)(2,1)} %collective-permute-done.refs_6_.refs_1_, ...), custom_call_target="tpu_custom_call" | custom-call | tf_op jit(solution)/shard_map/pallas_call | solution.py:956
  147.9 2.1 collective-permute-done.9
  150.2 1.9 collective-permute-done.11
  153.1 7.2 %collective-permute-done.12 = bf16[832,128]{1,0:T(8,128)(2,1)S(1)} collective-permute-done((bf16[832,128]{1,0:T(8,128)(2,1)S(1)}, bf16[832,128]{1,0:T(8,128)(2,1)S(1)}, u32[]{:S(2)}, u32[]{:S(2)}) %collective-permute-start.12) | collective-permute-done | bytes 213024 | tf_op jit(solution)/shard_map/ppermute | solution.py:815
  160.4 1.1 collective-permute-done.13
  161.7 1.7 collective-permute-start.15
  163.5 5.1 %collective-permute-done.14 = bf16[416,128]{1,0:T(8,128)(2,1)S(1)} collective-permute-done((bf16[416,128]{1,0:T(8,128)(2,1)S(1)}, bf16[416,128]{1,0:T(8,128)(2,1)S(1)}, u32[]{:S(2)}, u32[]{:S(2)}) %collective-permute-start.14) | collective-permute-done | bytes 106528 | tf_op jit(solution)/shard_map/ppermute | solution.py:815
  170.2 1.1 collective-permute-start.17
  171.3 1.9 collective-permute-start.16
  173.2 5.0 %collective-permute-done.17 = bf16[280,128]{1,0:T(8,128)(2,1)S(1)} collective-permute-done((bf16[280,128]{1,0:T(8,128)(2,1)S(1)}, bf16[280,128]{1,0:T(8,128)(2,1)S(1)}, u32[]{:S(2)}, u32[]{:S(2)}) %collective-permute-start.17) | collective-permute-done | bytes 71712 | tf_op jit(solution)/shard_map/ppermute | solution.py:815
  178.2 0.6 abs_reduce_fusion.1
  179.9 2.4 %collective-permute-start.18 = (f16[704,128]{1,0:T(8,128)(2,1)S(1)}, f16[704,128]{1,0:T(8,128)(2,1)S(1)}, u32[]{:S(2)}, u32[]{:S(2)}) collective-permute-start(f16[704,128]{1,0:T(8,128)(2,1)S(1)} %pad_maximum_fusion.10), channel_id=1, source_target_pairs={{0,8},{4,12},{8,0},{12,4},{16,24},{20,28},{24,16},{28,20},{1,9},{5... | collective-permute-start | bytes 540680 | tf_op jit(solution)/shard_map/ppermute | solution.py:815
  182.3 3.0 %collective-permute-done.19 = f16[272,128]{1,0:T(8,128)(2,1)S(1)} collective-permute-done((f16[272,128]{1,0:T(8,128)(2,1)S(1)}, f16[272,128]{1,0:T(8,128)(2,1)S(1)}, u32[]{:S(2)}, u32[]{:S(2)}) %collective-permute-start.19) | collective-permute-done | bytes 69664 | tf_op jit(solution)/shard_map/ppermute | solution.py:815
  185.4 1.1 collective-permute-done.18
  186.7 1.3 collective-permute-start.21
  188.9 2.7 %collective-permute-done.26 = f32[8,128]{1,0:T(8,128)S(1)} collective-permute-done((f32[8,128]{1,0:T(8,128)S(1)}, f32[8,128]{1,0:T(8,128)S(1)}, u32[]{:S(2)}, u32[]{:S(2)}) %collective-permute-start.26) | collective-permute-done | bytes 4128 | tf_op jit(solution)/shard_map/ppermute | solution.py:812
  192.3 1.2 collective-permute-start.20
  193.6 0.9 collective-permute-start.22
  194.5 7.4 %collective-permute-done.20 = f16[1408,128]{1,0:T(8,128)(2,1)S(1)} collective-permute-done((f16[1408,128]{1,0:T(8,128)(2,1)S(1)}, f16[1408,128]{1,0:T(8,128)(2,1)S(1)}, u32[]{:S(2)}, u32[]{:S(2)}) %collective-permute-start.20) | collective-permute-done | bytes 360480 | tf_op jit(solution)/shard_map/ppermute | solution.py:815
  203.0 0.8 fusion.3
  203.7 1.8 multiply_reduce_fusion.1
  207.0 1.2 collective-permute-done.24
  208.9 1.7 multiply_reduce_fusion
  211.3 0.7 collective-permute-start.23
  212.0 1.5 collective-permute-start.28
  214.5 1.3 slice_multiply_fusion
  216.4 11.4 %shard_map.507 = (f32[5,128]{1,0:T(8,128)}, f32[128,4096]{1,0:T(8,128)}, f32[32,128]{1,0:T(8,128)}, f32[2,128,384]{2,1,0:T(8,128)}, f32[384,512]{1,0:T(8,128)}, ...) custom-call(s32[4]{0:T(128)} %pad_add_fusion.refs_2_.place, ...), custom_call_target="tpu_custom_call" | custom-call | tf_op jit(solution)/shard_map/pallas_call | solution.py:1137
  (166 shorter events, 13.5 us)
Async XLA Ops:
  0.7 6.6 %copy-start = (bf16[5,8192]{1,0:T(8,128)(2,1)S(1)}, bf16[5,8192]{1,0:T(8,128)(2,1)}, u32[]{:S(2)}) copy-start(bf16[5,8192]{1,0:T(8,128)(2,1)} %param.32) | copy-start | bytes 245764
  0.7 6.7 %copy-start.2 = (f32[128,4096]{1,0:T(8,128)S(1)}, f32[128,4096]{1,0:T(8,128)}, u32[]{:S(2)}) copy-start(f32[128,4096]{1,0:T(8,128)} %refs_6_.1) | copy-start | bytes 6291460
  0.7 5.8 %copy-start.11 = (f32[4096]{0:T(1024)S(1)}, f32[4096]{0:T(1024)}, u32[]{:S(2)}) copy-start(f32[4096]{0:T(1024)} %param.40) | copy-start | bytes 49156
  0.7 6.3 %copy-start.12 = (s32[2,128,64]{1,2,0:T(8,128)S(1)}, s32[2,128,64]{1,2,0:T(8,128)}, u32[]{:S(2)}) copy-start(s32[2,128,64]{1,2,0:T(8,128)} %param.33) | copy-start | bytes 196612
  3.6 9.8 %collective-permute-start = (bf16[128,4096]{1,0:T(8,128)(2,1)}, bf16[128,4096]{1,0:T(8,128)(2,1)}, u32[]{:S(2)}, u32[]{:S(2)}) collective-permute-start(bf16[128,4096]{1,0:T(8,128)(2,1)} %convert_element_type.154.refs_5_.refs_0_), channel_id=1, source_target_pairs={{0,1},{1,0},{2,3},{3,2},{4,5},{5,4},{6,7},{7,6},{8,9},{9,8},{10,11... | collective-permute-start | bytes 3145736 | tf_op jit(solution)/shard_map/ppermute | solution.py:812
  4.0 27.0 %collective-permute-start.1 = (bf16[128,4096]{1,0:T(8,128)(2,1)}, bf16[128,4096]{1,0:T(8,128)(2,1)S(1)}, u32[]{:S(2)}, u32[]{:S(2)}) collective-permute-start(bf16[128,4096]{1,0:T(8,128)(2,1)} %convert_element_type.154.refs_5_.refs_0_), channel_id=1, source_target_pairs={{0,2},{1,3},{2,0},{3,1},{4,6},{5,7},{6,4},{7,5},{8,10},{9,11},{10,... | collective-permute-start | bytes 3145736 | tf_op jit(solution)/shard_map/ppermute | solution.py:812
  6.5 22.6 %collective-permute-start.2 = (f32[32,128]{1,0:T(8,128)S(1)}, f32[32,128]{1,0:T(8,128)S(1)}, u32[]{:S(2)}, u32[]{:S(2)}) collective-permute-start(f32[32,128]{1,0:T(8,128)S(1)} %bitcast.179), channel_id=1, source_target_pairs={{0,1},{1,0},{2,3},{3,2},{4,5},{5,4},{6,7},{7,6},{8,9},{9,8},{10,11... | collective-permute-start | bytes 49160 | tf_op jit(solution)/shard_map/ppermute | solution.py:812
  6.8 24.3 %collective-permute-start.3 = (f32[32,128]{1,0:T(8,128)S(1)}, f32[32,128]{1,0:T(8,128)}, u32[]{:S(2)}, u32[]{:S(2)}) collective-permute-start(f32[32,128]{1,0:T(8,128)S(1)} %bitcast.180), channel_id=1, source_target_pairs={{0,2},{1,3},{2,0},{3,1},{4,6},{5,7},{6,4},{7,5},{8,10},{9,11},{10,... | collective-permute-start | bytes 49160 | tf_op jit(solution)/shard_map/ppermute | solution.py:812
  7.4 1.2 copy-start.15
  7.4 2.5 %copy-start.10 = (bf16[32,29,128]{2,0,1:T(8,128)(2,1)S(1)}, bf16[32,29,128]{2,0,1:T(8,128)(2,1)}, u32[]{:S(2)}) copy-start(bf16[32,29,128]{2,0,1:T(8,128)(2,1)} %param.31) | copy-start | bytes 712708
  29.2 4.4 %copy-start.13 = (f32[32,128]{1,0:T(8,128)}, f32[32,128]{1,0:T(8,128)S(1)}, u32[]{:S(2)}) copy-start(f32[32,128]{1,0:T(8,128)S(1)} %collective-permute-done.2.refs_18_) | copy-start | bytes 49156
  31.0 2.5 %copy-start.3 = (bf16[128,4096]{1,0:T(8,128)(2,1)}, bf16[128,4096]{1,0:T(8,128)(2,1)S(1)}, u32[]{:S(2)}) copy-start(bf16[128,4096]{1,0:T(8,128)(2,1)S(1)} %collective-permute-done.1.refs_15_.refs_0_.refs_2_) | copy-start | bytes 3145732
  31.0 2.7 %collective-permute-start.4 = (bf16[128,4096]{1,0:T(8,128)(2,1)S(1)}, bf16[128,4096]{1,0:T(8,128)(2,1)S(1)}, u32[]{:S(2)}, u32[]{:S(2)}) collective-permute-start(bf16[128,4096]{1,0:T(8,128)(2,1)S(1)} %collective-permute-done.1.refs_15_.refs_0_.refs_2_), channel_id=1, source_target_pairs={{0,1},{1,0},{2,3},{3,2},{4,5},{5,4},{6,7},{7,6},{8,9},{9,8},{10,11... | collective-permute-start | bytes 3145736 | tf_op jit(solution)/shard_map/ppermute | solution.py:812
  31.0 4.1 %collective-permute-start.5 = (f32[32,128]{1,0:T(8,128)}, f32[32,128]{1,0:T(8,128)S(1)}, u32[]{:S(2)}, u32[]{:S(2)}) collective-permute-start(f32[32,128]{1,0:T(8,128)} %collective-permute-done.3.refs_19_), channel_id=1, source_target_pairs={{0,1},{1,0},{2,3},{3,2},{4,5},{5,4},{6,7},{7,6},{8,9},{9,8},{10,11... | collective-permute-start | bytes 49160 | tf_op jit(solution)/shard_map/ppermute | solution.py:812
  33.7 1.5 copy-start.4
  35.2 0.6 copy-start.14
  94.9 11.3 %copy-start.5 = (f32[2560,128]{1,0:T(8,128)S(1)}, f32[2560,128]{1,0:T(8,128)}, u32[]{:S(2)}) copy-start(f32[2560,128]{1,0:T(8,128)} %get-tuple-element.139.refs_6_) | copy-start | bytes 3932164
  106.1 3.1 %collective-permute-start.6 = (bf16[4608,128]{1,0:T(8,128)(2,1)}, bf16[4608,128]{1,0:T(8,128)(2,1)S(1)}, u32[]{:S(2)}, u32[]{:S(2)}) collective-permute-start(bf16[4608,128]{1,0:T(8,128)(2,1)} %get-tuple-element.141), channel_id=1, source_target_pairs={{0,1},{1,0},{2,3},{3,2},{4,5},{5,4},{6,7},{7,6},{8,9},{9,8},{10,11... | collective-permute-start | bytes 3538952 | tf_op jit(solution)/shard_map/ppermute | solution.py:812
  109.4 1.0 copy-start.7
  110.6 21.1 %collective-permute-start.7 = (bf16[3328,128]{1,0:T(8,128)(2,1)S(1)}, bf16[3328,128]{1,0:T(8,128)(2,1)S(1)}, u32[]{:S(2)}, u32[]{:S(2)}) collective-permute-start(bf16[3328,128]{1,0:T(8,128)(2,1)S(1)} %pad_maximum_fusion), channel_id=1, source_target_pairs={{0,2},{1,3},{2,0},{3,1},{4,6},{5,7},{6,4},{7,5},{8,10},{9,11},{10,... | collective-permute-start | bytes 2555912 | tf_op jit(solution)/shard_map/ppermute | solution.py:812
  131.7 2.9 %collective-permute-start.8 = (bf16[4096,128]{1,0:T(8,128)(2,1)}, bf16[4096,128]{1,0:T(8,128)(2,1)S(1)}, u32[]{:S(2)}, u32[]{:S(2)}) collective-permute-start(bf16[4096,128]{1,0:T(8,128)(2,1)} %get-tuple-element.147), channel_id=1, source_target_pairs={{0,1},{1,0},{2,3},{3,2},{4,5},{5,4},{6,7},{7,6},{8,9},{9,8},{10,11... | collective-permute-start | bytes 3145736 | tf_op jit(solution)/shard_map/ppermute | solution.py:812
  131.7 2.8 %copy-start.8 = (bf16[2048,128]{1,0:T(8,128)(2,1)S(1)}, bf16[2048,128]{1,0:T(8,128)(2,1)}, u32[]{:S(2)}) copy-start(bf16[2048,128]{1,0:T(8,128)(2,1)} %get-tuple-element.144) | copy-start | bytes 1572868
  131.7 2.8 %copy-start.9 = (bf16[2048,128]{1,0:T(8,128)(2,1)S(1)}, bf16[2048,128]{1,0:T(8,128)(2,1)}, u32[]{:S(2)}) copy-start(bf16[2048,128]{1,0:T(8,128)(2,1)} %get-tuple-element.149) | copy-start | bytes 1572868
  135.8 14.2 %collective-permute-start.9 = (bf16[2048,128]{1,0:T(8,128)(2,1)}, bf16[2048,128]{1,0:T(8,128)(2,1)S(1)}, u32[]{:S(2)}, u32[]{:S(2)}) collective-permute-start(bf16[2048,128]{1,0:T(8,128)(2,1)} %get-tuple-element.156), channel_id=1, source_target_pairs={{0,2},{1,3},{2,0},{3,1},{4,6},{5,7},{6,4},{7,5},{8,10},{9,11},{10,... | collective-permute-start | bytes 1572872 | tf_op jit(solution)/shard_map/ppermute | solution.py:812
  136.1 11.8 %collective-permute-start.10 = (bf16[1664,128]{1,0:T(8,128)(2,1)S(1)}, bf16[1664,128]{1,0:T(8,128)(2,1)S(1)}, u32[]{:S(2)}, u32[]{:S(2)}) collective-permute-start(bf16[1664,128]{1,0:T(8,128)(2,1)S(1)} %pad_maximum_fusion.4), channel_id=1, source_target_pairs={{0,4},{4,0},{8,12},{12,8},{16,20},{20,16},{24,28},{28,24},{1,5},{5... | collective-permute-start | bytes 1277960 | tf_op jit(solution)/shard_map/ppermute | solution.py:815
  150.0 2.1 collective-permute-start.11
  150.1 2.1 copy-start.6
  152.1 0.7 copy-start.18
  152.9 7.4 %collective-permute-start.12 = (bf16[832,128]{1,0:T(8,128)(2,1)S(1)}, bf16[832,128]{1,0:T(8,128)(2,1)S(1)}, u32[]{:S(2)}, u32[]{:S(2)}) collective-permute-start(bf16[832,128]{1,0:T(8,128)(2,1)S(1)} %pad_maximum_fusion.9), channel_id=1, source_target_pairs={{0,8},{4,12},{8,0},{12,4},{16,24},{20,28},{24,16},{28,20},{1,9},{5... | collective-permute-start | bytes 638984 | tf_op jit(solution)/shard_map/ppermute | solution.py:815
  153.0 8.5 %collective-permute-start.13 = (bf16[1048,128]{1,0:T(8,128)(2,1)S(1)}, bf16[1048,128]{1,0:T(8,128)(2,1)S(1)}, u32[]{:S(2)}, u32[]{:S(2)}) collective-permute-start(bf16[1048,128]{1,0:T(8,128)(2,1)S(1)} %pad_maximum_fusion.8), channel_id=1, source_target_pairs={{0,4},{4,0},{8,12},{12,8},{16,20},{20,16},{24,28},{28,24},{1,5},{5... | collective-permute-start | bytes 804872 | tf_op jit(solution)/shard_map/ppermute | solution.py:815
  161.7 6.9 %collective-permute-start.14 = (bf16[416,128]{1,0:T(8,128)(2,1)S(1)}, bf16[416,128]{1,0:T(8,128)(2,1)S(1)}, u32[]{:S(2)}, u32[]{:S(2)}) collective-permute-start(bf16[416,128]{1,0:T(8,128)(2,1)S(1)} %pad_maximum_fusion.14), channel_id=1, source_target_pairs={{0,16},{4,20},{8,24},{12,28},{16,0},{20,4},{24,8},{28,12},{1,17},{... | collective-permute-start | bytes 319496 | tf_op jit(solution)/shard_map/ppermute | solution.py:815
  161.7 8.3 %collective-permute-start.15 = (bf16[536,128]{1,0:T(8,128)(2,1)S(1)}, bf16[536,128]{1,0:T(8,128)(2,1)S(1)}, u32[]{:S(2)}, u32[]{:S(2)}) collective-permute-start(bf16[536,128]{1,0:T(8,128)(2,1)S(1)} %pad_maximum_fusion.13), channel_id=1, source_target_pairs={{0,8},{4,12},{8,0},{12,4},{16,24},{20,28},{24,16},{28,20},{1,9},{5... | collective-permute-start | bytes 411656 | tf_op jit(solution)/shard_map/ppermute | solution.py:815
  170.2 8.0 %collective-permute-start.17 = (bf16[280,128]{1,0:T(8,128)(2,1)S(1)}, bf16[280,128]{1,0:T(8,128)(2,1)S(1)}, u32[]{:S(2)}, u32[]{:S(2)}) collective-permute-start(bf16[280,128]{1,0:T(8,128)(2,1)S(1)} %pad_maximum_fusion.15), channel_id=1, source_target_pairs={{0,16},{4,20},{8,24},{12,28},{16,0},{20,4},{24,8},{28,12},{1,17},{... | collective-permute-start | bytes 215048 | tf_op jit(solution)/shard_map/ppermute | solution.py:815
  171.3 8.3 %collective-permute-start.16 = (f16[352,128]{1,0:T(8,128)(2,1)S(1)}, f16[352,128]{1,0:T(8,128)(2,1)S(1)}, u32[]{:S(2)}, u32[]{:S(2)}) collective-permute-start(f16[352,128]{1,0:T(8,128)(2,1)S(1)} %concatenate.88), channel_id=1, source_target_pairs={{0,16},{4,20},{8,24},{12,28},{16,0},{20,4},{24,8},{28,12},{1,17},{... | collective-permute-start | bytes 270344 | tf_op jit(solution)/shard_map/ppermute | solution.py:815
  179.6 8.8 %copy-start.16 = (f32[1572]{0:T(1024)S(1)}, f32[1572]{0:T(1024)}, u32[]{:S(2)}) copy-start(f32[1572]{0:T(1024)} %param.61) | copy-start | bytes 18868
  179.6 8.8 %copy-start.17 = (f32[1572]{0:T(1024)S(1)}, f32[1572]{0:T(1024)}, u32[]{:S(2)}) copy-start(f32[1572]{0:T(1024)} %param.53) | copy-start | bytes 18868
  179.8 5.5 %collective-permute-start.19 = (f16[272,128]{1,0:T(8,128)(2,1)S(1)}, f16[272,128]{1,0:T(8,128)(2,1)S(1)}, u32[]{:S(2)}, u32[]{:S(2)}) collective-permute-start(f16[272,128]{1,0:T(8,128)(2,1)S(1)} %concatenate.91), channel_id=1, source_target_pairs={{0,16},{4,20},{8,24},{12,28},{16,0},{20,4},{24,8},{28,12},{1,17},{... | collective-permute-start | bytes 208904 | tf_op jit(solution)/shard_map/ppermute | solution.py:815
  179.9 6.6 %collective-permute-start.18 = (f16[704,128]{1,0:T(8,128)(2,1)S(1)}, f16[704,128]{1,0:T(8,128)(2,1)S(1)}, u32[]{:S(2)}, u32[]{:S(2)}) collective-permute-start(f16[704,128]{1,0:T(8,128)(2,1)S(1)} %pad_maximum_fusion.10), channel_id=1, source_target_pairs={{0,8},{4,12},{8,0},{12,4},{16,24},{20,28},{24,16},{28,20},{1,9},{5... | collective-permute-start | bytes 540680 | tf_op jit(solution)/shard_map/ppermute | solution.py:815
  186.7 6.7 %collective-permute-start.21 = (f16[544,128]{1,0:T(8,128)(2,1)S(1)}, f16[544,128]{1,0:T(8,128)(2,1)S(1)}, u32[]{:S(2)}, u32[]{:S(2)}) collective-permute-start(f16[544,128]{1,0:T(8,128)(2,1)S(1)} %pad_maximum_fusion.12), channel_id=1, source_target_pairs={{0,8},{4,12},{8,0},{12,4},{16,24},{20,28},{24,16},{28,20},{1,9},{5... | collective-permute-start | bytes 417800 | tf_op jit(solution)/shard_map/ppermute | solution.py:815
  188.1 3.6 %collective-permute-start.26 = (f32[8,128]{1,0:T(8,128)S(1)}, f32[8,128]{1,0:T(8,128)S(1)}, u32[]{:S(2)}, u32[]{:S(2)}) collective-permute-start(f32[8,128]{1,0:T(8,128)S(1)} %fusion.26), channel_id=1, source_target_pairs={{0,2},{1,3},{2,0},{3,1},{4,6},{5,7},{6,4},{7,5},{8,10},{9,11},{10,... | collective-permute-start | bytes 12296 | tf_op jit(solution)/shard_map/ppermute | solution.py:812
  192.3 9.6 %collective-permute-start.20 = (f16[1408,128]{1,0:T(8,128)(2,1)S(1)}, f16[1408,128]{1,0:T(8,128)(2,1)S(1)}, u32[]{:S(2)}, u32[]{:S(2)}) collective-permute-start(f16[1408,128]{1,0:T(8,128)(2,1)S(1)} %pad_maximum_fusion.6), channel_id=1, source_target_pairs={{0,4},{4,0},{8,12},{12,8},{16,20},{20,16},{24,28},{28,24},{1,5},{5... | collective-permute-start | bytes 1081352 | tf_op jit(solution)/shard_map/ppermute | solution.py:815
  193.6 13.2 %collective-permute-start.22 = (f16[1088,128]{1,0:T(8,128)(2,1)S(1)}, f16[1088,128]{1,0:T(8,128)(2,1)S(1)}, u32[]{:S(2)}, u32[]{:S(2)}) collective-permute-start(f16[1088,128]{1,0:T(8,128)(2,1)S(1)} %pad_maximum_fusion.7), channel_id=1, source_target_pairs={{0,4},{4,0},{8,12},{12,8},{16,20},{20,16},{24,28},{28,24},{1,5},{5... | collective-permute-start | bytes 835592 | tf_op jit(solution)/shard_map/ppermute | solution.py:815
  202.5 5.7 %collective-permute-start.24 = (f16[768,128]{1,0:T(8,128)(2,1)S(1)}, f16[768,128]{1,0:T(8,128)(2,1)S(1)}, u32[]{:S(2)}, u32[]{:S(2)}) collective-permute-start(f16[768,128]{1,0:T(8,128)(2,1)S(1)} %bitcast.172), channel_id=1, source_target_pairs={{0,2},{1,3},{2,0},{3,1},{4,6},{5,7},{6,4},{7,5},{8,10},{9,11},{10,... | collective-permute-start | bytes 589832 | tf_op jit(solution)/shard_map/ppermute | solution.py:812
  208.4 5.1 %collective-permute-start.25 = (f16[1536,128]{1,0:T(8,128)(2,1)S(1)}, f16[1536,128]{1,0:T(8,128)(2,1)S(1)}, u32[]{:S(2)}, u32[]{:S(2)}) collective-permute-start(f16[1536,128]{1,0:T(8,128)(2,1)S(1)} %pad_maximum_fusion.5), channel_id=1, source_target_pairs={{0,1},{1,0},{2,3},{3,2},{4,5},{5,4},{6,7},{7,6},{8,9},{9,8},{10,11... | collective-permute-start | bytes 1179656 | tf_op jit(solution)/shard_map/ppermute | solution.py:812
  211.3 4.4 %collective-permute-start.23 = (f32[8,128]{1,0:T(8,128)S(1)}, f32[8,128]{1,0:T(8,128)S(1)}, u32[]{:S(2)}, u32[]{:S(2)}) collective-permute-start(f32[8,128]{1,0:T(8,128)S(1)} %broadcast_in_dim.2), channel_id=1, source_target_pairs={{0,3},{1,2},{2,1},{3,0},{4,7},{5,6},{6,5},{7,4},{8,11},{9,10},{10,... | collective-permute-start | bytes 12296 | tf_op jit(solution)/shard_map/ppermute | solution.py:812
  212.0 3.8 %collective-permute-start.27 = (f32[8,128]{1,0:T(8,128)S(1)}, f32[8,128]{1,0:T(8,128)S(1)}, u32[]{:S(2)}, u32[]{:S(2)}) collective-permute-start(f32[8,128]{1,0:T(8,128)S(1)} %broadcast_in_dim.2), channel_id=1, source_target_pairs={{0,1},{1,0},{2,3},{3,2},{4,5},{5,4},{6,7},{7,6},{8,9},{9,8},{10,11... | collective-permute-start | bytes 12296 | tf_op jit(solution)/shard_map/ppermute | solution.py:812
  212.0 3.7 %collective-permute-start.28 = (f32[8,128]{1,0:T(8,128)S(1)}, f32[8,128]{1,0:T(8,128)S(1)}, u32[]{:S(2)}, u32[]{:S(2)}) collective-permute-start(f32[8,128]{1,0:T(8,128)S(1)} %broadcast_in_dim.2), channel_id=1, source_target_pairs={{0,2},{1,3},{2,0},{3,1},{4,6},{5,7},{6,4},{7,5},{8,10},{9,11},{10,... | collective-permute-start | bytes 12296 | tf_op jit(solution)/shard_map/ppermute | solution.py:812
  216.4 11.5 %copy-start.1 = (bf16[5,8192]{1,0:T(8,128)(2,1)S(1)}, bf16[5,8192]{1,0:T(8,128)(2,1)}, u32[]{:S(2)}) copy-start(bf16[5,8192]{1,0:T(8,128)(2,1)} %param.32) | copy-start | bytes 245764

commit v6 on v5

--- a/solution.py
+++ b/solution.py
@@ -60,6 +60,26 @@
         both = mm(jnp.concatenate(a, axis=0), b[0], dims)
         return both[:rows] + (both[rows:] + mm(a[0], b[1], dims))
     return mm(a[0], b[0], dims) + (mm(a[0], b[1], dims) + mm(a[1], b[0], dims))
+
+
+def mm_stack(a, b):
+    high, low = split(a)
+    rows = a.shape[0]
+    left = jnp.concatenate(
+        [
+            jnp.concatenate([high, high], axis=1),
+            jnp.concatenate([low, jnp.zeros_like(low)], axis=1),
+        ],
+        axis=0,
+    )
+    both = mm(left, b)
+    return both[:rows] + both[rows:]
+
+
+def mm_stack_t(a, b):
+    rows, width = a.shape[0], b.shape[0] // 2
+    both = mm(jnp.concatenate(split(a), axis=0), b, NTR)
+    return both[:rows, :width] + (both[rows:, :width] + both[:rows, width:])
 
 
 def mm2(a, b, dims=NN):
@@ -383,7 +403,7 @@
     count_col = column_of(counts_s, mols).astype(f32)
     slot_of = lane - starts_of(count_col, mols)
     alive = (slot_of >= 0.0) & (slot_of < count_col)
-    x = split(st[LAYERS])
+    x = jnp.concatenate(split(st[LAYERS]), axis=0)
     lstm = jnp.concatenate(
         [lstm_rows[0:H, :] + lstm_rows[2 * H : 3 * H, :], lstm_rows[H : 2 * H, :]], axis=0
     )
@@ -405,11 +425,11 @@
         cell = forget * cell + in_gate * part
         squashed = jnp.tanh(cell)
         hidden = out_gate * squashed
-        scores = jnp.where(alive, mm3(split(hidden), x), -1e30)
+        scores = jnp.where(alive, mm_stack(hidden, x), -1e30)
         weights = jnp.where(alive, jnp.exp(scores - jnp.max(scores, axis=1, keepdims=True)), 0.0)
         weights = weights / jnp.sum(weights, axis=1, keepdims=True)
         w_all[step * mols : (step + 1) * mols, :] = weights
-        read = mm3(split(weights), x, NTR)
+        read = mm_stack_t(weights, x)
         saved.append((query, in_gate, forget, part, out_gate, before_cell, squashed, hidden))
     query = jnp.concatenate([hidden, read], axis=1)
     first_w = split(first[...])
@@ -458,12 +478,11 @@
     for step in reversed(range(STEPS)):
         query, in_gate, forget, part, out_gate, before_cell, squashed, hid_t = saved[step]
         weights = w_all[step * mols : (step + 1) * mols, :]
-        d_read_s = split(d_read)
         d_reads[step] = d_read
-        d_weights = mm3(d_read_s, x)
+        d_weights = mm_stack(d_read, x)
         d_scores = weights * (d_weights - jnp.sum(weights * d_weights, axis=1, keepdims=True))
         ds_all[step * mols : (step + 1) * mols, :] = d_scores
-        d_hidden = d_hidden + mm3(split(d_scores), x, NTR)
+        d_hidden = d_hidden + mm_stack_t(d_scores, x)
         d_out = d_hidden * squashed * out_gate * (1.0 - out_gate)
         d_cell = d_cell + d_hidden * out_gate * (1.0 - squashed * squashed)
         d_forget = d_cell * before_cell * forget * (1.0 - forget)
@@ -832,10 +851,14 @@
         part = part.reshape(EH, own_rows, H)
         return part.transpose(1, 0, 2).reshape(own_rows, EH * H)
 
-    parts, bias_parts = {0: sent}, {0: bias_sent}
+    parts, bias_parts = {}, {0: bias_sent}
     for bit in reversed(range(row_bits)):
+        for k in list(bias_parts):
+            bias_parts[k + (1 << bit)] = row_swap(bias_parts[k], 1 << bit)
+        if not parts:
+            sent, bias_parts = lax.optimization_barrier((sent, bias_parts))
+            parts[0] = sent
         parts[1 << bit] = row_swap(sent, 1 << bit)
-        bias_parts[1 << bit] = row_swap(bias_sent, 1 << bit)
 
     ends = lax.dynamic_slice_in_dim(edge_ends, row * mols, mols, 1)
     feats = lax.dynamic_slice_in_dim(edge_feats, row * mols * EM, mols * EM, 1)
@@ -867,14 +890,13 @@
         compiler_params=params,
     )(atom_counts, table, node_feats, edge_in, bias_rows, *at_hand)
     forward = {k: forward_order(part) for k, part in parts.items() if k < n // 2}
-    parts, bias_parts, prepared, forward = lax.optimization_barrier(
-        (parts, bias_parts, prepared, forward)
+    parts, bias_parts, places, prepared, forward = lax.optimization_barrier(
+        (parts, bias_parts, places, prepared, forward)
     )
     meta, nodes, hid, before, feat, hot_src, hot_dst, turned = prepared
     for bit in reversed(range(row_bits)):
         for k in [k for k in parts if k > 1 << bit and not k & (1 << bit)]:
             parts[k + (1 << bit)] = row_swap(parts[k], 1 << bit)
-            bias_parts[k + (1 << bit)] = row_swap(bias_parts[k], 1 << bit)
     parts = [parts[k] for k in range(n)]
     bias_parts = [bias_parts[k] for k in range(n)]
     w_fwd = [forward[k] if k in forward else forward_order(parts[k]) for k in range(n)]
@@ -1082,7 +1104,6 @@
     second_swap, second_sent = next(second)
     first_swap, first_sent = first.send(first_came)
     while True:
-        first_sent, second_sent = tie((first_sent, second_sent))
         first_came, second_came = first_swap(first_sent), second_swap(second_sent)
         second_swap, second_sent = second.send(second_came)
         try:
@@ -1091,21 +1112,24 @@
             first_own, pack, square = end.value
             break
     second_came, came = second_swap(second_sent), cross(pack)
-    grad_in = beside["rows"] + cross(beside["rows"])
-    pack = jnp.concatenate(
-        [jnp.where(cross_bit == 0, pack, came), jnp.where(cross_bit == 0, came, pack)], axis=0
-    )
-    came = core(pack)
-    pack = jnp.concatenate(
-        [jnp.where(core_bit == 0, pack, came), jnp.where(core_bit == 0, came, pack)], axis=0
-    )
-    pack = pack.astype(f32).reshape(n * 2**mol_bits, -1, 128)
-    pack = (pack[:, :-16] * jnp.exp2(-pack[:, -16:-15, 0:1])).reshape(-1, 128)
+    rows, pack = tie((beside["rows"], pack))
+    came_rows = cross(rows)
     try:
         second.send(second_came)
     except StopIteration as end:
         second_own, _, more = end.value
     squares = jnp.broadcast_to(square + more, (8, 128))
+    came, came_rows, _ = tie((came, came_rows, squares))
+    grad_in = rows + came_rows
+    pack = jnp.concatenate(
+        [jnp.where(cross_bit == 0, pack, came), jnp.where(cross_bit == 0, came, pack)], axis=0
+    )
+    came = core(pack)
+    pack = jnp.concatenate(
+        [jnp.where(core_bit == 0, pack, came), jnp.where(core_bit == 0, came, pack)], axis=0
+    )
+    pack = pack.astype(f32).reshape(n * 2**mol_bits, -1, 128)
+    pack = (pack[:, :-16] * jnp.exp2(-pack[:, -16:-15, 0:1])).reshape(-1, 128)
     came = row_swap(squares, 3)
     came, pack, grad_in = tie((came, pack, grad_in))
     squares = (squares + row_swap(squares, 1)) + (row_swap(squares, 2) + came)

time: 227 us -> 223 us (0.982)
  starting transfers between devices: 18.3 us -> 33.7 us
  Pallas kernels: 124 us -> 115 us
  waiting for transfers between devices: 48.8 us -> 41.4 us
  other arithmetic: 18 us -> 15.7 us
    ppermute x12, starting transfers between devices: 10.8 us -> 20.1 us  [mol_swap(): lax.ppermute(x, 'mol', [(i, i ^ 1 << bit) for i in range(2 ** mol_bits)])]
    ppermute x17, starting transfers between devices: 7.45 us -> 13.6 us  [row_swap(): return lax.ppermute(x, 'row', [(i, i ^ k) for i in range(row_count)])]
    pallas_call x3, Pallas kernels: 40.5 us -> 35.9 us  [edge_parts(): pl.pallas_call(functools.partial(body_edges, jobs, slots, kind, last), gr...]
    ppermute x17, waiting for transfers between devices: 18.9 us -> 14.4 us  [row_swap(): return lax.ppermute(x, 'row', [(i, i ^ k) for i in range(row_count)])]
    pallas_call x1, Pallas kernels: 59.1 us -> 54.7 us  [per_device(): pl.pallas_call(main, out_shape=(sds((R_PACK, 128), f32), sds((8, 128), f3...]
    ppermute x12, waiting for transfers between devices: 29.9 us -> 27 us  [mol_swap(): lax.ppermute(x, 'mol', [(i, i ^ 1 << bit) for i in range(2 ** mol_bits)])]
    unnamed x44 -> x46, local copies, waits for them, and re-layouts: 6.3 us -> 4.23 us
  transfers between devices with their start and end apart: 29 -> 29, of which waited for: 16 -> 18; matrix products, arithmetic and copies ran while one was open for 10% -> 9% of each run, Pallas kernels for 19% -> 18%
where the time goes in v6:
time: 223 us
  Pallas kernels  115 us (52%)
  waiting for transfers between devices  41.4 us (19%)
  starting transfers between devices  33.7 us (15%)
  other arithmetic  15.7 us (7%)
  local copies, waits for them, and re-layouts  11.5 us (5%)
  between operations  5.08 us (2%)
    pallas_call x1, Pallas kernels, per_device(): pl.pallas_call(main, out_shape=(sds((R_PACK, 128), f32), sds((8, 128), f3...  54.7 us
    pallas_call x3, Pallas kernels, edge_parts(): pl.pallas_call(functools.partial(body_edges, jobs, slots, kind, last), gr...  35.9 us
    ppermute x12, waiting for transfers between devices, mol_swap(): lax.ppermute(x, 'mol', [(i, i ^ 1 << bit) for i in range(2 ** mol_bits)])  27 us
    ppermute x12, starting transfers between devices, mol_swap(): lax.ppermute(x, 'mol', [(i, i ^ 1 << bit) for i in range(2 ** mol_bits)])  20.1 us
    ppermute x17, waiting for transfers between devices, row_swap(): return lax.ppermute(x, 'row', [(i, i ^ k) for i in range(row_count)])  14.4 us
    ppermute x17, starting transfers between devices, row_swap(): return lax.ppermute(x, 'row', [(i, i ^ k) for i in range(row_count)])  13.6 us
    pallas_call x1, Pallas kernels, per_device(): pl.pallas_call(prepare, out_shape=(sds((2 + space // LB,), jnp.int32), sd...  13.2 us
    pallas_call x1, Pallas kernels, per_device(): pl.pallas_call(functools.partial(body_adamw, own_rows), out_shape=tuple(s...  11.4 us
  transfers between devices with their start and end apart: 29, of which 18 were waited for; matrix products, arithmetic and copies ran while one was open for 9% of the time, Pallas kernels for 18%

profile of v6, /device:TPU:0, one launch (start us, length us, event | category | flops | bytes accessed | tf_op | source)
XLA Modules:
  0.0 222.7 jit_solution(17765968337797608570)
XLA Ops:
  0.7 3.0 %collective-permute-start = (f32[32,128]{1,0:T(8,128)}, f32[32,128]{1,0:T(8,128)S(1)}, u32[]{:S(2)}, u32[]{:S(2)}) collective-permute-start(f32[32,128]{1,0:T(8,128)} %bitcast.177), channel_id=1, source_target_pairs={{0,2},{1,3},{2,0},{3,1},{4,6},{5,7},{6,4},{7,5},{8,10},{9,11},{10,... | collective-permute-start | bytes 49160 | tf_op jit(solution)/shard_map/ppermute | solution.py:831
  3.7 1.7 convert_element_type.154.refs_5_.refs_0_
  5.7 2.0 collective-permute-start.2
  10.6 1.7 copy.76.refs_2_
  12.6 1.2 copy.97
  14.1 1.2 copy.96
  15.2 13.2 %shard_map.502 = (s32[10]{0:T(128)}, bf16[128,1024]{1,0:T(8,128)(2,1)}, bf16[128,2048]{1,0:T(8,128)(2,1)}, f32[128,2048]{1,0:T(8,128)}, f32[8,2048]{1,0:T(8,128)...) custom-call(s32[32]{0:T(128)} %refs_0_.3, bf16[32,448]{1,0:T(8,128)(2,1)} %reshape.258.refs_1_, ...), custom_call_target="tpu_custom_call" | custom-call | tf_op jit(solution)/shard_map/pallas_call | solution.py:875
  28.4 3.1 %collective-permute-done.2.refs_15_.refs_0_.refs_2_ = bf16[128,4096]{1,0:T(8,128)(2,1)S(1)} collective-permute-done((bf16[128,4096]{1,0:T(8,128)(2,1)S(1)}, bf16[128,4096]{1,0:T(8,128)(2,1)S(1)}, u32[]{:S(2)}, u32[]{:S(2)}) %collective-permute-start.2) | collective-permute-done | bytes 1048608 | tf_op jit(solution)/shard_map/ppermute | solution.py:831
  31.8 1.2 copy.95
  33.0 1.2 collective-permute-done.5.refs_16_.refs_1_.refs_3_
  34.4 1.2 copy.94
  35.7 54.7 %shard_map.503 = (f32[2560,128]{1,0:T(8,128)}, f32[8,128]{1,0:T(8,128)}, bf16[2,128,2048]{2,1,0:T(8,128)(2,1)}, bf16[2,128,2048]{2,1,0:T(8,128)(2,1)}) custom-call(s32[32]{0:T(128)} %refs_0_.3, s32[32]{0:T(128)} %refs_1_.1, s32[4]{0:T(128)} %pad_add_fusion.refs_2_.place, s32[10]{0:T(128)} %get-tuple-element.126.refs_3_.meta, f32[12,32]{1,0:T(8,128)} %bitcast.187, ...), custom_call_target="tpu_custom_call" | custom-call | tf_op jit(solution)/shard_map/pallas_call | solution.py:919
  90.4 10.0 %shard_map.504 = (bf16[4608,128]{1,0:T(8,128)(2,1)}, bf16[2048,128]{1,0:T(8,128)(2,1)}, f32[128,2048]{1,0:T(8,128)}) custom-call(s32[10]{0:T(128)} %get-tuple-element.126.refs_3_.meta, bf16[128,4096]{1,0:T(8,128)(2,1)} %copy-done.3, bf16[128,4096]{1,0:T(8,128)(2,1)} %copy-done.4, bf16[2,128,2048]{2,1,0:T(8,128)(2,1)} %get-tuple-element.141.refs_2_.refs_4_, ...), custom_call_target="tpu_custom_call" | custom-call | tf_op jit(solution)/shard_map/pallas_call | solution.py:978
  100.6 2.9 %collective-permute-done.6 = bf16[4608,128]{1,0:T(8,128)(2,1)S(1)} collective-permute-done((bf16[4608,128]{1,0:T(8,128)(2,1)}, bf16[4608,128]{1,0:T(8,128)(2,1)S(1)}, u32[]{:S(2)}, u32[]{:S(2)}) %collective-permute-start.6) | collective-permute-done | bytes 1179680 | tf_op jit(solution)/shard_map/ppermute | solution.py:831
  103.8 0.9 copy-done.8
  104.9 1.8 collective-permute-start.7
  106.7 15.5 %shard_map.505 = (bf16[4096,128]{1,0:T(8,128)(2,1)}, bf16[2048,128]{1,0:T(8,128)(2,1)}, bf16[2048,128]{1,0:T(8,128)(2,1)}, f32[128,2048]{1,0:T(8,128)}) custom-call(s32[10]{0:T(128)} %get-tuple-element.126.refs_3_.meta, bf16[128,4096]{1,0:T(8,128)(2,1)} %copy-done.2, bf16[128,4096]{1,0:T(8,128)(2,1)} %copy-done.5, bf16[128,4096]{1,0:T(8,128)(2,1)} %copy-done.3, ...), custom_call_target="tpu_custom_call" | custom-call | tf_op jit(solution)/shard_map/pallas_call | solution.py:978
  122.2 3.8 %collective-permute-done.7 = bf16[3328,128]{1,0:T(8,128)(2,1)S(1)} collective-permute-done((bf16[3328,128]{1,0:T(8,128)(2,1)S(1)}, bf16[3328,128]{1,0:T(8,128)(2,1)S(1)}, u32[]{:S(2)}, u32[]{:S(2)}) %collective-permute-start.7) | collective-permute-done | bytes 852000 | tf_op jit(solution)/shard_map/ppermute | solution.py:831
  126.2 2.6 %collective-permute-done.8 = bf16[4096,128]{1,0:T(8,128)(2,1)S(1)} collective-permute-done((bf16[4096,128]{1,0:T(8,128)(2,1)}, bf16[4096,128]{1,0:T(8,128)(2,1)S(1)}, u32[]{:S(2)}, u32[]{:S(2)}) %collective-permute-start.8) | collective-permute-done | bytes 1048608 | tf_op jit(solution)/shard_map/ppermute | solution.py:831
  128.8 1.1 convert_add_fusion.1
  130.0 1.8 collective-permute-start.9
  131.9 1.5 collective-permute-start.10
  133.4 10.5 %shard_map.506 = (bf16[2080,128]{1,0:T(8,128)(2,1)}, bf16[2048,128]{1,0:T(8,128)(2,1)}, f32[8,128]{1,0:T(8,128)}) custom-call(s32[10]{0:T(128)} %get-tuple-element.126.refs_3_.meta, bf16[128,4096]{1,0:T(8,128)(2,1)} %copy-done.2, bf16[128,4096]{1,0:T(8,128)(2,1)} %copy-done.5, bf16[2,128,2048]{2,1,0:T(8,128)(2,1)} %get-tuple-element.141.refs_2_.refs_4_, ...), custom_call_target="tpu_custom_call" | custom-call | tf_op jit(solution)/shard_map/pallas_call | solution.py:978
  144.5 1.9 collective-permute-start.11
  147.2 1.8 collective-permute-start.17
  149.0 3.4 %collective-permute-done.11 = bf16[832,128]{1,0:T(8,128)(2,1)S(1)} collective-permute-done((bf16[832,128]{1,0:T(8,128)(2,1)S(1)}, bf16[832,128]{1,0:T(8,128)(2,1)S(1)}, u32[]{:S(2)}, u32[]{:S(2)}) %collective-permute-start.11) | collective-permute-done | bytes 213024 | tf_op jit(solution)/shard_map/ppermute | solution.py:834
  152.4 3.4 %collective-permute-done.17 = bf16[1048,128]{1,0:T(8,128)(2,1)S(1)} collective-permute-done((bf16[1048,128]{1,0:T(8,128)(2,1)S(1)}, bf16[1048,128]{1,0:T(8,128)(2,1)S(1)}, u32[]{:S(2)}, u32[]{:S(2)}) %collective-permute-start.17) | collective-permute-done | bytes 268320 | tf_op jit(solution)/shard_map/ppermute | solution.py:834
  155.9 1.8 collective-permute-start.18
  157.8 3.2 %collective-permute-done.18 = bf16[536,128]{1,0:T(8,128)(2,1)S(1)} collective-permute-done((bf16[536,128]{1,0:T(8,128)(2,1)S(1)}, bf16[536,128]{1,0:T(8,128)(2,1)S(1)}, u32[]{:S(2)}, u32[]{:S(2)}) %collective-permute-start.18) | collective-permute-done | bytes 137248 | tf_op jit(solution)/shard_map/ppermute | solution.py:834
  161.2 2.8 %collective-permute-start.19 = (bf16[280,128]{1,0:T(8,128)(2,1)S(1)}, bf16[280,128]{1,0:T(8,128)(2,1)S(1)}, u32[]{:S(2)}, u32[]{:S(2)}) collective-permute-start(bf16[280,128]{1,0:T(8,128)(2,1)S(1)} %pad_maximum_fusion.15), channel_id=1, source_target_pairs={{0,16},{4,20},{8,24},{12,28},{16,0},{20,4},{24,8},{28,12},{1,17},{... | collective-permute-start | bytes 215048 | tf_op jit(solution)/shard_map/ppermute | solution.py:834
  164.2 4.9 %collective-permute-done.19 = bf16[280,128]{1,0:T(8,128)(2,1)S(1)} collective-permute-done((bf16[280,128]{1,0:T(8,128)(2,1)S(1)}, bf16[280,128]{1,0:T(8,128)(2,1)S(1)}, u32[]{:S(2)}, u32[]{:S(2)}) %collective-permute-start.19) | collective-permute-done | bytes 71712 | tf_op jit(solution)/shard_map/ppermute | solution.py:834
  170.8 2.2 collective-permute-done.12
  175.1 1.2 collective-permute-done.20
  176.4 2.5 %collective-permute-start.21 = (f16[544,128]{1,0:T(8,128)(2,1)S(1)}, f16[544,128]{1,0:T(8,128)(2,1)S(1)}, u32[]{:S(2)}, u32[]{:S(2)}) collective-permute-start(f16[544,128]{1,0:T(8,128)(2,1)S(1)} %pad_maximum_fusion.12), channel_id=1, source_target_pairs={{0,8},{4,12},{8,0},{12,4},{16,24},{20,28},{24,16},{28,20},{1,9},{5... | collective-permute-start | bytes 417800 | tf_op jit(solution)/shard_map/ppermute | solution.py:834
  178.9 1.2 collective-permute-done.13
  180.2 3.5 %collective-permute-start.14 = (f16[704,128]{1,0:T(8,128)(2,1)S(1)}, f16[704,128]{1,0:T(8,128)(2,1)S(1)}, u32[]{:S(2)}, u32[]{:S(2)}) collective-permute-start(f16[704,128]{1,0:T(8,128)(2,1)S(1)} %pad_maximum_fusion.10), channel_id=1, source_target_pairs={{0,8},{4,12},{8,0},{12,4},{16,24},{20,28},{24,16},{28,20},{1,9},{5... | collective-permute-start | bytes 540680 | tf_op jit(solution)/shard_map/ppermute | solution.py:834
  183.8 1.6 collective-permute-start.22
  185.4 1.7 collective-permute-done.14
  187.3 1.6 collective-permute-start.15
  188.9 4.3 %collective-permute-done.22 = f16[1088,128]{1,0:T(8,128)(2,1)S(1)} collective-permute-done((f16[1088,128]{1,0:T(8,128)(2,1)S(1)}, f16[1088,128]{1,0:T(8,128)(2,1)S(1)}, u32[]{:S(2)}, u32[]{:S(2)}) %collective-permute-start.22) | collective-permute-done | bytes 278560 | tf_op jit(solution)/shard_map/ppermute | solution.py:834
  193.8 1.8 multiply_reduce_fusion
  195.5 1.6 collective-permute-done.15
  197.6 1.5 collective-permute-start.24
  199.9 1.8 multiply_reduce_fusion.1
  201.7 0.8 fusion.3
  205.3 1.5 collective-permute-start.23
  209.0 1.3 slice_multiply_fusion
  211.1 11.4 %shard_map.507 = (f32[5,128]{1,0:T(8,128)}, f32[128,4096]{1,0:T(8,128)}, f32[32,128]{1,0:T(8,128)}, f32[2,128,384]{2,1,0:T(8,128)}, f32[384,512]{1,0:T(8,128)}, ...) custom-call(s32[4]{0:T(128)} %pad_add_fusion.refs_2_.place, ...), custom_call_target="tpu_custom_call" | custom-call | tf_op jit(solution)/shard_map/pallas_call | solution.py:1161
  (166 shorter events, 15.2 us)
Async XLA Ops:
  0.7 7.2 %copy-start = (bf16[5,8192]{1,0:T(8,128)(2,1)S(1)}, bf16[5,8192]{1,0:T(8,128)(2,1)}, u32[]{:S(2)}) copy-start(bf16[5,8192]{1,0:T(8,128)(2,1)} %param.32) | copy-start | bytes 245764
  0.7 7.0 %copy-start.12 = (s32[2,128,64]{1,2,0:T(8,128)S(1)}, s32[2,128,64]{1,2,0:T(8,128)}, u32[]{:S(2)}) copy-start(s32[2,128,64]{1,2,0:T(8,128)} %param.33) | copy-start | bytes 196612
  0.7 7.3 %copy-start.16 = (f32[1572]{0:T(1024)S(1)}, f32[1572]{0:T(1024)}, u32[]{:S(2)}) copy-start(f32[1572]{0:T(1024)} %param.45) | copy-start | bytes 18868
  0.7 7.9 %copy-start.11 = (f32[4096]{0:T(1024)S(1)}, f32[4096]{0:T(1024)}, u32[]{:S(2)}) copy-start(f32[4096]{0:T(1024)} %param.40) | copy-start | bytes 49156
  0.7 4.9 %collective-permute-start = (f32[32,128]{1,0:T(8,128)}, f32[32,128]{1,0:T(8,128)S(1)}, u32[]{:S(2)}, u32[]{:S(2)}) collective-permute-start(f32[32,128]{1,0:T(8,128)} %bitcast.177), channel_id=1, source_target_pairs={{0,2},{1,3},{2,0},{3,1},{4,6},{5,7},{6,4},{7,5},{8,10},{9,11},{10,... | collective-permute-start | bytes 49160 | tf_op jit(solution)/shard_map/ppermute | solution.py:831
  5.4 7.1 %copy-start.2 = (bf16[128,4096]{1,0:T(8,128)(2,1)}, bf16[128,4096]{1,0:T(8,128)(2,1)S(1)}, u32[]{:S(2)}) copy-start(bf16[128,4096]{1,0:T(8,128)(2,1)S(1)} %convert_element_type.154.refs_5_.refs_0_) | copy-start | bytes 3145732
  5.7 6.9 %copy-start.13 = (f32[32,128]{1,0:T(8,128)}, f32[32,128]{1,0:T(8,128)S(1)}, u32[]{:S(2)}) copy-start(f32[32,128]{1,0:T(8,128)S(1)} %collective-permute-done.refs_19_) | copy-start | bytes 49156
  5.7 8.2 %collective-permute-start.1 = (bf16[128,4096]{1,0:T(8,128)(2,1)S(1)}, bf16[128,4096]{1,0:T(8,128)(2,1)S(1)}, u32[]{:S(2)}, u32[]{:S(2)}) collective-permute-start(bf16[128,4096]{1,0:T(8,128)(2,1)S(1)} %convert_element_type.154.refs_5_.refs_0_), channel_id=1, source_target_pairs={{0,1},{1,0},{2,3},{3,2},{4,5},{5,4},{6,7},{7,6},{8,9},{9,8},{10,11... | collective-permute-start | bytes 3145736 | tf_op jit(solution)/shard_map/ppermute | solution.py:831
  5.7 25.8 %collective-permute-start.2 = (bf16[128,4096]{1,0:T(8,128)(2,1)S(1)}, bf16[128,4096]{1,0:T(8,128)(2,1)S(1)}, u32[]{:S(2)}, u32[]{:S(2)}) collective-permute-start(bf16[128,4096]{1,0:T(8,128)(2,1)S(1)} %convert_element_type.154.refs_5_.refs_0_), channel_id=1, source_target_pairs={{0,2},{1,3},{2,0},{3,1},{4,6},{5,7},{6,4},{7,5},{8,10},{9,11},{10,... | collective-permute-start | bytes 3145736 | tf_op jit(solution)/shard_map/ppermute | solution.py:831
  8.6 19.8 %collective-permute-start.3 = (f32[32,128]{1,0:T(8,128)S(1)}, f32[32,128]{1,0:T(8,128)S(1)}, u32[]{:S(2)}, u32[]{:S(2)}) collective-permute-start(f32[32,128]{1,0:T(8,128)S(1)} %bitcast.180), channel_id=1, source_target_pairs={{0,1},{1,0},{2,3},{3,2},{4,5},{5,4},{6,7},{7,6},{8,9},{9,8},{10,11... | collective-permute-start | bytes 49160 | tf_op jit(solution)/shard_map/ppermute | solution.py:831
  8.9 19.5 %collective-permute-start.4 = (f32[32,128]{1,0:T(8,128)S(1)}, f32[32,128]{1,0:T(8,128)S(1)}, u32[]{:S(2)}, u32[]{:S(2)}) collective-permute-start(f32[32,128]{1,0:T(8,128)S(1)} %collective-permute-done.refs_19_), channel_id=1, source_target_pairs={{0,1},{1,0},{2,3},{3,2},{4,5},{5,4},{6,7},{7,6},{8,9},{9,8},{10,11... | collective-permute-start | bytes 49160 | tf_op jit(solution)/shard_map/ppermute | solution.py:831
  13.8 1.4 copy-start.5
  28.4 4.6 %copy-start.14 = (f32[32,128]{1,0:T(8,128)}, f32[32,128]{1,0:T(8,128)S(1)}, u32[]{:S(2)}) copy-start(f32[32,128]{1,0:T(8,128)S(1)} %collective-permute-done.3.refs_18_) | copy-start | bytes 49156
  28.4 4.5 %copy-start.15 = (f32[32,128]{1,0:T(8,128)}, f32[32,128]{1,0:T(8,128)S(1)}, u32[]{:S(2)}) copy-start(f32[32,128]{1,0:T(8,128)S(1)} %collective-permute-done.4.refs_20_) | copy-start | bytes 49156
  31.5 1.5 copy-start.3
  31.5 2.7 %collective-permute-start.5 = (bf16[128,4096]{1,0:T(8,128)(2,1)S(1)}, bf16[128,4096]{1,0:T(8,128)(2,1)S(1)}, u32[]{:S(2)}, u32[]{:S(2)}) collective-permute-start(bf16[128,4096]{1,0:T(8,128)(2,1)S(1)} %collective-permute-done.2.refs_15_.refs_0_.refs_2_), channel_id=1, source_target_pairs={{0,1},{1,0},{2,3},{3,2},{4,5},{5,4},{6,7},{7,6},{8,9},{9,8},{10,11... | collective-permute-start | bytes 3145736 | tf_op jit(solution)/shard_map/ppermute | solution.py:831
  34.2 1.5 copy-start.4
  90.4 10.2 %copy-start.6 = (f32[2560,128]{1,0:T(8,128)S(1)}, f32[2560,128]{1,0:T(8,128)}, u32[]{:S(2)}) copy-start(f32[2560,128]{1,0:T(8,128)} %get-tuple-element.143.refs_6_) | copy-start | bytes 3932164
  100.4 3.1 %collective-permute-start.6 = (bf16[4608,128]{1,0:T(8,128)(2,1)}, bf16[4608,128]{1,0:T(8,128)(2,1)S(1)}, u32[]{:S(2)}, u32[]{:S(2)}) collective-permute-start(bf16[4608,128]{1,0:T(8,128)(2,1)} %get-tuple-element.145), channel_id=1, source_target_pairs={{0,1},{1,0},{2,3},{3,2},{4,5},{5,4},{6,7},{7,6},{8,9},{9,8},{10,11... | collective-permute-start | bytes 3538952 | tf_op jit(solution)/shard_map/ppermute | solution.py:831
  103.7 1.0 copy-start.8
  104.9 21.1 %collective-permute-start.7 = (bf16[3328,128]{1,0:T(8,128)(2,1)S(1)}, bf16[3328,128]{1,0:T(8,128)(2,1)S(1)}, u32[]{:S(2)}, u32[]{:S(2)}) collective-permute-start(bf16[3328,128]{1,0:T(8,128)(2,1)S(1)} %pad_maximum_fusion), channel_id=1, source_target_pairs={{0,2},{1,3},{2,0},{3,1},{4,6},{5,7},{6,4},{7,5},{8,10},{9,11},{10,... | collective-permute-start | bytes 2555912 | tf_op jit(solution)/shard_map/ppermute | solution.py:831
  126.0 2.9 %collective-permute-start.8 = (bf16[4096,128]{1,0:T(8,128)(2,1)}, bf16[4096,128]{1,0:T(8,128)(2,1)S(1)}, u32[]{:S(2)}, u32[]{:S(2)}) collective-permute-start(bf16[4096,128]{1,0:T(8,128)(2,1)} %get-tuple-element.151), channel_id=1, source_target_pairs={{0,1},{1,0},{2,3},{3,2},{4,5},{5,4},{6,7},{7,6},{8,9},{9,8},{10,11... | collective-permute-start | bytes 3145736 | tf_op jit(solution)/shard_map/ppermute | solution.py:831
  126.0 2.8 %copy-start.9 = (bf16[2048,128]{1,0:T(8,128)(2,1)S(1)}, bf16[2048,128]{1,0:T(8,128)(2,1)}, u32[]{:S(2)}) copy-start(bf16[2048,128]{1,0:T(8,128)(2,1)} %get-tuple-element.148) | copy-start | bytes 1572868
  126.0 2.8 %copy-start.10 = (bf16[2048,128]{1,0:T(8,128)(2,1)S(1)}, bf16[2048,128]{1,0:T(8,128)(2,1)}, u32[]{:S(2)}) copy-start(bf16[2048,128]{1,0:T(8,128)(2,1)} %get-tuple-element.153) | copy-start | bytes 1572868
  130.0 14.2 %collective-permute-start.9 = (bf16[2048,128]{1,0:T(8,128)(2,1)}, bf16[2048,128]{1,0:T(8,128)(2,1)S(1)}, u32[]{:S(2)}, u32[]{:S(2)}) collective-permute-start(bf16[2048,128]{1,0:T(8,128)(2,1)} %get-tuple-element.160), channel_id=1, source_target_pairs={{0,2},{1,3},{2,0},{3,1},{4,6},{5,7},{6,4},{7,5},{8,10},{9,11},{10,... | collective-permute-start | bytes 1572872 | tf_op jit(solution)/shard_map/ppermute | solution.py:831
  131.9 12.0 %collective-permute-start.10 = (bf16[1664,128]{1,0:T(8,128)(2,1)S(1)}, bf16[1664,128]{1,0:T(8,128)(2,1)S(1)}, u32[]{:S(2)}, u32[]{:S(2)}) collective-permute-start(bf16[1664,128]{1,0:T(8,128)(2,1)S(1)} %pad_maximum_fusion.4), channel_id=1, source_target_pairs={{0,4},{4,0},{8,12},{12,8},{16,20},{20,16},{24,28},{28,24},{1,5},{5... | collective-permute-start | bytes 1277960 | tf_op jit(solution)/shard_map/ppermute | solution.py:834
  144.3 2.1 collective-permute-start.16
  144.3 2.1 copy-start.7
  144.5 7.8 %collective-permute-start.11 = (bf16[832,128]{1,0:T(8,128)(2,1)S(1)}, bf16[832,128]{1,0:T(8,128)(2,1)S(1)}, u32[]{:S(2)}, u32[]{:S(2)}) collective-permute-start(bf16[832,128]{1,0:T(8,128)(2,1)S(1)} %pad_maximum_fusion.9), channel_id=1, source_target_pairs={{0,8},{4,12},{8,0},{12,4},{16,24},{20,28},{24,16},{28,20},{1,9},{5... | collective-permute-start | bytes 638984 | tf_op jit(solution)/shard_map/ppermute | solution.py:834
  147.2 8.6 %collective-permute-start.17 = (bf16[1048,128]{1,0:T(8,128)(2,1)S(1)}, bf16[1048,128]{1,0:T(8,128)(2,1)S(1)}, u32[]{:S(2)}, u32[]{:S(2)}) collective-permute-start(bf16[1048,128]{1,0:T(8,128)(2,1)S(1)} %pad_maximum_fusion.8), channel_id=1, source_target_pairs={{0,4},{4,0},{8,12},{12,8},{16,20},{20,16},{24,28},{28,24},{1,5},{5... | collective-permute-start | bytes 804872 | tf_op jit(solution)/shard_map/ppermute | solution.py:834
  155.9 5.1 %collective-permute-start.18 = (bf16[536,128]{1,0:T(8,128)(2,1)S(1)}, bf16[536,128]{1,0:T(8,128)(2,1)S(1)}, u32[]{:S(2)}, u32[]{:S(2)}) collective-permute-start(bf16[536,128]{1,0:T(8,128)(2,1)S(1)} %pad_maximum_fusion.13), channel_id=1, source_target_pairs={{0,8},{4,12},{8,0},{12,4},{16,24},{20,28},{24,16},{28,20},{1,9},{5... | collective-permute-start | bytes 411656 | tf_op jit(solution)/shard_map/ppermute | solution.py:834
  161.2 8.0 %collective-permute-start.19 = (bf16[280,128]{1,0:T(8,128)(2,1)S(1)}, bf16[280,128]{1,0:T(8,128)(2,1)S(1)}, u32[]{:S(2)}, u32[]{:S(2)}) collective-permute-start(bf16[280,128]{1,0:T(8,128)(2,1)S(1)} %pad_maximum_fusion.15), channel_id=1, source_target_pairs={{0,16},{4,20},{8,24},{12,28},{16,0},{20,4},{24,8},{28,12},{1,17},{... | collective-permute-start | bytes 215048 | tf_op jit(solution)/shard_map/ppermute | solution.py:834
  164.0 9.0 %collective-permute-start.12 = (bf16[416,128]{1,0:T(8,128)(2,1)S(1)}, bf16[416,128]{1,0:T(8,128)(2,1)S(1)}, u32[]{:S(2)}, u32[]{:S(2)}) collective-permute-start(bf16[416,128]{1,0:T(8,128)(2,1)S(1)} %pad_maximum_fusion.14), channel_id=1, source_target_pairs={{0,16},{4,20},{8,24},{12,28},{16,0},{20,4},{24,8},{28,12},{1,17},{... | collective-permute-start | bytes 319496 | tf_op jit(solution)/shard_map/ppermute | solution.py:834
  170.6 5.7 %collective-permute-start.20 = (f16[272,128]{1,0:T(8,128)(2,1)S(1)}, f16[272,128]{1,0:T(8,128)(2,1)S(1)}, u32[]{:S(2)}, u32[]{:S(2)}) collective-permute-start(f16[272,128]{1,0:T(8,128)(2,1)S(1)} %concatenate.94), channel_id=1, source_target_pairs={{0,16},{4,20},{8,24},{12,28},{16,0},{20,4},{24,8},{28,12},{1,17},{... | collective-permute-start | bytes 208904 | tf_op jit(solution)/shard_map/ppermute | solution.py:834
  174.5 5.5 %collective-permute-start.13 = (f16[352,128]{1,0:T(8,128)(2,1)S(1)}, f16[352,128]{1,0:T(8,128)(2,1)S(1)}, u32[]{:S(2)}, u32[]{:S(2)}) collective-permute-start(f16[352,128]{1,0:T(8,128)(2,1)S(1)} %concatenate.86), channel_id=1, source_target_pairs={{0,16},{4,20},{8,24},{12,28},{16,0},{20,4},{24,8},{28,12},{1,17},{... | collective-permute-start | bytes 270344 | tf_op jit(solution)/shard_map/ppermute | solution.py:834
  176.4 7.2 %collective-permute-start.21 = (f16[544,128]{1,0:T(8,128)(2,1)S(1)}, f16[544,128]{1,0:T(8,128)(2,1)S(1)}, u32[]{:S(2)}, u32[]{:S(2)}) collective-permute-start(f16[544,128]{1,0:T(8,128)(2,1)S(1)} %pad_maximum_fusion.12), channel_id=1, source_target_pairs={{0,8},{4,12},{8,0},{12,4},{16,24},{20,28},{24,16},{28,20},{1,9},{5... | collective-permute-start | bytes 417800 | tf_op jit(solution)/shard_map/ppermute | solution.py:834
  180.2 6.9 %collective-permute-start.14 = (f16[704,128]{1,0:T(8,128)(2,1)S(1)}, f16[704,128]{1,0:T(8,128)(2,1)S(1)}, u32[]{:S(2)}, u32[]{:S(2)}) collective-permute-start(f16[704,128]{1,0:T(8,128)(2,1)S(1)} %pad_maximum_fusion.10), channel_id=1, source_target_pairs={{0,8},{4,12},{8,0},{12,4},{16,24},{20,28},{24,16},{28,20},{1,9},{5... | collective-permute-start | bytes 540680 | tf_op jit(solution)/shard_map/ppermute | solution.py:834
  183.8 9.4 %collective-permute-start.22 = (f16[1088,128]{1,0:T(8,128)(2,1)S(1)}, f16[1088,128]{1,0:T(8,128)(2,1)S(1)}, u32[]{:S(2)}, u32[]{:S(2)}) collective-permute-start(f16[1088,128]{1,0:T(8,128)(2,1)S(1)} %pad_maximum_fusion.7), channel_id=1, source_target_pairs={{0,4},{4,0},{8,12},{12,8},{16,20},{20,16},{24,28},{28,24},{1,5},{5... | collective-permute-start | bytes 835592 | tf_op jit(solution)/shard_map/ppermute | solution.py:834
  187.3 9.7 %collective-permute-start.15 = (f16[1408,128]{1,0:T(8,128)(2,1)S(1)}, f16[1408,128]{1,0:T(8,128)(2,1)S(1)}, u32[]{:S(2)}, u32[]{:S(2)}) collective-permute-start(f16[1408,128]{1,0:T(8,128)(2,1)S(1)} %pad_maximum_fusion.6), channel_id=1, source_target_pairs={{0,4},{4,0},{8,12},{12,8},{16,20},{20,16},{24,28},{28,24},{1,5},{5... | collective-permute-start | bytes 1081352 | tf_op jit(solution)/shard_map/ppermute | solution.py:834
  197.6 6.7 %collective-permute-start.24 = (f16[768,128]{1,0:T(8,128)(2,1)S(1)}, f16[768,128]{1,0:T(8,128)(2,1)S(1)}, u32[]{:S(2)}, u32[]{:S(2)}) collective-permute-start(f16[768,128]{1,0:T(8,128)(2,1)S(1)} %bitcast.171), channel_id=1, source_target_pairs={{0,2},{1,3},{2,0},{3,1},{4,6},{5,7},{6,4},{7,5},{8,10},{9,11},{10,... | collective-permute-start | bytes 589832 | tf_op jit(solution)/shard_map/ppermute | solution.py:831
  199.2 5.2 %collective-permute-start.25 = (f32[8,128]{1,0:T(8,128)S(1)}, f32[8,128]{1,0:T(8,128)S(1)}, u32[]{:S(2)}, u32[]{:S(2)}) collective-permute-start(f32[8,128]{1,0:T(8,128)S(1)} %fusion.26), channel_id=1, source_target_pairs={{0,2},{1,3},{2,0},{3,1},{4,6},{5,7},{6,4},{7,5},{8,10},{9,11},{10,... | collective-permute-start | bytes 12296 | tf_op jit(solution)/shard_map/ppermute | solution.py:831
  201.7 3.1 %copy-start.17 = (f32[1572]{0:T(1024)S(1)}, f32[1572]{0:T(1024)}, u32[]{:S(2)}) copy-start(f32[1572]{0:T(1024)} %param.61) | copy-start | bytes 18868
  201.7 3.1 %copy-start.18 = (f32[1572]{0:T(1024)S(1)}, f32[1572]{0:T(1024)}, u32[]{:S(2)}) copy-start(f32[1572]{0:T(1024)} %param.53) | copy-start | bytes 18868
  204.6 3.4 %collective-permute-start.26 = (f16[1536,128]{1,0:T(8,128)(2,1)S(1)}, f16[1536,128]{1,0:T(8,128)(2,1)S(1)}, u32[]{:S(2)}, u32[]{:S(2)}) collective-permute-start(f16[1536,128]{1,0:T(8,128)(2,1)S(1)} %pad_maximum_fusion.5), channel_id=1, source_target_pairs={{0,1},{1,0},{2,3},{3,2},{4,5},{5,4},{6,7},{7,6},{8,9},{9,8},{10,11... | collective-permute-start | bytes 1179656 | tf_op jit(solution)/shard_map/ppermute | solution.py:831
  205.3 5.0 %collective-permute-start.23 = (f32[8,128]{1,0:T(8,128)S(1)}, f32[8,128]{1,0:T(8,128)S(1)}, u32[]{:S(2)}, u32[]{:S(2)}) collective-permute-start(f32[8,128]{1,0:T(8,128)S(1)} %broadcast_in_dim.2), channel_id=1, source_target_pairs={{0,3},{1,2},{2,1},{3,0},{4,7},{5,6},{6,5},{7,4},{8,11},{9,10},{10,... | collective-permute-start | bytes 12296 | tf_op jit(solution)/shard_map/ppermute | solution.py:831
  206.9 3.5 %collective-permute-start.27 = (f32[8,128]{1,0:T(8,128)S(1)}, f32[8,128]{1,0:T(8,128)S(1)}, u32[]{:S(2)}, u32[]{:S(2)}) collective-permute-start(f32[8,128]{1,0:T(8,128)S(1)} %broadcast_in_dim.2), channel_id=1, source_target_pairs={{0,1},{1,0},{2,3},{3,2},{4,5},{5,4},{6,7},{7,6},{8,9},{9,8},{10,11... | collective-permute-start | bytes 12296 | tf_op jit(solution)/shard_map/ppermute | solution.py:831
  206.9 3.6 %collective-permute-start.28 = (f32[8,128]{1,0:T(8,128)S(1)}, f32[8,128]{1,0:T(8,128)S(1)}, u32[]{:S(2)}, u32[]{:S(2)}) collective-permute-start(f32[8,128]{1,0:T(8,128)S(1)} %broadcast_in_dim.2), channel_id=1, source_target_pairs={{0,2},{1,3},{2,0},{3,1},{4,6},{5,7},{6,4},{7,5},{8,10},{9,11},{10,... | collective-permute-start | bytes 12296 | tf_op jit(solution)/shard_map/ppermute | solution.py:831
  211.1 11.5 %copy-start.1 = (bf16[5,8192]{1,0:T(8,128)(2,1)S(1)}, bf16[5,8192]{1,0:T(8,128)(2,1)}, u32[]{:S(2)}) copy-start(bf16[5,8192]{1,0:T(8,128)(2,1)} %param.32) | copy-start | bytes 245764
  (1 other events, 0.7 us)

commit v7 on v6

--- a/solution.py
+++ b/solution.py
@@ -665,11 +665,6 @@
             return carry
 
         lax.fori_loop(0, blocks, finish, 0)
-        high, low = split(result[...])
-        rest = result[...] - high.astype(f32) - low.astype(f32)
-        outs[0][span : span + 32, :] = jnp.concatenate(
-            [high.astype(f32), low.astype(f32), rest, jnp.zeros_like(rest)], axis=0
-        ).astype(bf16)
 
 
 def adamw(weight, grad, moment, second):
@@ -1075,9 +1070,9 @@
     sent, carry = tie((sent, carry))
     arrived = cross(sent)
     (message, near, far), carry = edge_parts(
-        ((0, 0), (1, 0), (2, 1), (3, 1)),
-        ((1, 0), (0, 0), (2, 0), (0, span)),
-        (2 * span, span, span),
+        ((0, 0), (1, 0), (2, 1), (3, 1), (1, 1)),
+        ((1, 0), (0, 0), (2, 0), (0, span), (0, 2 * span)),
+        (3 * span, span, span),
         (carry,),
         False,
     )
@@ -1085,25 +1080,24 @@
     came = core(message)
     own = near.astype(f32) + came[:span].astype(f32) + arrived[:span].astype(f32)
     pack = pack + from_low(arrived[span:], 2)
-    sent = (far.astype(f32) + came[span:].astype(f32)).astype(bf16)
+    sent = (far.astype(f32) + came[span : 2 * span].astype(f32)).astype(bf16)
+    near_came = came[2 * span :]
 
     first = chain(own, pack, None)
     first_swap, first_sent = next(first)
     sent, first_sent, carry = tie((sent, first_sent, carry))
     arrived = cross(sent)
     first_came = first_swap(first_sent)
-    (message, near), grad_in = edge_parts(
-        ((0, 1), (1, 1)), ((1, 0), (0, 0)), (span + 32, span), (carry,), True
-    )
-    message, arrived, first_came = tie((message, arrived, first_came))
-    came = core(message)
-    beside = {"rows": grad_in + from_low(came[span : span + 24], 3)}
-    own = near.astype(f32) + came[:span].astype(f32) + arrived.astype(f32)
+    (near,), grad_in = edge_parts(((0, 1),), ((0, 0),), (span,), (carry,), True)
+    near, arrived, first_came = tie((near, arrived, first_came))
+    beside = {"rows": grad_in}
+    own = near.astype(f32) + near_came.astype(f32) + arrived.astype(f32)
 
     second = chain(own, None, beside)
     second_swap, second_sent = next(second)
     first_swap, first_sent = first.send(first_came)
     while True:
+        first_sent, second_sent = tie((first_sent, second_sent))
         first_came, second_came = first_swap(first_sent), second_swap(second_sent)
         second_swap, second_sent = second.send(second_came)
         try:
@@ -1121,6 +1115,7 @@
     squares = jnp.broadcast_to(square + more, (8, 128))
     came, came_rows, _ = tie((came, came_rows, squares))
     grad_in = rows + came_rows
+    grad_in = grad_in + core(grad_in)
     pack = jnp.concatenate(
         [jnp.where(cross_bit == 0, pack, came), jnp.where(cross_bit == 0, came, pack)], axis=0
     )

time: 223 us -> 222 us (level)
  waiting for transfers between devices: 41.4 us -> 34.4 us
  other arithmetic: 15.7 us -> 20.1 us
    ppermute x12, waiting for transfers between devices: 27 us -> 22.3 us  [mol_swap(): lax.ppermute(x, 'mol', [(i, i ^ 1 << bit) for i in range(2 ** mol_bits)])]
    ppermute x17, waiting for transfers between devices: 14.4 us -> 12.1 us  [row_swap(): return lax.ppermute(x, 'row', [(i, i ^ k) for i in range(row_count)])]
    unnamed x46 -> x52, local copies, waits for them, and re-layouts: 4.23 us -> 4.54 us
  transfers between devices with their start and end apart: 29 -> 29, of which waited for: 18 -> 16; matrix products, arithmetic and copies ran while one was open for 9% -> 10% of each run, Pallas kernels for 18% -> 18%
where the time goes in v7:
time: 222 us; the launch traced here: 221 us
  Pallas kernels  115 us (52%)
  starting transfers between devices  35.1 us (16%)
  waiting for transfers between devices  34.4 us (15%)
  other arithmetic  20.1 us (9%)
  local copies, waits for them, and re-layouts  11.7 us (5%)
  between operations  5.13 us (2%)
    pallas_call x1, Pallas kernels, per_device(): pl.pallas_call(main, out_shape=(sds((R_PACK, 128), f32), sds((8, 128), f3...  54.7 us
    pallas_call x3, Pallas kernels, edge_parts(): pl.pallas_call(functools.partial(body_edges, jobs, slots, kind, last), gr...  35.8 us
    ppermute x12, waiting for transfers between devices, mol_swap(): lax.ppermute(x, 'mol', [(i, i ^ 1 << bit) for i in range(2 ** mol_bits)])  22.3 us
    ppermute x12, starting transfers between devices, mol_swap(): lax.ppermute(x, 'mol', [(i, i ^ 1 << bit) for i in range(2 ** mol_bits)])  21 us
    ppermute x17, starting transfers between devices, row_swap(): return lax.ppermute(x, 'row', [(i, i ^ k) for i in range(row_count)])  14.1 us
    pallas_call x1, Pallas kernels, per_device(): pl.pallas_call(prepare, out_shape=(sds((2 + space // LB,), jnp.int32), sd...  13.2 us
    ppermute x17, waiting for transfers between devices, row_swap(): return lax.ppermute(x, 'row', [(i, i ^ k) for i in range(row_count)])  12.1 us
    pallas_call x1, Pallas kernels, per_device(): pl.pallas_call(functools.partial(body_adamw, own_rows), out_shape=tuple(s...  11.4 us
  transfers between devices with their start and end apart: 29, of which 16 were waited for; matrix products, arithmetic and copies ran while one was open for 10% of the time, Pallas kernels for 18%

profile of v7, /device:TPU:0, one launch (start us, length us, event | category | flops | bytes accessed | tf_op | source)
XLA Modules:
  0.0 221.5 jit_solution(15365154856748059637)
XLA Ops:
  0.7 3.0 %collective-permute-start = (f32[32,128]{1,0:T(8,128)}, f32[32,128]{1,0:T(8,128)S(1)}, u32[]{:S(2)}, u32[]{:S(2)}) collective-permute-start(f32[32,128]{1,0:T(8,128)} %bitcast.177), channel_id=1, source_target_pairs={{0,2},{1,3},{2,0},{3,1},{4,6},{5,7},{6,4},{7,5},{8,10},{9,11},{10,... | collective-permute-start | bytes 49160 | tf_op jit(solution)/shard_map/ppermute | solution.py:826
  3.7 1.7 convert_element_type.151.refs_5_.refs_0_
  5.7 2.0 collective-permute-start.2
  10.5 1.7 copy.76.refs_2_
  12.6 1.1 copy.97
  14.0 1.2 copy.96
  15.1 13.2 %shard_map.502 = (s32[10]{0:T(128)}, bf16[128,1024]{1,0:T(8,128)(2,1)}, bf16[128,2048]{1,0:T(8,128)(2,1)}, f32[128,2048]{1,0:T(8,128)}, f32[8,2048]{1,0:T(8,128)...) custom-call(s32[32]{0:T(128)} %refs_0_.3, bf16[32,448]{1,0:T(8,128)(2,1)} %reshape.251.refs_1_, ...), custom_call_target="tpu_custom_call" | custom-call | tf_op jit(solution)/shard_map/pallas_call | solution.py:870
  28.3 3.2 %collective-permute-done.2.refs_15_.refs_0_.refs_2_ = bf16[128,4096]{1,0:T(8,128)(2,1)S(1)} collective-permute-done((bf16[128,4096]{1,0:T(8,128)(2,1)S(1)}, bf16[128,4096]{1,0:T(8,128)(2,1)S(1)}, u32[]{:S(2)}, u32[]{:S(2)}) %collective-permute-start.2) | collective-permute-done | bytes 1048608 | tf_op jit(solution)/shard_map/ppermute | solution.py:826
  31.8 1.2 copy.95
  33.0 1.2 collective-permute-done.5.refs_16_.refs_1_.refs_3_
  34.4 1.2 copy.94
  35.6 54.7 %shard_map.503 = (f32[2560,128]{1,0:T(8,128)}, f32[8,128]{1,0:T(8,128)}, bf16[2,128,2048]{2,1,0:T(8,128)(2,1)}, bf16[2,128,2048]{2,1,0:T(8,128)(2,1)}) custom-call(s32[32]{0:T(128)} %refs_0_.3, s32[32]{0:T(128)} %refs_1_.1, s32[4]{0:T(128)} %pad_add_fusion.refs_2_.place, s32[10]{0:T(128)} %get-tuple-element.135.refs_3_.meta, f32[12,32]{1,0:T(8,128)} %bitcast.187, ...), custom_call_target="tpu_custom_call" | custom-call | tf_op jit(solution)/shard_map/pallas_call | solution.py:914
  90.4 10.0 %shard_map.504 = (bf16[4608,128]{1,0:T(8,128)(2,1)}, bf16[2048,128]{1,0:T(8,128)(2,1)}, f32[128,2048]{1,0:T(8,128)}) custom-call(s32[10]{0:T(128)} %get-tuple-element.135.refs_3_.meta, bf16[128,4096]{1,0:T(8,128)(2,1)} %copy-done.3, bf16[128,4096]{1,0:T(8,128)(2,1)} %copy-done.4, bf16[2,128,2048]{2,1,0:T(8,128)(2,1)} %get-tuple-element.150.refs_2_.refs_5_.refs_1_, ...), custom_call_target="tpu_custom_call" | custom-call | tf_op jit(solution)/shard_map/pallas_call | solution.py:973
  100.6 2.9 %collective-permute-done.6 = bf16[4608,128]{1,0:T(8,128)(2,1)S(1)} collective-permute-done((bf16[4608,128]{1,0:T(8,128)(2,1)}, bf16[4608,128]{1,0:T(8,128)(2,1)S(1)}, u32[]{:S(2)}, u32[]{:S(2)}) %collective-permute-start.6) | collective-permute-done | bytes 1179680 | tf_op jit(solution)/shard_map/ppermute | solution.py:826
  104.9 1.8 collective-permute-start.7
  106.7 18.2 %shard_map.505 = (bf16[6144,128]{1,0:T(8,128)(2,1)}, bf16[2048,128]{1,0:T(8,128)(2,1)}, bf16[2048,128]{1,0:T(8,128)(2,1)}, f32[128,2048]{1,0:T(8,128)}) custom-call(s32[10]{0:T(128)} %get-tuple-element.135.refs_3_.meta, bf16[128,4096]{1,0:T(8,128)(2,1)} %copy-done.2, bf16[128,4096]{1,0:T(8,128)(2,1)} %copy-done.5, bf16[128,4096]{1,0:T(8,128)(2,1)} %copy-done.3, ...), custom_call_target="tpu_custom_call" | custom-call | tf_op jit(solution)/shard_map/pallas_call | solution.py:973
  125.0 1.0 collective-permute-done.7
  127.0 2.6 %collective-permute-done.8 = bf16[6144,128]{1,0:T(8,128)(2,1)S(1)} collective-permute-done((bf16[6144,128]{1,0:T(8,128)(2,1)}, bf16[6144,128]{1,0:T(8,128)(2,1)S(1)}, u32[]{:S(2)}, u32[]{:S(2)}) %collective-permute-start.8) | collective-permute-done | bytes 1572896 | tf_op jit(solution)/shard_map/ppermute | solution.py:826
  129.6 1.1 convert_add_fusion.1
  131.6 1.7 collective-permute-start.9
  133.3 1.5 collective-permute-start.10
  134.8 7.5 %shard_map.506 = (bf16[2048,128]{1,0:T(8,128)(2,1)}, f32[8,128]{1,0:T(8,128)}) custom-call(s32[10]{0:T(128)} %get-tuple-element.135.refs_3_.meta, bf16[128,4096]{1,0:T(8,128)(2,1)} %copy-done.2, bf16[2,128,2048]{2,1,0:T(8,128)(2,1)} %get-tuple-element.150.refs_2_.refs_5_.refs_1_, bf16[2,128,2048]{2,1,0:T(8,128)(2,1)} %get-tuple-element.151.refs_3_.refs_6_.refs_2_, ...), custom_call_target="tpu_custom_call" | custom-call | tf_op jit(solution)/shard_map/pallas_call | solution.py:973
  143.1 2.0 collective-permute-done.10
  145.8 1.0 bitcast_add_fusion.1
  147.8 1.2 convert_add_fusion
  149.2 1.9 collective-permute-start.11
  151.1 1.5 collective-permute-start.12
  152.6 3.2 %collective-permute-done.11 = bf16[832,128]{1,0:T(8,128)(2,1)S(1)} collective-permute-done((bf16[832,128]{1,0:T(8,128)(2,1)S(1)}, bf16[832,128]{1,0:T(8,128)(2,1)S(1)}, u32[]{:S(2)}, u32[]{:S(2)}) %collective-permute-start.11) | collective-permute-done | bytes 213024 | tf_op jit(solution)/shard_map/ppermute | solution.py:829
  156.0 2.5 %collective-permute-done.12 = bf16[1048,128]{1,0:T(8,128)(2,1)S(1)} collective-permute-done((bf16[1048,128]{1,0:T(8,128)(2,1)S(1)}, bf16[1048,128]{1,0:T(8,128)(2,1)S(1)}, u32[]{:S(2)}, u32[]{:S(2)}) %collective-permute-start.12) | collective-permute-done | bytes 268320 | tf_op jit(solution)/shard_map/ppermute | solution.py:829
  158.6 2.6 %collective-permute-start.13 = (bf16[416,128]{1,0:T(8,128)(2,1)S(1)}, bf16[416,128]{1,0:T(8,128)(2,1)S(1)}, u32[]{:S(2)}, u32[]{:S(2)}) collective-permute-start(bf16[416,128]{1,0:T(8,128)(2,1)S(1)} %pad_maximum_fusion.14), channel_id=1, source_target_pairs={{0,16},{4,20},{8,24},{12,28},{16,0},{20,4},{24,8},{28,12},{1,17},{... | collective-permute-start | bytes 319496 | tf_op jit(solution)/shard_map/ppermute | solution.py:829
  161.7 3.5 %collective-permute-done.13 = bf16[416,128]{1,0:T(8,128)(2,1)S(1)} collective-permute-done((bf16[416,128]{1,0:T(8,128)(2,1)S(1)}, bf16[416,128]{1,0:T(8,128)(2,1)S(1)}, u32[]{:S(2)}, u32[]{:S(2)}) %collective-permute-start.13) | collective-permute-done | bytes 106528 | tf_op jit(solution)/shard_map/ppermute | solution.py:829
  166.9 1.7 collective-permute-start.16
  168.6 1.2 collective-permute-start.15
  169.9 3.1 %collective-permute-done.16 = bf16[280,128]{1,0:T(8,128)(2,1)S(1)} collective-permute-done((bf16[280,128]{1,0:T(8,128)(2,1)S(1)}, bf16[280,128]{1,0:T(8,128)(2,1)S(1)}, u32[]{:S(2)}, u32[]{:S(2)}) %collective-permute-start.16) | collective-permute-done | bytes 71712 | tf_op jit(solution)/shard_map/ppermute | solution.py:829
  174.5 1.2 collective-permute-start.18
  175.7 4.0 %collective-permute-start.17 = (f16[704,128]{1,0:T(8,128)(2,1)S(1)}, f16[704,128]{1,0:T(8,128)(2,1)S(1)}, u32[]{:S(2)}, u32[]{:S(2)}) collective-permute-start(f16[704,128]{1,0:T(8,128)(2,1)S(1)} %pad_maximum_fusion.10), channel_id=1, source_target_pairs={{0,8},{4,12},{8,0},{12,4},{16,24},{20,28},{24,16},{28,20},{1,9},{5... | collective-permute-start | bytes 540680 | tf_op jit(solution)/shard_map/ppermute | solution.py:829
  179.9 4.0 %collective-permute-done.17 = f16[704,128]{1,0:T(8,128)(2,1)S(1)} collective-permute-done((f16[704,128]{1,0:T(8,128)(2,1)S(1)}, f16[704,128]{1,0:T(8,128)(2,1)S(1)}, u32[]{:S(2)}, u32[]{:S(2)}) %collective-permute-start.17) | collective-permute-done | bytes 180256 | tf_op jit(solution)/shard_map/ppermute | solution.py:829
  184.0 1.5 collective-permute-start.20
  185.6 1.6 collective-permute-start.19
  187.1 2.0 collective-permute-done.20
  189.3 1.6 collective-permute-start.21
  191.0 2.0 collective-permute-done.19
  193.6 1.6 collective-permute-start.23
  196.6 1.7 multiply_reduce_fusion.1
  200.2 1.7 multiply_reduce_fusion
  204.0 1.2 collective-permute-start.22
  207.7 1.3 slice_multiply_fusion
  209.9 11.4 %shard_map.507 = (f32[5,128]{1,0:T(8,128)}, f32[128,4096]{1,0:T(8,128)}, f32[32,128]{1,0:T(8,128)}, f32[2,128,384]{2,1,0:T(8,128)}, f32[384,512]{1,0:T(8,128)}, ...) custom-call(s32[4]{0:T(128)} %pad_add_fusion.refs_2_.place, ...), custom_call_target="tpu_custom_call" | custom-call | tf_op jit(solution)/shard_map/pallas_call | solution.py:1156
  (172 shorter events, 19.9 us)
Async XLA Ops:
  0.7 7.2 %copy-start = (bf16[5,8192]{1,0:T(8,128)(2,1)S(1)}, bf16[5,8192]{1,0:T(8,128)(2,1)}, u32[]{:S(2)}) copy-start(bf16[5,8192]{1,0:T(8,128)(2,1)} %param.32) | copy-start | bytes 245764
  0.7 7.0 %copy-start.15 = (s32[2,128,64]{1,2,0:T(8,128)S(1)}, s32[2,128,64]{1,2,0:T(8,128)}, u32[]{:S(2)}) copy-start(s32[2,128,64]{1,2,0:T(8,128)} %param.33) | copy-start | bytes 196612
  0.7 7.3 %copy-start.20 = (f32[1572]{0:T(1024)S(1)}, f32[1572]{0:T(1024)}, u32[]{:S(2)}) copy-start(f32[1572]{0:T(1024)} %param.45) | copy-start | bytes 18868
  0.7 7.9 %copy-start.14 = (f32[4096]{0:T(1024)S(1)}, f32[4096]{0:T(1024)}, u32[]{:S(2)}) copy-start(f32[4096]{0:T(1024)} %param.40) | copy-start | bytes 49156
  0.7 4.9 %collective-permute-start = (f32[32,128]{1,0:T(8,128)}, f32[32,128]{1,0:T(8,128)S(1)}, u32[]{:S(2)}, u32[]{:S(2)}) collective-permute-start(f32[32,128]{1,0:T(8,128)} %bitcast.177), channel_id=1, source_target_pairs={{0,2},{1,3},{2,0},{3,1},{4,6},{5,7},{6,4},{7,5},{8,10},{9,11},{10,... | collective-permute-start | bytes 49160 | tf_op jit(solution)/shard_map/ppermute | solution.py:826
  5.4 7.1 %copy-start.2 = (bf16[128,4096]{1,0:T(8,128)(2,1)}, bf16[128,4096]{1,0:T(8,128)(2,1)S(1)}, u32[]{:S(2)}) copy-start(bf16[128,4096]{1,0:T(8,128)(2,1)S(1)} %convert_element_type.151.refs_5_.refs_0_) | copy-start | bytes 3145732
  5.7 6.9 %copy-start.16 = (f32[32,128]{1,0:T(8,128)}, f32[32,128]{1,0:T(8,128)S(1)}, u32[]{:S(2)}) copy-start(f32[32,128]{1,0:T(8,128)S(1)} %collective-permute-done.refs_19_) | copy-start | bytes 49156
  5.7 8.0 %collective-permute-start.1 = (bf16[128,4096]{1,0:T(8,128)(2,1)S(1)}, bf16[128,4096]{1,0:T(8,128)(2,1)S(1)}, u32[]{:S(2)}, u32[]{:S(2)}) collective-permute-start(bf16[128,4096]{1,0:T(8,128)(2,1)S(1)} %convert_element_type.151.refs_5_.refs_0_), channel_id=1, source_target_pairs={{0,1},{1,0},{2,3},{3,2},{4,5},{5,4},{6,7},{7,6},{8,9},{9,8},{10,11... | collective-permute-start | bytes 3145736 | tf_op jit(solution)/shard_map/ppermute | solution.py:826
  5.7 25.8 %collective-permute-start.2 = (bf16[128,4096]{1,0:T(8,128)(2,1)S(1)}, bf16[128,4096]{1,0:T(8,128)(2,1)S(1)}, u32[]{:S(2)}, u32[]{:S(2)}) collective-permute-start(bf16[128,4096]{1,0:T(8,128)(2,1)S(1)} %convert_element_type.151.refs_5_.refs_0_), channel_id=1, source_target_pairs={{0,2},{1,3},{2,0},{3,1},{4,6},{5,7},{6,4},{7,5},{8,10},{9,11},{10,... | collective-permute-start | bytes 3145736 | tf_op jit(solution)/shard_map/ppermute | solution.py:826
  8.6 19.7 %collective-permute-start.3 = (f32[32,128]{1,0:T(8,128)S(1)}, f32[32,128]{1,0:T(8,128)S(1)}, u32[]{:S(2)}, u32[]{:S(2)}) collective-permute-start(f32[32,128]{1,0:T(8,128)S(1)} %bitcast.180), channel_id=1, source_target_pairs={{0,1},{1,0},{2,3},{3,2},{4,5},{5,4},{6,7},{7,6},{8,9},{9,8},{10,11... | collective-permute-start | bytes 49160 | tf_op jit(solution)/shard_map/ppermute | solution.py:826
  8.9 19.4 %collective-permute-start.4 = (f32[32,128]{1,0:T(8,128)S(1)}, f32[32,128]{1,0:T(8,128)S(1)}, u32[]{:S(2)}, u32[]{:S(2)}) collective-permute-start(f32[32,128]{1,0:T(8,128)S(1)} %collective-permute-done.refs_19_), channel_id=1, source_target_pairs={{0,1},{1,0},{2,3},{3,2},{4,5},{5,4},{6,7},{7,6},{8,9},{9,8},{10,11... | collective-permute-start | bytes 49160 | tf_op jit(solution)/shard_map/ppermute | solution.py:826
  28.3 4.7 %copy-start.17 = (f32[32,128]{1,0:T(8,128)}, f32[32,128]{1,0:T(8,128)S(1)}, u32[]{:S(2)}) copy-start(f32[32,128]{1,0:T(8,128)S(1)} %collective-permute-done.3.refs_18_) | copy-start | bytes 49156
  28.3 4.6 %copy-start.18 = (f32[32,128]{1,0:T(8,128)}, f32[32,128]{1,0:T(8,128)S(1)}, u32[]{:S(2)}) copy-start(f32[32,128]{1,0:T(8,128)S(1)} %collective-permute-done.4.refs_20_) | copy-start | bytes 49156
  31.5 1.4 copy-start.3
  31.5 2.7 %collective-permute-start.5 = (bf16[128,4096]{1,0:T(8,128)(2,1)S(1)}, bf16[128,4096]{1,0:T(8,128)(2,1)S(1)}, u32[]{:S(2)}, u32[]{:S(2)}) collective-permute-start(bf16[128,4096]{1,0:T(8,128)(2,1)S(1)} %collective-permute-done.2.refs_15_.refs_0_.refs_2_), channel_id=1, source_target_pairs={{0,1},{1,0},{2,3},{3,2},{4,5},{5,4},{6,7},{7,6},{8,9},{9,8},{10,11... | collective-permute-start | bytes 3145736 | tf_op jit(solution)/shard_map/ppermute | solution.py:826
  34.2 1.5 copy-start.4
  90.4 10.2 %copy-start.6 = (f32[2560,128]{1,0:T(8,128)S(1)}, f32[2560,128]{1,0:T(8,128)}, u32[]{:S(2)}) copy-start(f32[2560,128]{1,0:T(8,128)} %get-tuple-element.152.refs_6_) | copy-start | bytes 3932164
  100.4 3.1 %collective-permute-start.6 = (bf16[4608,128]{1,0:T(8,128)(2,1)}, bf16[4608,128]{1,0:T(8,128)(2,1)S(1)}, u32[]{:S(2)}, u32[]{:S(2)}) collective-permute-start(bf16[4608,128]{1,0:T(8,128)(2,1)} %get-tuple-element.154), channel_id=1, source_target_pairs={{0,1},{1,0},{2,3},{3,2},{4,5},{5,4},{6,7},{7,6},{8,9},{9,8},{10,11... | collective-permute-start | bytes 3538952 | tf_op jit(solution)/shard_map/ppermute | solution.py:826
  104.9 21.1 %collective-permute-start.7 = (bf16[3328,128]{1,0:T(8,128)(2,1)S(1)}, bf16[3328,128]{1,0:T(8,128)(2,1)S(1)}, u32[]{:S(2)}, u32[]{:S(2)}) collective-permute-start(bf16[3328,128]{1,0:T(8,128)(2,1)S(1)} %pad_maximum_fusion), channel_id=1, source_target_pairs={{0,2},{1,3},{2,0},{3,1},{4,6},{5,7},{6,4},{7,5},{8,10},{9,11},{10,... | collective-permute-start | bytes 2555912 | tf_op jit(solution)/shard_map/ppermute | solution.py:826
  126.0 3.6 %collective-permute-start.8 = (bf16[6144,128]{1,0:T(8,128)(2,1)}, bf16[6144,128]{1,0:T(8,128)(2,1)S(1)}, u32[]{:S(2)}, u32[]{:S(2)}) collective-permute-start(bf16[6144,128]{1,0:T(8,128)(2,1)} %get-tuple-element.160), channel_id=1, source_target_pairs={{0,1},{1,0},{2,3},{3,2},{4,5},{5,4},{6,7},{7,6},{8,9},{9,8},{10,11... | collective-permute-start | bytes 4718600 | tf_op jit(solution)/shard_map/ppermute | solution.py:826
  126.0 3.6 %copy-start.11 = (bf16[2048,128]{1,0:T(8,128)(2,1)S(1)}, bf16[2048,128]{1,0:T(8,128)(2,1)}, u32[]{:S(2)}) copy-start(bf16[2048,128]{1,0:T(8,128)(2,1)} %get-tuple-element.157) | copy-start | bytes 1572868
  126.0 3.6 %copy-start.12 = (bf16[2048,128]{1,0:T(8,128)(2,1)S(1)}, bf16[2048,128]{1,0:T(8,128)(2,1)}, u32[]{:S(2)}) copy-start(bf16[2048,128]{1,0:T(8,128)(2,1)} %get-tuple-element.162) | copy-start | bytes 1572868
  126.9 2.7 %copy-start.8 = (bf16[3328,128]{1,0:T(8,128)(2,1)S(1)}, bf16[3328,128]{1,0:T(8,128)(2,1)}, u32[]{:S(2)}) copy-start(bf16[3328,128]{1,0:T(8,128)(2,1)} %copy-done.7) | copy-start | bytes 2555908
  131.6 14.3 %collective-permute-start.9 = (bf16[2048,128]{1,0:T(8,128)(2,1)}, bf16[2048,128]{1,0:T(8,128)(2,1)}, u32[]{:S(2)}, u32[]{:S(2)}) collective-permute-start(bf16[2048,128]{1,0:T(8,128)(2,1)} %get-tuple-element.169), channel_id=1, source_target_pairs={{0,2},{1,3},{2,0},{3,1},{4,6},{5,7},{6,4},{7,5},{8,10},{9,11},{10,... | collective-permute-start | bytes 1572872 | tf_op jit(solution)/shard_map/ppermute | solution.py:826
  133.3 11.8 %collective-permute-start.10 = (bf16[1664,128]{1,0:T(8,128)(2,1)}, bf16[1664,128]{1,0:T(8,128)(2,1)S(1)}, u32[]{:S(2)}, u32[]{:S(2)}) collective-permute-start(bf16[1664,128]{1,0:T(8,128)(2,1)} %pad_maximum_fusion.4), channel_id=1, source_target_pairs={{0,4},{4,0},{8,12},{12,8},{16,20},{20,16},{24,28},{28,24},{1,5},{5... | collective-permute-start | bytes 1277960 | tf_op jit(solution)/shard_map/ppermute | solution.py:829
  142.4 5.4 %copy-start.10 = (bf16[2048,128]{1,0:T(8,128)(2,1)S(1)}, bf16[2048,128]{1,0:T(8,128)(2,1)}, u32[]{:S(2)}) copy-start(bf16[2048,128]{1,0:T(8,128)(2,1)} %get-tuple-element.172) | copy-start | bytes 1572868
  149.2 6.6 %collective-permute-start.11 = (bf16[832,128]{1,0:T(8,128)(2,1)S(1)}, bf16[832,128]{1,0:T(8,128)(2,1)S(1)}, u32[]{:S(2)}, u32[]{:S(2)}) collective-permute-start(bf16[832,128]{1,0:T(8,128)(2,1)S(1)} %pad_maximum_fusion.9), channel_id=1, source_target_pairs={{0,8},{4,12},{8,0},{12,4},{16,24},{20,28},{24,16},{28,20},{1,9},{5... | collective-permute-start | bytes 638984 | tf_op jit(solution)/shard_map/ppermute | solution.py:829
  151.1 7.4 %collective-permute-start.12 = (bf16[1048,128]{1,0:T(8,128)(2,1)S(1)}, bf16[1048,128]{1,0:T(8,128)(2,1)S(1)}, u32[]{:S(2)}, u32[]{:S(2)}) collective-permute-start(bf16[1048,128]{1,0:T(8,128)(2,1)S(1)} %pad_maximum_fusion.8), channel_id=1, source_target_pairs={{0,4},{4,0},{8,12},{12,8},{16,20},{20,16},{24,28},{28,24},{1,5},{5... | collective-permute-start | bytes 804872 | tf_op jit(solution)/shard_map/ppermute | solution.py:829
  155.8 2.7 %copy-start.19 = (f32[8,128]{1,0:T(8,128)S(1)}, f32[8,128]{1,0:T(8,128)}, u32[]{:S(2)}) copy-start(f32[8,128]{1,0:T(8,128)} %get-tuple-element.174) | copy-start | bytes 12292
  158.6 6.7 %collective-permute-start.13 = (bf16[416,128]{1,0:T(8,128)(2,1)S(1)}, bf16[416,128]{1,0:T(8,128)(2,1)S(1)}, u32[]{:S(2)}, u32[]{:S(2)}) collective-permute-start(bf16[416,128]{1,0:T(8,128)(2,1)S(1)} %pad_maximum_fusion.14), channel_id=1, source_target_pairs={{0,16},{4,20},{8,24},{12,28},{16,0},{20,4},{24,8},{28,12},{1,17},{... | collective-permute-start | bytes 319496 | tf_op jit(solution)/shard_map/ppermute | solution.py:829
  161.3 5.5 %collective-permute-start.14 = (bf16[536,128]{1,0:T(8,128)(2,1)S(1)}, bf16[536,128]{1,0:T(8,128)(2,1)S(1)}, u32[]{:S(2)}, u32[]{:S(2)}) collective-permute-start(bf16[536,128]{1,0:T(8,128)(2,1)S(1)} %pad_maximum_fusion.13), channel_id=1, source_target_pairs={{0,8},{4,12},{8,0},{12,4},{16,24},{20,28},{24,16},{28,20},{1,9},{5... | collective-permute-start | bytes 411656 | tf_op jit(solution)/shard_map/ppermute | solution.py:829
  166.9 6.1 %collective-permute-start.16 = (bf16[280,128]{1,0:T(8,128)(2,1)S(1)}, bf16[280,128]{1,0:T(8,128)(2,1)S(1)}, u32[]{:S(2)}, u32[]{:S(2)}) collective-permute-start(bf16[280,128]{1,0:T(8,128)(2,1)S(1)} %pad_maximum_fusion.15), channel_id=1, source_target_pairs={{0,16},{4,20},{8,24},{12,28},{16,0},{20,4},{24,8},{28,12},{1,17},{... | collective-permute-start | bytes 215048 | tf_op jit(solution)/shard_map/ppermute | solution.py:829
  168.6 5.7 %collective-permute-start.15 = (f16[352,128]{1,0:T(8,128)(2,1)S(1)}, f16[352,128]{1,0:T(8,128)(2,1)S(1)}, u32[]{:S(2)}, u32[]{:S(2)}) collective-permute-start(f16[352,128]{1,0:T(8,128)(2,1)S(1)} %concatenate.88), channel_id=1, source_target_pairs={{0,16},{4,20},{8,24},{12,28},{16,0},{20,4},{24,8},{28,12},{1,17},{... | collective-permute-start | bytes 270344 | tf_op jit(solution)/shard_map/ppermute | solution.py:829
  174.5 5.3 %collective-permute-start.18 = (f16[272,128]{1,0:T(8,128)(2,1)S(1)}, f16[272,128]{1,0:T(8,128)(2,1)S(1)}, u32[]{:S(2)}, u32[]{:S(2)}) collective-permute-start(f16[272,128]{1,0:T(8,128)(2,1)S(1)} %concatenate.91), channel_id=1, source_target_pairs={{0,16},{4,20},{8,24},{12,28},{16,0},{20,4},{24,8},{28,12},{1,17},{... | collective-permute-start | bytes 208904 | tf_op jit(solution)/shard_map/ppermute | solution.py:829
  175.7 8.1 %collective-permute-start.17 = (f16[704,128]{1,0:T(8,128)(2,1)S(1)}, f16[704,128]{1,0:T(8,128)(2,1)S(1)}, u32[]{:S(2)}, u32[]{:S(2)}) collective-permute-start(f16[704,128]{1,0:T(8,128)(2,1)S(1)} %pad_maximum_fusion.10), channel_id=1, source_target_pairs={{0,8},{4,12},{8,0},{12,4},{16,24},{20,28},{24,16},{28,20},{1,9},{5... | collective-permute-start | bytes 540680 | tf_op jit(solution)/shard_map/ppermute | solution.py:829
  184.0 5.1 %collective-permute-start.20 = (f16[544,128]{1,0:T(8,128)(2,1)S(1)}, f16[544,128]{1,0:T(8,128)(2,1)S(1)}, u32[]{:S(2)}, u32[]{:S(2)}) collective-permute-start(f16[544,128]{1,0:T(8,128)(2,1)S(1)} %pad_maximum_fusion.12), channel_id=1, source_target_pairs={{0,8},{4,12},{8,0},{12,4},{16,24},{20,28},{24,16},{28,20},{1,9},{5... | collective-permute-start | bytes 417800 | tf_op jit(solution)/shard_map/ppermute | solution.py:829
  185.6 7.4 %collective-permute-start.19 = (f16[1408,128]{1,0:T(8,128)(2,1)S(1)}, f16[1408,128]{1,0:T(8,128)(2,1)S(1)}, u32[]{:S(2)}, u32[]{:S(2)}) collective-permute-start(f16[1408,128]{1,0:T(8,128)(2,1)S(1)} %pad_maximum_fusion.6), channel_id=1, source_target_pairs={{0,4},{4,0},{8,12},{12,8},{16,20},{20,16},{24,28},{28,24},{1,5},{5... | collective-permute-start | bytes 1081352 | tf_op jit(solution)/shard_map/ppermute | solution.py:829
  189.3 10.3 %collective-permute-start.21 = (f16[1088,128]{1,0:T(8,128)(2,1)S(1)}, f16[1088,128]{1,0:T(8,128)(2,1)S(1)}, u32[]{:S(2)}, u32[]{:S(2)}) collective-permute-start(f16[1088,128]{1,0:T(8,128)(2,1)S(1)} %pad_maximum_fusion.7), channel_id=1, source_target_pairs={{0,4},{4,0},{8,12},{12,8},{16,20},{20,16},{24,28},{28,24},{1,5},{5... | collective-permute-start | bytes 835592 | tf_op jit(solution)/shard_map/ppermute | solution.py:829
  193.6 9.0 %collective-permute-start.23 = (f16[768,128]{1,0:T(8,128)(2,1)S(1)}, f16[768,128]{1,0:T(8,128)(2,1)S(1)}, u32[]{:S(2)}, u32[]{:S(2)}) collective-permute-start(f16[768,128]{1,0:T(8,128)(2,1)S(1)} %bitcast.171), channel_id=1, source_target_pairs={{0,2},{1,3},{2,0},{3,1},{4,6},{5,7},{6,4},{7,5},{8,10},{9,11},{10,... | collective-permute-start | bytes 589832 | tf_op jit(solution)/shard_map/ppermute | solution.py:826
  195.1 7.4 %collective-permute-start.24 = (f32[8,128]{1,0:T(8,128)S(1)}, f32[8,128]{1,0:T(8,128)S(1)}, u32[]{:S(2)}, u32[]{:S(2)}) collective-permute-start(f32[8,128]{1,0:T(8,128)S(1)} %fusion.26), channel_id=1, source_target_pairs={{0,2},{1,3},{2,0},{3,1},{4,6},{5,7},{6,4},{7,5},{8,10},{9,11},{10,... | collective-permute-start | bytes 12296 | tf_op jit(solution)/shard_map/ppermute | solution.py:826
  200.2 3.2 %copy-start.21 = (f32[1572]{0:T(1024)S(1)}, f32[1572]{0:T(1024)}, u32[]{:S(2)}) copy-start(f32[1572]{0:T(1024)} %param.61) | copy-start | bytes 18868
  200.2 3.2 %copy-start.22 = (f32[1572]{0:T(1024)S(1)}, f32[1572]{0:T(1024)}, u32[]{:S(2)}) copy-start(f32[1572]{0:T(1024)} %param.53) | copy-start | bytes 18868
  202.8 3.9 %collective-permute-start.25 = (f16[1536,128]{1,0:T(8,128)(2,1)S(1)}, f16[1536,128]{1,0:T(8,128)(2,1)S(1)}, u32[]{:S(2)}, u32[]{:S(2)}) collective-permute-start(f16[1536,128]{1,0:T(8,128)(2,1)S(1)} %pad_maximum_fusion.5), channel_id=1, source_target_pairs={{0,1},{1,0},{2,3},{3,2},{4,5},{5,4},{6,7},{7,6},{8,9},{9,8},{10,11... | collective-permute-start | bytes 1179656 | tf_op jit(solution)/shard_map/ppermute | solution.py:826
  202.9 3.2 %collective-permute-start.26 = (f32[8,128]{1,0:T(8,128)S(1)}, f32[8,128]{1,0:T(8,128)S(1)}, u32[]{:S(2)}, u32[]{:S(2)}) collective-permute-start(f32[8,128]{1,0:T(8,128)S(1)} %add.249), channel_id=1, source_target_pairs={{0,1},{1,0},{2,3},{3,2},{4,5},{5,4},{6,7},{7,6},{8,9},{9,8},{10,11... | collective-permute-start | bytes 12296 | tf_op jit(solution)/shard_map/ppermute | solution.py:826
  204.0 5.0 %collective-permute-start.22 = (f32[8,128]{1,0:T(8,128)S(1)}, f32[8,128]{1,0:T(8,128)S(1)}, u32[]{:S(2)}, u32[]{:S(2)}) collective-permute-start(f32[8,128]{1,0:T(8,128)S(1)} %broadcast_in_dim.2), channel_id=1, source_target_pairs={{0,3},{1,2},{2,1},{3,0},{4,7},{5,6},{6,5},{7,4},{8,11},{9,10},{10,... | collective-permute-start | bytes 12296 | tf_op jit(solution)/shard_map/ppermute | solution.py:826
  205.2 3.8 %collective-permute-start.27 = (f32[8,128]{1,0:T(8,128)S(1)}, f32[8,128]{1,0:T(8,128)S(1)}, u32[]{:S(2)}, u32[]{:S(2)}) collective-permute-start(f32[8,128]{1,0:T(8,128)S(1)} %broadcast_in_dim.2), channel_id=1, source_target_pairs={{0,1},{1,0},{2,3},{3,2},{4,5},{5,4},{6,7},{7,6},{8,9},{9,8},{10,11... | collective-permute-start | bytes 12296 | tf_op jit(solution)/shard_map/ppermute | solution.py:826
  205.7 3.6 %collective-permute-start.28 = (f32[8,128]{1,0:T(8,128)S(1)}, f32[8,128]{1,0:T(8,128)S(1)}, u32[]{:S(2)}, u32[]{:S(2)}) collective-permute-start(f32[8,128]{1,0:T(8,128)S(1)} %broadcast_in_dim.2), channel_id=1, source_target_pairs={{0,2},{1,3},{2,0},{3,1},{4,6},{5,7},{6,4},{7,5},{8,10},{9,11},{10,... | collective-permute-start | bytes 12296 | tf_op jit(solution)/shard_map/ppermute | solution.py:826
  209.9 11.5 %copy-start.1 = (bf16[5,8192]{1,0:T(8,128)(2,1)S(1)}, bf16[5,8192]{1,0:T(8,128)(2,1)}, u32[]{:S(2)}) copy-start(bf16[5,8192]{1,0:T(8,128)(2,1)} %param.32) | copy-start | bytes 245764
  (4 other events, 4.1 us)
